TPU v7x, 32 devices: a whole 2x2x4 slice. The times are simulated.
32 devices in a mesh: ens: 4 (over x, core), dom: 8 (over z, y).
Axes of the slice: x: 2, y: 2, z: 4, core: 2. Of those that a mesh axis runs over, the one named last changes fastest.
Arguments:
- nodes: bfloat16 [4, 4096, 512], P('ens', 'dom'), may hold values from -6 to 6
- senders: int32 [6, 4096], P(None, 'dom'), may hold values from 0 to 767
- send_next: int32 [1024], P('dom'), may hold values from 0 to 511
- send_prev: int32 [1024], P('dom'), may hold values from 0 to 511
- readout_vertex_list: int32 [3, 32768], P(None, 'dom'), may hold values from 0 to 767
- dec_weights: float32 [3, 32768], P(None, 'dom'), may hold values from 0.2 to 1
- base: bfloat16 [32768, 128], P('dom'), may hold values from -6 to 6
- observed_analysis: bfloat16 [32768, 128], P('dom'), may hold values from -8 to 8
- w_send: bfloat16 [512, 512], replicated, may hold values from -0.25 to 0.25
- w_recv: bfloat16 [512, 512], replicated, may hold values from -0.25 to 0.25
- vertex_refresh_matrix: bfloat16 [512, 512], replicated, may hold values from -0.25 to 0.25
- w_decode: bfloat16 [512, 128], replicated, may hold values from -0.25 to 0.25
Outputs:
- g_send: float32 [512, 512], replicated
- g_recv: float32 [512, 512], replicated
- g_update: float32 [512, 512], replicated
- g_decode: float32 [512, 128], replicated
- loss: float32 [], replicated
All inputs are finite; a program needn't handle non-finite values.
Results may differ from a plain program's by a relative error of at most 0.0045.
Values may be sent and summed in bfloat16 or wider, within the bound.
No kernel may reach another device: no remote copies, remote signals or barrier semaphores. Data moves between devices by JAX's collectives and lax.ppermute only.
A program may use at most 64 MiB of HBM per device.

v0:
```python
import jax
import jax.numpy as jnp
from jax import lax
from jax.sharding import PartitionSpec as P

smoothing_epsilon = 0.04


def passed_along(value, axis, steps):
    count = lax.axis_size(axis)
    pairs = [(source, (source + steps) % count) for source in range(count)]
    return lax.ppermute(value, axis, pairs)


def smooth_abs(diff):
    return jnp.sqrt(diff * diff + smoothing_epsilon)


def smooth_slope(diff):
    return diff / jnp.sqrt(diff * diff + smoothing_epsilon)


def silu_slope(value):
    sigma = jax.nn.sigmoid(value)
    return sigma * (1.0 + value * (1.0 - sigma))


def process(latent, extended, senders, w_send, w_recv, vertex_refresh_matrix):
    sent = jnp.dot(extended, w_send, preferred_element_type=jnp.float32)
    recv = jnp.dot(latent, w_recv, preferred_element_type=jnp.float32)
    pre = sent[senders] + recv[None]
    agg = (jnp.sum(jax.nn.silu(pre), axis=0) / senders.shape[0]).astype(jnp.bfloat16)
    upd = jnp.dot(agg, vertex_refresh_matrix, preferred_element_type=jnp.float32)
    hidden = (latent.astype(jnp.float32) + jax.nn.silu(upd)).astype(jnp.bfloat16)
    return (pre, agg, upd, hidden)


def backward(
    latent, extended, senders, pre, agg, upd, hidden, vertex_refresh_matrix, w_decode, grad_z
):
    g_decode = jnp.dot(hidden.T, grad_z, preferred_element_type=jnp.float32)
    grad_hidden = jnp.dot(grad_z, w_decode.T, preferred_element_type=jnp.float32)
    grad_upd = (grad_hidden * silu_slope(upd)).astype(jnp.bfloat16)
    g_update = jnp.dot(agg.T, grad_upd, preferred_element_type=jnp.float32)
    grad_agg = jnp.dot(grad_upd, vertex_refresh_matrix.T, preferred_element_type=jnp.float32)
    grad_pre = (grad_agg / senders.shape[0])[None] * silu_slope(pre)
    grad_recv = jnp.sum(grad_pre, axis=0).astype(jnp.bfloat16)
    g_recv = jnp.dot(latent.T, grad_recv, preferred_element_type=jnp.float32)
    grad_sent = (
        jnp.zeros(extended.shape, jnp.float32).at[senders].add(grad_pre).astype(jnp.bfloat16)
    )
    g_send = jnp.dot(extended.T, grad_sent, preferred_element_type=jnp.float32)
    return (g_send, g_recv, g_update, g_decode)


def member_parts(own, whole_ensemble_set, truth, line_span):
    count = whole_ensemble_set.shape[0]
    term = smooth_abs(own - truth) / count
    slope = smooth_slope(own - truth) / count
    for other in range(count):
        diff = own - whole_ensemble_set[other]
        term = term - smooth_abs(diff) / (2.0 * count * (count - 1))
        slope = slope - smooth_slope(diff) / (count * (count - 1.0))
    return (term, slope / line_span)


def extend(table, send_next, send_prev):
    from_prev = passed_along(table[send_next], "dom", 1)
    from_next = passed_along(table[send_prev], "dom", -1)
    return jnp.concatenate([table, from_prev, from_next], axis=0)


def per_device(
    nodes,
    senders,
    send_next,
    send_prev,
    readout_vertex_list,
    dec_weights,
    base,
    observed_analysis,
    w_send,
    w_recv,
    vertex_refresh_matrix,
    w_decode,
):
    latent = nodes[0]
    count = latent.shape[0]
    halo_rows = send_next.shape[0]
    line_span = base.shape[0]
    extended = extend(latent, send_next, send_prev)
    pre, agg, upd, hidden = process(
        latent, extended, senders, w_send, w_recv, vertex_refresh_matrix
    )
    field = jnp.dot(hidden, w_decode, preferred_element_type=jnp.float32).astype(jnp.bfloat16)
    field_ext = extend(field, send_next, send_prev)
    overall_aggregate = base.astype(jnp.float32)
    for k in range(readout_vertex_list.shape[0]):
        overall_aggregate = overall_aggregate + dec_weights[k][:, None] * field_ext[
            readout_vertex_list[k]
        ].astype(jnp.float32)
    outlook_grid_state = overall_aggregate.astype(jnp.bfloat16)
    whole_ensemble_set = lax.all_gather(outlook_grid_state[None], "ens", axis=0, tiled=True).astype(
        jnp.float32
    )
    term, grad_x = member_parts(
        outlook_grid_state.astype(jnp.float32),
        whole_ensemble_set,
        observed_analysis.astype(jnp.float32),
        line_span,
    )
    loss_local = jnp.sum(term) / line_span
    grad_ext = jnp.zeros((count + 2 * halo_rows, field.shape[1]), jnp.float32)
    for k in range(readout_vertex_list.shape[0]):
        grad_ext = grad_ext.at[readout_vertex_list[k]].add(dec_weights[k][:, None] * grad_x)
    got_a = passed_along(grad_ext[count : count + halo_rows], "dom", -1)
    got_b = passed_along(grad_ext[count + halo_rows :], "dom", 1)
    grad_z = grad_ext[:count].at[send_next].add(got_a).at[send_prev].add(got_b).astype(jnp.bfloat16)
    g_send, g_recv, g_update, g_decode = backward(
        latent, extended, senders, pre, agg, upd, hidden, vertex_refresh_matrix, w_decode, grad_z
    )
    summed = lax.psum((g_send, g_recv, g_update, g_decode, loss_local), ("ens", "dom"))
    return (summed[0], summed[1], summed[2], summed[3], summed[4])


def solution(mesh):
    return jax.shard_map(
        per_device,
        mesh=mesh,
        in_specs=(
            P("ens", "dom", None),
            P(None, "dom"),
            P("dom"),
            P("dom"),
            P(None, "dom"),
            P(None, "dom"),
            P("dom", None),
            P("dom", None),
            P(),
            P(),
            P(),
            P(),
        ),
        out_specs=(P(), P(), P(), P(), P()),
        check_vma=False,
    )
```

profile of v0, /device:TPU:0, one launch (start us, length us, event | category | flops | bytes accessed | tf_op | source)
XLA Modules:
  0.0 409.4 jit_solution(12629559679126089929)
XLA Ops:
  7.2 0.0 copy-start
  7.2 0.0 copy-start.1
  7.2 0.0 all-gather.3.cloned.1.call-start
  7.3 0.8 compare_select_fusion.4
  8.1 2.0 gather_fusion.1
  10.0 0.0 copy-start.24
  10.1 6.1 %collective-permute-start.1 = (bf16[128,512]{1,0:T(8,128)(2,1)S(1)}, bf16[128,512]{1,0:T(8,128)(2,1)S(1)}, u32[]{:S(2)}, u32[]{:S(2)}) collective-permute-start(bf16[128,512]{1,0:T(8,128)(2,1)S(1)} %gather_fusion.1), channel_id=1, source_target_pairs={{0,7},{1,0},{2,1},{3,2},{4,3},{5,4},{6,5},{7,6},{8,15},{9,8},{10,9... | collective-permute-start | bytes 393224 | tf_op jit(solution)/shard_map/ppermute | solution.py:12
  16.1 0.7 compare_select_fusion.5
  16.8 2.0 gather_fusion
  18.8 0.1 collective-permute-start
  18.9 0.1 compare_select_fusion.1
  19.0 0.0 copy-start.17
  19.1 1.4 fusion.25
  20.6 5.9 %collective-permute-done = bf16[128,512]{1,0:T(8,128)(2,1)S(1)} collective-permute-done((bf16[128,512]{1,0:T(8,128)(2,1)S(1)}, bf16[128,512]{1,0:T(8,128)(2,1)S(1)}, u32[]{:S(2)}, u32[]{:S(2)}) %collective-permute-start) | collective-permute-done | bytes 131104 | tf_op jit(solution)/shard_map/ppermute | solution.py:12
  26.5 0.6 fusion.15
  27.1 12.8 %gather_fusion.2 = f32[3072,512]{1,0:T(8,128)} fusion(f32[768,512]{1,0:T(8,128)S(1)} %fusion.15, s32[3072]{0:T(1024)S(1)} %broadcast_clamp_fusion.3), kind=kCustom, calls=%fused_computation.2 | custom fusion | bytes 12595200 | tf_op jit(solution)/shard_map/gather | solution.py:31
  39.8 5.0 %multiply_reduce_fusion = f32[512,512]{1,0:T(8,128)S(1)} fusion(f32[6,512,512]{2,1,0:T(8,128)} %bitcast.33, f32[512,512]{1,0:T(8,128)} %fusion.25), kind=kLoop, calls=%fused_computation.15 | loop fusion | flops 9175040 | bytes 8388608 | tf_op jit(solution)/shard_map/reduce_sum | solution.py:32
  44.9 1.5 add_convert_fusion.1
  46.3 0.8 copy-done.6
  47.1 0.3 convolution_convert_fusion
  47.4 0.7 gather_fusion.4
  48.1 0.7 gather_fusion.3
  48.9 0.1 collective-permute-start.2
  48.9 4.7 %collective-permute-start.3 = (bf16[128,128]{1,0:T(8,128)(2,1)S(1)}, bf16[128,128]{1,0:T(8,128)(2,1)S(1)}, u32[]{:S(2)}, u32[]{:S(2)}) collective-permute-start(bf16[128,128]{1,0:T(8,128)(2,1)S(1)} %gather_fusion.4), channel_id=1, source_target_pairs={{0,7},{1,0},{2,1},{3,2},{4,3},{5,4},{6,5},{7,6},{8,15},{9,8},{10,9... | collective-permute-start | bytes 98312 | tf_op jit(solution)/shard_map/ppermute | solution.py:12
  53.6 1.9 collective-permute-done.2
  55.5 12.1 %gather_fusion.7 = bf16[4096,128]{1,0:T(8,128)(2,1)S(1)} fusion(bf16[768,128]{1,0:T(8,128)(2,1)S(1)} %pad_maximum_fusion.3, s32[4096]{0:T(1024)S(1)} %broadcast_clamp_fusion), kind=kCustom, calls=%fused_computation.7 | custom fusion | bytes 2113536 | tf_op jit(solution)/shard_map/gather | solution.py:99
  67.7 12.1 %gather_fusion.6 = bf16[4096,128]{1,0:T(8,128)(2,1)S(1)} fusion(bf16[768,128]{1,0:T(8,128)(2,1)S(1)} %pad_maximum_fusion.3, s32[4096]{0:T(1024)S(1)} %broadcast_clamp_fusion.1), kind=kCustom, calls=%fused_computation.6 | custom fusion | bytes 2113536 | tf_op jit(solution)/shard_map/gather | solution.py:99
  79.8 15.0 %gather_fusion.5 = bf16[4096,128]{1,0:T(8,128)(2,1)} fusion(bf16[768,128]{1,0:T(8,128)(2,1)S(1)} %pad_maximum_fusion.3, s32[4096]{0:T(1024)S(1)} %broadcast_clamp_fusion.2), kind=kCustom, calls=%fused_computation.5 | custom fusion | bytes 2113536 | tf_op jit(solution)/shard_map/gather | solution.py:99
  94.8 4.5 %add_convert_fusion = bf16[4096,128]{1,0:T(8,128)(2,1)} fusion(bf16[4096,128]{1,0:T(8,128)(2,1)S(1)} %gather_fusion.7, bf16[4096,128]{1,0:T(8,128)(2,1)S(1)} %gather_fusion.6, bf16[4096,128]{1,0:T(8,128)(2,1)} %gather_fusion.5, bf16[4096,128]{1,0:T(8,128)(2,1)} %param.18, f32[4096]{0:T(1024)S(1)} %bitcast.46, f32[4096]{0:T(1024)S(1)} %bitcast.42, ...), kind=kLoop, calls=%fused_computation.35 | loop fusion | flops 5767168 | bytes 5292032 | tf_op jit(solution)/shard_map/convert_element_type | solution.py:102
  99.3 0.0 all-gather.3.cloned.1.call-update
  99.3 0.0 all-reduce.3.cloned.1.call-start
  99.4 0.6 broadcast_multiply_fusion.2
  100.0 0.6 broadcast_multiply_fusion.1
  100.6 34.8 %all-gather.3.cloned.1.call-done = bf16[16384,128]{1,0:T(8,128)(2,1)} async-done(((bf16[4096,128]{1,0:T(8,128)(2,1)}), bf16[16384,128]{1,0:T(8,128)(2,1)}) %all-gather.3.cloned.1.call-update) | async-done | bytes 4194320 | tf_op jit(solution)/shard_map/all_gather | solution.py:103
  135.4 2.7 convert_element_type.64
  138.0 0.1 copy-done.8
  138.2 6.1 %subtract_reduce_fusion = (f32[]{:T(128)}, f32[4096,128]{1,0:T(8,128)S(1)}) fusion(bf16[4096,128]{1,0:T(8,128)(2,1)S(1)} %copy-done.8, bf16[4096,128]{1,0:T(8,128)(2,1)S(1)} %copy-done.2, f32[16384,128]{1,0:T(8,128)S(1)} %convert_element_type.64), kind=kLoop, calls=%fused_computation.22 | loop fusion | flops 21495808 | bytes 12582916 | tf_op jit(solution)/shard_map/reduce_sum | solution.py:112
  144.3 24.4 %scatter_custom_fusion = f32[768,128]{1,0:T(8,128)S(1)} fusion(s32[4096]{0:T(1024)} %bitcast.53, f32[4096,128]{1,0:T(8,128)S(1)} %get-tuple-element.22, f32[4096]{0:T(1024)} %broadcast_multiply_fusion.2, f32[]{:T(128)} %constant.18.clone.1), kind=kCustom, calls=%fused_computation.27 | custom fusion | flops 1048576 | bytes 2507264 | tf_op jit(solution)/shard_map/scatter-add | solution.py:115
  168.7 22.6 %scatter_custom_fusion.1 = f32[768,128]{1,0:T(8,128)S(1)} fusion(f32[768,128]{1,0:T(8,128)S(1)} %scatter_custom_fusion, s32[4096]{0:T(1024)} %bitcast.51, f32[4096,128]{1,0:T(8,128)S(1)} %get-tuple-element.22, f32[4096]{0:T(1024)} %broadcast_multiply_fusion.1), kind=kCustom, calls=%fused_computation.25 | custom fusion | flops 1048576 | bytes 2506752 | tf_op jit(solution)/shard_map/scatter-add | solution.py:115
  191.3 24.7 %scatter_custom_fusion.2 = f32[768,128]{1,0:T(8,128)S(1)} fusion(f32[768,128]{1,0:T(8,128)S(1)} %scatter_custom_fusion.1, s32[4096]{0:T(1024)} %bitcast.49, f32[4096,128]{1,0:T(8,128)S(1)} %get-tuple-element.22, f32[4096]{0:T(1024)S(1)} %broadcast_multiply_fusion), kind=kCustom, calls=%fused_computation.23 | custom fusion | flops 1048576 | bytes 2506752 | tf_op jit(solution)/shard_map/scatter-add | solution.py:115
  216.0 4.3 %collective-permute-start.4 = (f32[128,128]{1,0:T(8,128)S(1)}, f32[128,128]{1,0:T(8,128)S(1)}, u32[]{:S(2)}, u32[]{:S(2)}) collective-permute-start(f32[128,128]{1,0:T(8,128)S(1)} %get-tuple-element.24), channel_id=1, source_target_pairs={{0,7},{1,0},{2,1},{3,2},{4,3},{5,4},{6,5},{7,6},{8,15},{9,8},{10,9... | collective-permute-start | bytes 196616 | tf_op jit(solution)/shard_map/ppermute | solution.py:12
  220.3 0.0 copy-start.29
  220.3 1.9 collective-permute-done.4
  222.2 1.5 scatter_fusion
  223.7 3.6 collective-permute-done.5
  227.3 1.5 scatter_fusion.1
  228.8 1.0 fusion.19
  229.8 0.5 fusion.6
  230.3 0.0 copy-start.3
  230.3 1.4 fusion.16
  231.8 0.5 convolution_multiply_fusion
  232.3 0.3 slice-done.1
  232.6 0.2 copy-done.3
  232.8 4.2 %fusion.29 = (bf16[512,512]{1,0:T(8,128)(2,1)S(1)}, f32[6,512,512]{2,1,0:T(8,128)}) fusion(f32[6,512,512]{2,1,0:T(8,128)S(1)} %bitcast.36, f32[512,512]{1,0:T(8,128)S(1)} %copy-done.3, f32[512,512]{1,0:T(8,128)S(1)} %convolution_multiply_fusion), kind=kLoop, calls=%fused_computation.83 | loop fusion | flops 15466496 | bytes 15204352 | tf_op jit(solution)/shard_map/reduce_sum | solution.py:47
  237.1 19.6 %scatter_custom_fusion.5 = f32[768,512]{1,0:T(8,128)S(1)} fusion(s32[3072]{0:T(1024)} %copy-done.18, f32[3072,512]{1,0:T(8,128)} %bitcast.41, f32[]{:T(128)} %constant.18.clone.1), kind=kCustom, calls=%fused_computation.50 | custom fusion | flops 1572864 | bytes 1573376 | tf_op jit(solution)/shard_map/scatter-add | solution.py:50
  256.7 1.4 convolution_bitcast_fusion
  258.1 1.6 fusion.10
  259.7 0.0 all-reduce.3.cloned.1.call-update
  260.4 37.4 %psum.39 = f32[]{:T(128)} all-reduce(f32[]{:T(128)S(6)} %div.85), channel_id=1, replica_groups=mesh['ens'=4,'dom'=8] {'ens','dom'}, use_global_device_ids=true, to_apply=%region_13.14 | all-reduce | flops 1 | bytes 8 | tf_op jit(solution)/shard_map/psum | solution.py:122
  297.7 99.5 %all-reduce.3.cloned.1.call-done = (f32[512,512]{1,0:T(8,128)}, f32[512,512]{0,1:T(8,128)}, f32[512,512]{1,0:T(8,128)}, f32[512,128]{1,0:T(8,128)}) async-done(((f32[512,512]{1,0:T(8,128)}, f32[512,512]{0,1:T(8,128)}, f32[512,512]{1,0:T(8,128)}, f32[512,128]{1,0:T(8,128)}), (f32[512,512]{1,0:T(8,128)}, f32[512,512]{0,1:T(8,128)}, f32[512,512]{1,0:T(8,128)}, ...) | async-done | bytes 3407888 | tf_op jit(solution)/shard_map/psum | solution.py:122
  397.2 2.7 copy.18
  399.9 1.0 copy.27
  400.9 1.0 copy.28
  401.9 0.7 copy.29
  (71 shorter events, 0.2 us)
Async XLA Ops:
  7.2 37.7 %copy-start = (bf16[512,512]{1,0:T(8,128)(2,1)S(1)}, bf16[512,512]{1,0:T(8,128)(2,1)}, u32[]{:S(2)}) copy-start(bf16[512,512]{1,0:T(8,128)(2,1)} %param.22) | copy-start | bytes 1572868
  7.2 11.9 %copy-start.1 = (bf16[1,512,512]{2,1,0:T(8,128)(2,1)S(1)}, bf16[1,512,512]{2,1,0:T(8,128)(2,1)}, u32[]{:S(2)}) copy-start(bf16[1,512,512]{2,1,0:T(8,128)(2,1)} %param.12) | copy-start | bytes 1572868
  7.2 11.7 %copy-start.21 = (s32[6,512]{1,0:T(8,128)S(1)}, s32[6,512]{1,0:T(8,128)}, u32[]{:S(2)}) copy-start(s32[6,512]{1,0:T(8,128)} %param.13) | copy-start | bytes 36868
  7.2 11.7 %copy-start.19 = (s32[3,4096]{1,0:T(4,128)S(1)}, s32[3,4096]{1,0:T(4,128)}, u32[]{:S(2)}) copy-start(s32[3,4096]{1,0:T(4,128)} %param.16) | copy-start | bytes 147460
  7.2 11.8 %copy-start.20 = (f32[3,4096]{1,0:T(4,128)S(1)}, f32[3,4096]{1,0:T(4,128)}, u32[]{:S(2)}) copy-start(f32[3,4096]{1,0:T(4,128)} %param.17) | copy-start | bytes 147460
  7.2 11.9 %copy-start.11 = (bf16[512,512]{1,0:T(8,128)(2,1)S(1)}, bf16[512,512]{1,0:T(8,128)(2,1)}, u32[]{:S(2)}) copy-start(bf16[512,512]{1,0:T(8,128)(2,1)} %param.21) | copy-start | bytes 1572868
  7.2 128.1 %all-gather.3.cloned.1.call-start = ((), (), s32[]{:S(2)}) async-start(), calls=%async_computation | async-start | bytes 5242880 | tf_op jit(solution)/shard_map/all_gather | solution.py:103
  8.0 10.8 %copy-start.22 = (s32[128]{0:T(128)}, s32[128]{0:T(128)S(1)}, u32[]{:S(2)}) copy-start(s32[128]{0:T(128)S(1)} %compare_select_fusion.4) | copy-start | bytes 1540
  10.0 16.4 %copy-start.24 = (bf16[512,512]{1,0:T(8,128)(2,1)S(1)}, bf16[512,512]{1,0:T(8,128)(2,1)}, u32[]{:S(2)}) copy-start(bf16[512,512]{1,0:T(8,128)(2,1)} %param.20) | copy-start | bytes 1572868
  10.1 10.5 %collective-permute-start.1 = (bf16[128,512]{1,0:T(8,128)(2,1)S(1)}, bf16[128,512]{1,0:T(8,128)(2,1)S(1)}, u32[]{:S(2)}, u32[]{:S(2)}) collective-permute-start(bf16[128,512]{1,0:T(8,128)(2,1)S(1)} %gather_fusion.1), channel_id=1, source_target_pairs={{0,7},{1,0},{2,1},{3,2},{4,3},{5,4},{6,5},{7,6},{8,15},{9,8},{10,9... | collective-permute-start | bytes 393224 | tf_op jit(solution)/shard_map/ppermute | solution.py:12
  16.8 2.1 copy-start.23
  18.8 7.7 %collective-permute-start = (bf16[128,512]{1,0:T(8,128)(2,1)S(1)}, bf16[128,512]{1,0:T(8,128)(2,1)S(1)}, u32[]{:S(2)}, u32[]{:S(2)}) collective-permute-start(bf16[128,512]{1,0:T(8,128)(2,1)S(1)} %gather_fusion), channel_id=1, source_target_pairs={{0,1},{1,2},{2,3},{3,4},{4,5},{5,6},{6,7},{7,0},{8,9},{9,10},{10,1... | collective-permute-start | bytes 393224 | tf_op jit(solution)/shard_map/ppermute | solution.py:12
  18.9 1.6 copy-start.18
  19.0 1.6 copy-start.16
  19.0 1.6 copy-start.17
  19.0 34.6 %copy-start.15 = (s32[4096,1]{0,1:T(1,128)}, s32[4096,1]{0,1:T(1,128)S(1)}, u32[]{:S(2)}) copy-start(s32[4096,1]{0,1:T(1,128)S(1)} %get-tuple-element.30) | copy-start | bytes 49156
  20.6 19.3 %copy-start.25 = (bf16[128,512]{1,0:T(8,128)(2,1)}, bf16[128,512]{1,0:T(8,128)(2,1)S(1)}, u32[]{:S(2)}) copy-start(bf16[128,512]{1,0:T(8,128)(2,1)S(1)} %collective-permute-done.1) | copy-start | bytes 393220
  26.5 13.4 %copy-start.27 = (bf16[128,512]{1,0:T(8,128)(2,1)}, bf16[128,512]{1,0:T(8,128)(2,1)S(1)}, u32[]{:S(2)}) copy-start(bf16[128,512]{1,0:T(8,128)(2,1)S(1)} %collective-permute-done) | copy-start | bytes 393220
  44.8 1.5 copy-start.4
  44.8 2.3 copy-start.13
  46.3 0.8 copy-start.6
  48.9 6.7 %collective-permute-start.2 = (bf16[128,128]{1,0:T(8,128)(2,1)S(1)}, bf16[128,128]{1,0:T(8,128)(2,1)S(1)}, u32[]{:S(2)}, u32[]{:S(2)}) collective-permute-start(bf16[128,128]{1,0:T(8,128)(2,1)S(1)} %gather_fusion.3), channel_id=1, source_target_pairs={{0,1},{1,2},{2,3},{3,4},{4,5},{5,6},{6,7},{7,0},{8,9},{9,10},{10,1... | collective-permute-start | bytes 98312 | tf_op jit(solution)/shard_map/ppermute | solution.py:12
  48.9 6.6 %collective-permute-start.3 = (bf16[128,128]{1,0:T(8,128)(2,1)S(1)}, bf16[128,128]{1,0:T(8,128)(2,1)S(1)}, u32[]{:S(2)}, u32[]{:S(2)}) collective-permute-start(bf16[128,128]{1,0:T(8,128)(2,1)S(1)} %gather_fusion.4), channel_id=1, source_target_pairs={{0,7},{1,0},{2,1},{3,2},{4,3},{5,4},{6,5},{7,6},{8,15},{9,8},{10,9... | collective-permute-start | bytes 98312 | tf_op jit(solution)/shard_map/ppermute | solution.py:12
  99.3 297.9 %all-reduce.3.cloned.1.call-start = ((), (), s32[]{:S(2)}) async-start(), calls=%async_computation.1 | async-start | bytes 6815744 | tf_op jit(solution)/shard_map/psum | solution.py:122
  135.4 2.7 copy-start.2
  135.4 2.8 copy-start.8
  216.0 12.8 %copy-start.7 = (bf16[512,512]{1,0:T(8,128)(2,1)S(1)}, bf16[512,512]{1,0:T(8,128)(2,1)}, u32[]{:S(2)}) copy-start(bf16[512,512]{1,0:T(8,128)(2,1)} %copy-done.6) | copy-start | bytes 1572868
  216.0 13.8 %copy-start.14 = (bf16[512,128]{1,0:T(8,128)(2,1)S(1)}, bf16[512,128]{1,0:T(8,128)(2,1)}, u32[]{:S(2)}) copy-start(bf16[512,128]{1,0:T(8,128)(2,1)} %param.23) | copy-start | bytes 393220
  216.0 6.2 %collective-permute-start.4 = (f32[128,128]{1,0:T(8,128)S(1)}, f32[128,128]{1,0:T(8,128)S(1)}, u32[]{:S(2)}, u32[]{:S(2)}) collective-permute-start(f32[128,128]{1,0:T(8,128)S(1)} %get-tuple-element.24), channel_id=1, source_target_pairs={{0,7},{1,0},{2,1},{3,2},{4,3},{5,4},{6,5},{7,6},{8,15},{9,8},{10,9... | collective-permute-start | bytes 196616 | tf_op jit(solution)/shard_map/ppermute | solution.py:12
  220.3 7.0 %collective-permute-start.5 = (f32[128,128]{1,0:T(8,128)S(1)}, f32[128,128]{1,0:T(8,128)S(1)}, u32[]{:S(2)}, u32[]{:S(2)}) collective-permute-start(f32[128,128]{1,0:T(8,128)S(1)} %get-tuple-element.23), channel_id=1, source_target_pairs={{0,1},{1,2},{2,3},{3,4},{4,5},{5,6},{6,7},{7,0},{8,9},{9,10},{10,1... | collective-permute-start | bytes 196616 | tf_op jit(solution)/shard_map/ppermute | solution.py:12
  220.3 9.5 %copy-start.29 = (f32[512,512]{1,0:T(8,128)S(1)}, f32[512,512]{1,0:T(8,128)}, u32[]{:S(2)}) copy-start(f32[512,512]{1,0:T(8,128)} %get-tuple-element.32) | copy-start | bytes 3145732
  228.8 1.6 copy-start.5
  228.8 3.5 slice-start
  229.8 2.8 slice-start.1
  230.3 2.5 copy-start.3
  237.1 21.1 %copy-start.26 = (bf16[128,512]{1,0:T(8,128)(2,1)S(1)}, bf16[128,512]{1,0:T(8,128)(2,1)}, u32[]{:S(2)}) copy-start(bf16[128,512]{1,0:T(8,128)(2,1)} %copy-done.25) | copy-start | bytes 393220
  237.1 21.1 %copy-start.28 = (bf16[128,512]{1,0:T(8,128)(2,1)S(1)}, bf16[128,512]{1,0:T(8,128)(2,1)}, u32[]{:S(2)}) copy-start(bf16[128,512]{1,0:T(8,128)(2,1)} %copy-done.27) | copy-start | bytes 393220
  397.2 2.7 copy-start.10
  397.2 3.7 copy-start.9
  399.9 1.9 copy-start.12
Sparse Core Ops, SparseCore 0:
  99.4 35.8 all-gather.2
  259.8 137.3 all-reduce.2
where the time goes:
time: 410 us; the launch traced here: 409 us
  waiting for transfers between devices  148 us (36%)
  other arithmetic  119 us (29%)
  local copies, waits for them, and re-layouts  64.5 us (16%)
  blocking collectives  37.4 us (9%)
  starting transfers between devices  15.3 us (4%)
  between operations  15.2 us (4%)
  matrix products  10.2 us (2%)
    psum x1, waiting for transfers between devices, per_device(): lax.psum((g_send, g_recv, g_update, g_decode, loss_local), ('ens', 'dom'))  99.5 us
    scatter-add x3, other arithmetic, per_device(): grad_ext.at[readout_vertex_list[k]].add(dec_weights[k][:, None] * grad_x)  71.6 us
    gather x3, local copies, waits for them, and re-layouts, per_device(): field_ext[readout_vertex_list[k]].astype(jnp.float32)  39.3 us
    psum x1, blocking collectives, per_device(): lax.psum((g_send, g_recv, g_update, g_decode, loss_local), ('ens', 'dom'))  37.4 us
    all_gather x1, waiting for transfers between devices, per_device(): lax.all_gather(outlook_grid_state[None], 'ens', axis=0, tiled=True)  34.8 us
    scatter-add x1, other arithmetic, backward(): jnp.zeros(extended.shape, jnp.float32).at[senders].add(grad_pre)  19.6 us
    ppermute x6, starting transfers between devices, passed_along(): return lax.ppermute(value, axis, pairs)  15.2 us
    ppermute x6, waiting for transfers between devices, passed_along(): return lax.ppermute(value, axis, pairs)  13.3 us
  transfers between devices with their start and end apart: 8, of which 6 were waited for; matrix products, arithmetic and copies ran while one was open for 2% of the time, Pallas kernels for 0%

commit v1 on v0

v1 whole, which is shorter than its diff:
```python
import functools

import jax
import jax.numpy as jnp
from jax import lax
from jax.experimental import pallas as pl
from jax.experimental.pallas import tpu as pltpu
from jax.sharding import PartitionSpec as P

EPS = 0.04
F32 = jnp.float32
BF16 = jnp.bfloat16
VMEM_BYTES = 56 * 1024 * 1024


def dot(a, b, ca=1, cb=0):
    return lax.dot_general(a, b, (((ca,), (cb,)), ((), ())), preferred_element_type=F32)


def dot_nt(a, b):
    return dot(a, b, 1, 1)


def one_hot(rows, index_row):
    shape = (rows, index_row.shape[1])
    hit = lax.broadcasted_iota(jnp.int32, shape, 0) == index_row
    return jnp.where(hit, 1.0, 0.0).astype(BF16)


def params(**kw):
    return pltpu.CompilerParams(vmem_limit_bytes=VMEM_BYTES, **kw)


def vmem(n):
    return [pl.BlockSpec(memory_space=pltpu.VMEM)] * n


def cost(flops, size):
    return pl.CostEstimate(flops=int(flops), bytes_accessed=int(size), transcendentals=0)


def sds(shape, dtype):
    return jax.ShapeDtypeStruct(shape, dtype)


def lend_kernel(nodes, to_next, to_prev, nodes_t, next_t, prev_t):
    table = nodes[...].T
    nodes_t[...] = table
    count = table.shape[1]
    next_t[...] = dot(table, one_hot(count, to_next[...])).astype(BF16)
    prev_t[...] = dot(table, one_hot(count, to_prev[...])).astype(BF16)


def prepare_kernel(
    w_send, w_recv, vertex, w_decode, nodes_t, vertices, weights, base, truth,
    w_send_t, vertex_t, w_decode_t, recv_t, mat_hi, mat_lo, base_t, truth_t,
):
    @pl.when(pl.program_id(0) == 0)
    def _():
        w_send_t[...] = w_send[...].T
        vertex_t[...] = vertex[...].T
        w_decode_t[...] = w_decode[...].T
        recv_t[...] = dot(w_recv[...].T, nodes_t[...])

    shape = mat_hi.shape
    row = lax.broadcasted_iota(jnp.int32, shape, 0)
    mat = jnp.zeros(shape, F32)
    for k in range(vertices.shape[0]):
        mat += jnp.where(row == vertices[k : k + 1, :], weights[k : k + 1, :], 0.0)
    hi = mat.astype(BF16)
    mat_hi[...] = hi
    mat_lo[...] = (mat - hi.astype(F32)).astype(BF16)
    base_t[...] = base[...].T
    truth_t[...] = truth[...].T


def forward_kernel(
    nodes_t, from_prev, from_next, senders, w_send_t, recv_t, vertex_t, w_decode_t, to_next, to_prev,
    picked_t, slope_t, slope_sum_t, agg_t, upd_slope_t, hidden_t, field_t, next_t, prev_t,
):
    degree, count = senders.shape
    halo = from_prev.shape[1]
    ext = jnp.concatenate([nodes_t[...], from_prev[...], from_next[...]], axis=1)
    total = jnp.zeros(recv_t.shape, F32)
    slopes = jnp.zeros(recv_t.shape, F32)
    for k in range(degree):
        picked = dot(ext, one_hot(count + 2 * halo, senders[k : k + 1, :])).astype(BF16)
        picked_t[k] = picked
        pre = dot(w_send_t[...], picked) + recv_t[...]
        sigma = 0.5 * jnp.tanh(0.5 * pre) + 0.5
        value = pre * sigma
        total += value
        slope = sigma * (1.0 + (pre - value)) * (1.0 / degree)
        slopes += slope
        slope_t[k] = slope.astype(slope_t.dtype)
    slope_sum_t[...] = slopes
    agg = (total * (1.0 / degree)).astype(BF16)
    agg_t[...] = agg
    upd = dot(vertex_t[...], agg)
    sigma = 0.5 * jnp.tanh(0.5 * upd) + 0.5
    value = upd * sigma
    upd_slope_t[...] = sigma * (1.0 + (upd - value))
    hidden = (nodes_t[...].astype(F32) + value).astype(BF16)
    hidden_t[...] = hidden
    field = dot(w_decode_t[...], hidden).astype(BF16)
    field_t[...] = field
    next_t[...] = dot(field, one_hot(count, to_next[...])).astype(BF16)
    prev_t[...] = dot(field, one_hot(count, to_prev[...])).astype(BF16)


def readout_kernel(line_span, own_index, fields, mat_hi, mat_lo, base_t, truth_t, grad_t, loss, states):
    step = pl.program_id(0)
    members = states.shape[0]
    variables = base_t.shape[0]

    @pl.when(step == 0)
    def _():
        grad_t[...] = jnp.zeros_like(grad_t)
        loss[...] = jnp.zeros_like(loss)

    ready = base_t[...].astype(F32)
    for m in range(members):
        table = fields[m * variables : (m + 1) * variables, :]
        x = ready + (dot(table, mat_hi[...]) + dot(table, mat_lo[...]))
        states[m] = x.astype(BF16).astype(F32)
    own = states[own_index[0]]
    diff = own - truth_t[...].astype(F32)
    square = diff * diff + EPS
    inverse = lax.rsqrt(square)
    term = square * inverse * (1.0 / members)
    slope = diff * inverse * (1.0 / members)
    spread = jnp.zeros_like(term)
    push = jnp.zeros_like(term)
    for m in range(members):
        diff = own - states[m]
        square = diff * diff + EPS
        inverse = lax.rsqrt(square)
        spread += square * inverse
        push += diff * inverse
    term = term - spread * (1.0 / (2.0 * members * (members - 1)))
    slope = (slope - push * (1.0 / (members * (members - 1.0)))) * (1.0 / line_span)
    grad_t[...] += dot_nt(slope.astype(BF16), mat_hi[...])
    loss[...] += jnp.sum(term.reshape(-1, 8, term.shape[1]), axis=0)


def split(value):
    hi = value.astype(BF16)
    return hi, (value - hi.astype(F32)).astype(BF16)


def backward_kernel(
    half, grad_ext_t, from_next, from_prev, to_next, to_prev, w_decode, vertex, nodes_t, picked_t,
    slope_t, slope_sum_t, agg_t, upd_slope_t, hidden_t,
    keep, send, whole,
):
    count = nodes_t.shape[1]
    width = nodes_t.shape[0]
    grad_z = grad_ext_t[:, :count]
    for got, rows in ((from_next, to_next), (from_prev, to_prev)):
        place = one_hot(count, rows[...])
        hi, lo = split(got[...])
        grad_z += dot_nt(hi, place) + dot_nt(lo, place)
    grad_z = grad_z.astype(BF16)
    whole[:, 3 * width :] = dot_nt(hidden_t[...], grad_z)
    grad_upd = (dot(w_decode[...], grad_z) * upd_slope_t[...]).astype(BF16)
    whole[:, 2 * width : 3 * width] = dot_nt(agg_t[...], grad_upd)
    grad_agg = dot(vertex[...], grad_upd)
    grad_recv = (grad_agg * slope_sum_t[...]).astype(BF16)
    whole[:, width : 2 * width] = dot_nt(nodes_t[...], grad_recv)
    total = jnp.zeros((width, width), F32)
    for k in range(picked_t.shape[0]):
        grad_pre = (grad_agg * slope_t[k].astype(F32)).astype(BF16)
        total += dot_nt(picked_t[k], grad_pre)
    whole[:, :width] = total
    rows = keep.shape[0]
    keep[...] = whole[pl.ds(pl.multiple_of(half[0] * rows, rows), rows), :]
    send[...] = whole[pl.ds(pl.multiple_of((1 - half[0]) * rows, rows), rows), :].astype(BF16)


def halve_kernel(half, mine, got, keep, send, total):
    total[...] = mine[...] + got[...].astype(F32)
    rows = keep.shape[0]
    keep[...] = total[pl.ds(pl.multiple_of(half[0] * rows, rows), rows), :]
    send[...] = total[pl.ds(pl.multiple_of((1 - half[0]) * rows, rows), rows), :].astype(BF16)


def shares_kernel(here, mine, got, *outs):
    total = outs[-1]
    total[...] = mine[...] + got[...].astype(F32)
    parts = len(outs) - 1
    rows = outs[0].shape[0]
    for k in range(parts):
        place = lax.rem(here[0] + k, parts)
        block = total[pl.ds(pl.multiple_of(place * rows, rows), rows), :]
        outs[k][...] = block.astype(outs[k].dtype)


def sum_kernel(*refs):
    total = refs[0][...]
    for ref in refs[1:-1]:
        total += ref[...].astype(F32)
    refs[-1][...] = total.astype(BF16)


def line_up_kernel(here, *refs):
    out = refs[-1]
    parts = len(refs) - 1
    rows = refs[0].shape[0]
    for k in range(parts):
        place = lax.rem(here[0] + (parts - k), parts)
        out[pl.ds(pl.multiple_of(place * rows, rows), rows), :] = refs[k][...]


def finish_kernel(order, p0, p1, p2, p3, g_send, g_recv, g_update, g_decode):
    rows, width = p0.shape[0], g_send.shape[1]
    for k, piece in enumerate((p0, p1, p2, p3)):
        place = pl.ds(pl.multiple_of(order[k] * rows, rows), rows)
        g_send[place, :] = piece[:, :width].astype(F32)
        g_recv[place, :] = piece[:, width : 2 * width].astype(F32)
        g_update[place, :] = piece[:, 2 * width : 3 * width].astype(F32)
        g_decode[place, :] = piece[:, 3 * width :].astype(F32)


SCALAR = pl.BlockSpec(memory_space=pltpu.SMEM)


def along(value, axis, steps):
    size = lax.axis_size(axis)
    return lax.ppermute(value, axis, [(i, (i + steps) % size) for i in range(size)])


def flip(value, axis, bit):
    size = lax.axis_size(axis)
    return lax.ppermute(value, axis, [(i, i ^ bit) for i in range(size)])


def call(kernel, ins, outs, scratch=(), flops=0, scalars=0):
    size = sum(x.size * x.dtype.itemsize for x in list(ins) + list(outs))
    many = isinstance(outs, (list, tuple))
    return pl.pallas_call(
        kernel,
        out_shape=outs,
        in_specs=[SCALAR] * scalars + vmem(len(ins) - scalars),
        out_specs=vmem(len(outs)),
        scratch_shapes=list(scratch),
        compiler_params=params(),
        cost_estimate=cost(flops, size),
    )(*ins)


def scalar(value):
    return jnp.reshape(value, (1,)).astype(jnp.int32)


def spread(quarter):
    across = flip(quarter, "ens", 2)
    beside = flip(quarter, "ens", 1)
    corner = flip(across, "ens", 1)
    return quarter, across, beside, corner


def reduced(keep, send, ens, dom):
    parts = lax.axis_size("dom")
    rows, cols = keep.shape
    got = flip(send, "ens", 1)
    keep, send = call(
        halve_kernel,
        [scalar(ens // 2), keep, got],
        [sds((rows // 2, cols), F32), sds((rows // 2, cols), BF16)],
        [pltpu.VMEM((rows, cols), F32)],
        scalars=1,
    )
    rows //= 2
    got = flip(send, "ens", 2)
    share = rows // parts
    if share % 16:
        quarter = lax.psum(keep + got.astype(F32), "dom").astype(BF16)
        return spread(quarter)
    shares = call(
        shares_kernel,
        [scalar(dom), keep, got],
        [sds((share, cols), F32)] + [sds((share, cols), BF16)] * (parts - 1),
        [pltpu.VMEM((rows, cols), F32)],
        scalars=1,
    )
    terms = [shares[0]] + [along(shares[k], "dom", k) for k in range(1, parts)]
    (own,) = call(sum_kernel, terms, [sds((share, cols), BF16)])
    pieces = [own] + [along(own, "dom", k) for k in range(1, parts)]
    (quarter,) = call(line_up_kernel, [scalar(dom)] + pieces, [sds((rows, cols), BF16)], scalars=1)
    return spread(quarter)


def per_device(
    nodes, senders, send_next, send_prev, readout_vertex_list, dec_weights, base, observed_analysis,
    w_send, w_recv, vertex_refresh_matrix, w_decode,
):
    latent = nodes[0]
    count, width = latent.shape
    halo = send_next.shape[0]
    line_span, variables = base.shape
    degree = senders.shape[0]
    fan = readout_vertex_list.shape[0]
    ext_rows = count + 2 * halo
    members = lax.axis_size("ens")
    ens, dom = lax.axis_index("ens"), lax.axis_index("dom")
    to_next, to_prev = send_next.reshape(1, halo), send_prev.reshape(1, halo)

    nodes_t, next_t, prev_t = call(
        lend_kernel,
        [latent, to_next, to_prev],
        [sds((width, count), BF16), sds((width, halo), BF16), sds((width, halo), BF16)],
        flops=4 * width * count * halo,
    )
    lat_prev = along(next_t, "dom", 1)
    lat_next = along(prev_t, "dom", -1)

    block = 512
    steps = line_span // block
    fixed = lambda shape: pl.BlockSpec(shape, lambda i: (0,) * len(shape))
    tall = lambda rows: pl.BlockSpec((rows, block), lambda i: (0, i))
    flat = pl.BlockSpec((block, variables), lambda i: (i, 0))
    w_send_t, vertex_t, w_decode_t, recv_t, mat_hi, mat_lo, base_t, truth_t = pl.pallas_call(
        prepare_kernel,
        grid=(steps,),
        out_shape=[
            sds((width, width), BF16), sds((width, width), BF16), sds((variables, width), BF16),
            sds((width, count), F32), sds((ext_rows, line_span), BF16), sds((ext_rows, line_span), BF16),
            sds((variables, line_span), BF16), sds((variables, line_span), BF16),
        ],
        in_specs=[
            fixed((width, width)), fixed((width, width)), fixed((width, width)), fixed((width, variables)),
            fixed((width, count)), tall(fan), tall(fan), flat, flat,
        ],
        out_specs=[
            fixed((width, width)), fixed((width, width)), fixed((variables, width)), fixed((width, count)),
            tall(ext_rows), tall(ext_rows), tall(variables), tall(variables),
        ],
        compiler_params=params(),
        cost_estimate=cost(2 * width * width * count, 20e6),
    )(w_send, w_recv, vertex_refresh_matrix, w_decode, nodes_t, readout_vertex_list, dec_weights, base, observed_analysis)

    picked_t, slope_t, slope_sum_t, agg_t, upd_slope_t, hidden_t, field_t, next_t, prev_t = call(
        forward_kernel,
        [nodes_t, lat_prev, lat_next, senders, w_send_t, recv_t, vertex_t, w_decode_t, to_next, to_prev],
        [
            sds((degree, width, count), BF16), sds((degree, width, count), BF16), sds((width, count), F32),
            sds((width, count), BF16), sds((width, count), F32), sds((width, count), BF16),
            sds((variables, count), BF16), sds((variables, halo), BF16), sds((variables, halo), BF16),
        ],
        flops=2 * degree * width * count * (ext_rows + width),
    )
    field_ext = jnp.concatenate([field_t, along(next_t, "dom", 1), along(prev_t, "dom", -1)], axis=1)
    fields = lax.all_gather(field_ext, "ens", axis=0, tiled=True)

    grad_ext_t, term = pl.pallas_call(
        functools.partial(readout_kernel, line_span),
        grid=(steps,),
        out_shape=[sds((variables, ext_rows), F32), sds((8, block), F32)],
        in_specs=[
            SCALAR, fixed((members * variables, ext_rows)), tall(ext_rows), tall(ext_rows),
            tall(variables), tall(variables),
        ],
        out_specs=[fixed((variables, ext_rows)), fixed((8, block))],
        scratch_shapes=[pltpu.VMEM((members, variables, block), F32)],
        compiler_params=params(),
        cost_estimate=cost(4 * members * variables * ext_rows * line_span, 14e6),
    )(scalar(ens), fields, mat_hi, mat_lo, base_t, truth_t)

    got_next = along(grad_ext_t[:, count : count + halo], "dom", -1)
    got_prev = along(grad_ext_t[:, count + halo :], "dom", 1)
    losses = lax.all_gather(term[:, :128] + term[:, 128:256] + term[:, 256:384] + term[:, 384:], ("ens", "dom"), axis=0, tiled=True)
    loss = jnp.sum(losses) / line_span

    cols = 3 * width + variables
    keep, send = call(
        backward_kernel,
        [
            scalar(lax.rem(ens, 2)), grad_ext_t, got_next, got_prev, to_next, to_prev, w_decode, vertex_refresh_matrix,
            nodes_t, picked_t, slope_t, slope_sum_t, agg_t, upd_slope_t, hidden_t,
        ],
        [sds((width // 2, cols), F32), sds((width // 2, cols), BF16)],
        [pltpu.VMEM((width, cols), F32)],
        flops=2 * (degree + 3) * width * width * count,
        scalars=1,
    )
    pieces = reduced(keep, send, ens, dom)
    spot = 2 * lax.rem(ens, 2) + ens // 2
    order = jnp.stack([spot, spot ^ 1, spot ^ 2, spot ^ 3]).astype(jnp.int32)
    g_send, g_recv, g_update, g_decode = call(
        finish_kernel,
        [order] + list(pieces),
        [sds((width, width), F32)] * 3 + [sds((width, variables), F32)],
        scalars=1,
    )
    return g_send, g_recv, g_update, g_decode, loss


def solution(mesh):
    return jax.shard_map(
        per_device,
        mesh=mesh,
        in_specs=(
            P("ens", "dom", None), P(None, "dom"), P("dom"), P("dom"), P(None, "dom"), P(None, "dom"),
            P("dom", None), P("dom", None), P(), P(), P(), P(),
        ),
        out_specs=(P(), P(), P(), P(), P()),
        check_vma=False,
    )
```

time: 410 us -> 231 us (0.56)
  other arithmetic: 119 us -> 2.2 us
  waiting for transfers between devices: 148 us -> 42.8 us
  Pallas kernels: 0 us -> 68.1 us
  local copies, waits for them, and re-layouts: 64.5 us -> 6.57 us
  blocking collectives: 37.4 us -> 76.9 us
  starting transfers between devices: 15.3 us -> 31.8 us
  between operations: 15.2 us -> 2.65 us
  matrix products: 10.2 us -> 0 us
    psum x1 -> x0, waiting for transfers between devices: 99.5 us -> none  [per_device(): lax.psum((g_send, g_recv, g_update, g_decode, loss_local), ('ens', 'dom'))]
    scatter-add x6 -> x0, other arithmetic: 94.2 us -> none  [the longest x3 71.6 us: per_device(): grad_ext.at[readout_vertex_list[k]].add(dec_weights[k][:, None] * grad_x)]
    all_gather x0 -> x2, blocking collectives: none -> 76.9 us  [the longest x1 67.7 us: per_device(): lax.all_gather(term[:, :128] + term[:, 128:256] + term[:, 256:384] + term...]
    pallas_call x0 -> x10, Pallas kernels: none -> 68.1 us  [the longest x8 35.9 us: call(): pl.pallas_call(kernel, out_shape=outs, in_specs=[SCALAR] * scalars + vmem...]
    gather x8 -> x0, local copies, waits for them, and re-layouts: 57.5 us -> none  [the longest x3 39.3 us: per_device(): field_ext[readout_vertex_list[k]].astype(jnp.float32)]
    psum x1 -> x0, blocking collectives: 37.4 us -> none  [per_device(): lax.psum((g_send, g_recv, g_update, g_decode, loss_local), ('ens', 'dom'))]
    all_gather x1 -> x0, waiting for transfers between devices: 34.8 us -> none  [per_device(): lax.all_gather(outlook_grid_state[None], 'ens', axis=0, tiled=True)]
    ppermute x6 -> x25, waiting for transfers between devices: 13.3 us -> 42.8 us  [the longest x5 22.2 us: flip(): return lax.ppermute(value, axis, [(i, i ^ bit) for i in range(size)])]
  transfers between devices with their start and end apart: 8 -> 25, of which waited for: 6 -> 13; matrix products, arithmetic and copies ran while one was open for 2% -> 1% of each run, Pallas kernels for 0% -> 7%
where the time goes in v1:
time: 231 us
  blocking collectives  76.9 us (33%)
  Pallas kernels  68.1 us (29%)
  waiting for transfers between devices  42.8 us (19%)
  starting transfers between devices  31.8 us (14%)
  local copies, waits for them, and re-layouts  6.57 us (3%)
  between operations  2.65 us (1%)
    all_gather x1, blocking collectives, per_device(): lax.all_gather(term[:, :128] + term[:, 128:256] + term[:, 256:384] + term...  67.7 us
    pallas_call x8, Pallas kernels, call(): pl.pallas_call(kernel, out_shape=outs, in_specs=[SCALAR] * scalars + vmem...  35.9 us
    ppermute x20, starting transfers between devices, along(): lax.ppermute(value, axis, [(i, (i + steps) % size) for i in range(size)])  31 us
    ppermute x5, waiting for transfers between devices, flip(): return lax.ppermute(value, axis, [(i, i ^ bit) for i in range(size)])  22.2 us
    ppermute x20, waiting for transfers between devices, along(): lax.ppermute(value, axis, [(i, (i + steps) % size) for i in range(size)])  20.6 us
    pallas_call x1, Pallas kernels, per_device(): pl.pallas_call(prepare_kernel, grid=(steps,), out_shape=[sds((width, widt...  16.1 us
    pallas_call x1, Pallas kernels, per_device(): pl.pallas_call(functools.partial(readout_kernel, line_span), grid=(steps,...  16 us
    all_gather x1, blocking collectives, per_device(): fields = lax.all_gather(field_ext, 'ens', axis=0, tiled=True)  9.2 us
  transfers between devices with their start and end apart: 25, of which 13 were waited for; matrix products, arithmetic and copies ran while one was open for 1% of the time, Pallas kernels for 7%

profile of v1, /device:TPU:0, one launch (start us, length us, event | category | flops | bytes accessed | tf_op | source)
XLA Modules:
  0.0 230.9 jit_solution(17499753340663407261)
XLA Ops:
  0.6 2.2 shard_map.155
  2.9 3.0 %collective-permute-start = (bf16[512,128]{1,0:T(8,128)(2,1)}, bf16[512,128]{1,0:T(8,128)(2,1)S(1)}, u32[]{:S(2)}, u32[]{:S(2)}) collective-permute-start(bf16[512,128]{1,0:T(8,128)(2,1)} %get-tuple-element.44), channel_id=1, source_target_pairs={{0,1},{1,2},{2,3},{3,4},{4,5},{5,6},{6,7},{7,0},{8,9},{9,10},{10,1... | collective-permute-start | bytes 393224 | tf_op jit(solution)/shard_map/ppermute | solution.py:229
  5.8 3.0 %collective-permute-start.1 = (bf16[512,128]{1,0:T(8,128)(2,1)}, bf16[512,128]{1,0:T(8,128)(2,1)S(1)}, u32[]{:S(2)}, u32[]{:S(2)}) collective-permute-start(bf16[512,128]{1,0:T(8,128)(2,1)} %get-tuple-element.45), channel_id=1, source_target_pairs={{0,7},{1,0},{2,1},{3,2},{4,3},{5,4},{6,5},{7,6},{8,15},{9,8},{10,9... | collective-permute-start | bytes 393224 | tf_op jit(solution)/shard_map/ppermute | solution.py:229
  8.9 16.1 %shard_map.156 = (bf16[512,512]{1,0:T(8,128)(2,1)}, bf16[512,512]{1,0:T(8,128)(2,1)}, bf16[128,512]{1,0:T(8,128)(2,1)}, f32[512,512]{1,0:T(8,128)}, bf16[768,409...) custom-call(bf16[512,512]{1,0:T(8,128)(2,1)} %w_send.1, ...), custom_call_target="tpu_custom_call" | custom-call | flops 268435456 | bytes 20000000 | tf_op jit(solution)/shard_map/pallas_call | solution.py:322
  25.0 0.0 copy-start.22
  25.0 0.0 collective-permute-done.1.from_next
  25.0 0.6 copy-done.22
  25.7 0.0 copy-done.23
  25.7 12.4 %shard_map.157 = (bf16[6,512,512]{2,1,0:T(8,128)(2,1)}, bf16[6,512,512]{2,1,0:T(8,128)(2,1)}, f32[512,512]{1,0:T(8,128)}, bf16[512,512]{1,0:T(8,128)(2,1)}, f32[...) custom-call(bf16[512,512]{1,0:T(8,128)(2,1)} %get-tuple-element.43.n, ...), custom_call_target="tpu_custom_call" | custom-call | flops 4026531840 | bytes 12661760 | tf_op jit(solution)/shard_map/pallas_call | solution.py:240
  38.1 0.0 collective-permute-start.2
  38.1 4.7 %collective-permute-start.3 = (bf16[128,128]{1,0:T(8,128)(2,1)}, bf16[128,128]{1,0:T(8,128)(2,1)S(1)}, u32[]{:S(2)}, u32[]{:S(2)}) collective-permute-start(bf16[128,128]{1,0:T(8,128)(2,1)} %get-tuple-element.52), channel_id=1, source_target_pairs={{0,7},{1,0},{2,1},{3,2},{4,3},{5,4},{6,5},{7,6},{8,15},{9,8},{10,9... | collective-permute-start | bytes 98312 | tf_op jit(solution)/shard_map/ppermute | solution.py:229
  42.9 2.1 collective-permute-done.2
  45.0 0.9 pad_maximum_fusion
  45.9 9.2 %all_gather.6.fields = bf16[512,768]{1,0:T(8,128)(2,1)} all-gather(bf16[128,768]{1,0:T(8,128)(2,1)S(1)} %pad_maximum_fusion), channel_id=1, replica_groups=mesh['ens'=4,'dom'=8] {'ens'}, dimensions={0}, use_global_device_ids=true | all-gather | bytes 983040 | tf_op jit(solution)/shard_map/all_gather | solution.py:353
  55.1 16.0 %shard_map.158 = (f32[128,768]{1,0:T(8,128)}, f32[8,512]{1,0:T(8,128)}) custom-call(s32[1]{0:T(128)} %bitcast.7.own_index, bf16[512,768]{1,0:T(8,128)(2,1)} %all_gather.6.fields, bf16[768,4096]{1,0:T(8,128)(2,1)} %get-tuple-element.53.mat_hi, bf16[768,4096]{1,0:T(8,128)(2,1)} %get-tuple-element.54.mat_lo, bf16[128,4096]{1,0:T(8,128)(2,1)} %get-tuple-element.55.base_t, ...), custom_call_target="tpu_custom_call" | custom-call | flops 6442450944 | bytes 14000000 | tf_op jit(solution)/shard_map/pallas_call | solution.py:355
  71.1 0.9 fusion
  72.0 4.8 %collective-permute-start.4 = (f32[128,128]{1,0:T(8,128)S(1)}, f32[128,128]{1,0:T(8,128)S(1)}, u32[]{:S(2)}, u32[]{:S(2)}) collective-permute-start(f32[128,128]{1,0:T(8,128)S(1)} %get-tuple-element.82), channel_id=1, source_target_pairs={{0,7},{1,0},{2,1},{3,2},{4,3},{5,4},{6,5},{7,6},{8,15},{9,8},{10,9... | collective-permute-start | bytes 196616 | tf_op jit(solution)/shard_map/ppermute | solution.py:229
  76.8 0.0 collective-permute-start.5
  76.8 1.9 collective-permute-done.4.from_next
  78.7 5.1 %collective-permute-done.5.from_prev = f32[128,128]{1,0:T(8,128)S(1)} collective-permute-done((f32[128,128]{1,0:T(8,128)S(1)}, f32[128,128]{1,0:T(8,128)S(1)}, u32[]{:S(2)}, u32[]{:S(2)}) %collective-permute-start.5) | collective-permute-done | bytes 65568 | tf_op jit(solution)/shard_map/ppermute | solution.py:229
  83.8 0.6 copy-done.6
  84.4 9.3 %shard_map.159 = (f32[256,1664]{1,0:T(8,128)}, bf16[256,1664]{1,0:T(8,128)(2,1)}) custom-call(s32[1]{0:T(128)} %bitcast.6.half, f32[128,768]{1,0:T(8,128)} %get-tuple-element.57.grad_ext_t, f32[128,128]{1,0:T(8,128)} %copy-done.5, f32[128,128]{1,0:T(8,128)} %copy-done.6, s32[1,128]{1,0:T(1,128)} %bitcast.14, s32[1,128]{1,0:T(1,128)} %bitcast.17, ...), custom_call_target="tpu_custom_call" | custom-call | flops 2415919104 | bytes 13698052 | tf_op jit(solution)/shard_map/pallas_call | solution.py:240
  93.7 0.0 collective-permute-start.6
  93.7 2.6 %collective-permute-done.6.got = bf16[256,1664]{1,0:T(8,128)(2,1)S(1)} collective-permute-done((bf16[256,1664]{1,0:T(8,128)(2,1)}, bf16[256,1664]{1,0:T(8,128)(2,1)S(1)}, u32[]{:S(2)}, u32[]{:S(2)}) %collective-permute-start.6) | collective-permute-done | bytes 852000 | tf_op jit(solution)/shard_map/ppermute | solution.py:234
  96.3 0.9 copy-done
  97.2 3.0 %shard_map.160 = (f32[128,1664]{1,0:T(8,128)}, bf16[128,1664]{1,0:T(8,128)(2,1)}) custom-call(s32[1]{0:T(128)} %bitcast.5.half, f32[256,1664]{1,0:T(8,128)} %get-tuple-element.64.mine, bf16[256,1664]{1,0:T(8,128)(2,1)} %copy-done), custom_call_target="tpu_custom_call" | custom-call | bytes 3833860 | tf_op jit(solution)/shard_map/pallas_call | solution.py:240
  100.2 0.4 collective-permute-start.7
  100.6 11.7 %collective-permute-done.7.got = bf16[128,1664]{1,0:T(8,128)(2,1)S(1)} collective-permute-done((bf16[128,1664]{1,0:T(8,128)(2,1)}, bf16[128,1664]{1,0:T(8,128)(2,1)S(1)}, u32[]{:S(2)}, u32[]{:S(2)}) %collective-permute-start.7) | collective-permute-done | bytes 426016 | tf_op jit(solution)/shard_map/ppermute | solution.py:234
  112.2 0.8 copy-done.4
  113.0 2.1 shard_map.161
  115.1 0.7 collective-permute-start.11
  115.8 3.2 %collective-permute-start.12 = (bf16[16,1664]{1,0:T(8,128)(2,1)}, bf16[16,1664]{1,0:T(8,128)(2,1)S(1)}, u32[]{:S(2)}, u32[]{:S(2)}) collective-permute-start(bf16[16,1664]{1,0:T(8,128)(2,1)} %get-tuple-element.73), channel_id=1, source_target_pairs={{0,5},{1,6},{2,7},{3,0},{4,1},{5,2},{6,3},{7,4},{8,13},{9,14},{10,... | collective-permute-start | bytes 159752 | tf_op jit(solution)/shard_map/ppermute | solution.py:229
  119.0 0.0 collective-permute-start.13
  119.0 1.5 collective-permute-start.14
  120.5 1.5 collective-permute-done.10.refs_3_
  122.0 0.0 collective-permute-start.8
  122.0 0.0 collective-permute-done.11.refs_4_
  122.0 1.0 collective-permute-start.9
  123.0 0.3 collective-permute-done.13.refs_6_
  123.3 0.0 collective-permute-done.14.refs_7_
  123.3 5.7 %collective-permute-done.8.refs_1_ = bf16[16,1664]{1,0:T(8,128)(2,1)S(1)} collective-permute-done((bf16[16,1664]{1,0:T(8,128)(2,1)}, bf16[16,1664]{1,0:T(8,128)(2,1)S(1)}, u32[]{:S(2)}, u32[]{:S(2)}) %collective-permute-start.8) | collective-permute-done | bytes 53280 | tf_op jit(solution)/shard_map/ppermute | solution.py:229
  129.1 0.6 copy-done.16
  129.7 0.0 copy-done.19
  129.7 1.7 shard_map.162.refs_0_
  131.4 1.1 collective-permute-start.15
  132.5 1.6 collective-permute-start.17
  134.1 2.6 %collective-permute-start.18 = (bf16[16,1664]{1,0:T(8,128)(2,1)}, bf16[16,1664]{1,0:T(8,128)(2,1)S(1)}, u32[]{:S(2)}, u32[]{:S(2)}) collective-permute-start(bf16[16,1664]{1,0:T(8,128)(2,1)} %shard_map.162.refs_0_), channel_id=1, source_target_pairs={{0,4},{1,5},{2,6},{3,7},{4,0},{5,1},{6,2},{7,3},{8,12},{9,13},{10,... | collective-permute-start | bytes 159752 | tf_op jit(solution)/shard_map/ppermute | solution.py:229
  136.7 1.7 collective-permute-start.19
  138.3 0.8 collective-permute-done.15.refs_1_
  139.1 1.0 collective-permute-start.20
  140.2 1.2 collective-permute-start.21
  141.3 0.6 collective-permute-done.19.refs_5_
  141.9 1.7 collective-permute-done.20.refs_6_
  143.6 0.9 collective-permute-done.21.refs_7_
  144.5 0.6 copy-done.20
  145.2 1.8 shard_map.163.p0
  147.0 0.4 collective-permute-start.22
  147.4 7.9 %collective-permute-done.22.p1 = bf16[128,1664]{1,0:T(8,128)(2,1)S(1)} collective-permute-done((bf16[128,1664]{1,0:T(8,128)(2,1)}, bf16[128,1664]{1,0:T(8,128)(2,1)S(1)}, u32[]{:S(2)}, u32[]{:S(2)}) %collective-permute-start.22) | collective-permute-done | bytes 426016 | tf_op jit(solution)/shard_map/ppermute | solution.py:234
  155.3 0.6 pad_add_fusion.order
  156.0 67.7 %all_gather.7 = f32[256,128]{1,0:T(8,128)S(1)} all-gather(f32[8,128]{1,0:T(8,128)S(1)} %slice_add_fusion), channel_id=1, replica_groups=mesh['ens'=4,'dom'=8] {'ens','dom'}, dimensions={0}, use_global_device_ids=true | all-gather | bytes 135168 | tf_op jit(solution)/shard_map/all_gather | solution.py:371
  223.7 0.6 reduce_sum.9
  225.0 0.7 copy-done.2
  225.7 0.8 copy-done.3
  226.5 3.3 %shard_map.164 = (f32[512,512]{1,0:T(8,128)}, f32[512,512]{1,0:T(8,128)}, f32[512,512]{1,0:T(8,128)}, f32[512,128]{1,0:T(8,128)}) custom-call(s32[4]{0:T(128)} %pad_add_fusion.order, bf16[128,1664]{1,0:T(8,128)(2,1)} %shard_map.163.p0, bf16[128,1664]{1,0:T(8,128)(2,1)} %copy-done.1, bf16[128,1664]{1,0:T(8,128)(2,1)} %copy-done.2, bf16[128,1664]{1,0:T(8,128)(2,1)} %copy-done.3), custom_call_target="tpu_custom_call" | custom-call | bytes 5111824 | tf_op jit(solution)/shard_map/pallas_call | solution.py:240
  (51 shorter events, 0.1 us)
Async XLA Ops:
  2.9 22.1 %collective-permute-start = (bf16[512,128]{1,0:T(8,128)(2,1)}, bf16[512,128]{1,0:T(8,128)(2,1)S(1)}, u32[]{:S(2)}, u32[]{:S(2)}) collective-permute-start(bf16[512,128]{1,0:T(8,128)(2,1)} %get-tuple-element.44), channel_id=1, source_target_pairs={{0,1},{1,2},{2,3},{3,4},{4,5},{5,6},{6,7},{7,0},{8,9},{9,10},{10,1... | collective-permute-start | bytes 393224 | tf_op jit(solution)/shard_map/ppermute | solution.py:229
  5.8 19.2 %collective-permute-start.1 = (bf16[512,128]{1,0:T(8,128)(2,1)}, bf16[512,128]{1,0:T(8,128)(2,1)S(1)}, u32[]{:S(2)}, u32[]{:S(2)}) collective-permute-start(bf16[512,128]{1,0:T(8,128)(2,1)} %get-tuple-element.45), channel_id=1, source_target_pairs={{0,7},{1,0},{2,1},{3,2},{4,3},{5,4},{6,5},{7,6},{8,15},{9,8},{10,9... | collective-permute-start | bytes 393224 | tf_op jit(solution)/shard_map/ppermute | solution.py:229
  25.0 0.7 copy-start.22
  25.0 0.7 copy-start.23
  38.1 6.8 %collective-permute-start.2 = (bf16[128,128]{1,0:T(8,128)(2,1)}, bf16[128,128]{1,0:T(8,128)(2,1)S(1)}, u32[]{:S(2)}, u32[]{:S(2)}) collective-permute-start(bf16[128,128]{1,0:T(8,128)(2,1)} %get-tuple-element.51), channel_id=1, source_target_pairs={{0,1},{1,2},{2,3},{3,4},{4,5},{5,6},{6,7},{7,0},{8,9},{9,10},{10,1... | collective-permute-start | bytes 98312 | tf_op jit(solution)/shard_map/ppermute | solution.py:229
  38.1 6.8 %collective-permute-start.3 = (bf16[128,128]{1,0:T(8,128)(2,1)}, bf16[128,128]{1,0:T(8,128)(2,1)S(1)}, u32[]{:S(2)}, u32[]{:S(2)}) collective-permute-start(bf16[128,128]{1,0:T(8,128)(2,1)} %get-tuple-element.52), channel_id=1, source_target_pairs={{0,7},{1,0},{2,1},{3,2},{4,3},{5,4},{6,5},{7,6},{8,15},{9,8},{10,9... | collective-permute-start | bytes 98312 | tf_op jit(solution)/shard_map/ppermute | solution.py:229
  72.0 6.7 %collective-permute-start.4 = (f32[128,128]{1,0:T(8,128)S(1)}, f32[128,128]{1,0:T(8,128)S(1)}, u32[]{:S(2)}, u32[]{:S(2)}) collective-permute-start(f32[128,128]{1,0:T(8,128)S(1)} %get-tuple-element.82), channel_id=1, source_target_pairs={{0,7},{1,0},{2,1},{3,2},{4,3},{5,4},{6,5},{7,6},{8,15},{9,8},{10,9... | collective-permute-start | bytes 196616 | tf_op jit(solution)/shard_map/ppermute | solution.py:229
  76.8 7.0 %collective-permute-start.5 = (f32[128,128]{1,0:T(8,128)S(1)}, f32[128,128]{1,0:T(8,128)S(1)}, u32[]{:S(2)}, u32[]{:S(2)}) collective-permute-start(f32[128,128]{1,0:T(8,128)S(1)} %get-tuple-element.81), channel_id=1, source_target_pairs={{0,1},{1,2},{2,3},{3,4},{4,5},{5,6},{6,7},{7,0},{8,9},{9,10},{10,1... | collective-permute-start | bytes 196616 | tf_op jit(solution)/shard_map/ppermute | solution.py:229
  78.7 5.1 %copy-start.5 = (f32[128,128]{1,0:T(8,128)}, f32[128,128]{1,0:T(8,128)S(1)}, u32[]{:S(2)}) copy-start(f32[128,128]{1,0:T(8,128)S(1)} %collective-permute-done.4.from_next) | copy-start | bytes 196612
  83.8 0.6 copy-start.6
  93.7 62.3 %copy-start.21 = (f32[8,512]{1,0:T(8,128)S(1)}, f32[8,512]{1,0:T(8,128)}, u32[]{:S(2)}) copy-start(f32[8,512]{1,0:T(8,128)} %get-tuple-element.80) | copy-start | bytes 49156
  93.7 2.6 %collective-permute-start.6 = (bf16[256,1664]{1,0:T(8,128)(2,1)}, bf16[256,1664]{1,0:T(8,128)(2,1)S(1)}, u32[]{:S(2)}, u32[]{:S(2)}) collective-permute-start(bf16[256,1664]{1,0:T(8,128)(2,1)} %get-tuple-element.65), channel_id=1, source_target_pairs={{0,8},{8,0},{16,24},{24,16},{1,9},{9,1},{17,25},{25,17},{2,10},{10... | collective-permute-start | bytes 2555912 | tf_op jit(solution)/shard_map/ppermute | solution.py:234
  96.3 0.9 copy-start
  100.2 12.1 %collective-permute-start.7 = (bf16[128,1664]{1,0:T(8,128)(2,1)}, bf16[128,1664]{1,0:T(8,128)(2,1)S(1)}, u32[]{:S(2)}, u32[]{:S(2)}) collective-permute-start(bf16[128,1664]{1,0:T(8,128)(2,1)} %get-tuple-element.67), channel_id=1, source_target_pairs={{0,16},{8,24},{16,0},{24,8},{1,17},{9,25},{17,1},{25,9},{2,18},{10... | collective-permute-start | bytes 1277960 | tf_op jit(solution)/shard_map/ppermute | solution.py:234
  112.2 0.8 copy-start.4
  115.1 6.9 %collective-permute-start.10 = (bf16[16,1664]{1,0:T(8,128)(2,1)}, bf16[16,1664]{1,0:T(8,128)(2,1)S(1)}, u32[]{:S(2)}, u32[]{:S(2)}) collective-permute-start(bf16[16,1664]{1,0:T(8,128)(2,1)} %get-tuple-element.71), channel_id=1, source_target_pairs={{0,3},{1,4},{2,5},{3,6},{4,7},{5,0},{6,1},{7,2},{8,11},{9,12},{10,... | collective-permute-start | bytes 159752 | tf_op jit(solution)/shard_map/ppermute | solution.py:229
  115.1 6.9 %collective-permute-start.11 = (bf16[16,1664]{1,0:T(8,128)(2,1)}, bf16[16,1664]{1,0:T(8,128)(2,1)S(1)}, u32[]{:S(2)}, u32[]{:S(2)}) collective-permute-start(bf16[16,1664]{1,0:T(8,128)(2,1)} %get-tuple-element.72), channel_id=1, source_target_pairs={{0,4},{1,5},{2,6},{3,7},{4,0},{5,1},{6,2},{7,3},{8,12},{9,13},{10,... | collective-permute-start | bytes 159752 | tf_op jit(solution)/shard_map/ppermute | solution.py:229
  115.8 7.2 %collective-permute-start.12 = (bf16[16,1664]{1,0:T(8,128)(2,1)}, bf16[16,1664]{1,0:T(8,128)(2,1)S(1)}, u32[]{:S(2)}, u32[]{:S(2)}) collective-permute-start(bf16[16,1664]{1,0:T(8,128)(2,1)} %get-tuple-element.73), channel_id=1, source_target_pairs={{0,5},{1,6},{2,7},{3,0},{4,1},{5,2},{6,3},{7,4},{8,13},{9,14},{10,... | collective-permute-start | bytes 159752 | tf_op jit(solution)/shard_map/ppermute | solution.py:229
  119.0 4.3 %collective-permute-start.13 = (bf16[16,1664]{1,0:T(8,128)(2,1)}, bf16[16,1664]{1,0:T(8,128)(2,1)S(1)}, u32[]{:S(2)}, u32[]{:S(2)}) collective-permute-start(bf16[16,1664]{1,0:T(8,128)(2,1)} %get-tuple-element.74), channel_id=1, source_target_pairs={{0,6},{1,7},{2,0},{3,1},{4,2},{5,3},{6,4},{7,5},{8,14},{9,15},{10,... | collective-permute-start | bytes 159752 | tf_op jit(solution)/shard_map/ppermute | solution.py:229
  119.0 4.4 %collective-permute-start.14 = (bf16[16,1664]{1,0:T(8,128)(2,1)}, bf16[16,1664]{1,0:T(8,128)(2,1)S(1)}, u32[]{:S(2)}, u32[]{:S(2)}) collective-permute-start(bf16[16,1664]{1,0:T(8,128)(2,1)} %get-tuple-element.75), channel_id=1, source_target_pairs={{0,7},{1,0},{2,1},{3,2},{4,3},{5,4},{6,5},{7,6},{8,15},{9,8},{10,9... | collective-permute-start | bytes 159752 | tf_op jit(solution)/shard_map/ppermute | solution.py:229
  122.0 7.1 %copy-start.7 = (bf16[16,1664]{1,0:T(8,128)(2,1)}, bf16[16,1664]{1,0:T(8,128)(2,1)S(1)}, u32[]{:S(2)}) copy-start(bf16[16,1664]{1,0:T(8,128)(2,1)S(1)} %collective-permute-done.10.refs_3_) | copy-start | bytes 159748
  122.0 7.0 %collective-permute-start.8 = (bf16[16,1664]{1,0:T(8,128)(2,1)}, bf16[16,1664]{1,0:T(8,128)(2,1)S(1)}, u32[]{:S(2)}, u32[]{:S(2)}) collective-permute-start(bf16[16,1664]{1,0:T(8,128)(2,1)} %get-tuple-element.69), channel_id=1, source_target_pairs={{0,1},{1,2},{2,3},{3,4},{4,5},{5,6},{6,7},{7,0},{8,9},{9,10},{10,1... | collective-permute-start | bytes 159752 | tf_op jit(solution)/shard_map/ppermute | solution.py:229
  122.0 7.0 %copy-start.8 = (bf16[16,1664]{1,0:T(8,128)(2,1)}, bf16[16,1664]{1,0:T(8,128)(2,1)S(1)}, u32[]{:S(2)}) copy-start(bf16[16,1664]{1,0:T(8,128)(2,1)S(1)} %collective-permute-done.11.refs_4_) | copy-start | bytes 159748
  122.0 7.0 %collective-permute-start.9 = (bf16[16,1664]{1,0:T(8,128)(2,1)}, bf16[16,1664]{1,0:T(8,128)(2,1)S(1)}, u32[]{:S(2)}, u32[]{:S(2)}) collective-permute-start(bf16[16,1664]{1,0:T(8,128)(2,1)} %get-tuple-element.70), channel_id=1, source_target_pairs={{0,2},{1,3},{2,4},{3,5},{4,6},{5,7},{6,0},{7,1},{8,10},{9,11},{10,... | collective-permute-start | bytes 159752 | tf_op jit(solution)/shard_map/ppermute | solution.py:229
  123.0 6.0 %copy-start.9 = (bf16[16,1664]{1,0:T(8,128)(2,1)}, bf16[16,1664]{1,0:T(8,128)(2,1)S(1)}, u32[]{:S(2)}) copy-start(bf16[16,1664]{1,0:T(8,128)(2,1)S(1)} %collective-permute-done.12.refs_5_) | copy-start | bytes 159748
  123.3 5.8 %copy-start.11 = (bf16[16,1664]{1,0:T(8,128)(2,1)}, bf16[16,1664]{1,0:T(8,128)(2,1)S(1)}, u32[]{:S(2)}) copy-start(bf16[16,1664]{1,0:T(8,128)(2,1)S(1)} %collective-permute-done.13.refs_6_) | copy-start | bytes 159748
  123.3 5.7 %copy-start.13 = (bf16[16,1664]{1,0:T(8,128)(2,1)}, bf16[16,1664]{1,0:T(8,128)(2,1)S(1)}, u32[]{:S(2)}) copy-start(bf16[16,1664]{1,0:T(8,128)(2,1)S(1)} %collective-permute-done.14.refs_7_) | copy-start | bytes 159748
  129.0 0.6 copy-start.16
  129.0 0.6 copy-start.19
  131.4 7.8 %collective-permute-start.15 = (bf16[16,1664]{1,0:T(8,128)(2,1)}, bf16[16,1664]{1,0:T(8,128)(2,1)S(1)}, u32[]{:S(2)}, u32[]{:S(2)}) collective-permute-start(bf16[16,1664]{1,0:T(8,128)(2,1)} %shard_map.162.refs_0_), channel_id=1, source_target_pairs={{0,1},{1,2},{2,3},{3,4},{4,5},{5,6},{6,7},{7,0},{8,9},{9,10},{10,1... | collective-permute-start | bytes 159752 | tf_op jit(solution)/shard_map/ppermute | solution.py:229
  132.5 7.7 %collective-permute-start.16 = (bf16[16,1664]{1,0:T(8,128)(2,1)}, bf16[16,1664]{1,0:T(8,128)(2,1)S(1)}, u32[]{:S(2)}, u32[]{:S(2)}) collective-permute-start(bf16[16,1664]{1,0:T(8,128)(2,1)} %shard_map.162.refs_0_), channel_id=1, source_target_pairs={{0,2},{1,3},{2,4},{3,5},{4,6},{5,7},{6,0},{7,1},{8,10},{9,11},{10,... | collective-permute-start | bytes 159752 | tf_op jit(solution)/shard_map/ppermute | solution.py:229
  132.5 8.8 %collective-permute-start.17 = (bf16[16,1664]{1,0:T(8,128)(2,1)}, bf16[16,1664]{1,0:T(8,128)(2,1)S(1)}, u32[]{:S(2)}, u32[]{:S(2)}) collective-permute-start(bf16[16,1664]{1,0:T(8,128)(2,1)} %shard_map.162.refs_0_), channel_id=1, source_target_pairs={{0,3},{1,4},{2,5},{3,6},{4,7},{5,0},{6,1},{7,2},{8,11},{9,12},{10,... | collective-permute-start | bytes 159752 | tf_op jit(solution)/shard_map/ppermute | solution.py:229
  134.1 7.3 %collective-permute-start.18 = (bf16[16,1664]{1,0:T(8,128)(2,1)}, bf16[16,1664]{1,0:T(8,128)(2,1)S(1)}, u32[]{:S(2)}, u32[]{:S(2)}) collective-permute-start(bf16[16,1664]{1,0:T(8,128)(2,1)} %shard_map.162.refs_0_), channel_id=1, source_target_pairs={{0,4},{1,5},{2,6},{3,7},{4,0},{5,1},{6,2},{7,3},{8,12},{9,13},{10,... | collective-permute-start | bytes 159752 | tf_op jit(solution)/shard_map/ppermute | solution.py:229
  136.7 5.2 %collective-permute-start.19 = (bf16[16,1664]{1,0:T(8,128)(2,1)}, bf16[16,1664]{1,0:T(8,128)(2,1)S(1)}, u32[]{:S(2)}, u32[]{:S(2)}) collective-permute-start(bf16[16,1664]{1,0:T(8,128)(2,1)} %shard_map.162.refs_0_), channel_id=1, source_target_pairs={{0,5},{1,6},{2,7},{3,0},{4,1},{5,2},{6,3},{7,4},{8,13},{9,14},{10,... | collective-permute-start | bytes 159752 | tf_op jit(solution)/shard_map/ppermute | solution.py:229
  139.1 5.4 %copy-start.10 = (bf16[16,1664]{1,0:T(8,128)(2,1)}, bf16[16,1664]{1,0:T(8,128)(2,1)S(1)}, u32[]{:S(2)}) copy-start(bf16[16,1664]{1,0:T(8,128)(2,1)S(1)} %collective-permute-done.15.refs_1_) | copy-start | bytes 159748
  139.1 4.5 %collective-permute-start.20 = (bf16[16,1664]{1,0:T(8,128)(2,1)}, bf16[16,1664]{1,0:T(8,128)(2,1)S(1)}, u32[]{:S(2)}, u32[]{:S(2)}) collective-permute-start(bf16[16,1664]{1,0:T(8,128)(2,1)} %shard_map.162.refs_0_), channel_id=1, source_target_pairs={{0,6},{1,7},{2,0},{3,1},{4,2},{5,3},{6,4},{7,5},{8,14},{9,15},{10,... | collective-permute-start | bytes 159752 | tf_op jit(solution)/shard_map/ppermute | solution.py:229
  140.1 4.4 %copy-start.12 = (bf16[16,1664]{1,0:T(8,128)(2,1)}, bf16[16,1664]{1,0:T(8,128)(2,1)S(1)}, u32[]{:S(2)}) copy-start(bf16[16,1664]{1,0:T(8,128)(2,1)S(1)} %collective-permute-done.16.refs_2_) | copy-start | bytes 159748
  140.2 4.3 %collective-permute-start.21 = (bf16[16,1664]{1,0:T(8,128)(2,1)}, bf16[16,1664]{1,0:T(8,128)(2,1)S(1)}, u32[]{:S(2)}, u32[]{:S(2)}) collective-permute-start(bf16[16,1664]{1,0:T(8,128)(2,1)} %shard_map.162.refs_0_), channel_id=1, source_target_pairs={{0,7},{1,0},{2,1},{3,2},{4,3},{5,4},{6,5},{7,6},{8,15},{9,8},{10,9... | collective-permute-start | bytes 159752 | tf_op jit(solution)/shard_map/ppermute | solution.py:229
  141.3 3.2 %copy-start.14 = (bf16[16,1664]{1,0:T(8,128)(2,1)}, bf16[16,1664]{1,0:T(8,128)(2,1)S(1)}, u32[]{:S(2)}) copy-start(bf16[16,1664]{1,0:T(8,128)(2,1)S(1)} %collective-permute-done.17.refs_3_) | copy-start | bytes 159748
  141.3 3.2 %copy-start.15 = (bf16[16,1664]{1,0:T(8,128)(2,1)}, bf16[16,1664]{1,0:T(8,128)(2,1)S(1)}, u32[]{:S(2)}) copy-start(bf16[16,1664]{1,0:T(8,128)(2,1)S(1)} %collective-permute-done.18.refs_4_) | copy-start | bytes 159748
  141.9 2.6 %copy-start.17 = (bf16[16,1664]{1,0:T(8,128)(2,1)}, bf16[16,1664]{1,0:T(8,128)(2,1)S(1)}, u32[]{:S(2)}) copy-start(bf16[16,1664]{1,0:T(8,128)(2,1)S(1)} %collective-permute-done.19.refs_5_) | copy-start | bytes 159748
  143.6 0.9 copy-start.18
  144.5 0.6 copy-start.20
  147.0 8.3 %collective-permute-start.22 = (bf16[128,1664]{1,0:T(8,128)(2,1)}, bf16[128,1664]{1,0:T(8,128)(2,1)S(1)}, u32[]{:S(2)}, u32[]{:S(2)}) collective-permute-start(bf16[128,1664]{1,0:T(8,128)(2,1)} %shard_map.163.p0), channel_id=1, source_target_pairs={{0,16},{8,24},{16,0},{24,8},{1,17},{9,25},{17,1},{25,9},{2,18},{10... | collective-permute-start | bytes 1277960 | tf_op jit(solution)/shard_map/ppermute | solution.py:234
  147.3 77.6 %collective-permute-start.23 = (bf16[128,1664]{1,0:T(8,128)(2,1)}, bf16[128,1664]{1,0:T(8,128)(2,1)S(1)}, u32[]{:S(2)}, u32[]{:S(2)}) collective-permute-start(bf16[128,1664]{1,0:T(8,128)(2,1)} %shard_map.163.p0), channel_id=1, source_target_pairs={{0,8},{8,0},{16,24},{24,16},{1,9},{9,1},{17,25},{25,17},{2,10},{10... | collective-permute-start | bytes 1277960 | tf_op jit(solution)/shard_map/ppermute | solution.py:234
  155.3 69.7 %copy-start.1 = (bf16[128,1664]{1,0:T(8,128)(2,1)}, bf16[128,1664]{1,0:T(8,128)(2,1)S(1)}, u32[]{:S(2)}) copy-start(bf16[128,1664]{1,0:T(8,128)(2,1)S(1)} %collective-permute-done.22.p1) | copy-start | bytes 1277956
  155.3 69.7 %collective-permute-start.24 = (bf16[128,1664]{1,0:T(8,128)(2,1)S(1)}, bf16[128,1664]{1,0:T(8,128)(2,1)S(1)}, u32[]{:S(2)}, u32[]{:S(2)}) collective-permute-start(bf16[128,1664]{1,0:T(8,128)(2,1)S(1)} %collective-permute-done.22.p1), channel_id=1, source_target_pairs={{0,8},{8,0},{16,24},{24,16},{1,9},{9,1},{17,25},{25,17},{2,10},{10... | collective-permute-start | bytes 1277960 | tf_op jit(solution)/shard_map/ppermute | solution.py:234
  225.0 0.8 copy-start.2
  225.7 0.8 copy-start.3

commit v2 on v1

v2 whole, which is shorter than its diff:
```python
import functools

import jax
import jax.numpy as jnp
from jax import lax
from jax.experimental import pallas as pl
from jax.experimental.pallas import tpu as pltpu
from jax.sharding import PartitionSpec as P

EPS = 0.04
F32 = jnp.float32
BF16 = jnp.bfloat16
VMEM_BYTES = 56 * 1024 * 1024


def dot(a, b, ca=1, cb=0):
    return lax.dot_general(a, b, (((ca,), (cb,)), ((), ())), preferred_element_type=F32)


def dot_nt(a, b):
    return dot(a, b, 1, 1)


def one_hot(rows, index_row):
    shape = (rows, index_row.shape[1])
    hit = lax.broadcasted_iota(jnp.int32, shape, 0) == index_row
    return jnp.where(hit, 1.0, 0.0).astype(BF16)


def params(**kw):
    return pltpu.CompilerParams(vmem_limit_bytes=VMEM_BYTES, **kw)


def vmem(n):
    return [pl.BlockSpec(memory_space=pltpu.VMEM)] * n


def cost(flops, size):
    return pl.CostEstimate(flops=int(flops), bytes_accessed=int(size), transcendentals=0)


def sds(shape, dtype):
    return jax.ShapeDtypeStruct(shape, dtype)


def lend_kernel(nodes, to_next, to_prev, nodes_t, next_t, prev_t):
    table = nodes[...].T
    nodes_t[...] = table
    count = table.shape[1]
    next_t[...] = dot(table, one_hot(count, to_next[...])).astype(BF16)
    prev_t[...] = dot(table, one_hot(count, to_prev[...])).astype(BF16)


def weights_kernel(w_send, w_recv, vertex, w_decode, nodes_t, w_send_t, vertex_t, w_decode_t, recv_t):
    w_send_t[...] = w_send[...].T
    vertex_t[...] = vertex[...].T
    w_decode_t[...] = w_decode[...].T
    recv_t[...] = dot(w_recv[...].T, nodes_t[...])


def decoder_kernel(core, vertices, weights, base, truth, after, mat_hi, mat_lo, base_t, truth_t):
    del core, after
    shape = mat_hi.shape
    row = lax.broadcasted_iota(jnp.int32, shape, 0)
    mat = jnp.zeros(shape, F32)
    for k in range(vertices.shape[0]):
        mat += jnp.where(row == vertices[k : k + 1, :], weights[k : k + 1, :], 0.0)
    mat_hi[...], mat_lo[...] = split(mat)
    base_t[...] = base[...].T
    truth_t[...] = truth[...].T


def forward_kernel(
    nodes_t, from_prev, from_next, senders, w_send_t, recv_t, vertex_t, w_decode_t, to_next, to_prev,
    picked_t, slope_t, slope_sum_t, agg_t, upd_slope_t, hidden_t, field_t, next_t, prev_t,
):
    degree, count = senders.shape
    halo = from_prev.shape[1]
    ext = jnp.concatenate([nodes_t[...], from_prev[...], from_next[...]], axis=1)
    total = jnp.zeros(recv_t.shape, F32)
    slopes = jnp.zeros(recv_t.shape, F32)
    for k in range(degree):
        picked = dot(ext, one_hot(count + 2 * halo, senders[k : k + 1, :])).astype(BF16)
        picked_t[k] = picked
        pre = dot(w_send_t[...], picked) + recv_t[...]
        sigma = 0.5 * jnp.tanh(0.5 * pre) + 0.5
        value = pre * sigma
        total += value
        slope = sigma * (1.0 + (pre - value)) * (1.0 / degree)
        slopes += slope
        slope_t[k] = slope.astype(slope_t.dtype)
    slope_sum_t[...] = slopes
    agg = (total * (1.0 / degree)).astype(BF16)
    agg_t[...] = agg
    upd = dot(vertex_t[...], agg)
    sigma = 0.5 * jnp.tanh(0.5 * upd) + 0.5
    value = upd * sigma
    upd_slope_t[...] = sigma * (1.0 + (upd - value))
    hidden = (nodes_t[...].astype(F32) + value).astype(BF16)
    hidden_t[...] = hidden
    field = dot(w_decode_t[...], hidden).astype(BF16)
    field_t[...] = field
    next_t[...] = dot(field, one_hot(count, to_next[...])).astype(BF16)
    prev_t[...] = dot(field, one_hot(count, to_prev[...])).astype(BF16)


def readout_kernel(line_span, *refs):
    mids, ends = refs[0:4], refs[4:8]
    mat_hi, mat_lo, base_t, truth_t = refs[8:12]
    own_mid, own_next, own_prev, pair_mid, pair_next, pair_prev, loss = refs[12:19]
    table, grad = refs[19:21]
    step = pl.program_id(0)
    members = len(mids)
    variables, count = own_mid.shape
    halo = own_next.shape[1]

    @pl.when(step == 0)
    def _():
        grad[...] = jnp.zeros_like(grad)
        loss[...] = jnp.zeros_like(loss)
        for m in range(members):
            table[m * variables : (m + 1) * variables, :count] = mids[m][...]
            table[m * variables : (m + 1) * variables, count:] = ends[m][...]

    ready = base_t[...].astype(F32)
    states = []
    for m in range(members):
        one = table[m * variables : (m + 1) * variables, :]
        x = ready + (dot(one, mat_hi[...]) + dot(one, mat_lo[...]))
        states.append(x.astype(BF16).astype(F32))
    truth = truth_t[...].astype(F32)

    def bend(diff):
        square = diff * diff + EPS
        inverse = lax.rsqrt(square)
        return square * inverse, diff * inverse

    sizes = {}
    for i in range(2):
        for j in range(i + 1, members):
            sizes[i, j] = bend(states[i] - states[j])
    alone = EPS**0.5
    total = jnp.zeros_like(truth)
    slopes = []
    for i in range(2):
        near, push = bend(states[i] - truth)
        apart, pull = alone, 0.0
        for j in range(members):
            if j != i:
                size, slope = sizes[min(i, j), max(i, j)]
                apart = apart + size
                pull = pull + slope if i < j else pull - slope
        total += near * (1.0 / members) - apart * (1.0 / (2.0 * members * (members - 1)))
        slope = push * (1.0 / members) - pull * (1.0 / (members * (members - 1.0)))
        slopes.append((slope * (1.0 / line_span)).astype(BF16))
    grad[...] += dot_nt(jnp.concatenate(slopes, axis=0), mat_hi[...])
    loss[...] += jnp.sum(total.reshape(-1, 8, total.shape[1]), axis=0)

    @pl.when(step == pl.num_programs(0) - 1)
    def _():
        for i, (mid, after, before) in enumerate(((own_mid, own_next, own_prev), (pair_mid, pair_next, pair_prev))):
            rows = slice(i * variables, (i + 1) * variables)
            mid[...] = grad[rows, :count]
            after[...] = grad[rows, count : count + halo]
            before[...] = grad[rows, count + halo :]


def split(value):
    hi = value.astype(BF16)
    return hi, (value - hi.astype(F32)).astype(BF16)


LANES = 128


def encoded(total):
    tile = total[:, -LANES:]
    value = tile + pltpu.roll(tile, LANES // 2, 1)
    hi = value.astype(BF16).astype(F32)
    lane = lax.broadcasted_iota(jnp.int32, tile.shape, 1)
    tile = jnp.where(lane < LANES // 2, hi, value - hi)
    return jnp.concatenate([total[:, :-LANES].astype(BF16), tile.astype(BF16)], axis=1)


def backward_kernel(
    half, own_mid, pair_mid, next_a, next_b, prev_a, prev_b, to_next, to_prev, term, w_decode, vertex, nodes_t,
    picked_t, slope_t, slope_sum_t, agg_t, upd_slope_t, hidden_t,
    keep, send, whole,
):
    count = nodes_t.shape[1]
    width = nodes_t.shape[0]
    grad_z = own_mid[...] + pair_mid[...]
    for got, rows in ((next_a[...] + next_b[...], to_next), (prev_a[...] + prev_b[...], to_prev)):
        place = one_hot(count, rows[...])
        hi, lo = split(got)
        grad_z += dot_nt(hi, place) + dot_nt(lo, place)
    grad_z = grad_z.astype(BF16)
    main = whole.shape[1] - LANES
    whole[:, 3 * width : main] = dot_nt(hidden_t[...], grad_z)
    grad_upd = (dot(w_decode[...], grad_z) * upd_slope_t[...]).astype(BF16)
    whole[:, 2 * width : 3 * width] = dot_nt(agg_t[...], grad_upd)
    grad_agg = dot(vertex[...], grad_upd)
    grad_recv = (grad_agg * slope_sum_t[...]).astype(BF16)
    whole[:, width : 2 * width] = dot_nt(nodes_t[...], grad_recv)
    total = jnp.zeros((width, width), F32)
    for k in range(picked_t.shape[0]):
        grad_pre = (grad_agg * slope_t[k].astype(F32)).astype(BF16)
        total += dot_nt(picked_t[k], grad_pre)
    whole[:, :width] = total
    whole[:, main:] = jnp.zeros((width, LANES), F32)
    spot = (lax.broadcasted_iota(jnp.int32, (8, LANES), 0) == 0) & (lax.broadcasted_iota(jnp.int32, (8, LANES), 1) == 0)
    whole[0:8, main:] = jnp.where(spot, jnp.sum(term[...]), 0.0)
    rows = keep.shape[0]
    keep[...] = whole[pl.ds(pl.multiple_of(half[0] * rows, rows), rows), :]
    send[...] = encoded(whole[pl.ds(pl.multiple_of((1 - half[0]) * rows, rows), rows), :])


def halve_kernel(half, mine, got, keep, send, total):
    total[...] = mine[...] + got[...].astype(F32)
    rows = keep.shape[0]
    keep[...] = total[pl.ds(pl.multiple_of(half[0] * rows, rows), rows), :]
    send[...] = encoded(total[pl.ds(pl.multiple_of((1 - half[0]) * rows, rows), rows), :])


def shares_kernel(here, mine, got, *outs):
    total = outs[-1]
    total[...] = mine[...] + got[...].astype(F32)
    parts = len(outs) - 1
    rows = outs[0].shape[0]
    for k in range(parts):
        place = lax.rem(here[0] + k, parts)
        block = total[pl.ds(pl.multiple_of(place * rows, rows), rows), :]
        outs[k][...] = encoded(block) if k else block


def sum_kernel(*refs):
    total = refs[0][...]
    for ref in refs[1:-1]:
        total += ref[...].astype(F32)
    refs[-1][...] = encoded(total)


def line_up_kernel(here, *refs):
    out = refs[-1]
    parts = len(refs) - 1
    rows = refs[0].shape[0]
    for k in range(parts):
        place = lax.rem(here[0] + (parts - k), parts)
        out[pl.ds(pl.multiple_of(place * rows, rows), rows), :] = refs[k][...]


def finish_kernel(scale, place, piece, *refs):
    g_send, g_recv, g_update, g_decode, loss = refs[-5:]
    width = g_send.shape[1]
    g_send[...] = piece[:, :width].astype(F32)
    g_recv[...] = piece[:, width : 2 * width].astype(F32)
    g_update[...] = piece[:, 2 * width : 3 * width].astype(F32)
    g_decode[...] = piece[:, 3 * width : -LANES].astype(F32)
    part = jnp.sum(piece[:, -LANES:].astype(F32)) * scale
    loss[0, 0] = part if len(refs) == 5 else refs[4][0, 0] + part


def finish(piece, place, shapes, scale, before=()):
    rows = piece.shape[0]
    block = lambda shape: pl.BlockSpec((rows, shape.shape[1]), lambda i, at: (at[0], 0))
    cell = pl.BlockSpec(memory_space=pltpu.SMEM)
    whole = pl.BlockSpec(memory_space=pl.ANY)
    return pl.pallas_call(
        functools.partial(finish_kernel, scale),
        grid_spec=pltpu.PrefetchScalarGridSpec(
            num_scalar_prefetch=1,
            grid=(1,),
            in_specs=[pl.BlockSpec(piece.shape, lambda i, at: (0, 0))] + ([whole] * 4 + [cell] if before else []),
            out_specs=[block(s) for s in shapes] + [cell],
        ),
        out_shape=list(shapes) + [sds((1, 1), F32)],
        input_output_aliases={2 + i: i for i in range(4)} if before else {},
        compiler_params=params(),
        cost_estimate=cost(0, 6 * piece.size),
    )(scalar(place), piece, *before)


SCALAR = pl.BlockSpec(memory_space=pltpu.SMEM)


def crossed(value, bit, steps):
    ens, dom = lax.axis_size("ens"), lax.axis_size("dom")
    pairs = [(e * dom + d, (e ^ bit) * dom + (d + steps) % dom) for e in range(ens) for d in range(dom)]
    return lax.ppermute(value, ("ens", "dom"), pairs)


def along(value, axis, steps):
    size = lax.axis_size(axis)
    return lax.ppermute(value, axis, [(i, (i + steps) % size) for i in range(size)])


def flip(value, axis, bit):
    size = lax.axis_size(axis)
    return lax.ppermute(value, axis, [(i, i ^ bit) for i in range(size)])


def call(kernel, ins, outs, scratch=(), flops=0, scalars=0):
    size = sum(x.size * x.dtype.itemsize for x in list(ins) + list(outs))
    many = isinstance(outs, (list, tuple))
    return pl.pallas_call(
        kernel,
        out_shape=outs,
        in_specs=[SCALAR] * scalars + vmem(len(ins) - scalars),
        out_specs=vmem(len(outs)),
        scratch_shapes=list(scratch),
        compiler_params=params(),
        cost_estimate=cost(flops, size),
    )(*ins)


def scalar(value):
    return jnp.reshape(value, (1,)).astype(jnp.int32)


def reduced(keep, send, ens, dom):
    parts = lax.axis_size("dom")
    rows, cols = keep.shape
    got = flip(send, "ens", 1)
    keep, send = call(
        halve_kernel,
        [scalar(ens // 2), keep, got],
        [sds((rows // 2, cols), F32), sds((rows // 2, cols), BF16)],
        [pltpu.VMEM((rows, cols), F32)],
        scalars=1,
    )
    rows //= 2
    got = flip(send, "ens", 2)
    share = rows // parts
    if share % 16:
        total = lax.psum(keep + got.astype(F32), "dom")
        return call(sum_kernel, [total], [sds((rows, cols), BF16)])[0]
    shares = call(
        shares_kernel,
        [scalar(dom), keep, got],
        [sds((share, cols), F32)] + [sds((share, cols), BF16)] * (parts - 1),
        [pltpu.VMEM((rows, cols), F32)],
        scalars=1,
    )
    terms = [shares[0]] + [along(shares[k], "dom", k) for k in range(1, parts)]
    (own,) = call(sum_kernel, terms, [sds((share, cols), BF16)])
    pieces = [own] + [along(own, "dom", k) for k in range(1, parts)]
    (quarter,) = call(line_up_kernel, [scalar(dom)] + pieces, [sds((rows, cols), BF16)], scalars=1)
    return quarter


def per_device(
    nodes, senders, send_next, send_prev, readout_vertex_list, dec_weights, base, observed_analysis,
    w_send, w_recv, vertex_refresh_matrix, w_decode,
):
    latent = nodes[0]
    count, width = latent.shape
    halo = send_next.shape[0]
    line_span, variables = base.shape
    degree = senders.shape[0]
    fan = readout_vertex_list.shape[0]
    ext_rows = count + 2 * halo
    members = lax.axis_size("ens")
    ens, dom = lax.axis_index("ens"), lax.axis_index("dom")
    to_next, to_prev = send_next.reshape(1, halo), send_prev.reshape(1, halo)

    nodes_t, next_t, prev_t = call(
        lend_kernel,
        [latent, to_next, to_prev],
        [sds((width, count), BF16), sds((width, halo), BF16), sds((width, halo), BF16)],
        flops=4 * width * count * halo,
    )
    lat_prev = along(next_t, "dom", 1)
    lat_next = along(prev_t, "dom", -1)

    core = scalar(lax.rem(ens, 2))
    w_send_t, vertex_t, w_decode_t, recv_t = call(
        weights_kernel,
        [w_send, w_recv, vertex_refresh_matrix, w_decode, nodes_t],
        [sds((width, width), BF16), sds((width, width), BF16), sds((variables, width), BF16), sds((width, count), F32)],
        flops=2 * width * width * count,
    )

    picked_t, slope_t, slope_sum_t, agg_t, upd_slope_t, hidden_t, field_t, next_t, prev_t = call(
        forward_kernel,
        [nodes_t, lat_prev, lat_next, senders, w_send_t, recv_t, vertex_t, w_decode_t, to_next, to_prev],
        [
            sds((degree, width, count), BF16), sds((degree, width, count), BF16), sds((width, count), F32),
            sds((width, count), BF16), sds((width, count), F32), sds((width, count), BF16),
            sds((variables, count), BF16), sds((variables, halo), BF16), sds((variables, halo), BF16),
        ],
        flops=2 * degree * width * count * (ext_rows + width),
    )
    lent = (along(next_t, "dom", 1), along(prev_t, "dom", -1))
    mids = [field_t] + [flip(field_t, "ens", m) for m in range(1, members)]

    block = 512
    steps = line_span // 2 // block
    fixed = lambda shape: pl.BlockSpec(shape, lambda i, *at: (0,) * len(shape))
    tall = lambda rows: pl.BlockSpec((rows, block), lambda i, *at: (0, i))
    tall_half = lambda rows: pl.BlockSpec((rows, block), lambda i, at: (0, i + at[0] * steps))
    flat_half = pl.BlockSpec((block, variables), lambda i, at: (i + at[0] * steps, 0))
    half_span = line_span // 2
    mat_hi, mat_lo, base_t, truth_t = pl.pallas_call(
        decoder_kernel,
        grid_spec=pltpu.PrefetchScalarGridSpec(
            num_scalar_prefetch=1,
            grid=(steps,),
            in_specs=[tall_half(fan), tall_half(fan), flat_half, flat_half, pl.BlockSpec(memory_space=pl.ANY)],
            out_specs=[tall(ext_rows), tall(ext_rows), tall(variables), tall(variables)],
        ),
        out_shape=[sds((ext_rows, half_span), BF16)] * 2 + [sds((variables, half_span), BF16)] * 2,
        compiler_params=params(),
        cost_estimate=cost(10 * ext_rows * half_span, 16e6),
    )(core, readout_vertex_list, dec_weights, base, observed_analysis, field_t)

    end = jnp.concatenate(lent, axis=1)
    ends = [end] + [flip(end, "ens", m) for m in range(1, members)]

    grads = pl.pallas_call(
        functools.partial(readout_kernel, line_span),
        grid=(steps,),
        out_shape=[sds((variables, count), F32), sds((variables, halo), F32), sds((variables, halo), F32)] * 2 + [sds((8, block), F32)],
        in_specs=[fixed((variables, count))] * members + [fixed((variables, 2 * halo))] * members + [
            tall(ext_rows), tall(ext_rows), tall(variables), tall(variables),
        ],
        out_specs=[fixed((variables, count)), fixed((variables, halo)), fixed((variables, halo))] * 2 + [fixed((8, block))],
        scratch_shapes=[pltpu.VMEM((members * variables, ext_rows), BF16), pltpu.VMEM((2 * variables, ext_rows), F32)],
        compiler_params=params(),
        cost_estimate=cost(4 * members * variables * ext_rows * half_span, 14e6),
    )(*mids, *ends, mat_hi, mat_lo, base_t, truth_t)
    own_mid, own_next, own_prev, pair_mid, pair_next, pair_prev, term = grads
    next_a, prev_a = along(own_next, "dom", -1), along(own_prev, "dom", 1)
    next_b, prev_b = crossed(pair_next, 1, -1), crossed(pair_prev, 1, 1)
    pair_mid = flip(pair_mid, "ens", 1)

    cols = 3 * width + variables + LANES
    keep, send = call(
        backward_kernel,
        [
            core, own_mid, pair_mid, next_a, next_b, prev_a, prev_b, to_next, to_prev, term, w_decode,
            vertex_refresh_matrix, nodes_t, picked_t, slope_t, slope_sum_t, agg_t, upd_slope_t, hidden_t,
        ],
        [sds((width // 2, cols), F32), sds((width // 2, cols), BF16)],
        [pltpu.VMEM((width, cols), F32)],
        flops=2 * (degree + 3) * width * width * count,
        scalars=1,
    )
    quarter = reduced(keep, send, ens, dom)
    across = flip(quarter, "ens", 2)
    beside = flip(quarter, "ens", 1)
    corner = flip(across, "ens", 1)
    spot = 2 * lax.rem(ens, 2) + ens // 2
    shapes = [sds((width, width), F32)] * 3 + [sds((width, variables), F32)]
    scale = 1.0 / line_span
    outs = finish(quarter, spot, shapes, scale)
    outs = finish(beside, spot ^ 2, shapes, scale, outs)
    outs = finish(across, spot ^ 1, shapes, scale, outs)
    g_send, g_recv, g_update, g_decode, loss = finish(corner, spot ^ 3, shapes, scale, outs)
    return g_send, g_recv, g_update, g_decode, loss[0, 0]


def solution(mesh):
    return jax.shard_map(
        per_device,
        mesh=mesh,
        in_specs=(
            P("ens", "dom", None), P(None, "dom"), P("dom"), P("dom"), P(None, "dom"), P(None, "dom"),
            P("dom", None), P("dom", None), P(), P(), P(), P(),
        ),
        out_specs=(P(), P(), P(), P(), P()),
        check_vma=False,
    )
```

time: 231 us -> 159 us (0.69)
  blocking collectives: 76.9 us -> 0 us
  starting transfers between devices: 31.8 us -> 44.9 us
  Pallas kernels: 68.1 us -> 64.7 us
  waiting for transfers between devices: 42.8 us -> 40.1 us
    all_gather x2 -> x0, blocking collectives: 76.9 us -> none  [the longest x1 67.7 us: per_device(): lax.all_gather(term[:, :128] + term[:, 128:256] + term[:, 256:384] + term...]
    ppermute x5 -> x12, starting transfers between devices: 0.78 us -> 7.51 us  [flip(): return lax.ppermute(value, axis, [(i, i ^ bit) for i in range(size)])]
    ppermute x20, starting transfers between devices: 31 us -> 37.3 us  [along(): lax.ppermute(value, axis, [(i, (i + steps) % size) for i in range(size)])]
    pallas_call x1, Pallas kernels: 16 us -> 10 us  [per_device(): pl.pallas_call(functools.partial(readout_kernel, line_span), grid=(steps,...]
    ppermute x20, waiting for transfers between devices: 20.6 us -> 14.9 us  [along(): lax.ppermute(value, axis, [(i, (i + steps) % size) for i in range(size)])]
    ppermute x0 -> x2, waiting for transfers between devices: none -> 3.07 us  [crossed(): return lax.ppermute(value, ('ens', 'dom'), pairs)]
    pallas_call x1 -> x5, Pallas kernels: 16.1 us -> 18.3 us  [the longest x4 9.81 us: finish(): pl.pallas_call(functools.partial(finish_kernel, scale), grid_spec=pltpu.P...]
    unnamed x48 -> x67, local copies, waits for them, and re-layouts: 5.69 us -> 6.8 us
  transfers between devices with their start and end apart: 25 -> 34, of which waited for: 13 -> 18; matrix products, arithmetic and copies ran while one was open for 1% -> 0% of each run, Pallas kernels for 7% -> 12%
where the time goes in v2:
time: 159 us; the launch traced here: 158 us
  Pallas kernels  64.7 us (41%)
  starting transfers between devices  44.9 us (28%)
  waiting for transfers between devices  40.1 us (25%)
  local copies, waits for them, and re-layouts  6.81 us (4%)
    ppermute x20, starting transfers between devices, along(): lax.ppermute(value, axis, [(i, (i + steps) % size) for i in range(size)])  37.3 us
    pallas_call x8, Pallas kernels, call(): pl.pallas_call(kernel, out_shape=outs, in_specs=[SCALAR] * scalars + vmem...  36.3 us
    ppermute x12, waiting for transfers between devices, flip(): return lax.ppermute(value, axis, [(i, i ^ bit) for i in range(size)])  22.1 us
    ppermute x20, waiting for transfers between devices, along(): lax.ppermute(value, axis, [(i, (i + steps) % size) for i in range(size)])  14.9 us
    pallas_call x1, Pallas kernels, per_device(): pl.pallas_call(functools.partial(readout_kernel, line_span), grid=(steps,...  10 us
    pallas_call x4, Pallas kernels, finish(): pl.pallas_call(functools.partial(finish_kernel, scale), grid_spec=pltpu.P...  9.81 us
    pallas_call x1, Pallas kernels, per_device(): pl.pallas_call(decoder_kernel, grid_spec=pltpu.PrefetchScalarGridSpec(num...  8.51 us
    ppermute x12, starting transfers between devices, flip(): return lax.ppermute(value, axis, [(i, i ^ bit) for i in range(size)])  7.51 us
  transfers between devices with their start and end apart: 34, of which 18 were waited for; matrix products, arithmetic and copies ran while one was open for 0% of the time, Pallas kernels for 12%

profile of v2, /device:TPU:0, one launch (start us, length us, event | category | flops | bytes accessed | tf_op | source)
XLA Modules:
  0.0 157.6 jit_solution(5964296217038021312)
XLA Ops:
  0.6 2.2 %shard_map.155 = (bf16[512,512]{1,0:T(8,128)(2,1)}, bf16[512,128]{1,0:T(8,128)(2,1)}, bf16[512,128]{1,0:T(8,128)(2,1)}) custom-call(bf16[512,512]{1,0:T(8,128)(2,1)} %bitcast.11, s32[1,128]{1,0:T(1,128)} %bitcast.12, s32[1,128]{1,0:T(1,128)} %bitcast.15), custom_call_target="tpu_custom_call" | custom-call | flops 134217728 | bytes 1311744 | tf_op jit(solution)/shard_map/pallas_call | solution.py:305
  2.9 3.0 %collective-permute-start = (bf16[512,128]{1,0:T(8,128)(2,1)}, bf16[512,128]{1,0:T(8,128)(2,1)S(1)}, u32[]{:S(2)}, u32[]{:S(2)}) collective-permute-start(bf16[512,128]{1,0:T(8,128)(2,1)} %get-tuple-element.65), channel_id=1, source_target_pairs={{0,1},{1,2},{2,3},{3,4},{4,5},{5,6},{6,7},{7,0},{8,9},{9,10},{10,1... | collective-permute-start | bytes 393224 | tf_op jit(solution)/shard_map/ppermute | solution.py:294
  5.8 3.0 %collective-permute-start.1 = (bf16[512,128]{1,0:T(8,128)(2,1)}, bf16[512,128]{1,0:T(8,128)(2,1)S(1)}, u32[]{:S(2)}, u32[]{:S(2)}) collective-permute-start(bf16[512,128]{1,0:T(8,128)(2,1)} %get-tuple-element.66), channel_id=1, source_target_pairs={{0,7},{1,0},{2,1},{3,2},{4,3},{5,4},{6,5},{7,6},{8,15},{9,8},{10,9... | collective-permute-start | bytes 393224 | tf_op jit(solution)/shard_map/ppermute | solution.py:294
  8.9 3.2 %shard_map.156 = (bf16[512,512]{1,0:T(8,128)(2,1)}, bf16[512,512]{1,0:T(8,128)(2,1)}, bf16[128,512]{1,0:T(8,128)(2,1)}, f32[512,512]{1,0:T(8,128)}) custom-call(bf16[512,512]{1,0:T(8,128)(2,1)} %w_send.1, bf16[512,512]{1,0:T(8,128)(2,1)} %w_recv.1, bf16[512,512]{1,0:T(8,128)(2,1)} %vertex.3, bf16[512,128]{1,0:T(8,128)(2,1)} %w_decode.3, ...), custom_call_target="tpu_custom_call" | custom-call | flops 268435456 | bytes 4456448 | tf_op jit(solution)/shard_map/pallas_call | solution.py:305
  12.1 0.6 collective-permute-done.from_prev
  12.7 1.1 collective-permute-done.1.from_next
  13.8 0.6 copy-done.29
  14.5 12.4 %shard_map.157 = (bf16[6,512,512]{2,1,0:T(8,128)(2,1)}, bf16[6,512,512]{2,1,0:T(8,128)(2,1)}, f32[512,512]{1,0:T(8,128)}, bf16[512,512]{1,0:T(8,128)(2,1)}, f32[...) custom-call(bf16[512,512]{1,0:T(8,128)(2,1)} %get-tuple-element.64.n, ...), custom_call_target="tpu_custom_call" | custom-call | flops 4026531840 | bytes 12661760 | tf_op jit(solution)/shard_map/pallas_call | solution.py:305
  26.9 0.3 collective-permute-start.5
  27.2 4.4 %collective-permute-start.6 = (bf16[128,128]{1,0:T(8,128)(2,1)}, bf16[128,128]{1,0:T(8,128)(2,1)S(1)}, u32[]{:S(2)}, u32[]{:S(2)}) collective-permute-start(bf16[128,128]{1,0:T(8,128)(2,1)} %get-tuple-element.73), channel_id=1, source_target_pairs={{0,7},{1,0},{2,1},{3,2},{4,3},{5,4},{6,5},{7,6},{8,15},{9,8},{10,9... | collective-permute-start | bytes 98312 | tf_op jit(solution)/shard_map/ppermute | solution.py:294
  31.6 2.1 %collective-permute-done.5 = bf16[128,128]{1,0:T(8,128)(2,1)S(1)} collective-permute-done((bf16[128,128]{1,0:T(8,128)(2,1)}, bf16[128,128]{1,0:T(8,128)(2,1)S(1)}, u32[]{:S(2)}, u32[]{:S(2)}) %collective-permute-start.5) | collective-permute-done | bytes 32800 | tf_op jit(solution)/shard_map/ppermute | solution.py:294
  33.9 0.5 collective-permute-start.2
  34.4 1.5 collective-permute-start.3
  35.8 1.4 collective-permute-start.8
  37.3 0.6 collective-permute-start.9
  37.9 8.5 %shard_map.158 = (bf16[768,2048]{1,0:T(8,128)(2,1)}, bf16[768,2048]{1,0:T(8,128)(2,1)}, bf16[128,2048]{1,0:T(8,128)(2,1)}, bf16[128,2048]{1,0:T(8,128)(2,1)}) custom-call(s32[1]{0:T(128)} %bitcast.3.core.half, s32[3,4096]{1,0:T(4,128)} %vertices.1, f32[3,4096]{1,0:T(4,128)} %weights.1, bf16[4096,128]{1,0:T(8,128)(2,1)} %base.1, bf16[4096,128]{1,0:T(8,128)(2,1)} %truth.1, ...), custom_call_target="tpu_custom_call" | custom-call | flops 15728640 | bytes 16000000 | tf_op jit(solution)/shard_map/pallas_call | solution.py:403
  46.5 0.5 copy-done.31
  47.2 10.0 %shard_map.159 = (f32[128,512]{1,0:T(8,128)}, f32[128,128]{1,0:T(8,128)}, f32[128,128]{1,0:T(8,128)}, f32[128,512]{1,0:T(8,128)}, f32[128,128]{1,0:T(8,128)}, /*index=5*/f32[128,128]{1,0:T(8,128)}, f32[8,512]{1,0:T(8,128)}) custom-call(bf16[128,512]{1,0:T(8,128)(2,1)} %get-tuple-element.71.after.refs_0_, bf16[128,512]{1,0:T(8,128)(2,1)} %copy-done.25, ...), custom_call_target="tpu_custom_call" | custom-call | flops 3221225472 | bytes 14000000 | tf_op jit(solution)/shard_map/pallas_call | solution.py:419
  57.5 4.8 %collective-permute-start.11 = (f32[128,128]{1,0:T(8,128)}, f32[128,128]{1,0:T(8,128)S(1)}, u32[]{:S(2)}, u32[]{:S(2)}) collective-permute-start(f32[128,128]{1,0:T(8,128)} %get-tuple-element.80), channel_id=1, source_target_pairs={{0,7},{1,0},{2,1},{3,2},{4,3},{5,4},{6,5},{7,6},{8,15},{9,8},{10,9... | collective-permute-start | bytes 196616 | tf_op jit(solution)/shard_map/ppermute | solution.py:294
  62.2 1.6 %collective-permute-start.13 = (f32[128,128]{1,0:T(8,128)}, f32[128,128]{1,0:T(8,128)S(1)}, u32[]{:S(2)}, u32[]{:S(2)}) collective-permute-start(f32[128,128]{1,0:T(8,128)} %get-tuple-element.82), channel_id=1, source_target_pairs={{0,1},{1,2},{2,3},{3,4},{4,5},{5,6},{6,7},{7,0},{8,9},{9,10},{10,1... | collective-permute-start | bytes 196616 | tf_op jit(solution)/shard_map/ppermute | solution.py:294
  64.0 1.0 collective-permute-done.11.next_a
  65.0 1.7 %collective-permute-done.12.next_b = f32[128,128]{1,0:T(8,128)S(1)} collective-permute-done((f32[128,128]{1,0:T(8,128)}, f32[128,128]{1,0:T(8,128)S(1)}, u32[]{:S(2)}, u32[]{:S(2)}) %collective-permute-start.12) | collective-permute-done | bytes 65568 | tf_op jit(solution)/shard_map/ppermute | solution.py:289
  66.7 2.7 %collective-permute-done.13.prev_a = f32[128,128]{1,0:T(8,128)S(1)} collective-permute-done((f32[128,128]{1,0:T(8,128)}, f32[128,128]{1,0:T(8,128)S(1)}, u32[]{:S(2)}, u32[]{:S(2)}) %collective-permute-start.13) | collective-permute-done | bytes 65568 | tf_op jit(solution)/shard_map/ppermute | solution.py:294
  69.4 1.4 collective-permute-done.14.prev_b
  70.8 0.6 copy-done.9
  71.5 9.5 %shard_map.160 = (f32[256,1792]{1,0:T(8,128)}, bf16[256,1792]{1,0:T(8,128)(2,1)}) custom-call(s32[1]{0:T(128)} %bitcast.3.core.half, f32[128,512]{1,0:T(8,128)} %get-tuple-element.78.own_mid, f32[128,512]{1,0:T(8,128)} %copy-done.5, f32[128,128]{1,0:T(8,128)} %copy-done.6, f32[128,128]{1,0:T(8,128)} %copy-done.7, f32[128,128]{1,0:T(8,128)} %copy-done.8, ...), custom_call_target="tpu_custom_call" | custom-call | flops 2415919104 | bytes 14173188 | tf_op jit(solution)/shard_map/pallas_call | solution.py:305
  81.2 2.5 %collective-permute-done.15.got = bf16[256,1792]{1,0:T(8,128)(2,1)S(1)} collective-permute-done((bf16[256,1792]{1,0:T(8,128)(2,1)}, bf16[256,1792]{1,0:T(8,128)(2,1)S(1)}, u32[]{:S(2)}, u32[]{:S(2)}) %collective-permute-start.15) | collective-permute-done | bytes 917536 | tf_op jit(solution)/shard_map/ppermute | solution.py:299
  83.7 0.9 copy-done
  84.6 3.1 %shard_map.161 = (f32[128,1792]{1,0:T(8,128)}, bf16[128,1792]{1,0:T(8,128)(2,1)}) custom-call(s32[1]{0:T(128)} %bitcast.2.half, f32[256,1792]{1,0:T(8,128)} %get-tuple-element.91.mine, bf16[256,1792]{1,0:T(8,128)(2,1)} %copy-done), custom_call_target="tpu_custom_call" | custom-call | bytes 4128772 | tf_op jit(solution)/shard_map/pallas_call | solution.py:305
  87.8 1.5 collective-permute-start.16
  89.3 11.3 %collective-permute-done.16.got = bf16[128,1792]{1,0:T(8,128)(2,1)S(1)} collective-permute-done((bf16[128,1792]{1,0:T(8,128)(2,1)}, bf16[128,1792]{1,0:T(8,128)(2,1)S(1)}, u32[]{:S(2)}, u32[]{:S(2)}) %collective-permute-start.16) | collective-permute-done | bytes 458784 | tf_op jit(solution)/shard_map/ppermute | solution.py:299
  100.6 0.8 copy-done.1
  101.3 2.2 %shard_map.162 = (f32[16,1792]{1,0:T(8,128)}, bf16[16,1792]{1,0:T(8,128)(2,1)}, bf16[16,1792]{1,0:T(8,128)(2,1)}, bf16[16,1792]{1,0:T(8,128)(2,1)}, bf16[16,1792...) custom-call(s32[1]{0:T(128)} %bitcast.1.here, ...), custom_call_target="tpu_custom_call" | custom-call | bytes 1892356 | tf_op jit(solution)/shard_map/pallas_call | solution.py:305
  103.6 1.5 collective-permute-start.19
  105.1 3.7 %collective-permute-start.20 = (bf16[16,1792]{1,0:T(8,128)(2,1)}, bf16[16,1792]{1,0:T(8,128)(2,1)S(1)}, u32[]{:S(2)}, u32[]{:S(2)}) collective-permute-start(bf16[16,1792]{1,0:T(8,128)(2,1)} %get-tuple-element.99), channel_id=1, source_target_pairs={{0,4},{1,5},{2,6},{3,7},{4,0},{5,1},{6,2},{7,3},{8,12},{9,13},{10,... | collective-permute-start | bytes 172040 | tf_op jit(solution)/shard_map/ppermute | solution.py:294
  108.8 1.0 collective-permute-start.21
  109.9 1.2 collective-permute-done.17.refs_1_
  111.1 0.8 collective-permute-start.22
  111.8 1.4 collective-permute-start.23
  113.2 1.4 collective-permute-done.19.refs_3_
  114.6 1.8 %collective-permute-done.21.refs_5_ = bf16[16,1792]{1,0:T(8,128)(2,1)S(1)} collective-permute-done((bf16[16,1792]{1,0:T(8,128)(2,1)}, bf16[16,1792]{1,0:T(8,128)(2,1)S(1)}, u32[]{:S(2)}, u32[]{:S(2)}) %collective-permute-start.21) | collective-permute-done | bytes 57376 | tf_op jit(solution)/shard_map/ppermute | solution.py:294
  116.6 0.5 copy-done.16
  117.2 1.8 %shard_map.163.refs_0_ = bf16[16,1792]{1,0:T(8,128)(2,1)} custom-call(f32[16,1792]{1,0:T(8,128)} %get-tuple-element.95.refs_0_, bf16[16,1792]{1,0:T(8,128)(2,1)} %copy-done.10, bf16[16,1792]{1,0:T(8,128)(2,1)} %copy-done.11, bf16[16,1792]{1,0:T(8,128)(2,1)} %copy-done.12, bf16[16,1792]{1,0:T(8,128)(2,1)} %copy-done.14, bf16[16,1792]{1,0:T(8,128)(2,1)} %copy-done.16, ...), custom_call_target="tpu_custom_call" | custom-call | bytes 573440 | tf_op jit(solution)/shard_map/pallas_call | solution.py:305
  118.9 2.1 %collective-permute-start.24 = (bf16[16,1792]{1,0:T(8,128)(2,1)}, bf16[16,1792]{1,0:T(8,128)(2,1)S(1)}, u32[]{:S(2)}, u32[]{:S(2)}) collective-permute-start(bf16[16,1792]{1,0:T(8,128)(2,1)} %shard_map.163.refs_0_), channel_id=1, source_target_pairs={{0,1},{1,2},{2,3},{3,4},{4,5},{5,6},{6,7},{7,0},{8,9},{9,10},{10,1... | collective-permute-start | bytes 172040 | tf_op jit(solution)/shard_map/ppermute | solution.py:294
  121.0 2.0 %collective-permute-start.25 = (bf16[16,1792]{1,0:T(8,128)(2,1)}, bf16[16,1792]{1,0:T(8,128)(2,1)S(1)}, u32[]{:S(2)}, u32[]{:S(2)}) collective-permute-start(bf16[16,1792]{1,0:T(8,128)(2,1)} %shard_map.163.refs_0_), channel_id=1, source_target_pairs={{0,2},{1,3},{2,4},{3,5},{4,6},{5,7},{6,0},{7,1},{8,10},{9,11},{10,... | collective-permute-start | bytes 172040 | tf_op jit(solution)/shard_map/ppermute | solution.py:294
  122.9 0.4 collective-permute-start.26
  123.3 2.5 %collective-permute-start.27 = (bf16[16,1792]{1,0:T(8,128)(2,1)}, bf16[16,1792]{1,0:T(8,128)(2,1)S(1)}, u32[]{:S(2)}, u32[]{:S(2)}) collective-permute-start(bf16[16,1792]{1,0:T(8,128)(2,1)} %shard_map.163.refs_0_), channel_id=1, source_target_pairs={{0,4},{1,5},{2,6},{3,7},{4,0},{5,1},{6,2},{7,3},{8,12},{9,13},{10,... | collective-permute-start | bytes 172040 | tf_op jit(solution)/shard_map/ppermute | solution.py:294
  125.8 2.4 %collective-permute-start.28 = (bf16[16,1792]{1,0:T(8,128)(2,1)}, bf16[16,1792]{1,0:T(8,128)(2,1)S(1)}, u32[]{:S(2)}, u32[]{:S(2)}) collective-permute-start(bf16[16,1792]{1,0:T(8,128)(2,1)} %shard_map.163.refs_0_), channel_id=1, source_target_pairs={{0,5},{1,6},{2,7},{3,0},{4,1},{5,2},{6,3},{7,4},{8,13},{9,14},{10,... | collective-permute-start | bytes 172040 | tf_op jit(solution)/shard_map/ppermute | solution.py:294
  128.2 0.9 collective-permute-start.29
  129.1 1.5 collective-permute-start.30
  130.6 0.5 collective-permute-done.27.refs_4_
  131.1 1.3 collective-permute-done.28.refs_5_
  132.3 0.8 collective-permute-done.29.refs_6_
  133.1 0.4 collective-permute-done.30.refs_7_
  133.7 0.6 copy-done.23
  134.3 1.8 %shard_map.164.piece = bf16[128,1792]{1,0:T(8,128)(2,1)} custom-call(s32[1]{0:T(128)} %bitcast.1.here, bf16[16,1792]{1,0:T(8,128)(2,1)} %shard_map.163.refs_0_, bf16[16,1792]{1,0:T(8,128)(2,1)} %copy-done.13, bf16[16,1792]{1,0:T(8,128)(2,1)} %copy-done.15, bf16[16,1792]{1,0:T(8,128)(2,1)} %copy-done.17, bf16[16,1792]{1,0:T(8,128)(2,1)} %copy-done.18, ...), custom_call_target="tpu_custom_call" | custom-call | bytes 917508 | tf_op jit(solution)/shard_map/pallas_call | solution.py:305
  136.2 1.5 collective-permute-start.31
  137.7 8.3 %collective-permute-done.31.piece = bf16[128,1792]{1,0:T(8,128)(2,1)S(1)} collective-permute-done((bf16[128,1792]{1,0:T(8,128)(2,1)}, bf16[128,1792]{1,0:T(8,128)(2,1)S(1)}, u32[]{:S(2)}, u32[]{:S(2)}) %collective-permute-start.31) | collective-permute-done | bytes 458784 | tf_op jit(solution)/shard_map/ppermute | solution.py:299
  146.0 2.1 %shard_map.165 = (f32[512,512]{1,0:T(8,128)}, f32[512,512]{1,0:T(8,128)}, f32[512,512]{1,0:T(8,128)}, f32[512,128]{1,0:T(8,128)}, f32[1,1]{1,0:T(1,128)}) custom-call(s32[1]{0:T(128)} %bitcast.9.place, bf16[128,1792]{1,0:T(8,128)(2,1)} %shard_map.164.piece), custom_call_target="tpu_custom_call" | custom-call | bytes 1376256 | tf_op jit(solution)/shard_map/pallas_call | solution.py:268
  148.1 0.8 copy-done.4
  148.9 2.6 %shard_map.166 = (f32[512,512]{1,0:T(8,128)}, f32[512,512]{1,0:T(8,128)}, f32[512,512]{1,0:T(8,128)}, f32[512,128]{1,0:T(8,128)}, f32[1,1]{1,0:T(1,128)}) custom-call(s32[1]{0:T(128)} %bitcast.8.place, bf16[128,1792]{1,0:T(8,128)(2,1)} %copy-done.4, ...), custom_call_target="tpu_custom_call", output_to_operand_aliasing={{0}: (2, {}), {1}: (3, {}), {2}: (4, {}), {3}: (5, {})} | custom-call | bytes 1376256 | tf_op jit(solution)/shard_map/pallas_call | solution.py:268
  151.5 2.6 %shard_map.167 = (f32[512,512]{1,0:T(8,128)}, f32[512,512]{1,0:T(8,128)}, f32[512,512]{1,0:T(8,128)}, f32[512,128]{1,0:T(8,128)}, f32[1,1]{1,0:T(1,128)}) custom-call(s32[1]{0:T(128)} %bitcast.7.place, bf16[128,1792]{1,0:T(8,128)(2,1)} %copy-done.2, ...), custom_call_target="tpu_custom_call", output_to_operand_aliasing={{0}: (2, {}), {1}: (3, {}), {2}: (4, {}), {3}: (5, {})} | custom-call | bytes 1376256 | tf_op jit(solution)/shard_map/pallas_call | solution.py:268
  154.1 0.8 copy-done.3
  154.9 2.6 %shard_map.168 = (f32[512,512]{1,0:T(8,128)}, f32[512,512]{1,0:T(8,128)}, f32[512,512]{1,0:T(8,128)}, f32[512,128]{1,0:T(8,128)}, f32[1,1]{1,0:T(1,128)}) custom-call(s32[1]{0:T(128)} %bitcast.place, bf16[128,1792]{1,0:T(8,128)(2,1)} %copy-done.3, ...), custom_call_target="tpu_custom_call", output_to_operand_aliasing={{0}: (2, {}), {1}: (3, {}), {2}: (4, {}), {3}: (5, {})} | custom-call | bytes 1376256 | tf_op jit(solution)/shard_map/pallas_call | solution.py:268
  (86 shorter events, 1.5 us)
Async XLA Ops:
  2.9 9.8 %collective-permute-start = (bf16[512,128]{1,0:T(8,128)(2,1)}, bf16[512,128]{1,0:T(8,128)(2,1)S(1)}, u32[]{:S(2)}, u32[]{:S(2)}) collective-permute-start(bf16[512,128]{1,0:T(8,128)(2,1)} %get-tuple-element.65), channel_id=1, source_target_pairs={{0,1},{1,2},{2,3},{3,4},{4,5},{5,6},{6,7},{7,0},{8,9},{9,10},{10,1... | collective-permute-start | bytes 393224 | tf_op jit(solution)/shard_map/ppermute | solution.py:294
  5.8 8.0 %collective-permute-start.1 = (bf16[512,128]{1,0:T(8,128)(2,1)}, bf16[512,128]{1,0:T(8,128)(2,1)S(1)}, u32[]{:S(2)}, u32[]{:S(2)}) collective-permute-start(bf16[512,128]{1,0:T(8,128)(2,1)} %get-tuple-element.66), channel_id=1, source_target_pairs={{0,7},{1,0},{2,1},{3,2},{4,3},{5,4},{6,5},{7,6},{8,15},{9,8},{10,9... | collective-permute-start | bytes 393224 | tf_op jit(solution)/shard_map/ppermute | solution.py:294
  12.7 1.1 copy-start.28
  13.8 0.7 copy-start.29
  26.9 6.8 %collective-permute-start.5 = (bf16[128,128]{1,0:T(8,128)(2,1)}, bf16[128,128]{1,0:T(8,128)(2,1)S(1)}, u32[]{:S(2)}, u32[]{:S(2)}) collective-permute-start(bf16[128,128]{1,0:T(8,128)(2,1)} %get-tuple-element.72), channel_id=1, source_target_pairs={{0,1},{1,2},{2,3},{3,4},{4,5},{5,6},{6,7},{7,0},{8,9},{9,10},{10,1... | collective-permute-start | bytes 98312 | tf_op jit(solution)/shard_map/ppermute | solution.py:294
  27.2 6.5 %collective-permute-start.6 = (bf16[128,128]{1,0:T(8,128)(2,1)}, bf16[128,128]{1,0:T(8,128)(2,1)S(1)}, u32[]{:S(2)}, u32[]{:S(2)}) collective-permute-start(bf16[128,128]{1,0:T(8,128)(2,1)} %get-tuple-element.73), channel_id=1, source_target_pairs={{0,7},{1,0},{2,1},{3,2},{4,3},{5,4},{6,5},{7,6},{8,15},{9,8},{10,9... | collective-permute-start | bytes 98312 | tf_op jit(solution)/shard_map/ppermute | solution.py:294
  33.8 12.7 %copy-start.24 = (bf16[128,256]{1,0:T(8,128)(2,1)}, bf16[128,256]{1,0:T(8,128)(2,1)S(1)}, u32[]{:S(2)}) copy-start(bf16[128,256]{1,0:T(8,128)(2,1)S(1)} %constant_dynamic-update-slice_fusion.refs_4_) | copy-start | bytes 196612
  33.8 3.5 %collective-permute-start.7 = (bf16[128,256]{1,0:T(8,128)(2,1)S(1)}, bf16[128,256]{1,0:T(8,128)(2,1)S(1)}, u32[]{:S(2)}, u32[]{:S(2)}) collective-permute-start(bf16[128,256]{1,0:T(8,128)(2,1)S(1)} %constant_dynamic-update-slice_fusion.refs_4_), channel_id=1, source_target_pairs={{0,8},{8,0},{16,24},{24,16},{1,9},{9,1},{17,25},{25,17},{2,10},{10... | collective-permute-start | bytes 196616 | tf_op jit(solution)/shard_map/ppermute | solution.py:299
  33.9 12.6 %collective-permute-start.2 = (bf16[128,512]{1,0:T(8,128)(2,1)}, bf16[128,512]{1,0:T(8,128)(2,1)S(1)}, u32[]{:S(2)}, u32[]{:S(2)}) collective-permute-start(bf16[128,512]{1,0:T(8,128)(2,1)} %get-tuple-element.71.after.refs_0_), channel_id=1, source_target_pairs={{0,8},{8,0},{16,24},{24,16},{1,9},{9,1},{17,25},{25,17},{2,10},{10... | collective-permute-start | bytes 393224 | tf_op jit(solution)/shard_map/ppermute | solution.py:299
  34.4 12.1 %collective-permute-start.3 = (bf16[128,512]{1,0:T(8,128)(2,1)}, bf16[128,512]{1,0:T(8,128)(2,1)S(1)}, u32[]{:S(2)}, u32[]{:S(2)}) collective-permute-start(bf16[128,512]{1,0:T(8,128)(2,1)} %get-tuple-element.71.after.refs_0_), channel_id=1, source_target_pairs={{0,16},{8,24},{16,0},{24,8},{1,17},{9,25},{17,1},{25,9},{2,18},{10... | collective-permute-start | bytes 393224 | tf_op jit(solution)/shard_map/ppermute | solution.py:299
  35.8 10.6 %collective-permute-start.4 = (bf16[128,512]{1,0:T(8,128)(2,1)}, bf16[128,512]{1,0:T(8,128)(2,1)S(1)}, u32[]{:S(2)}, u32[]{:S(2)}) collective-permute-start(bf16[128,512]{1,0:T(8,128)(2,1)} %get-tuple-element.71.after.refs_0_), channel_id=1, source_target_pairs={{0,24},{8,16},{16,8},{24,0},{1,25},{9,17},{17,9},{25,1},{2,26},{10... | collective-permute-start | bytes 393224 | tf_op jit(solution)/shard_map/ppermute | solution.py:299
  35.8 10.5 %collective-permute-start.8 = (bf16[128,256]{1,0:T(8,128)(2,1)S(1)}, bf16[128,256]{1,0:T(8,128)(2,1)S(1)}, u32[]{:S(2)}, u32[]{:S(2)}) collective-permute-start(bf16[128,256]{1,0:T(8,128)(2,1)S(1)} %constant_dynamic-update-slice_fusion.refs_4_), channel_id=1, source_target_pairs={{0,16},{8,24},{16,0},{24,8},{1,17},{9,25},{17,1},{25,9},{2,18},{10... | collective-permute-start | bytes 196616 | tf_op jit(solution)/shard_map/ppermute | solution.py:299
  37.3 9.2 %copy-start.30 = (bf16[128,256]{1,0:T(8,128)(2,1)}, bf16[128,256]{1,0:T(8,128)(2,1)S(1)}, u32[]{:S(2)}) copy-start(bf16[128,256]{1,0:T(8,128)(2,1)S(1)} %collective-permute-done.7.refs_5_) | copy-start | bytes 196612
  37.3 9.1 %collective-permute-start.9 = (bf16[128,256]{1,0:T(8,128)(2,1)S(1)}, bf16[128,256]{1,0:T(8,128)(2,1)S(1)}, u32[]{:S(2)}, u32[]{:S(2)}) collective-permute-start(bf16[128,256]{1,0:T(8,128)(2,1)S(1)} %constant_dynamic-update-slice_fusion.refs_4_), channel_id=1, source_target_pairs={{0,24},{8,16},{16,8},{24,0},{1,25},{9,17},{17,9},{25,1},{2,26},{10... | collective-permute-start | bytes 196616 | tf_op jit(solution)/shard_map/ppermute | solution.py:299
  46.4 0.6 copy-start.31
  46.4 0.6 copy-start.32
  46.4 0.7 copy-start.25
  46.4 0.7 copy-start.26
  46.5 0.7 copy-start.27
  57.2 13.6 %collective-permute-start.10 = (f32[128,512]{1,0:T(8,128)}, f32[128,512]{1,0:T(8,128)S(1)}, u32[]{:S(2)}, u32[]{:S(2)}) collective-permute-start(f32[128,512]{1,0:T(8,128)} %get-tuple-element.79), channel_id=1, source_target_pairs={{0,8},{8,0},{16,24},{24,16},{1,9},{9,1},{17,25},{25,17},{2,10},{10... | collective-permute-start | bytes 786440 | tf_op jit(solution)/shard_map/ppermute | solution.py:299
  57.5 7.5 %collective-permute-start.11 = (f32[128,128]{1,0:T(8,128)}, f32[128,128]{1,0:T(8,128)S(1)}, u32[]{:S(2)}, u32[]{:S(2)}) collective-permute-start(f32[128,128]{1,0:T(8,128)} %get-tuple-element.80), channel_id=1, source_target_pairs={{0,7},{1,0},{2,1},{3,2},{4,3},{5,4},{6,5},{7,6},{8,15},{9,8},{10,9... | collective-permute-start | bytes 196616 | tf_op jit(solution)/shard_map/ppermute | solution.py:294
  62.2 4.4 %collective-permute-start.12 = (f32[128,128]{1,0:T(8,128)}, f32[128,128]{1,0:T(8,128)S(1)}, u32[]{:S(2)}, u32[]{:S(2)}) collective-permute-start(f32[128,128]{1,0:T(8,128)} %get-tuple-element.81), channel_id=1, source_target_pairs={{0,15},{1,8},{2,9},{3,10},{4,11},{5,12},{6,13},{7,14},{8,7},{9,0},... | collective-permute-start | bytes 196616 | tf_op jit(solution)/shard_map/ppermute | solution.py:289
  62.2 7.2 %collective-permute-start.13 = (f32[128,128]{1,0:T(8,128)}, f32[128,128]{1,0:T(8,128)S(1)}, u32[]{:S(2)}, u32[]{:S(2)}) collective-permute-start(f32[128,128]{1,0:T(8,128)} %get-tuple-element.82), channel_id=1, source_target_pairs={{0,1},{1,2},{2,3},{3,4},{4,5},{5,6},{6,7},{7,0},{8,9},{9,10},{10,1... | collective-permute-start | bytes 196616 | tf_op jit(solution)/shard_map/ppermute | solution.py:294
  63.8 7.0 %collective-permute-start.14 = (f32[128,128]{1,0:T(8,128)}, f32[128,128]{1,0:T(8,128)S(1)}, u32[]{:S(2)}, u32[]{:S(2)}) collective-permute-start(f32[128,128]{1,0:T(8,128)} %get-tuple-element.83), channel_id=1, source_target_pairs={{0,9},{1,10},{2,11},{3,12},{4,13},{5,14},{6,15},{7,8},{8,1},{9,2},... | collective-permute-start | bytes 196616 | tf_op jit(solution)/shard_map/ppermute | solution.py:289
  65.0 5.8 %copy-start.6 = (f32[128,128]{1,0:T(8,128)}, f32[128,128]{1,0:T(8,128)S(1)}, u32[]{:S(2)}) copy-start(f32[128,128]{1,0:T(8,128)S(1)} %collective-permute-done.11.next_a) | copy-start | bytes 196612
  66.7 4.1 %copy-start.7 = (f32[128,128]{1,0:T(8,128)}, f32[128,128]{1,0:T(8,128)S(1)}, u32[]{:S(2)}) copy-start(f32[128,128]{1,0:T(8,128)S(1)} %collective-permute-done.12.next_b) | copy-start | bytes 196612
  69.4 1.4 copy-start.8
  70.8 0.7 copy-start.5
  81.0 2.7 %collective-permute-start.15 = (bf16[256,1792]{1,0:T(8,128)(2,1)}, bf16[256,1792]{1,0:T(8,128)(2,1)S(1)}, u32[]{:S(2)}, u32[]{:S(2)}) collective-permute-start(bf16[256,1792]{1,0:T(8,128)(2,1)} %get-tuple-element.92), channel_id=1, source_target_pairs={{0,8},{8,0},{16,24},{24,16},{1,9},{9,1},{17,25},{25,17},{2,10},{10... | collective-permute-start | bytes 2752520 | tf_op jit(solution)/shard_map/ppermute | solution.py:299
  83.7 0.9 copy-start
  87.8 12.8 %collective-permute-start.16 = (bf16[128,1792]{1,0:T(8,128)(2,1)}, bf16[128,1792]{1,0:T(8,128)(2,1)S(1)}, u32[]{:S(2)}, u32[]{:S(2)}) collective-permute-start(bf16[128,1792]{1,0:T(8,128)(2,1)} %get-tuple-element.94), channel_id=1, source_target_pairs={{0,16},{8,24},{16,0},{24,8},{1,17},{9,25},{17,1},{25,9},{2,18},{10... | collective-permute-start | bytes 1376264 | tf_op jit(solution)/shard_map/ppermute | solution.py:299
  100.6 0.8 copy-start.1
  103.5 7.5 %collective-permute-start.17 = (bf16[16,1792]{1,0:T(8,128)(2,1)}, bf16[16,1792]{1,0:T(8,128)(2,1)S(1)}, u32[]{:S(2)}, u32[]{:S(2)}) collective-permute-start(bf16[16,1792]{1,0:T(8,128)(2,1)} %get-tuple-element.96), channel_id=1, source_target_pairs={{0,1},{1,2},{2,3},{3,4},{4,5},{5,6},{6,7},{7,0},{8,9},{9,10},{10,1... | collective-permute-start | bytes 172040 | tf_op jit(solution)/shard_map/ppermute | solution.py:294
  103.5 8.3 %collective-permute-start.18 = (bf16[16,1792]{1,0:T(8,128)(2,1)}, bf16[16,1792]{1,0:T(8,128)(2,1)S(1)}, u32[]{:S(2)}, u32[]{:S(2)}) collective-permute-start(bf16[16,1792]{1,0:T(8,128)(2,1)} %get-tuple-element.97), channel_id=1, source_target_pairs={{0,2},{1,3},{2,4},{3,5},{4,6},{5,7},{6,0},{7,1},{8,10},{9,11},{10,... | collective-permute-start | bytes 172040 | tf_op jit(solution)/shard_map/ppermute | solution.py:294
  103.6 11.0 %collective-permute-start.19 = (bf16[16,1792]{1,0:T(8,128)(2,1)}, bf16[16,1792]{1,0:T(8,128)(2,1)S(1)}, u32[]{:S(2)}, u32[]{:S(2)}) collective-permute-start(bf16[16,1792]{1,0:T(8,128)(2,1)} %get-tuple-element.98), channel_id=1, source_target_pairs={{0,3},{1,4},{2,5},{3,6},{4,7},{5,0},{6,1},{7,2},{8,11},{9,12},{10,... | collective-permute-start | bytes 172040 | tf_op jit(solution)/shard_map/ppermute | solution.py:294
  105.1 9.5 %collective-permute-start.20 = (bf16[16,1792]{1,0:T(8,128)(2,1)}, bf16[16,1792]{1,0:T(8,128)(2,1)S(1)}, u32[]{:S(2)}, u32[]{:S(2)}) collective-permute-start(bf16[16,1792]{1,0:T(8,128)(2,1)} %get-tuple-element.99), channel_id=1, source_target_pairs={{0,4},{1,5},{2,6},{3,7},{4,0},{5,1},{6,2},{7,3},{8,12},{9,13},{10,... | collective-permute-start | bytes 172040 | tf_op jit(solution)/shard_map/ppermute | solution.py:294
  108.8 7.6 %collective-permute-start.21 = (bf16[16,1792]{1,0:T(8,128)(2,1)}, bf16[16,1792]{1,0:T(8,128)(2,1)S(1)}, u32[]{:S(2)}, u32[]{:S(2)}) collective-permute-start(bf16[16,1792]{1,0:T(8,128)(2,1)} %get-tuple-element.100), channel_id=1, source_target_pairs={{0,5},{1,6},{2,7},{3,0},{4,1},{5,2},{6,3},{7,4},{8,13},{9,14},{10,... | collective-permute-start | bytes 172040 | tf_op jit(solution)/shard_map/ppermute | solution.py:294
  111.1 5.5 %copy-start.10 = (bf16[16,1792]{1,0:T(8,128)(2,1)}, bf16[16,1792]{1,0:T(8,128)(2,1)S(1)}, u32[]{:S(2)}) copy-start(bf16[16,1792]{1,0:T(8,128)(2,1)S(1)} %collective-permute-done.17.refs_1_) | copy-start | bytes 172036
  111.1 5.4 %collective-permute-start.22 = (bf16[16,1792]{1,0:T(8,128)(2,1)}, bf16[16,1792]{1,0:T(8,128)(2,1)S(1)}, u32[]{:S(2)}, u32[]{:S(2)}) collective-permute-start(bf16[16,1792]{1,0:T(8,128)(2,1)} %get-tuple-element.101), channel_id=1, source_target_pairs={{0,6},{1,7},{2,0},{3,1},{4,2},{5,3},{6,4},{7,5},{8,14},{9,15},{10,... | collective-permute-start | bytes 172040 | tf_op jit(solution)/shard_map/ppermute | solution.py:294
  111.8 4.7 %copy-start.11 = (bf16[16,1792]{1,0:T(8,128)(2,1)}, bf16[16,1792]{1,0:T(8,128)(2,1)S(1)}, u32[]{:S(2)}) copy-start(bf16[16,1792]{1,0:T(8,128)(2,1)S(1)} %collective-permute-done.18.refs_2_) | copy-start | bytes 172036
  111.8 4.7 %collective-permute-start.23 = (bf16[16,1792]{1,0:T(8,128)(2,1)}, bf16[16,1792]{1,0:T(8,128)(2,1)S(1)}, u32[]{:S(2)}, u32[]{:S(2)}) collective-permute-start(bf16[16,1792]{1,0:T(8,128)(2,1)} %get-tuple-element.102), channel_id=1, source_target_pairs={{0,7},{1,0},{2,1},{3,2},{4,3},{5,4},{6,5},{7,6},{8,15},{9,8},{10,9... | collective-permute-start | bytes 172040 | tf_op jit(solution)/shard_map/ppermute | solution.py:294
  114.6 1.9 %copy-start.12 = (bf16[16,1792]{1,0:T(8,128)(2,1)}, bf16[16,1792]{1,0:T(8,128)(2,1)S(1)}, u32[]{:S(2)}) copy-start(bf16[16,1792]{1,0:T(8,128)(2,1)S(1)} %collective-permute-done.19.refs_3_) | copy-start | bytes 172036
  114.6 1.9 %copy-start.14 = (bf16[16,1792]{1,0:T(8,128)(2,1)}, bf16[16,1792]{1,0:T(8,128)(2,1)S(1)}, u32[]{:S(2)}) copy-start(bf16[16,1792]{1,0:T(8,128)(2,1)S(1)} %collective-permute-done.20.refs_4_) | copy-start | bytes 172036
  116.4 0.6 copy-start.16
  116.4 0.7 copy-start.19
  118.9 9.3 %collective-permute-start.24 = (bf16[16,1792]{1,0:T(8,128)(2,1)}, bf16[16,1792]{1,0:T(8,128)(2,1)S(1)}, u32[]{:S(2)}, u32[]{:S(2)}) collective-permute-start(bf16[16,1792]{1,0:T(8,128)(2,1)} %shard_map.163.refs_0_), channel_id=1, source_target_pairs={{0,1},{1,2},{2,3},{3,4},{4,5},{5,6},{6,7},{7,0},{8,9},{9,10},{10,1... | collective-permute-start | bytes 172040 | tf_op jit(solution)/shard_map/ppermute | solution.py:294
  121.0 8.2 %collective-permute-start.25 = (bf16[16,1792]{1,0:T(8,128)(2,1)}, bf16[16,1792]{1,0:T(8,128)(2,1)S(1)}, u32[]{:S(2)}, u32[]{:S(2)}) collective-permute-start(bf16[16,1792]{1,0:T(8,128)(2,1)} %shard_map.163.refs_0_), channel_id=1, source_target_pairs={{0,2},{1,3},{2,4},{3,5},{4,6},{5,7},{6,0},{7,1},{8,10},{9,11},{10,... | collective-permute-start | bytes 172040 | tf_op jit(solution)/shard_map/ppermute | solution.py:294
  122.9 7.7 %collective-permute-start.26 = (bf16[16,1792]{1,0:T(8,128)(2,1)}, bf16[16,1792]{1,0:T(8,128)(2,1)S(1)}, u32[]{:S(2)}, u32[]{:S(2)}) collective-permute-start(bf16[16,1792]{1,0:T(8,128)(2,1)} %shard_map.163.refs_0_), channel_id=1, source_target_pairs={{0,3},{1,4},{2,5},{3,6},{4,7},{5,0},{6,1},{7,2},{8,11},{9,12},{10,... | collective-permute-start | bytes 172040 | tf_op jit(solution)/shard_map/ppermute | solution.py:294
  123.3 7.8 %collective-permute-start.27 = (bf16[16,1792]{1,0:T(8,128)(2,1)}, bf16[16,1792]{1,0:T(8,128)(2,1)S(1)}, u32[]{:S(2)}, u32[]{:S(2)}) collective-permute-start(bf16[16,1792]{1,0:T(8,128)(2,1)} %shard_map.163.refs_0_), channel_id=1, source_target_pairs={{0,4},{1,5},{2,6},{3,7},{4,0},{5,1},{6,2},{7,3},{8,12},{9,13},{10,... | collective-permute-start | bytes 172040 | tf_op jit(solution)/shard_map/ppermute | solution.py:294
  125.8 6.5 %collective-permute-start.28 = (bf16[16,1792]{1,0:T(8,128)(2,1)}, bf16[16,1792]{1,0:T(8,128)(2,1)S(1)}, u32[]{:S(2)}, u32[]{:S(2)}) collective-permute-start(bf16[16,1792]{1,0:T(8,128)(2,1)} %shard_map.163.refs_0_), channel_id=1, source_target_pairs={{0,5},{1,6},{2,7},{3,0},{4,1},{5,2},{6,3},{7,4},{8,13},{9,14},{10,... | collective-permute-start | bytes 172040 | tf_op jit(solution)/shard_map/ppermute | solution.py:294
  128.2 5.3 %copy-start.13 = (bf16[16,1792]{1,0:T(8,128)(2,1)}, bf16[16,1792]{1,0:T(8,128)(2,1)S(1)}, u32[]{:S(2)}) copy-start(bf16[16,1792]{1,0:T(8,128)(2,1)S(1)} %collective-permute-done.24.refs_1_) | copy-start | bytes 172036
  128.2 4.9 %collective-permute-start.29 = (bf16[16,1792]{1,0:T(8,128)(2,1)}, bf16[16,1792]{1,0:T(8,128)(2,1)S(1)}, u32[]{:S(2)}, u32[]{:S(2)}) collective-permute-start(bf16[16,1792]{1,0:T(8,128)(2,1)} %shard_map.163.refs_0_), channel_id=1, source_target_pairs={{0,6},{1,7},{2,0},{3,1},{4,2},{5,3},{6,4},{7,5},{8,14},{9,15},{10,... | collective-permute-start | bytes 172040 | tf_op jit(solution)/shard_map/ppermute | solution.py:294
  129.1 4.4 %copy-start.15 = (bf16[16,1792]{1,0:T(8,128)(2,1)}, bf16[16,1792]{1,0:T(8,128)(2,1)S(1)}, u32[]{:S(2)}) copy-start(bf16[16,1792]{1,0:T(8,128)(2,1)S(1)} %collective-permute-done.25.refs_2_) | copy-start | bytes 172036
  129.1 4.4 %collective-permute-start.30 = (bf16[16,1792]{1,0:T(8,128)(2,1)}, bf16[16,1792]{1,0:T(8,128)(2,1)S(1)}, u32[]{:S(2)}, u32[]{:S(2)}) collective-permute-start(bf16[16,1792]{1,0:T(8,128)(2,1)} %shard_map.163.refs_0_), channel_id=1, source_target_pairs={{0,7},{1,0},{2,1},{3,2},{4,3},{5,4},{6,5},{7,6},{8,15},{9,8},{10,9... | collective-permute-start | bytes 172040 | tf_op jit(solution)/shard_map/ppermute | solution.py:294
  130.6 2.9 %copy-start.17 = (bf16[16,1792]{1,0:T(8,128)(2,1)}, bf16[16,1792]{1,0:T(8,128)(2,1)S(1)}, u32[]{:S(2)}) copy-start(bf16[16,1792]{1,0:T(8,128)(2,1)S(1)} %collective-permute-done.26.refs_3_) | copy-start | bytes 172036
  131.1 2.4 %copy-start.18 = (bf16[16,1792]{1,0:T(8,128)(2,1)}, bf16[16,1792]{1,0:T(8,128)(2,1)S(1)}, u32[]{:S(2)}) copy-start(bf16[16,1792]{1,0:T(8,128)(2,1)S(1)} %collective-permute-done.27.refs_4_) | copy-start | bytes 172036
  132.3 1.2 copy-start.20
  133.7 0.6 copy-start.23
  136.2 9.8 %collective-permute-start.31 = (bf16[128,1792]{1,0:T(8,128)(2,1)}, bf16[128,1792]{1,0:T(8,128)(2,1)S(1)}, u32[]{:S(2)}, u32[]{:S(2)}) collective-permute-start(bf16[128,1792]{1,0:T(8,128)(2,1)} %shard_map.164.piece), channel_id=1, source_target_pairs={{0,16},{8,24},{16,0},{24,8},{1,17},{9,25},{17,1},{25,9},{2,18},{10... | collective-permute-start | bytes 1376264 | tf_op jit(solution)/shard_map/ppermute | solution.py:299
  137.7 10.4 %collective-permute-start.33 = (bf16[128,1792]{1,0:T(8,128)(2,1)}, bf16[128,1792]{1,0:T(8,128)(2,1)S(1)}, u32[]{:S(2)}, u32[]{:S(2)}) collective-permute-start(bf16[128,1792]{1,0:T(8,128)(2,1)} %shard_map.164.piece), channel_id=1, source_target_pairs={{0,8},{8,0},{16,24},{24,16},{1,9},{9,1},{17,25},{25,17},{2,10},{10... | collective-permute-start | bytes 1376264 | tf_op jit(solution)/shard_map/ppermute | solution.py:299
  146.0 5.5 %copy-start.2 = (bf16[128,1792]{1,0:T(8,128)(2,1)}, bf16[128,1792]{1,0:T(8,128)(2,1)S(1)}, u32[]{:S(2)}) copy-start(bf16[128,1792]{1,0:T(8,128)(2,1)S(1)} %collective-permute-done.31.piece) | copy-start | bytes 1376260
  146.0 8.1 %collective-permute-start.32 = (bf16[128,1792]{1,0:T(8,128)(2,1)S(1)}, bf16[128,1792]{1,0:T(8,128)(2,1)S(1)}, u32[]{:S(2)}, u32[]{:S(2)}) collective-permute-start(bf16[128,1792]{1,0:T(8,128)(2,1)S(1)} %collective-permute-done.31.piece), channel_id=1, source_target_pairs={{0,8},{8,0},{16,24},{24,16},{1,9},{9,1},{17,25},{25,17},{2,10},{10... | collective-permute-start | bytes 1376264 | tf_op jit(solution)/shard_map/ppermute | solution.py:299
  148.1 0.8 copy-start.4
  154.1 0.8 copy-start.3
  (3 other events, 1.9 us)

commit v3 on v2

--- a/solution.py
+++ b/solution.py
@@ -107,12 +107,11 @@
 def readout_kernel(line_span, *refs):
     mids, ends = refs[0:4], refs[4:8]
     mat_hi, mat_lo, base_t, truth_t = refs[8:12]
-    own_mid, own_next, own_prev, pair_mid, pair_next, pair_prev, loss = refs[12:19]
-    table, grad = refs[19:21]
+    own_mid, own_end, pair_mid, pair_end, loss = refs[12:17]
+    table, grad = refs[17:19]
     step = pl.program_id(0)
     members = len(mids)
     variables, count = own_mid.shape
-    halo = own_next.shape[1]
 
     @pl.when(step == 0)
     def _():
@@ -158,11 +157,17 @@
 
     @pl.when(step == pl.num_programs(0) - 1)
     def _():
-        for i, (mid, after, before) in enumerate(((own_mid, own_next, own_prev), (pair_mid, pair_next, pair_prev))):
+        for i, (mid, end) in enumerate(((own_mid, own_end), (pair_mid, pair_end))):
             rows = slice(i * variables, (i + 1) * variables)
             mid[...] = grad[rows, :count]
-            after[...] = grad[rows, count : count + halo]
-            before[...] = grad[rows, count + halo :]
+            end[...] = grad[rows, count:]
+
+
+def ends_kernel(mine, got, after, before):
+    halo = after.shape[1]
+    total = mine[...] + got[...]
+    after[...] = total[:, :halo]
+    before[...] = total[:, halo:]
 
 
 def split(value):
@@ -183,14 +188,14 @@
 
 
 def backward_kernel(
-    half, own_mid, pair_mid, next_a, next_b, prev_a, prev_b, to_next, to_prev, term, w_decode, vertex, nodes_t,
+    parts, own_mid, pair_mid, from_next, from_prev, to_next, to_prev, term, w_decode, vertex, nodes_t,
     picked_t, slope_t, slope_sum_t, agg_t, upd_slope_t, hidden_t,
-    keep, send, whole,
+    keep, send_far, send_near, whole,
 ):
     count = nodes_t.shape[1]
     width = nodes_t.shape[0]
     grad_z = own_mid[...] + pair_mid[...]
-    for got, rows in ((next_a[...] + next_b[...], to_next), (prev_a[...] + prev_b[...], to_prev)):
+    for got, rows in ((from_next[...], to_next), (from_prev[...], to_prev)):
         place = one_hot(count, rows[...])
         hi, lo = split(got)
         grad_z += dot_nt(hi, place) + dot_nt(lo, place)
@@ -210,27 +215,37 @@
     whole[:, main:] = jnp.zeros((width, LANES), F32)
     spot = (lax.broadcasted_iota(jnp.int32, (8, LANES), 0) == 0) & (lax.broadcasted_iota(jnp.int32, (8, LANES), 1) == 0)
     whole[0:8, main:] = jnp.where(spot, jnp.sum(term[...]), 0.0)
-    rows = keep.shape[0]
-    keep[...] = whole[pl.ds(pl.multiple_of(half[0] * rows, rows), rows), :]
-    send[...] = encoded(whole[pl.ds(pl.multiple_of((1 - half[0]) * rows, rows), rows), :])
-
-
-def halve_kernel(half, mine, got, keep, send, total):
-    total[...] = mine[...] + got[...].astype(F32)
-    rows = keep.shape[0]
-    keep[...] = total[pl.ds(pl.multiple_of(half[0] * rows, rows), rows), :]
-    send[...] = encoded(total[pl.ds(pl.multiple_of((1 - half[0]) * rows, rows), rows), :])
-
-
-def shares_kernel(here, mine, got, *outs):
-    total = outs[-1]
-    total[...] = mine[...] + got[...].astype(F32)
-    parts = len(outs) - 1
+    ens, dom = lax.axis_index("ens"), lax.axis_index("dom")
+    core, chip = lax.rem(ens, 2), lax.div(ens, 2)
+    rows = send_far.shape[0]
+    share = rows // parts
+
+    def block(c, x, k):
+        start = ((2 * c + x) * parts + lax.rem(dom + k, parts)) * share
+        return whole[pl.ds(pl.multiple_of(start, share), share), :]
+
+    for place, k in enumerate(list(range(1, parts)) + [0]):
+        here = slice(place * share, (place + 1) * share)
+        there = slice(rows + place * share, rows + (place + 1) * share)
+        keep[here, :] = block(core, chip, k)
+        keep[there, :] = block(core, 1 - chip, k)
+        send_far[here, :] = encoded(block(1 - core, 1 - chip, k))
+        send_near[here, :] = encoded(block(1 - core, chip, k))
+
+
+def chip_kernel(mine, got, first, second):
+    total = encoded(mine[...] + got[...].astype(F32))
+    rows = first.shape[0]
+    first[...] = total[:rows]
+    second[...] = total[rows:]
+
+
+def shares_kernel(mine, near, far, *outs):
+    total = mine[...] + near[...].astype(F32) + far[...].astype(F32)
     rows = outs[0].shape[0]
-    for k in range(parts):
-        place = lax.rem(here[0] + k, parts)
-        block = total[pl.ds(pl.multiple_of(place * rows, rows), rows), :]
-        outs[k][...] = encoded(block) if k else block
+    for k, out in enumerate(outs):
+        block = total[k * rows : (k + 1) * rows]
+        out[...] = encoded(block) if out.dtype == BF16 else block
 
 
 def sum_kernel(*refs):
@@ -240,53 +255,41 @@
     refs[-1][...] = encoded(total)
 
 
-def line_up_kernel(here, *refs):
-    out = refs[-1]
-    parts = len(refs) - 1
+def join_kernel(*refs):
     rows = refs[0].shape[0]
-    for k in range(parts):
-        place = lax.rem(here[0] + (parts - k), parts)
-        out[pl.ds(pl.multiple_of(place * rows, rows), rows), :] = refs[k][...]
-
-
-def finish_kernel(scale, place, piece, *refs):
+    for k, ref in enumerate(refs[:-1]):
+        refs[-1][k * rows : (k + 1) * rows, :] = ref[...]
+
+
+def finish_kernel(scale, parts, *refs):
     g_send, g_recv, g_update, g_decode, loss = refs[-5:]
+    pieces = refs[:-5]
     width = g_send.shape[1]
-    g_send[...] = piece[:, :width].astype(F32)
-    g_recv[...] = piece[:, width : 2 * width].astype(F32)
-    g_update[...] = piece[:, 2 * width : 3 * width].astype(F32)
-    g_decode[...] = piece[:, 3 * width : -LANES].astype(F32)
-    part = jnp.sum(piece[:, -LANES:].astype(F32)) * scale
-    loss[0, 0] = part if len(refs) == 5 else refs[4][0, 0] + part
-
-
-def finish(piece, place, shapes, scale, before=()):
-    rows = piece.shape[0]
-    block = lambda shape: pl.BlockSpec((rows, shape.shape[1]), lambda i, at: (at[0], 0))
-    cell = pl.BlockSpec(memory_space=pltpu.SMEM)
-    whole = pl.BlockSpec(memory_space=pl.ANY)
-    return pl.pallas_call(
-        functools.partial(finish_kernel, scale),
-        grid_spec=pltpu.PrefetchScalarGridSpec(
-            num_scalar_prefetch=1,
-            grid=(1,),
-            in_specs=[pl.BlockSpec(piece.shape, lambda i, at: (0, 0))] + ([whole] * 4 + [cell] if before else []),
-            out_specs=[block(s) for s in shapes] + [cell],
-        ),
-        out_shape=list(shapes) + [sds((1, 1), F32)],
-        input_output_aliases={2 + i: i for i in range(4)} if before else {},
-        compiler_params=params(),
-        cost_estimate=cost(0, 6 * piece.size),
-    )(scalar(place), piece, *before)
+    turn = parts if parts > 1 else 2
+    share = width // 4 // turn
+    ens, dom = lax.axis_index("ens"), lax.axis_index("dom")
+    spot = 2 * lax.rem(ens, 2) + lax.div(ens, 2)
+    total = jnp.zeros((share, LANES), F32)
+    each = len(pieces) // 4
+    for q, other in enumerate((0, 2, 1, 3)):
+        quarter = lax.bitwise_xor(spot, other)
+        step = 0
+        for piece in pieces[q * each : (q + 1) * each]:
+            for j in range(piece.shape[0] // share):
+                spin = lax.rem(dom + parts - step, parts) if parts > 1 else step
+                start = (quarter * turn + spin) * share
+                place = pl.ds(pl.multiple_of(start, share), share)
+                block = piece[j * share : (j + 1) * share, :].astype(F32)
+                g_send[place, :] = block[:, :width]
+                g_recv[place, :] = block[:, width : 2 * width]
+                g_update[place, :] = block[:, 2 * width : 3 * width]
+                g_decode[place, :] = block[:, 3 * width : -LANES]
+                total += block[:, -LANES:]
+                step += 1
+    loss[0, 0] = jnp.sum(total) * scale
 
 
 SCALAR = pl.BlockSpec(memory_space=pltpu.SMEM)
-
-
-def crossed(value, bit, steps):
-    ens, dom = lax.axis_size("ens"), lax.axis_size("dom")
-    pairs = [(e * dom + d, (e ^ bit) * dom + (d + steps) % dom) for e in range(ens) for d in range(dom)]
-    return lax.ppermute(value, ("ens", "dom"), pairs)
 
 
 def along(value, axis, steps):
@@ -317,35 +320,49 @@
     return jnp.reshape(value, (1,)).astype(jnp.int32)
 
 
-def reduced(keep, send, ens, dom):
-    parts = lax.axis_size("dom")
-    rows, cols = keep.shape
-    got = flip(send, "ens", 1)
-    keep, send = call(
-        halve_kernel,
-        [scalar(ens // 2), keep, got],
-        [sds((rows // 2, cols), F32), sds((rows // 2, cols), BF16)],
-        [pltpu.VMEM((rows, cols), F32)],
-        scalars=1,
-    )
-    rows //= 2
-    got = flip(send, "ens", 2)
-    share = rows // parts
-    if share % 16:
-        total = lax.psum(keep + got.astype(F32), "dom")
-        return call(sum_kernel, [total], [sds((rows, cols), BF16)])[0]
-    shares = call(
-        shares_kernel,
-        [scalar(dom), keep, got],
-        [sds((share, cols), F32)] + [sds((share, cols), BF16)] * (parts - 1),
-        [pltpu.VMEM((rows, cols), F32)],
-        scalars=1,
-    )
-    terms = [shares[0]] + [along(shares[k], "dom", k) for k in range(1, parts)]
-    (own,) = call(sum_kernel, terms, [sds((share, cols), BF16)])
+def reduced(keep, send_far, send_near, parts):
+    quarter, cols = send_far.shape
+    half, share = quarter // 2, quarter // parts
+    got_far, got_near = flip(send_far, "ens", 1), flip(send_near, "ens", 1)
+    whole = lambda x: pl.BlockSpec(x.shape, lambda i: (0, 0))
+    rows = lambda size, at: pl.BlockSpec((size, cols), lambda i: (at, 0))
+    piece = sds((half, cols), BF16)
+    first, second = pl.pallas_call(
+        chip_kernel,
+        grid=(1,),
+        out_shape=[piece, piece],
+        in_specs=[rows(quarter, 1), whole(got_far)],
+        out_specs=[whole(piece)] * 2,
+        compiler_params=params(),
+        cost_estimate=cost(0, 8 * keep.size),
+    )(keep, got_far)
+    first, second = flip(first, "ens", 2), flip(second, "ens", 2)
+
+    def shares(at, far, outs):
+        return pl.pallas_call(
+            shares_kernel,
+            grid=(1,),
+            out_shape=outs,
+            in_specs=[rows(half, at), rows(half, at), whole(far)],
+            out_specs=[whole(x) for x in outs],
+            compiler_params=params(),
+            cost_estimate=cost(0, 8 * keep.size),
+        )(keep, got_near, far)
+
+    if parts == 1:
+        sums = [shares(at, far, [sds((half, cols), F32)])[0] for at, far in enumerate((first, second))]
+        return [call(sum_kernel, [lax.psum(x, "dom")], [piece])[0] for x in sums]
+    terms = []
+    count = half // share
+    for at, far in enumerate((first, second)):
+        outs = [sds((share, cols), BF16)] * count
+        if at == 1:
+            outs[-1] = sds((share, cols), F32)
+        steps = range(at * count + 1, at * count + 1 + count)
+        terms += [along(x, "dom", k) if k < parts else x for k, x in zip(steps, shares(at, far, outs))]
+    (own,) = call(sum_kernel, terms[::-1], [sds((share, cols), BF16)])
     pieces = [own] + [along(own, "dom", k) for k in range(1, parts)]
-    (quarter,) = call(line_up_kernel, [scalar(dom)] + pieces, [sds((rows, cols), BF16)], scalars=1)
-    return quarter
+    return [call(join_kernel, pieces[at * count : (at + 1) * count], [piece])[0] for at in range(2)]
 
 
 def per_device(
@@ -419,43 +436,48 @@
     grads = pl.pallas_call(
         functools.partial(readout_kernel, line_span),
         grid=(steps,),
-        out_shape=[sds((variables, count), F32), sds((variables, halo), F32), sds((variables, halo), F32)] * 2 + [sds((8, block), F32)],
+        out_shape=[sds((variables, count), F32), sds((variables, 2 * halo), F32)] * 2 + [sds((8, block), F32)],
         in_specs=[fixed((variables, count))] * members + [fixed((variables, 2 * halo))] * members + [
             tall(ext_rows), tall(ext_rows), tall(variables), tall(variables),
         ],
-        out_specs=[fixed((variables, count)), fixed((variables, halo)), fixed((variables, halo))] * 2 + [fixed((8, block))],
+        out_specs=[fixed((variables, count)), fixed((variables, 2 * halo))] * 2 + [fixed((8, block))],
         scratch_shapes=[pltpu.VMEM((members * variables, ext_rows), BF16), pltpu.VMEM((2 * variables, ext_rows), F32)],
         compiler_params=params(),
         cost_estimate=cost(4 * members * variables * ext_rows * half_span, 14e6),
     )(*mids, *ends, mat_hi, mat_lo, base_t, truth_t)
-    own_mid, own_next, own_prev, pair_mid, pair_next, pair_prev, term = grads
-    next_a, prev_a = along(own_next, "dom", -1), along(own_prev, "dom", 1)
-    next_b, prev_b = crossed(pair_next, 1, -1), crossed(pair_prev, 1, 1)
-    pair_mid = flip(pair_mid, "ens", 1)
+    own_mid, own_end, pair_mid, pair_end, term = grads
+    got_end = flip(pair_end, "ens", 1)
+    got_mid = flip(pair_mid, "ens", 1)
+    to_before, to_after = call(ends_kernel, [own_end, got_end], [sds((variables, halo), F32)] * 2)
+    from_next, from_prev = along(to_before, "dom", -1), along(to_after, "dom", 1)
 
     cols = 3 * width + variables + LANES
-    keep, send = call(
-        backward_kernel,
+    quarter = width // 4
+    parts = lax.axis_size("dom")
+    if quarter % (16 * parts):
+        parts = 1
+    keep, send_far, send_near = call(
+        functools.partial(backward_kernel, parts),
         [
-            core, own_mid, pair_mid, next_a, next_b, prev_a, prev_b, to_next, to_prev, term, w_decode,
+            own_mid, got_mid, from_next, from_prev, to_next, to_prev, term, w_decode,
             vertex_refresh_matrix, nodes_t, picked_t, slope_t, slope_sum_t, agg_t, upd_slope_t, hidden_t,
         ],
-        [sds((width // 2, cols), F32), sds((width // 2, cols), BF16)],
+        [sds((2 * quarter, cols), F32), sds((quarter, cols), BF16), sds((quarter, cols), BF16)],
         [pltpu.VMEM((width, cols), F32)],
         flops=2 * (degree + 3) * width * width * count,
-        scalars=1,
     )
-    quarter = reduced(keep, send, ens, dom)
-    across = flip(quarter, "ens", 2)
-    beside = flip(quarter, "ens", 1)
-    corner = flip(across, "ens", 1)
-    spot = 2 * lax.rem(ens, 2) + ens // 2
-    shapes = [sds((width, width), F32)] * 3 + [sds((width, variables), F32)]
-    scale = 1.0 / line_span
-    outs = finish(quarter, spot, shapes, scale)
-    outs = finish(beside, spot ^ 2, shapes, scale, outs)
-    outs = finish(across, spot ^ 1, shapes, scale, outs)
-    g_send, g_recv, g_update, g_decode, loss = finish(corner, spot ^ 3, shapes, scale, outs)
+    mine = reduced(keep, send_far, send_near, parts)
+    across = [flip(x, "ens", 2) for x in mine]
+    beside = [flip(x, "ens", 1) for x in mine]
+    corner = [flip(x, "ens", 1) for x in across]
+    g_send, g_recv, g_update, g_decode, loss = pl.pallas_call(
+        functools.partial(finish_kernel, 1.0 / line_span, parts),
+        out_shape=[sds((width, width), F32)] * 3 + [sds((width, variables), F32), sds((1, 1), F32)],
+        in_specs=vmem(8),
+        out_specs=vmem(4) + [SCALAR],
+        compiler_params=params(),
+        cost_estimate=cost(0, 6 * width * cols),
+    )(*mine, *beside, *across, *corner)
     return g_send, g_recv, g_update, g_decode, loss[0, 0]
 
 

time: 159 us -> 148 us (0.931)
  waiting for transfers between devices: 40.1 us -> 34.6 us
  starting transfers between devices: 44.9 us -> 41.9 us
  Pallas kernels: 64.7 us -> 62 us
    ppermute x20, starting transfers between devices: 37.3 us -> 32.1 us  [along(): lax.ppermute(value, axis, [(i, (i + steps) % size) for i in range(size)])]
    ppermute x12 -> x18, waiting for transfers between devices: 22.1 us -> 17.6 us  [flip(): return lax.ppermute(value, axis, [(i, i ^ bit) for i in range(size)])]
    ppermute x2 -> x0, waiting for transfers between devices: 3.07 us -> none  [crossed(): return lax.ppermute(value, ('ens', 'dom'), pairs)]
    pallas_call x8, Pallas kernels: 36.3 us -> 33.9 us  [call(): pl.pallas_call(kernel, out_shape=outs, in_specs=[SCALAR] * scalars + vmem...]
    ppermute x12 -> x18, starting transfers between devices: 7.51 us -> 9.72 us  [flip(): return lax.ppermute(value, axis, [(i, i ^ bit) for i in range(size)])]
    ppermute x20, waiting for transfers between devices: 14.9 us -> 17 us  [along(): lax.ppermute(value, axis, [(i, (i + steps) % size) for i in range(size)])]
    unnamed x67 -> x75, local copies, waits for them, and re-layouts: 6.8 us -> 7.77 us
  transfers between devices with their start and end apart: 34 -> 38, of which waited for: 18 -> 18; matrix products, arithmetic and copies ran while one was open for 0% -> 0% of each run, Pallas kernels for 12% -> 15%
where the time goes in v3:
time: 148 us; the launch traced here: 147 us
  Pallas kernels  62 us (42%)
  starting transfers between devices  41.9 us (28%)
  waiting for transfers between devices  34.6 us (23%)
  local copies, waits for them, and re-layouts  7.79 us (5%)
    pallas_call x8, Pallas kernels, call(): pl.pallas_call(kernel, out_shape=outs, in_specs=[SCALAR] * scalars + vmem...  33.9 us
    ppermute x20, starting transfers between devices, along(): lax.ppermute(value, axis, [(i, (i + steps) % size) for i in range(size)])  32.1 us
    ppermute x18, waiting for transfers between devices, flip(): return lax.ppermute(value, axis, [(i, i ^ bit) for i in range(size)])  17.6 us
    ppermute x20, waiting for transfers between devices, along(): lax.ppermute(value, axis, [(i, (i + steps) % size) for i in range(size)])  17 us
    pallas_call x1, Pallas kernels, per_device(): pl.pallas_call(functools.partial(readout_kernel, line_span), grid=(steps,...  9.95 us
    ppermute x18, starting transfers between devices, flip(): return lax.ppermute(value, axis, [(i, i ^ bit) for i in range(size)])  9.72 us
    pallas_call x1, Pallas kernels, per_device(): pl.pallas_call(decoder_kernel, grid_spec=pltpu.PrefetchScalarGridSpec(num...  8.54 us
    unnamed x75, local copies, waits for them, and re-layouts  7.77 us
  transfers between devices with their start and end apart: 38, of which 18 were waited for; matrix products, arithmetic and copies ran while one was open for 0% of the time, Pallas kernels for 15%

profile of v3, /device:TPU:0, one launch (start us, length us, event | category | flops | bytes accessed | tf_op | source)
XLA Modules:
  0.0 147.4 jit_solution(17319854624534694029)
XLA Ops:
  0.6 2.2 %shard_map.155 = (bf16[512,512]{1,0:T(8,128)(2,1)}, bf16[512,128]{1,0:T(8,128)(2,1)}, bf16[512,128]{1,0:T(8,128)(2,1)}) custom-call(bf16[512,512]{1,0:T(8,128)(2,1)} %bitcast.5, s32[1,128]{1,0:T(1,128)} %bitcast.6, s32[1,128]{1,0:T(1,128)} %bitcast.9), custom_call_target="tpu_custom_call" | custom-call | flops 134217728 | bytes 1311744 | tf_op jit(solution)/shard_map/pallas_call | solution.py:308
  2.9 3.0 %collective-permute-start = (bf16[512,128]{1,0:T(8,128)(2,1)}, bf16[512,128]{1,0:T(8,128)(2,1)S(1)}, u32[]{:S(2)}, u32[]{:S(2)}) collective-permute-start(bf16[512,128]{1,0:T(8,128)(2,1)} %get-tuple-element.51), channel_id=1, source_target_pairs={{0,1},{1,2},{2,3},{3,4},{4,5},{5,6},{6,7},{7,0},{8,9},{9,10},{10,1... | collective-permute-start | bytes 393224 | tf_op jit(solution)/shard_map/ppermute | solution.py:297
  5.8 3.0 %collective-permute-start.1 = (bf16[512,128]{1,0:T(8,128)(2,1)}, bf16[512,128]{1,0:T(8,128)(2,1)S(1)}, u32[]{:S(2)}, u32[]{:S(2)}) collective-permute-start(bf16[512,128]{1,0:T(8,128)(2,1)} %get-tuple-element.52), channel_id=1, source_target_pairs={{0,7},{1,0},{2,1},{3,2},{4,3},{5,4},{6,5},{7,6},{8,15},{9,8},{10,9... | collective-permute-start | bytes 393224 | tf_op jit(solution)/shard_map/ppermute | solution.py:297
  8.9 3.2 %shard_map.156 = (bf16[512,512]{1,0:T(8,128)(2,1)}, bf16[512,512]{1,0:T(8,128)(2,1)}, bf16[128,512]{1,0:T(8,128)(2,1)}, f32[512,512]{1,0:T(8,128)}) custom-call(bf16[512,512]{1,0:T(8,128)(2,1)} %w_send.1, bf16[512,512]{1,0:T(8,128)(2,1)} %w_recv.1, bf16[512,512]{1,0:T(8,128)(2,1)} %vertex.3, bf16[512,128]{1,0:T(8,128)(2,1)} %w_decode.3, ...), custom_call_target="tpu_custom_call" | custom-call | flops 268435456 | bytes 4456448 | tf_op jit(solution)/shard_map/pallas_call | solution.py:308
  12.1 0.6 collective-permute-done.from_prev
  12.7 1.1 collective-permute-done.1.from_next
  13.8 0.6 copy-done.33
  14.5 12.4 %shard_map.157 = (bf16[6,512,512]{2,1,0:T(8,128)(2,1)}, bf16[6,512,512]{2,1,0:T(8,128)(2,1)}, f32[512,512]{1,0:T(8,128)}, bf16[512,512]{1,0:T(8,128)(2,1)}, f32[...) custom-call(bf16[512,512]{1,0:T(8,128)(2,1)} %get-tuple-element.50.n, ...), custom_call_target="tpu_custom_call" | custom-call | flops 4026531840 | bytes 12661760 | tf_op jit(solution)/shard_map/pallas_call | solution.py:308
  27.2 4.4 %collective-permute-start.6 = (bf16[128,128]{1,0:T(8,128)(2,1)}, bf16[128,128]{1,0:T(8,128)(2,1)S(1)}, u32[]{:S(2)}, u32[]{:S(2)}) collective-permute-start(bf16[128,128]{1,0:T(8,128)(2,1)} %get-tuple-element.59), channel_id=1, source_target_pairs={{0,7},{1,0},{2,1},{3,2},{4,3},{5,4},{6,5},{7,6},{8,15},{9,8},{10,9... | collective-permute-start | bytes 98312 | tf_op jit(solution)/shard_map/ppermute | solution.py:297
  31.6 2.1 %collective-permute-done.5 = bf16[128,128]{1,0:T(8,128)(2,1)S(1)} collective-permute-done((bf16[128,128]{1,0:T(8,128)(2,1)}, bf16[128,128]{1,0:T(8,128)(2,1)S(1)}, u32[]{:S(2)}, u32[]{:S(2)}) %collective-permute-start.5) | collective-permute-done | bytes 32800 | tf_op jit(solution)/shard_map/ppermute | solution.py:297
  33.8 1.7 %collective-permute-start.4 = (bf16[128,512]{1,0:T(8,128)(2,1)}, bf16[128,512]{1,0:T(8,128)(2,1)S(1)}, u32[]{:S(2)}, u32[]{:S(2)}) collective-permute-start(bf16[128,512]{1,0:T(8,128)(2,1)} %get-tuple-element.57.after.refs_0_), channel_id=1, source_target_pairs={{0,24},{8,16},{16,8},{24,0},{1,25},{9,17},{17,9},{25,1},{2,26},{10... | collective-permute-start | bytes 393224 | tf_op jit(solution)/shard_map/ppermute | solution.py:302
  35.6 1.5 %collective-permute-start.3 = (bf16[128,512]{1,0:T(8,128)(2,1)}, bf16[128,512]{1,0:T(8,128)(2,1)S(1)}, u32[]{:S(2)}, u32[]{:S(2)}) collective-permute-start(bf16[128,512]{1,0:T(8,128)(2,1)} %get-tuple-element.57.after.refs_0_), channel_id=1, source_target_pairs={{0,16},{8,24},{16,0},{24,8},{1,17},{9,25},{17,1},{25,9},{2,18},{10... | collective-permute-start | bytes 393224 | tf_op jit(solution)/shard_map/ppermute | solution.py:302
  37.1 0.5 collective-permute-start.8
  37.6 0.6 collective-permute-done.9.refs_7_
  38.4 8.5 %shard_map.158 = (bf16[768,2048]{1,0:T(8,128)(2,1)}, bf16[768,2048]{1,0:T(8,128)(2,1)}, bf16[128,2048]{1,0:T(8,128)(2,1)}, bf16[128,2048]{1,0:T(8,128)(2,1)}) custom-call(s32[1]{0:T(128)} %bitcast.3.core, s32[3,4096]{1,0:T(4,128)} %vertices.1, f32[3,4096]{1,0:T(4,128)} %weights.1, bf16[4096,128]{1,0:T(8,128)(2,1)} %base.1, bf16[4096,128]{1,0:T(8,128)(2,1)} %truth.1, ...), custom_call_target="tpu_custom_call" | custom-call | flops 15728640 | bytes 16000000 | tf_op jit(solution)/shard_map/pallas_call | solution.py:420
  47.1 0.5 copy-done.35
  47.8 9.9 %shard_map.159 = (f32[128,512]{1,0:T(8,128)}, f32[128,256]{1,0:T(8,128)}, f32[128,512]{1,0:T(8,128)}, f32[128,256]{1,0:T(8,128)}, f32[8,512]{1,0:T(8,128)}) custom-call(bf16[128,512]{1,0:T(8,128)(2,1)} %get-tuple-element.57.after.refs_0_, bf16[128,512]{1,0:T(8,128)(2,1)} %copy-done.31, bf16[128,512]{1,0:T(8,128)(2,1)} %copy-done.30, ...), custom_call_target="tpu_custom_call" | custom-call | flops 3221225472 | bytes 14000000 | tf_op jit(solution)/shard_map/pallas_call | solution.py:436
  58.3 1.4 collective-permute-done.11.got
  59.7 0.7 copy-done.11
  60.4 1.6 %shard_map.160 = (f32[128,128]{1,0:T(8,128)}, f32[128,128]{1,0:T(8,128)}) custom-call(f32[128,256]{1,0:T(8,128)} %get-tuple-element.66.mine, f32[128,256]{1,0:T(8,128)} %copy-done.11), custom_call_target="tpu_custom_call" | custom-call | bytes 393216 | tf_op jit(solution)/shard_map/pallas_call | solution.py:308
  62.0 4.7 %collective-permute-start.12 = (f32[128,128]{1,0:T(8,128)}, f32[128,128]{1,0:T(8,128)S(1)}, u32[]{:S(2)}, u32[]{:S(2)}) collective-permute-start(f32[128,128]{1,0:T(8,128)} %get-tuple-element.68), channel_id=1, source_target_pairs={{0,7},{1,0},{2,1},{3,2},{4,3},{5,4},{6,5},{7,6},{8,15},{9,8},{10,9... | collective-permute-start | bytes 196616 | tf_op jit(solution)/shard_map/ppermute | solution.py:297
  66.7 2.2 %collective-permute-done.12.from_next = f32[128,128]{1,0:T(8,128)S(1)} collective-permute-done((f32[128,128]{1,0:T(8,128)}, f32[128,128]{1,0:T(8,128)S(1)}, u32[]{:S(2)}, u32[]{:S(2)}) %collective-permute-start.12) | collective-permute-done | bytes 65568 | tf_op jit(solution)/shard_map/ppermute | solution.py:297
  69.0 4.9 %collective-permute-done.13.from_prev = f32[128,128]{1,0:T(8,128)S(1)} collective-permute-done((f32[128,128]{1,0:T(8,128)}, f32[128,128]{1,0:T(8,128)S(1)}, u32[]{:S(2)}, u32[]{:S(2)}) %collective-permute-start.13) | collective-permute-done | bytes 65568 | tf_op jit(solution)/shard_map/ppermute | solution.py:297
  73.9 0.6 copy-done.13
  74.7 9.4 %shard_map.161 = (f32[256,1792]{1,0:T(8,128)}, bf16[128,1792]{1,0:T(8,128)(2,1)}, bf16[128,1792]{1,0:T(8,128)(2,1)}) custom-call(f32[128,512]{1,0:T(8,128)} %get-tuple-element.64.own_mid, f32[128,512]{1,0:T(8,128)} %copy-done.2, f32[128,128]{1,0:T(8,128)} %copy-done.12, f32[128,128]{1,0:T(8,128)} %copy-done.13, s32[1,128]{1,0:T(1,128)} %bitcast.8, ...), custom_call_target="tpu_custom_call" | custom-call | flops 2415919104 | bytes 14042112 | tf_op jit(solution)/shard_map/pallas_call | solution.py:308
  84.0 0.5 collective-permute-start.14
  84.6 1.5 %collective-permute-done.15.got = bf16[128,1792]{1,0:T(8,128)(2,1)S(1)} collective-permute-done((bf16[128,1792]{1,0:T(8,128)(2,1)}, bf16[128,1792]{1,0:T(8,128)(2,1)S(1)}, u32[]{:S(2)}, u32[]{:S(2)}) %collective-permute-start.15) | collective-permute-done | bytes 458784 | tf_op jit(solution)/shard_map/ppermute | solution.py:302
  86.1 0.8 copy-done.1
  86.8 2.1 %shard_map.162 = (bf16[64,1792]{1,0:T(8,128)(2,1)}, bf16[64,1792]{1,0:T(8,128)(2,1)}) custom-call(f32[256,1792]{1,0:T(8,128)} %get-tuple-element.77.mine, bf16[128,1792]{1,0:T(8,128)(2,1)} %copy-done.1), custom_call_target="tpu_custom_call" | custom-call | bytes 3670016 | tf_op jit(solution)/shard_map/pallas_call | solution.py:330
  89.0 0.9 collective-permute-start.16
  89.9 1.1 collective-permute-start.20
  91.0 6.6 %collective-permute-done.16.far = bf16[64,1792]{1,0:T(8,128)(2,1)S(1)} collective-permute-done((bf16[64,1792]{1,0:T(8,128)(2,1)}, bf16[64,1792]{1,0:T(8,128)(2,1)S(1)}, u32[]{:S(2)}, u32[]{:S(2)}) %collective-permute-start.16) | collective-permute-done | bytes 229408 | tf_op jit(solution)/shard_map/ppermute | solution.py:302
  97.6 0.7 copy-done.4
  98.3 2.0 %shard_map.163 = (bf16[16,1792]{1,0:T(8,128)(2,1)}, bf16[16,1792]{1,0:T(8,128)(2,1)}, bf16[16,1792]{1,0:T(8,128)(2,1)}, f32[16,1792]{1,0:T(8,128)}) custom-call(f32[256,1792]{1,0:T(8,128)} %get-tuple-element.77.mine, bf16[128,1792]{1,0:T(8,128)(2,1)} %copy-done, bf16[64,1792]{1,0:T(8,128)(2,1)} %copy-done.4), custom_call_target="tpu_custom_call" | custom-call | bytes 3670016 | tf_op jit(solution)/shard_map/pallas_call | solution.py:342
  100.4 1.4 collective-permute-done.20.far
  101.8 0.7 copy-done.3
  102.4 2.0 %shard_map.164 = (bf16[16,1792]{1,0:T(8,128)(2,1)}, bf16[16,1792]{1,0:T(8,128)(2,1)}, bf16[16,1792]{1,0:T(8,128)(2,1)}, bf16[16,1792]{1,0:T(8,128)(2,1)}) custom-call(f32[256,1792]{1,0:T(8,128)} %get-tuple-element.77.mine, bf16[128,1792]{1,0:T(8,128)(2,1)} %copy-done, bf16[64,1792]{1,0:T(8,128)(2,1)} %copy-done.3), custom_call_target="tpu_custom_call" | custom-call | bytes 3670016 | tf_op jit(solution)/shard_map/pallas_call | solution.py:342
  104.4 2.9 %collective-permute-start.21 = (bf16[16,1792]{1,0:T(8,128)(2,1)}, bf16[16,1792]{1,0:T(8,128)(2,1)S(1)}, u32[]{:S(2)}, u32[]{:S(2)}) collective-permute-start(bf16[16,1792]{1,0:T(8,128)(2,1)} %get-tuple-element.86), channel_id=1, source_target_pairs={{0,4},{1,5},{2,6},{3,7},{4,0},{5,1},{6,2},{7,3},{8,12},{9,13},{10,... | collective-permute-start | bytes 172040 | tf_op jit(solution)/shard_map/ppermute | solution.py:297
  107.4 2.1 %collective-permute-start.23 = (bf16[16,1792]{1,0:T(8,128)(2,1)}, bf16[16,1792]{1,0:T(8,128)(2,1)S(1)}, u32[]{:S(2)}, u32[]{:S(2)}) collective-permute-start(bf16[16,1792]{1,0:T(8,128)(2,1)} %get-tuple-element.88), channel_id=1, source_target_pairs={{0,2},{1,3},{2,4},{3,5},{4,6},{5,7},{6,0},{7,1},{8,10},{9,11},{10,... | collective-permute-start | bytes 172040 | tf_op jit(solution)/shard_map/ppermute | solution.py:297
  109.4 1.4 collective-permute-start.24
  110.9 0.9 collective-permute-done.21.refs_4_
  111.7 1.9 %collective-permute-done.22.refs_5_ = bf16[16,1792]{1,0:T(8,128)(2,1)S(1)} collective-permute-done((bf16[16,1792]{1,0:T(8,128)(2,1)}, bf16[16,1792]{1,0:T(8,128)(2,1)S(1)}, u32[]{:S(2)}, u32[]{:S(2)}) %collective-permute-start.22) | collective-permute-done | bytes 57376 | tf_op jit(solution)/shard_map/ppermute | solution.py:297
  113.6 0.5 collective-permute-done.23.refs_6_
  114.2 2.3 %collective-permute-done.24.refs_7_ = bf16[16,1792]{1,0:T(8,128)(2,1)S(1)} collective-permute-done((bf16[16,1792]{1,0:T(8,128)(2,1)}, bf16[16,1792]{1,0:T(8,128)(2,1)S(1)}, u32[]{:S(2)}, u32[]{:S(2)}) %collective-permute-start.24) | collective-permute-done | bytes 57376 | tf_op jit(solution)/shard_map/ppermute | solution.py:297
  116.6 0.6 copy-done.20
  117.2 1.7 %shard_map.165.refs_0_ = bf16[16,1792]{1,0:T(8,128)(2,1)} custom-call(f32[16,1792]{1,0:T(8,128)} %get-tuple-element.81.refs_0_, bf16[16,1792]{1,0:T(8,128)(2,1)} %copy-done.14, bf16[16,1792]{1,0:T(8,128)(2,1)} %copy-done.15, bf16[16,1792]{1,0:T(8,128)(2,1)} %copy-done.16, bf16[16,1792]{1,0:T(8,128)(2,1)} %copy-done.17, bf16[16,1792]{1,0:T(8,128)(2,1)} %copy-done.18, ...), custom_call_target="tpu_custom_call" | custom-call | bytes 573440 | tf_op jit(solution)/shard_map/pallas_call | solution.py:308
  118.9 1.6 %collective-permute-start.26 = (bf16[16,1792]{1,0:T(8,128)(2,1)}, bf16[16,1792]{1,0:T(8,128)(2,1)S(1)}, u32[]{:S(2)}, u32[]{:S(2)}) collective-permute-start(bf16[16,1792]{1,0:T(8,128)(2,1)} %shard_map.165.refs_0_), channel_id=1, source_target_pairs={{0,2},{1,3},{2,4},{3,5},{4,6},{5,7},{6,0},{7,1},{8,10},{9,11},{10,... | collective-permute-start | bytes 172040 | tf_op jit(solution)/shard_map/ppermute | solution.py:297
  120.5 1.5 %collective-permute-start.25 = (bf16[16,1792]{1,0:T(8,128)(2,1)}, bf16[16,1792]{1,0:T(8,128)(2,1)S(1)}, u32[]{:S(2)}, u32[]{:S(2)}) collective-permute-start(bf16[16,1792]{1,0:T(8,128)(2,1)} %shard_map.165.refs_0_), channel_id=1, source_target_pairs={{0,1},{1,2},{2,3},{3,4},{4,5},{5,6},{6,7},{7,0},{8,9},{9,10},{10,1... | collective-permute-start | bytes 172040 | tf_op jit(solution)/shard_map/ppermute | solution.py:297
  122.0 3.2 %collective-permute-start.31 = (bf16[16,1792]{1,0:T(8,128)(2,1)}, bf16[16,1792]{1,0:T(8,128)(2,1)S(1)}, u32[]{:S(2)}, u32[]{:S(2)}) collective-permute-start(bf16[16,1792]{1,0:T(8,128)(2,1)} %shard_map.165.refs_0_), channel_id=1, source_target_pairs={{0,7},{1,0},{2,1},{3,2},{4,3},{5,4},{6,5},{7,6},{8,15},{9,8},{10,9... | collective-permute-start | bytes 172040 | tf_op jit(solution)/shard_map/ppermute | solution.py:297
  125.3 0.4 collective-permute-start.30
  125.7 1.1 collective-permute-start.29
  126.8 2.3 %collective-permute-start.28 = (bf16[16,1792]{1,0:T(8,128)(2,1)}, bf16[16,1792]{1,0:T(8,128)(2,1)S(1)}, u32[]{:S(2)}, u32[]{:S(2)}) collective-permute-start(bf16[16,1792]{1,0:T(8,128)(2,1)} %shard_map.165.refs_0_), channel_id=1, source_target_pairs={{0,4},{1,5},{2,6},{3,7},{4,0},{5,1},{6,2},{7,3},{8,12},{9,13},{10,... | collective-permute-start | bytes 172040 | tf_op jit(solution)/shard_map/ppermute | solution.py:297
  129.1 0.6 copy-done.26
  129.8 1.6 %shard_map.166.refs_0_ = bf16[64,1792]{1,0:T(8,128)(2,1)} custom-call(bf16[16,1792]{1,0:T(8,128)(2,1)} %shard_map.165.refs_0_, bf16[16,1792]{1,0:T(8,128)(2,1)} %copy-done.26, bf16[16,1792]{1,0:T(8,128)(2,1)} %copy-done.25, bf16[16,1792]{1,0:T(8,128)(2,1)} %copy-done.23), custom_call_target="tpu_custom_call" | custom-call | bytes 458752 | tf_op jit(solution)/shard_map/pallas_call | solution.py:308
  131.4 1.0 collective-permute-start.34
  133.0 0.6 copy-done.27
  133.6 1.6 %shard_map.167.refs_1_ = bf16[64,1792]{1,0:T(8,128)(2,1)} custom-call(bf16[16,1792]{1,0:T(8,128)(2,1)} %copy-done.27, bf16[16,1792]{1,0:T(8,128)(2,1)} %copy-done.24, bf16[16,1792]{1,0:T(8,128)(2,1)} %copy-done.22, bf16[16,1792]{1,0:T(8,128)(2,1)} %copy-done.21), custom_call_target="tpu_custom_call" | custom-call | bytes 458752 | tf_op jit(solution)/shard_map/pallas_call | solution.py:308
  135.2 1.1 collective-permute-start.35
  136.3 0.5 collective-permute-start.33
  136.8 1.0 collective-permute-done.34.refs_4_
  137.8 3.7 %collective-permute-done.35.refs_5_ = bf16[64,1792]{1,0:T(8,128)(2,1)S(1)} collective-permute-done((bf16[64,1792]{1,0:T(8,128)(2,1)}, bf16[64,1792]{1,0:T(8,128)(2,1)S(1)}, u32[]{:S(2)}, u32[]{:S(2)}) %collective-permute-start.35) | collective-permute-done | bytes 229408 | tf_op jit(solution)/shard_map/ppermute | solution.py:302
  141.5 1.4 collective-permute-done.37.refs_7_
  143.0 0.7 copy-done.10
  143.7 3.5 %shard_map.168 = (f32[512,512]{1,0:T(8,128)}, f32[512,512]{1,0:T(8,128)}, f32[512,512]{1,0:T(8,128)}, f32[512,128]{1,0:T(8,128)}, f32[1,1]{1,0:T(1,128)}) custom-call(bf16[64,1792]{1,0:T(8,128)(2,1)} %shard_map.166.refs_0_, bf16[64,1792]{1,0:T(8,128)(2,1)} %shard_map.167.refs_1_, bf16[64,1792]{1,0:T(8,128)(2,1)} %copy-done.7, bf16[64,1792]{1,0:T(8,128)(2,1)} %copy-done.8, ...), custom_call_target="tpu_custom_call" | custom-call | bytes 5505024 | tf_op jit(solution)/shard_map/pallas_call | solution.py:473
  (102 shorter events, 2.4 us)
Async XLA Ops:
  2.9 9.8 %collective-permute-start = (bf16[512,128]{1,0:T(8,128)(2,1)}, bf16[512,128]{1,0:T(8,128)(2,1)S(1)}, u32[]{:S(2)}, u32[]{:S(2)}) collective-permute-start(bf16[512,128]{1,0:T(8,128)(2,1)} %get-tuple-element.51), channel_id=1, source_target_pairs={{0,1},{1,2},{2,3},{3,4},{4,5},{5,6},{6,7},{7,0},{8,9},{9,10},{10,1... | collective-permute-start | bytes 393224 | tf_op jit(solution)/shard_map/ppermute | solution.py:297
  5.8 8.0 %collective-permute-start.1 = (bf16[512,128]{1,0:T(8,128)(2,1)}, bf16[512,128]{1,0:T(8,128)(2,1)S(1)}, u32[]{:S(2)}, u32[]{:S(2)}) collective-permute-start(bf16[512,128]{1,0:T(8,128)(2,1)} %get-tuple-element.52), channel_id=1, source_target_pairs={{0,7},{1,0},{2,1},{3,2},{4,3},{5,4},{6,5},{7,6},{8,15},{9,8},{10,9... | collective-permute-start | bytes 393224 | tf_op jit(solution)/shard_map/ppermute | solution.py:297
  12.7 1.1 copy-start.32
  26.9 6.8 %collective-permute-start.5 = (bf16[128,128]{1,0:T(8,128)(2,1)}, bf16[128,128]{1,0:T(8,128)(2,1)S(1)}, u32[]{:S(2)}, u32[]{:S(2)}) collective-permute-start(bf16[128,128]{1,0:T(8,128)(2,1)} %get-tuple-element.58), channel_id=1, source_target_pairs={{0,1},{1,2},{2,3},{3,4},{4,5},{5,6},{6,7},{7,0},{8,9},{9,10},{10,1... | collective-permute-start | bytes 98312 | tf_op jit(solution)/shard_map/ppermute | solution.py:297
  27.2 6.5 %collective-permute-start.6 = (bf16[128,128]{1,0:T(8,128)(2,1)}, bf16[128,128]{1,0:T(8,128)(2,1)S(1)}, u32[]{:S(2)}, u32[]{:S(2)}) collective-permute-start(bf16[128,128]{1,0:T(8,128)(2,1)} %get-tuple-element.59), channel_id=1, source_target_pairs={{0,7},{1,0},{2,1},{3,2},{4,3},{5,4},{6,5},{7,6},{8,15},{9,8},{10,9... | collective-permute-start | bytes 98312 | tf_op jit(solution)/shard_map/ppermute | solution.py:297
  33.8 13.3 %copy-start.28 = (bf16[128,256]{1,0:T(8,128)(2,1)}, bf16[128,256]{1,0:T(8,128)(2,1)S(1)}, u32[]{:S(2)}) copy-start(bf16[128,256]{1,0:T(8,128)(2,1)S(1)} %constant_dynamic-update-slice_fusion.refs_4_) | copy-start | bytes 196612
  33.8 4.4 %collective-permute-start.9 = (bf16[128,256]{1,0:T(8,128)(2,1)S(1)}, bf16[128,256]{1,0:T(8,128)(2,1)S(1)}, u32[]{:S(2)}, u32[]{:S(2)}) collective-permute-start(bf16[128,256]{1,0:T(8,128)(2,1)S(1)} %constant_dynamic-update-slice_fusion.refs_4_), channel_id=1, source_target_pairs={{0,24},{8,16},{16,8},{24,0},{1,25},{9,17},{17,9},{25,1},{2,26},{10... | collective-permute-start | bytes 196616 | tf_op jit(solution)/shard_map/ppermute | solution.py:302
  33.8 13.1 %collective-permute-start.4 = (bf16[128,512]{1,0:T(8,128)(2,1)}, bf16[128,512]{1,0:T(8,128)(2,1)S(1)}, u32[]{:S(2)}, u32[]{:S(2)}) collective-permute-start(bf16[128,512]{1,0:T(8,128)(2,1)} %get-tuple-element.57.after.refs_0_), channel_id=1, source_target_pairs={{0,24},{8,16},{16,8},{24,0},{1,25},{9,17},{17,9},{25,1},{2,26},{10... | collective-permute-start | bytes 393224 | tf_op jit(solution)/shard_map/ppermute | solution.py:302
  35.6 11.4 %collective-permute-start.3 = (bf16[128,512]{1,0:T(8,128)(2,1)}, bf16[128,512]{1,0:T(8,128)(2,1)S(1)}, u32[]{:S(2)}, u32[]{:S(2)}) collective-permute-start(bf16[128,512]{1,0:T(8,128)(2,1)} %get-tuple-element.57.after.refs_0_), channel_id=1, source_target_pairs={{0,16},{8,24},{16,0},{24,8},{1,17},{9,25},{17,1},{25,9},{2,18},{10... | collective-permute-start | bytes 393224 | tf_op jit(solution)/shard_map/ppermute | solution.py:302
  37.1 9.9 %collective-permute-start.2 = (bf16[128,512]{1,0:T(8,128)(2,1)}, bf16[128,512]{1,0:T(8,128)(2,1)S(1)}, u32[]{:S(2)}, u32[]{:S(2)}) collective-permute-start(bf16[128,512]{1,0:T(8,128)(2,1)} %get-tuple-element.57.after.refs_0_), channel_id=1, source_target_pairs={{0,8},{8,0},{16,24},{24,16},{1,9},{9,1},{17,25},{25,17},{2,10},{10... | collective-permute-start | bytes 393224 | tf_op jit(solution)/shard_map/ppermute | solution.py:302
  37.1 9.9 %collective-permute-start.8 = (bf16[128,256]{1,0:T(8,128)(2,1)S(1)}, bf16[128,256]{1,0:T(8,128)(2,1)S(1)}, u32[]{:S(2)}, u32[]{:S(2)}) collective-permute-start(bf16[128,256]{1,0:T(8,128)(2,1)S(1)} %constant_dynamic-update-slice_fusion.refs_4_), channel_id=1, source_target_pairs={{0,16},{8,24},{16,0},{24,8},{1,17},{9,25},{17,1},{25,9},{2,18},{10... | collective-permute-start | bytes 196616 | tf_op jit(solution)/shard_map/ppermute | solution.py:302
  38.2 8.9 %copy-start.34 = (bf16[128,256]{1,0:T(8,128)(2,1)}, bf16[128,256]{1,0:T(8,128)(2,1)S(1)}, u32[]{:S(2)}) copy-start(bf16[128,256]{1,0:T(8,128)(2,1)S(1)} %collective-permute-done.9.refs_7_) | copy-start | bytes 196612
  38.2 8.8 %collective-permute-start.7 = (bf16[128,256]{1,0:T(8,128)(2,1)S(1)}, bf16[128,256]{1,0:T(8,128)(2,1)S(1)}, u32[]{:S(2)}, u32[]{:S(2)}) collective-permute-start(bf16[128,256]{1,0:T(8,128)(2,1)S(1)} %constant_dynamic-update-slice_fusion.refs_4_), channel_id=1, source_target_pairs={{0,8},{8,0},{16,24},{24,16},{1,9},{9,1},{17,25},{25,17},{2,10},{10... | collective-permute-start | bytes 196616 | tf_op jit(solution)/shard_map/ppermute | solution.py:302
  47.0 0.7 copy-start.29
  47.0 0.7 copy-start.30
  47.0 0.7 copy-start.31
  57.7 16.2 %collective-permute-start.10 = (f32[128,512]{1,0:T(8,128)}, f32[128,512]{1,0:T(8,128)S(1)}, u32[]{:S(2)}, u32[]{:S(2)}) collective-permute-start(f32[128,512]{1,0:T(8,128)} %get-tuple-element.65), channel_id=1, source_target_pairs={{0,8},{8,0},{16,24},{24,16},{1,9},{9,1},{17,25},{25,17},{2,10},{10... | collective-permute-start | bytes 786440 | tf_op jit(solution)/shard_map/ppermute | solution.py:302
  58.1 1.7 %collective-permute-start.11 = (f32[128,256]{1,0:T(8,128)}, f32[128,256]{1,0:T(8,128)S(1)}, u32[]{:S(2)}, u32[]{:S(2)}) collective-permute-start(f32[128,256]{1,0:T(8,128)} %get-tuple-element.67), channel_id=1, source_target_pairs={{0,8},{8,0},{16,24},{24,16},{1,9},{9,1},{17,25},{25,17},{2,10},{10... | collective-permute-start | bytes 393224 | tf_op jit(solution)/shard_map/ppermute | solution.py:302
  62.0 6.9 %collective-permute-start.12 = (f32[128,128]{1,0:T(8,128)}, f32[128,128]{1,0:T(8,128)S(1)}, u32[]{:S(2)}, u32[]{:S(2)}) collective-permute-start(f32[128,128]{1,0:T(8,128)} %get-tuple-element.68), channel_id=1, source_target_pairs={{0,7},{1,0},{2,1},{3,2},{4,3},{5,4},{6,5},{7,6},{8,15},{9,8},{10,9... | collective-permute-start | bytes 196616 | tf_op jit(solution)/shard_map/ppermute | solution.py:297
  66.7 7.2 %collective-permute-start.13 = (f32[128,128]{1,0:T(8,128)}, f32[128,128]{1,0:T(8,128)S(1)}, u32[]{:S(2)}, u32[]{:S(2)}) collective-permute-start(f32[128,128]{1,0:T(8,128)} %get-tuple-element.69), channel_id=1, source_target_pairs={{0,1},{1,2},{2,3},{3,4},{4,5},{5,6},{6,7},{7,0},{8,9},{9,10},{10,1... | collective-permute-start | bytes 196616 | tf_op jit(solution)/shard_map/ppermute | solution.py:297
  69.0 5.0 %copy-start.12 = (f32[128,128]{1,0:T(8,128)}, f32[128,128]{1,0:T(8,128)S(1)}, u32[]{:S(2)}) copy-start(f32[128,128]{1,0:T(8,128)S(1)} %collective-permute-done.12.from_next) | copy-start | bytes 196612
  73.9 0.7 copy-start.2
  84.0 2.0 %collective-permute-start.15 = (bf16[128,1792]{1,0:T(8,128)(2,1)}, bf16[128,1792]{1,0:T(8,128)(2,1)S(1)}, u32[]{:S(2)}, u32[]{:S(2)}) collective-permute-start(bf16[128,1792]{1,0:T(8,128)(2,1)} %get-tuple-element.79), channel_id=1, source_target_pairs={{0,8},{8,0},{16,24},{24,16},{1,9},{9,1},{17,25},{25,17},{2,10},{10... | collective-permute-start | bytes 1376264 | tf_op jit(solution)/shard_map/ppermute | solution.py:302
  84.0 7.0 %collective-permute-start.14 = (bf16[128,1792]{1,0:T(8,128)(2,1)}, bf16[128,1792]{1,0:T(8,128)(2,1)S(1)}, u32[]{:S(2)}, u32[]{:S(2)}) collective-permute-start(bf16[128,1792]{1,0:T(8,128)(2,1)} %get-tuple-element.78), channel_id=1, source_target_pairs={{0,8},{8,0},{16,24},{24,16},{1,9},{9,1},{17,25},{25,17},{2,10},{10... | collective-permute-start | bytes 1376264 | tf_op jit(solution)/shard_map/ppermute | solution.py:302
  86.1 0.8 copy-start.1
  89.0 8.7 %collective-permute-start.16 = (bf16[64,1792]{1,0:T(8,128)(2,1)}, bf16[64,1792]{1,0:T(8,128)(2,1)S(1)}, u32[]{:S(2)}, u32[]{:S(2)}) collective-permute-start(bf16[64,1792]{1,0:T(8,128)(2,1)} %get-tuple-element.80), channel_id=1, source_target_pairs={{0,16},{8,24},{16,0},{24,8},{1,17},{9,25},{17,1},{25,9},{2,18},{10... | collective-permute-start | bytes 688136 | tf_op jit(solution)/shard_map/ppermute | solution.py:302
  89.9 11.8 %collective-permute-start.20 = (bf16[64,1792]{1,0:T(8,128)(2,1)}, bf16[64,1792]{1,0:T(8,128)(2,1)S(1)}, u32[]{:S(2)}, u32[]{:S(2)}) collective-permute-start(bf16[64,1792]{1,0:T(8,128)(2,1)} %get-tuple-element.85), channel_id=1, source_target_pairs={{0,16},{8,24},{16,0},{24,8},{1,17},{9,25},{17,1},{25,9},{2,18},{10... | collective-permute-start | bytes 688136 | tf_op jit(solution)/shard_map/ppermute | solution.py:302
  91.0 6.6 %copy-start = (bf16[128,1792]{1,0:T(8,128)(2,1)}, bf16[128,1792]{1,0:T(8,128)(2,1)S(1)}, u32[]{:S(2)}) copy-start(bf16[128,1792]{1,0:T(8,128)(2,1)S(1)} %collective-permute-done.14.near) | copy-start | bytes 1376260
  97.6 0.7 copy-start.4
  100.3 7.1 %collective-permute-start.17 = (bf16[16,1792]{1,0:T(8,128)(2,1)}, bf16[16,1792]{1,0:T(8,128)(2,1)S(1)}, u32[]{:S(2)}, u32[]{:S(2)}) collective-permute-start(bf16[16,1792]{1,0:T(8,128)(2,1)} %get-tuple-element.82), channel_id=1, source_target_pairs={{0,7},{1,0},{2,1},{3,2},{4,3},{5,4},{6,5},{7,6},{8,15},{9,8},{10,9... | collective-permute-start | bytes 172040 | tf_op jit(solution)/shard_map/ppermute | solution.py:297
  100.3 9.1 %collective-permute-start.18 = (bf16[16,1792]{1,0:T(8,128)(2,1)}, bf16[16,1792]{1,0:T(8,128)(2,1)S(1)}, u32[]{:S(2)}, u32[]{:S(2)}) collective-permute-start(bf16[16,1792]{1,0:T(8,128)(2,1)} %get-tuple-element.83), channel_id=1, source_target_pairs={{0,6},{1,7},{2,0},{3,1},{4,2},{5,3},{6,4},{7,5},{8,14},{9,15},{10,... | collective-permute-start | bytes 172040 | tf_op jit(solution)/shard_map/ppermute | solution.py:297
  100.3 10.5 %collective-permute-start.19 = (bf16[16,1792]{1,0:T(8,128)(2,1)}, bf16[16,1792]{1,0:T(8,128)(2,1)S(1)}, u32[]{:S(2)}, u32[]{:S(2)}) collective-permute-start(bf16[16,1792]{1,0:T(8,128)(2,1)} %get-tuple-element.84), channel_id=1, source_target_pairs={{0,5},{1,6},{2,7},{3,0},{4,1},{5,2},{6,3},{7,4},{8,13},{9,14},{10,... | collective-permute-start | bytes 172040 | tf_op jit(solution)/shard_map/ppermute | solution.py:297
  101.8 0.7 copy-start.3
  104.4 7.3 %collective-permute-start.21 = (bf16[16,1792]{1,0:T(8,128)(2,1)}, bf16[16,1792]{1,0:T(8,128)(2,1)S(1)}, u32[]{:S(2)}, u32[]{:S(2)}) collective-permute-start(bf16[16,1792]{1,0:T(8,128)(2,1)} %get-tuple-element.86), channel_id=1, source_target_pairs={{0,4},{1,5},{2,6},{3,7},{4,0},{5,1},{6,2},{7,3},{8,12},{9,13},{10,... | collective-permute-start | bytes 172040 | tf_op jit(solution)/shard_map/ppermute | solution.py:297
  107.4 6.3 %collective-permute-start.22 = (bf16[16,1792]{1,0:T(8,128)(2,1)}, bf16[16,1792]{1,0:T(8,128)(2,1)S(1)}, u32[]{:S(2)}, u32[]{:S(2)}) collective-permute-start(bf16[16,1792]{1,0:T(8,128)(2,1)} %get-tuple-element.87), channel_id=1, source_target_pairs={{0,3},{1,4},{2,5},{3,6},{4,7},{5,0},{6,1},{7,2},{8,11},{9,12},{10,... | collective-permute-start | bytes 172040 | tf_op jit(solution)/shard_map/ppermute | solution.py:297
  107.4 9.2 %copy-start.14 = (bf16[16,1792]{1,0:T(8,128)(2,1)}, bf16[16,1792]{1,0:T(8,128)(2,1)S(1)}, u32[]{:S(2)}) copy-start(bf16[16,1792]{1,0:T(8,128)(2,1)S(1)} %collective-permute-done.17.refs_1_) | copy-start | bytes 172036
  107.4 6.8 %collective-permute-start.23 = (bf16[16,1792]{1,0:T(8,128)(2,1)}, bf16[16,1792]{1,0:T(8,128)(2,1)S(1)}, u32[]{:S(2)}, u32[]{:S(2)}) collective-permute-start(bf16[16,1792]{1,0:T(8,128)(2,1)} %get-tuple-element.88), channel_id=1, source_target_pairs={{0,2},{1,3},{2,4},{3,5},{4,6},{5,7},{6,0},{7,1},{8,10},{9,11},{10,... | collective-permute-start | bytes 172040 | tf_op jit(solution)/shard_map/ppermute | solution.py:297
  109.4 7.1 %copy-start.15 = (bf16[16,1792]{1,0:T(8,128)(2,1)}, bf16[16,1792]{1,0:T(8,128)(2,1)S(1)}, u32[]{:S(2)}) copy-start(bf16[16,1792]{1,0:T(8,128)(2,1)S(1)} %collective-permute-done.18.refs_2_) | copy-start | bytes 172036
  109.4 7.1 %collective-permute-start.24 = (bf16[16,1792]{1,0:T(8,128)(2,1)}, bf16[16,1792]{1,0:T(8,128)(2,1)S(1)}, u32[]{:S(2)}, u32[]{:S(2)}) collective-permute-start(bf16[16,1792]{1,0:T(8,128)(2,1)} %get-tuple-element.89), channel_id=1, source_target_pairs={{0,1},{1,2},{2,3},{3,4},{4,5},{5,6},{6,7},{7,0},{8,9},{9,10},{10,1... | collective-permute-start | bytes 172040 | tf_op jit(solution)/shard_map/ppermute | solution.py:297
  110.9 5.7 %copy-start.16 = (bf16[16,1792]{1,0:T(8,128)(2,1)}, bf16[16,1792]{1,0:T(8,128)(2,1)S(1)}, u32[]{:S(2)}) copy-start(bf16[16,1792]{1,0:T(8,128)(2,1)S(1)} %collective-permute-done.19.refs_3_) | copy-start | bytes 172036
  111.7 4.8 %copy-start.17 = (bf16[16,1792]{1,0:T(8,128)(2,1)}, bf16[16,1792]{1,0:T(8,128)(2,1)S(1)}, u32[]{:S(2)}) copy-start(bf16[16,1792]{1,0:T(8,128)(2,1)S(1)} %collective-permute-done.21.refs_4_) | copy-start | bytes 172036
  113.6 2.9 %copy-start.18 = (bf16[16,1792]{1,0:T(8,128)(2,1)}, bf16[16,1792]{1,0:T(8,128)(2,1)S(1)}, u32[]{:S(2)}) copy-start(bf16[16,1792]{1,0:T(8,128)(2,1)S(1)} %collective-permute-done.22.refs_5_) | copy-start | bytes 172036
  114.2 2.4 %copy-start.19 = (bf16[16,1792]{1,0:T(8,128)(2,1)}, bf16[16,1792]{1,0:T(8,128)(2,1)S(1)}, u32[]{:S(2)}) copy-start(bf16[16,1792]{1,0:T(8,128)(2,1)S(1)} %collective-permute-done.23.refs_6_) | copy-start | bytes 172036
  118.9 6.8 %collective-permute-start.27 = (bf16[16,1792]{1,0:T(8,128)(2,1)}, bf16[16,1792]{1,0:T(8,128)(2,1)S(1)}, u32[]{:S(2)}, u32[]{:S(2)}) collective-permute-start(bf16[16,1792]{1,0:T(8,128)(2,1)} %shard_map.165.refs_0_), channel_id=1, source_target_pairs={{0,3},{1,4},{2,5},{3,6},{4,7},{5,0},{6,1},{7,2},{8,11},{9,12},{10,... | collective-permute-start | bytes 172040 | tf_op jit(solution)/shard_map/ppermute | solution.py:297
  118.9 7.9 %collective-permute-start.26 = (bf16[16,1792]{1,0:T(8,128)(2,1)}, bf16[16,1792]{1,0:T(8,128)(2,1)S(1)}, u32[]{:S(2)}, u32[]{:S(2)}) collective-permute-start(bf16[16,1792]{1,0:T(8,128)(2,1)} %shard_map.165.refs_0_), channel_id=1, source_target_pairs={{0,2},{1,3},{2,4},{3,5},{4,6},{5,7},{6,0},{7,1},{8,10},{9,11},{10,... | collective-permute-start | bytes 172040 | tf_op jit(solution)/shard_map/ppermute | solution.py:297
  120.5 8.6 %collective-permute-start.25 = (bf16[16,1792]{1,0:T(8,128)(2,1)}, bf16[16,1792]{1,0:T(8,128)(2,1)S(1)}, u32[]{:S(2)}, u32[]{:S(2)}) collective-permute-start(bf16[16,1792]{1,0:T(8,128)(2,1)} %shard_map.165.refs_0_), channel_id=1, source_target_pairs={{0,1},{1,2},{2,3},{3,4},{4,5},{5,6},{6,7},{7,0},{8,9},{9,10},{10,1... | collective-permute-start | bytes 172040 | tf_op jit(solution)/shard_map/ppermute | solution.py:297
  122.0 10.3 %collective-permute-start.31 = (bf16[16,1792]{1,0:T(8,128)(2,1)}, bf16[16,1792]{1,0:T(8,128)(2,1)S(1)}, u32[]{:S(2)}, u32[]{:S(2)}) collective-permute-start(bf16[16,1792]{1,0:T(8,128)(2,1)} %shard_map.165.refs_0_), channel_id=1, source_target_pairs={{0,7},{1,0},{2,1},{3,2},{4,3},{5,4},{6,5},{7,6},{8,15},{9,8},{10,9... | collective-permute-start | bytes 172040 | tf_op jit(solution)/shard_map/ppermute | solution.py:297
  125.3 7.1 %collective-permute-start.30 = (bf16[16,1792]{1,0:T(8,128)(2,1)}, bf16[16,1792]{1,0:T(8,128)(2,1)S(1)}, u32[]{:S(2)}, u32[]{:S(2)}) collective-permute-start(bf16[16,1792]{1,0:T(8,128)(2,1)} %shard_map.165.refs_0_), channel_id=1, source_target_pairs={{0,6},{1,7},{2,0},{3,1},{4,2},{5,3},{6,4},{7,5},{8,14},{9,15},{10,... | collective-permute-start | bytes 172040 | tf_op jit(solution)/shard_map/ppermute | solution.py:297
  125.7 3.5 %copy-start.23 = (bf16[16,1792]{1,0:T(8,128)(2,1)}, bf16[16,1792]{1,0:T(8,128)(2,1)S(1)}, u32[]{:S(2)}) copy-start(bf16[16,1792]{1,0:T(8,128)(2,1)S(1)} %collective-permute-done.27.refs_3_) | copy-start | bytes 172036
  125.7 6.7 %collective-permute-start.29 = (bf16[16,1792]{1,0:T(8,128)(2,1)}, bf16[16,1792]{1,0:T(8,128)(2,1)S(1)}, u32[]{:S(2)}, u32[]{:S(2)}) collective-permute-start(bf16[16,1792]{1,0:T(8,128)(2,1)} %shard_map.165.refs_0_), channel_id=1, source_target_pairs={{0,5},{1,6},{2,7},{3,0},{4,1},{5,2},{6,3},{7,4},{8,13},{9,14},{10,... | collective-permute-start | bytes 172040 | tf_op jit(solution)/shard_map/ppermute | solution.py:297
  126.8 2.3 %copy-start.25 = (bf16[16,1792]{1,0:T(8,128)(2,1)}, bf16[16,1792]{1,0:T(8,128)(2,1)S(1)}, u32[]{:S(2)}) copy-start(bf16[16,1792]{1,0:T(8,128)(2,1)S(1)} %collective-permute-done.26.refs_2_) | copy-start | bytes 172036
  126.8 5.9 %collective-permute-start.28 = (bf16[16,1792]{1,0:T(8,128)(2,1)}, bf16[16,1792]{1,0:T(8,128)(2,1)S(1)}, u32[]{:S(2)}, u32[]{:S(2)}) collective-permute-start(bf16[16,1792]{1,0:T(8,128)(2,1)} %shard_map.165.refs_0_), channel_id=1, source_target_pairs={{0,4},{1,5},{2,6},{3,7},{4,0},{5,1},{6,2},{7,3},{8,12},{9,13},{10,... | collective-permute-start | bytes 172040 | tf_op jit(solution)/shard_map/ppermute | solution.py:297
  131.4 6.4 %collective-permute-start.34 = (bf16[64,1792]{1,0:T(8,128)(2,1)}, bf16[64,1792]{1,0:T(8,128)(2,1)S(1)}, u32[]{:S(2)}, u32[]{:S(2)}) collective-permute-start(bf16[64,1792]{1,0:T(8,128)(2,1)} %shard_map.166.refs_0_), channel_id=1, source_target_pairs={{0,16},{8,24},{16,0},{24,8},{1,17},{9,25},{17,1},{25,9},{2,18},{10... | collective-permute-start | bytes 688136 | tf_op jit(solution)/shard_map/ppermute | solution.py:302
  135.2 6.2 %collective-permute-start.35 = (bf16[64,1792]{1,0:T(8,128)(2,1)}, bf16[64,1792]{1,0:T(8,128)(2,1)S(1)}, u32[]{:S(2)}, u32[]{:S(2)}) collective-permute-start(bf16[64,1792]{1,0:T(8,128)(2,1)} %shard_map.167.refs_1_), channel_id=1, source_target_pairs={{0,16},{8,24},{16,0},{24,8},{1,17},{9,25},{17,1},{25,9},{2,18},{10... | collective-permute-start | bytes 688136 | tf_op jit(solution)/shard_map/ppermute | solution.py:302
  136.3 5.2 %collective-permute-start.32 = (bf16[64,1792]{1,0:T(8,128)(2,1)}, bf16[64,1792]{1,0:T(8,128)(2,1)S(1)}, u32[]{:S(2)}, u32[]{:S(2)}) collective-permute-start(bf16[64,1792]{1,0:T(8,128)(2,1)} %shard_map.166.refs_0_), channel_id=1, source_target_pairs={{0,8},{8,0},{16,24},{24,16},{1,9},{9,1},{17,25},{25,17},{2,10},{10... | collective-permute-start | bytes 688136 | tf_op jit(solution)/shard_map/ppermute | solution.py:302
  136.3 5.2 %collective-permute-start.33 = (bf16[64,1792]{1,0:T(8,128)(2,1)}, bf16[64,1792]{1,0:T(8,128)(2,1)S(1)}, u32[]{:S(2)}, u32[]{:S(2)}) collective-permute-start(bf16[64,1792]{1,0:T(8,128)(2,1)} %shard_map.167.refs_1_), channel_id=1, source_target_pairs={{0,8},{8,0},{16,24},{24,16},{1,9},{9,1},{17,25},{25,17},{2,10},{10... | collective-permute-start | bytes 688136 | tf_op jit(solution)/shard_map/ppermute | solution.py:302
  137.8 5.2 %copy-start.5 = (bf16[64,1792]{1,0:T(8,128)(2,1)}, bf16[64,1792]{1,0:T(8,128)(2,1)S(1)}, u32[]{:S(2)}) copy-start(bf16[64,1792]{1,0:T(8,128)(2,1)S(1)} %collective-permute-done.34.refs_4_) | copy-start | bytes 688132
  137.8 3.7 %collective-permute-start.36 = (bf16[64,1792]{1,0:T(8,128)(2,1)S(1)}, bf16[64,1792]{1,0:T(8,128)(2,1)S(1)}, u32[]{:S(2)}, u32[]{:S(2)}) collective-permute-start(bf16[64,1792]{1,0:T(8,128)(2,1)S(1)} %collective-permute-done.34.refs_4_), channel_id=1, source_target_pairs={{0,8},{8,0},{16,24},{24,16},{1,9},{9,1},{17,25},{25,17},{2,10},{10... | collective-permute-start | bytes 688136 | tf_op jit(solution)/shard_map/ppermute | solution.py:302
  141.5 1.5 %copy-start.6 = (bf16[64,1792]{1,0:T(8,128)(2,1)}, bf16[64,1792]{1,0:T(8,128)(2,1)S(1)}, u32[]{:S(2)}) copy-start(bf16[64,1792]{1,0:T(8,128)(2,1)S(1)} %collective-permute-done.35.refs_5_) | copy-start | bytes 688132
  141.5 1.5 %collective-permute-start.37 = (bf16[64,1792]{1,0:T(8,128)(2,1)S(1)}, bf16[64,1792]{1,0:T(8,128)(2,1)S(1)}, u32[]{:S(2)}, u32[]{:S(2)}) collective-permute-start(bf16[64,1792]{1,0:T(8,128)(2,1)S(1)} %collective-permute-done.35.refs_5_), channel_id=1, source_target_pairs={{0,8},{8,0},{16,24},{24,16},{1,9},{9,1},{17,25},{25,17},{2,10},{10... | collective-permute-start | bytes 688136 | tf_op jit(solution)/shard_map/ppermute | solution.py:302
  141.5 1.5 %copy-start.7 = (bf16[64,1792]{1,0:T(8,128)(2,1)}, bf16[64,1792]{1,0:T(8,128)(2,1)S(1)}, u32[]{:S(2)}) copy-start(bf16[64,1792]{1,0:T(8,128)(2,1)S(1)} %collective-permute-done.32.refs_2_) | copy-start | bytes 688132
  141.5 1.5 copy-start.8
  141.5 1.5 copy-start.9
  143.0 0.7 copy-start.10
  (11 other events, 6.9 us)

commit v4 on v3

--- a/solution.py
+++ b/solution.py
@@ -10,7 +10,7 @@
 EPS = 0.04
 F32 = jnp.float32
 BF16 = jnp.bfloat16
-VMEM_BYTES = 56 * 1024 * 1024
+MIB = 1024 * 1024
 
 
 def dot(a, b, ca=1, cb=0):
@@ -27,8 +27,8 @@
     return jnp.where(hit, 1.0, 0.0).astype(BF16)
 
 
-def params(**kw):
-    return pltpu.CompilerParams(vmem_limit_bytes=VMEM_BYTES, **kw)
+def params(mib):
+    return pltpu.CompilerParams(vmem_limit_bytes=int(mib * MIB))
 
 
 def vmem(n):
@@ -52,53 +52,74 @@
 
 
 def weights_kernel(w_send, w_recv, vertex, w_decode, nodes_t, w_send_t, vertex_t, w_decode_t, recv_t):
-    w_send_t[...] = w_send[...].T
-    vertex_t[...] = vertex[...].T
+    w_send_t[...] = w_send[...].T * 0.5
+    vertex_t[...] = vertex[...].T * 0.5
     w_decode_t[...] = w_decode[...].T
-    recv_t[...] = dot(w_recv[...].T, nodes_t[...])
-
-
-def decoder_kernel(core, vertices, weights, base, truth, after, mat_hi, mat_lo, base_t, truth_t):
+    recv_t[...] = dot(w_recv[...].T, nodes_t[...]) * 0.5
+
+
+def decoder_kernel(core, vertices, weights, base, truth, after, mat, base_t, truth_t):
     del core, after
-    shape = mat_hi.shape
+    rows, tile = mat.shape[0] // 2, 16
+    shape = (tile, mat.shape[1])
+    spread = lambda ref, k: jnp.broadcast_to(ref[k : k + 1, :], shape)
+    vertex = [spread(vertices, k) for k in range(vertices.shape[0])]
+    weight = [spread(weights, k) for k in range(vertices.shape[0])]
     row = lax.broadcasted_iota(jnp.int32, shape, 0)
-    mat = jnp.zeros(shape, F32)
-    for k in range(vertices.shape[0]):
-        mat += jnp.where(row == vertices[k : k + 1, :], weights[k : k + 1, :], 0.0)
-    mat_hi[...], mat_lo[...] = split(mat)
+
+    for start in range(0, rows, tile):
+        here = row + start
+        total = jnp.where(here == vertex[0], weight[0], 0.0)
+        for k in range(1, len(vertex)):
+            total += jnp.where(here == vertex[k], weight[k], 0.0)
+        hi, lo = split(total)
+        mat[start : start + tile, :] = hi
+        mat[rows + start : rows + start + tile, :] = lo
     base_t[...] = base[...].T
     truth_t[...] = truth[...].T
+
+
+TILE = 16
+
+
+def bent(half):
+    t = jnp.tanh(half)
+    u = half * t
+    return half + u, (1.0 + t) * (1.0 + half - u)
 
 
 def forward_kernel(
     nodes_t, from_prev, from_next, senders, w_send_t, recv_t, vertex_t, w_decode_t, to_next, to_prev,
     picked_t, slope_t, slope_sum_t, agg_t, upd_slope_t, hidden_t, field_t, next_t, prev_t,
+    pre,
 ):
     degree, count = senders.shape
     halo = from_prev.shape[1]
+    width = nodes_t.shape[0]
     ext = jnp.concatenate([nodes_t[...], from_prev[...], from_next[...]], axis=1)
-    total = jnp.zeros(recv_t.shape, F32)
-    slopes = jnp.zeros(recv_t.shape, F32)
     for k in range(degree):
-        picked = dot(ext, one_hot(count + 2 * halo, senders[k : k + 1, :])).astype(BF16)
-        picked_t[k] = picked
-        pre = dot(w_send_t[...], picked) + recv_t[...]
-        sigma = 0.5 * jnp.tanh(0.5 * pre) + 0.5
-        value = pre * sigma
-        total += value
-        slope = sigma * (1.0 + (pre - value)) * (1.0 / degree)
-        slopes += slope
-        slope_t[k] = slope.astype(slope_t.dtype)
-    slope_sum_t[...] = slopes
-    agg = (total * (1.0 / degree)).astype(BF16)
-    agg_t[...] = agg
-    upd = dot(vertex_t[...], agg)
-    sigma = 0.5 * jnp.tanh(0.5 * upd) + 0.5
-    value = upd * sigma
-    upd_slope_t[...] = sigma * (1.0 + (upd - value))
-    hidden = (nodes_t[...].astype(F32) + value).astype(BF16)
-    hidden_t[...] = hidden
-    field = dot(w_decode_t[...], hidden).astype(BF16)
+        here = slice(k * count, (k + 1) * count)
+        picked_t[:, here] = dot(ext, one_hot(count + 2 * halo, senders[k : k + 1, :])).astype(BF16)
+        pre[:, here] = dot(w_send_t[...], picked_t[:, here])
+    for start in range(0, width, TILE):
+        rows = slice(start, start + TILE)
+        recv = recv_t[rows, :]
+        total = slopes = None
+        for k in range(degree):
+            here = slice(k * count, (k + 1) * count)
+            value, slope = bent(pre[rows, here] + recv)
+            slope_t[rows, here] = slope.astype(BF16)
+            total = value if k == 0 else total + value
+            slopes = slope if k == 0 else slopes + slope
+        slope_sum_t[rows, :] = slopes
+        agg_t[rows, :] = (total * (1.0 / degree)).astype(BF16)
+    pre[:, :count] = dot(vertex_t[...], agg_t[...])
+    for start in range(0, width, TILE):
+        rows = slice(start, start + TILE)
+        value, slope = bent(pre[rows, :count])
+        upd_slope_t[rows, :] = slope * 0.5
+        hidden_t[rows, :] = (nodes_t[rows, :].astype(F32) + value).astype(BF16)
+    field = dot(w_decode_t[...], hidden_t[...]).astype(BF16)
     field_t[...] = field
     next_t[...] = dot(field, one_hot(count, to_next[...])).astype(BF16)
     prev_t[...] = dot(field, one_hot(count, to_prev[...])).astype(BF16)
@@ -106,54 +127,64 @@
 
 def readout_kernel(line_span, *refs):
     mids, ends = refs[0:4], refs[4:8]
-    mat_hi, mat_lo, base_t, truth_t = refs[8:12]
-    own_mid, own_end, pair_mid, pair_end, loss = refs[12:17]
-    table, grad = refs[17:19]
+    mat, base_t, truth_t = refs[8:11]
+    own_mid, own_end, pair_mid, pair_end, loss = refs[11:16]
+    table, grad, states, slopes = refs[16:20]
     step = pl.program_id(0)
     members = len(mids)
     variables, count = own_mid.shape
+    ext_rows = grad.shape[1]
 
     @pl.when(step == 0)
     def _():
         grad[...] = jnp.zeros_like(grad)
         loss[...] = jnp.zeros_like(loss)
         for m in range(members):
-            table[m * variables : (m + 1) * variables, :count] = mids[m][...]
-            table[m * variables : (m + 1) * variables, count:] = ends[m][...]
-
-    ready = base_t[...].astype(F32)
-    states = []
-    for m in range(members):
-        one = table[m * variables : (m + 1) * variables, :]
-        x = ready + (dot(one, mat_hi[...]) + dot(one, mat_lo[...]))
-        states.append(x.astype(BF16).astype(F32))
-    truth = truth_t[...].astype(F32)
+            for base in (0, ext_rows):
+                table[m * variables : (m + 1) * variables, base : base + count] = mids[m][...]
+                table[m * variables : (m + 1) * variables, base + count : base + ext_rows] = ends[m][...]
+
+    states[...] = dot(table[...], mat[...])
 
     def bend(diff):
         square = diff * diff + EPS
         inverse = lax.rsqrt(square)
         return square * inverse, diff * inverse
 
-    sizes = {}
-    for i in range(2):
-        for j in range(i + 1, members):
-            sizes[i, j] = bend(states[i] - states[j])
     alone = EPS**0.5
-    total = jnp.zeros_like(truth)
-    slopes = []
-    for i in range(2):
-        near, push = bend(states[i] - truth)
-        apart, pull = alone, 0.0
-        for j in range(members):
-            if j != i:
-                size, slope = sizes[min(i, j), max(i, j)]
-                apart = apart + size
-                pull = pull + slope if i < j else pull - slope
-        total += near * (1.0 / members) - apart * (1.0 / (2.0 * members * (members - 1)))
-        slope = push * (1.0 / members) - pull * (1.0 / (members * (members - 1.0)))
-        slopes.append((slope * (1.0 / line_span)).astype(BF16))
-    grad[...] += dot_nt(jnp.concatenate(slopes, axis=0), mat_hi[...])
-    loss[...] += jnp.sum(total.reshape(-1, 8, total.shape[1]), axis=0)
+    across = states.shape[1]
+    wide = min(256, across)
+    for left in range(0, across, wide):
+        cols = slice(left, left + wide)
+        summed = jnp.zeros((8, wide), F32)
+        for start in range(0, variables, TILE):
+            rows = slice(start, start + TILE)
+            ready = base_t[rows, cols].astype(F32)
+            truth = truth_t[rows, cols].astype(F32)
+            x = [
+                (states[m * variables + start : m * variables + start + TILE, cols] + ready).astype(BF16).astype(F32)
+                for m in range(members)
+            ]
+            apart = [alone, alone]
+            pull = [0.0, 0.0]
+            for i in range(2):
+                for j in range(i + 1, members):
+                    size, slope = bend(x[i] - x[j])
+                    apart[i] = apart[i] + size
+                    pull[i] = pull[i] + slope
+                    if j < 2:
+                        apart[j] = apart[j] + size
+                        pull[j] = pull[j] - slope
+            near = 0.0
+            for i in range(2):
+                size, push = bend(x[i] - truth)
+                near = near + size
+                slope = push * (1.0 / members / line_span) - pull[i] * (1.0 / (members * (members - 1.0)) / line_span)
+                slopes[i * variables + start : i * variables + start + TILE, cols] = slope.astype(BF16)
+            term = near * (1.0 / members) - (apart[0] + apart[1]) * (1.0 / (2.0 * members * (members - 1)))
+            summed += term[:8] + term[8:]
+        loss[:, cols] += summed
+    grad[...] += dot_nt(slopes[...], mat[:ext_rows, :])
 
     @pl.when(step == pl.num_programs(0) - 1)
     def _():
@@ -190,7 +221,7 @@
 def backward_kernel(
     parts, own_mid, pair_mid, from_next, from_prev, to_next, to_prev, term, w_decode, vertex, nodes_t,
     picked_t, slope_t, slope_sum_t, agg_t, upd_slope_t, hidden_t,
-    keep, send_far, send_near, whole,
+    keep, send_far, send_near, whole, back, grad_pre,
 ):
     count = nodes_t.shape[1]
     width = nodes_t.shape[0]
@@ -204,14 +235,17 @@
     whole[:, 3 * width : main] = dot_nt(hidden_t[...], grad_z)
     grad_upd = (dot(w_decode[...], grad_z) * upd_slope_t[...]).astype(BF16)
     whole[:, 2 * width : 3 * width] = dot_nt(agg_t[...], grad_upd)
-    grad_agg = dot(vertex[...], grad_upd)
-    grad_recv = (grad_agg * slope_sum_t[...]).astype(BF16)
-    whole[:, width : 2 * width] = dot_nt(nodes_t[...], grad_recv)
-    total = jnp.zeros((width, width), F32)
-    for k in range(picked_t.shape[0]):
-        grad_pre = (grad_agg * slope_t[k].astype(F32)).astype(BF16)
-        total += dot_nt(picked_t[k], grad_pre)
-    whole[:, :width] = total
+    degree = slope_t.shape[1] // count
+    back[...] = dot(vertex[...], grad_upd)
+    for start in range(0, width, TILE):
+        rows = slice(start, start + TILE)
+        grad_agg = back[rows, :] * (0.5 / degree)
+        grad_pre[rows, degree * count :] = (grad_agg * slope_sum_t[rows, :]).astype(BF16)
+        for k in range(degree):
+            here = slice(k * count, (k + 1) * count)
+            grad_pre[rows, here] = (grad_agg * slope_t[rows, here].astype(F32)).astype(BF16)
+    whole[:, width : 2 * width] = dot_nt(nodes_t[...], grad_pre[:, degree * count :])
+    whole[:, :width] = dot_nt(picked_t[...], grad_pre[:, : degree * count])
     whole[:, main:] = jnp.zeros((width, LANES), F32)
     spot = (lax.broadcasted_iota(jnp.int32, (8, LANES), 0) == 0) & (lax.broadcasted_iota(jnp.int32, (8, LANES), 1) == 0)
     whole[0:8, main:] = jnp.where(spot, jnp.sum(term[...]), 0.0)
@@ -302,16 +336,19 @@
     return lax.ppermute(value, axis, [(i, i ^ bit) for i in range(size)])
 
 
-def call(kernel, ins, outs, scratch=(), flops=0, scalars=0):
-    size = sum(x.size * x.dtype.itemsize for x in list(ins) + list(outs))
-    many = isinstance(outs, (list, tuple))
+def nbytes(arrays):
+    return sum(x.size * x.dtype.itemsize for x in arrays)
+
+
+def call(kernel, ins, outs, scratch=(), flops=0, room=4):
+    size = nbytes(list(ins) + list(outs))
     return pl.pallas_call(
         kernel,
         out_shape=outs,
-        in_specs=[SCALAR] * scalars + vmem(len(ins) - scalars),
+        in_specs=vmem(len(ins)),
         out_specs=vmem(len(outs)),
         scratch_shapes=list(scratch),
-        compiler_params=params(),
+        compiler_params=params(1.1 * size / MIB + room),
         cost_estimate=cost(flops, size),
     )(*ins)
 
@@ -333,7 +370,7 @@
         out_shape=[piece, piece],
         in_specs=[rows(quarter, 1), whole(got_far)],
         out_specs=[whole(piece)] * 2,
-        compiler_params=params(),
+        compiler_params=params(12),
         cost_estimate=cost(0, 8 * keep.size),
     )(keep, got_far)
     first, second = flip(first, "ens", 2), flip(second, "ens", 2)
@@ -345,7 +382,7 @@
             out_shape=outs,
             in_specs=[rows(half, at), rows(half, at), whole(far)],
             out_specs=[whole(x) for x in outs],
-            compiler_params=params(),
+            compiler_params=params(12),
             cost_estimate=cost(0, 8 * keep.size),
         )(keep, got_near, far)
 
@@ -401,11 +438,13 @@
         forward_kernel,
         [nodes_t, lat_prev, lat_next, senders, w_send_t, recv_t, vertex_t, w_decode_t, to_next, to_prev],
         [
-            sds((degree, width, count), BF16), sds((degree, width, count), BF16), sds((width, count), F32),
+            sds((width, degree * count), BF16), sds((width, degree * count), BF16), sds((width, count), F32),
             sds((width, count), BF16), sds((width, count), F32), sds((width, count), BF16),
             sds((variables, count), BF16), sds((variables, halo), BF16), sds((variables, halo), BF16),
         ],
+        [pltpu.VMEM((width, degree * count), F32)],
         flops=2 * degree * width * count * (ext_rows + width),
+        room=14,
     )
     lent = (along(next_t, "dom", 1), along(prev_t, "dom", -1))
     mids = [field_t] + [flip(field_t, "ens", m) for m in range(1, members)]
@@ -417,16 +456,16 @@
     tall_half = lambda rows: pl.BlockSpec((rows, block), lambda i, at: (0, i + at[0] * steps))
     flat_half = pl.BlockSpec((block, variables), lambda i, at: (i + at[0] * steps, 0))
     half_span = line_span // 2
-    mat_hi, mat_lo, base_t, truth_t = pl.pallas_call(
+    mat, base_t, truth_t = pl.pallas_call(
         decoder_kernel,
         grid_spec=pltpu.PrefetchScalarGridSpec(
             num_scalar_prefetch=1,
             grid=(steps,),
             in_specs=[tall_half(fan), tall_half(fan), flat_half, flat_half, pl.BlockSpec(memory_space=pl.ANY)],
-            out_specs=[tall(ext_rows), tall(ext_rows), tall(variables), tall(variables)],
+            out_specs=[tall(2 * ext_rows), tall(variables), tall(variables)],
         ),
-        out_shape=[sds((ext_rows, half_span), BF16)] * 2 + [sds((variables, half_span), BF16)] * 2,
-        compiler_params=params(),
+        out_shape=[sds((2 * ext_rows, half_span), BF16)] + [sds((variables, half_span), BF16)] * 2,
+        compiler_params=params(12),
         cost_estimate=cost(10 * ext_rows * half_span, 16e6),
     )(core, readout_vertex_list, dec_weights, base, observed_analysis, field_t)
 
@@ -438,13 +477,16 @@
         grid=(steps,),
         out_shape=[sds((variables, count), F32), sds((variables, 2 * halo), F32)] * 2 + [sds((8, block), F32)],
         in_specs=[fixed((variables, count))] * members + [fixed((variables, 2 * halo))] * members + [
-            tall(ext_rows), tall(ext_rows), tall(variables), tall(variables),
+            tall(2 * ext_rows), tall(variables), tall(variables),
         ],
         out_specs=[fixed((variables, count)), fixed((variables, 2 * halo))] * 2 + [fixed((8, block))],
-        scratch_shapes=[pltpu.VMEM((members * variables, ext_rows), BF16), pltpu.VMEM((2 * variables, ext_rows), F32)],
-        compiler_params=params(),
+        scratch_shapes=[
+            pltpu.VMEM((members * variables, 2 * ext_rows), BF16), pltpu.VMEM((2 * variables, ext_rows), F32),
+            pltpu.VMEM((members * variables, block), F32), pltpu.VMEM((2 * variables, block), BF16),
+        ],
+        compiler_params=params(20),
         cost_estimate=cost(4 * members * variables * ext_rows * half_span, 14e6),
-    )(*mids, *ends, mat_hi, mat_lo, base_t, truth_t)
+    )(*mids, *ends, mat, base_t, truth_t)
     own_mid, own_end, pair_mid, pair_end, term = grads
     got_end = flip(pair_end, "ens", 1)
     got_mid = flip(pair_mid, "ens", 1)
@@ -463,8 +505,9 @@
             vertex_refresh_matrix, nodes_t, picked_t, slope_t, slope_sum_t, agg_t, upd_slope_t, hidden_t,
         ],
         [sds((2 * quarter, cols), F32), sds((quarter, cols), BF16), sds((quarter, cols), BF16)],
-        [pltpu.VMEM((width, cols), F32)],
+        [pltpu.VMEM((width, cols), F32), pltpu.VMEM((width, count), F32), pltpu.VMEM((width, (degree + 1) * count), BF16)],
         flops=2 * (degree + 3) * width * width * count,
+        room=16,
     )
     mine = reduced(keep, send_far, send_near, parts)
     across = [flip(x, "ens", 2) for x in mine]
@@ -475,7 +518,7 @@
         out_shape=[sds((width, width), F32)] * 3 + [sds((width, variables), F32), sds((1, 1), F32)],
         in_specs=vmem(8),
         out_specs=vmem(4) + [SCALAR],
-        compiler_params=params(),
+        compiler_params=params(14),
         cost_estimate=cost(0, 6 * width * cols),
     )(*mine, *beside, *across, *corner)
     return g_send, g_recv, g_update, g_decode, loss[0, 0]

time: 148 us -> 124 us (0.84)
  Pallas kernels: 62 us -> 27.2 us
  local copies, waits for them, and re-layouts: 7.79 us -> 16.1 us
  waiting for transfers between devices: 34.6 us -> 40.4 us
  starting transfers between devices: 41.9 us -> 38.7 us
    pallas_call x8, Pallas kernels: 33.9 us -> 12.3 us  [call(): pl.pallas_call(kernel, out_shape=outs, in_specs=vmem(len(ins)), out_specs...]
    unnamed x75 -> x61, local copies, waits for them, and re-layouts: 7.77 us -> 16.1 us
    pallas_call x1, Pallas kernels: 8.54 us -> 3.44 us  [per_device(): pl.pallas_call(decoder_kernel, grid_spec=pltpu.PrefetchScalarGridSpec(num...]
    ppermute x18, waiting for transfers between devices: 17.6 us -> 21.7 us  [flip(): return lax.ppermute(value, axis, [(i, i ^ bit) for i in range(size)])]
    pallas_call x2, Pallas kernels: 3.94 us -> 0.2 us  [shares(): pl.pallas_call(shares_kernel, grid=(1,), out_shape=outs, in_specs=[rows(h...]
    ppermute x20, starting transfers between devices: 32.1 us -> 29 us  [along(): lax.ppermute(value, axis, [(i, (i + steps) % size) for i in range(size)])]
    pallas_call x1, Pallas kernels: 2.14 us -> 0.14 us  [reduced(): pl.pallas_call(chip_kernel, grid=(1,), out_shape=[piece, piece], in_specs...]
    ppermute x20, waiting for transfers between devices: 17 us -> 18.7 us  [along(): lax.ppermute(value, axis, [(i, (i + steps) % size) for i in range(size)])]
  transfers between devices with their start and end apart: 38 -> 38, of which waited for: 18 -> 18; matrix products, arithmetic and copies ran while one was open for 0% -> 0% of each run, Pallas kernels for 15% -> 4%
where the time goes in v4:
time: 124 us
  waiting for transfers between devices  40.4 us (33%)
  starting transfers between devices  38.7 us (31%)
  Pallas kernels  27.2 us (22%)
  local copies, waits for them, and re-layouts  16.1 us (13%)
    ppermute x20, starting transfers between devices, along(): lax.ppermute(value, axis, [(i, (i + steps) % size) for i in range(size)])  29 us
    ppermute x18, waiting for transfers between devices, flip(): return lax.ppermute(value, axis, [(i, i ^ bit) for i in range(size)])  21.7 us
    ppermute x20, waiting for transfers between devices, along(): lax.ppermute(value, axis, [(i, (i + steps) % size) for i in range(size)])  18.7 us
    unnamed x61, local copies, waits for them, and re-layouts  16.1 us
    pallas_call x8, Pallas kernels, call(): pl.pallas_call(kernel, out_shape=outs, in_specs=vmem(len(ins)), out_specs...  12.3 us
    ppermute x18, starting transfers between devices, flip(): return lax.ppermute(value, axis, [(i, i ^ bit) for i in range(size)])  9.66 us
    pallas_call x1, Pallas kernels, per_device(): pl.pallas_call(functools.partial(readout_kernel, line_span), grid=(steps,...  9.2 us
    pallas_call x1, Pallas kernels, per_device(): pl.pallas_call(decoder_kernel, grid_spec=pltpu.PrefetchScalarGridSpec(num...  3.44 us
  transfers between devices with their start and end apart: 38, of which 18 were waited for; matrix products, arithmetic and copies ran while one was open for 0% of the time, Pallas kernels for 4%

profile of v4, /device:TPU:0, one launch (start us, length us, event | category | flops | bytes accessed | tf_op | source)
XLA Modules:
  0.0 123.5 jit_solution(6558638380269726130)
XLA Ops:
  0.6 1.0 copy-done.20
  1.7 0.7 copy-done.23
  2.3 0.7 copy-done.26
  3.0 0.5 shard_map.155
  3.5 3.0 %collective-permute-start = (bf16[512,128]{1,0:T(8,128)(2,1)S(1)}, bf16[512,128]{1,0:T(8,128)(2,1)S(1)}, u32[]{:S(2)}, u32[]{:S(2)}) collective-permute-start(bf16[512,128]{1,0:T(8,128)(2,1)S(1)} %get-tuple-element.50), channel_id=1, source_target_pairs={{0,1},{1,2},{2,3},{3,4},{4,5},{5,6},{6,7},{7,0},{8,9},{9,10},{10,1... | collective-permute-start | bytes 393224 | tf_op jit(solution)/shard_map/ppermute | solution.py:331
  6.5 3.1 %collective-permute-start.1 = (bf16[512,128]{1,0:T(8,128)(2,1)S(1)}, bf16[512,128]{1,0:T(8,128)(2,1)S(1)}, u32[]{:S(2)}, u32[]{:S(2)}) collective-permute-start(bf16[512,128]{1,0:T(8,128)(2,1)S(1)} %get-tuple-element.51), channel_id=1, source_target_pairs={{0,7},{1,0},{2,1},{3,2},{4,3},{5,4},{6,5},{7,6},{8,15},{9,8},{10,9... | collective-permute-start | bytes 393224 | tf_op jit(solution)/shard_map/ppermute | solution.py:331
  9.6 1.0 copy-done.2
  10.6 0.9 copy-done.12
  11.5 1.0 copy-done.14
  12.6 1.0 copy-done.15
  13.6 0.5 shard_map.156
  14.3 0.7 copy-done.24
  14.9 0.7 copy-done.27
  15.6 0.7 copy-done.29
  16.3 7.5 %shard_map.157 = (bf16[512,3072]{1,0:T(8,128)(2,1)S(1)}, bf16[512,3072]{1,0:T(8,128)(2,1)S(1)}, f32[512,512]{1,0:T(8,128)S(1)}, bf16[512,512]{1,0:T(8,128)(2,1)S...) custom-call(bf16[512,512]{1,0:T(8,128)(2,1)S(1)} %get-tuple-element., ...), custom_call_target="tpu_custom_call" | custom-call | flops 4026531840 | bytes 12661760 | tf_op jit(solution)/shard_map/pallas_call | solution.py:345
  23.8 1.6 %copy-done = bf16[512,3072]{1,0:T(8,128)(2,1)} copy-done((bf16[512,3072]{1,0:T(8,128)(2,1)}, bf16[512,3072]{1,0:T(8,128)(2,1)S(1)}, u32[]{:S(2)}) %copy-start) | copy-done | bytes 3145752
  25.5 1.0 copy-done.6
  26.4 1.0 copy-done.8
  27.4 0.8 copy-done.16
  28.2 0.8 copy-done.18
  29.3 4.5 %collective-permute-start.6 = (bf16[128,128]{1,0:T(8,128)(2,1)S(1)}, bf16[128,128]{1,0:T(8,128)(2,1)S(1)}, u32[]{:S(2)}, u32[]{:S(2)}) collective-permute-start(bf16[128,128]{1,0:T(8,128)(2,1)S(1)} %get-tuple-element.58), channel_id=1, source_target_pairs={{0,7},{1,0},{2,1},{3,2},{4,3},{5,4},{6,5},{7,6},{8,15},{9,8},{10,9... | collective-permute-start | bytes 98312 | tf_op jit(solution)/shard_map/ppermute | solution.py:331
  33.7 1.9 %collective-permute-done.5 = bf16[128,128]{1,0:T(8,128)(2,1)S(1)} collective-permute-done((bf16[128,128]{1,0:T(8,128)(2,1)S(1)}, bf16[128,128]{1,0:T(8,128)(2,1)S(1)}, u32[]{:S(2)}, u32[]{:S(2)}) %collective-permute-start.5) | collective-permute-done | bytes 32800 | tf_op jit(solution)/shard_map/ppermute | solution.py:331
  35.7 1.7 %collective-permute-start.4 = (bf16[128,512]{1,0:T(8,128)(2,1)S(1)}, bf16[128,512]{1,0:T(8,128)(2,1)}, u32[]{:S(2)}, u32[]{:S(2)}) collective-permute-start(bf16[128,512]{1,0:T(8,128)(2,1)S(1)} %get-tuple-element.56.after.refs_0_), channel_id=1, source_target_pairs={{0,24},{8,16},{16,8},{24,0},{1,25},{9,17},{17,9},{25,1},{2,26},{10... | collective-permute-start | bytes 393224 | tf_op jit(solution)/shard_map/ppermute | solution.py:336
  37.5 1.5 %collective-permute-start.3 = (bf16[128,512]{1,0:T(8,128)(2,1)S(1)}, bf16[128,512]{1,0:T(8,128)(2,1)}, u32[]{:S(2)}, u32[]{:S(2)}) collective-permute-start(bf16[128,512]{1,0:T(8,128)(2,1)S(1)} %get-tuple-element.56.after.refs_0_), channel_id=1, source_target_pairs={{0,16},{8,24},{16,0},{24,8},{1,17},{9,25},{17,1},{25,9},{2,18},{10... | collective-permute-start | bytes 393224 | tf_op jit(solution)/shard_map/ppermute | solution.py:336
  39.0 0.5 collective-permute-start.8
  39.5 0.6 collective-permute-done.9.refs_7_
  40.0 0.3 collective-permute-start.7
  40.4 1.2 copy-done.10
  41.6 1.2 copy-done.11
  42.8 3.4 %shard_map.158 = (bf16[1536,2048]{1,0:T(8,128)(2,1)S(1)}, bf16[128,2048]{1,0:T(8,128)(2,1)S(1)}, bf16[128,2048]{1,0:T(8,128)(2,1)S(1)}) custom-call(s32[1]{0:T(128)} %bitcast.3.core, s32[3,4096]{1,0:T(4,128)S(1)} %copy-done.21, f32[3,4096]{1,0:T(4,128)S(1)} %copy-done.22, bf16[4096,128]{1,0:T(8,128)(2,1)S(1)} %copy-done.10, ...), custom_call_target="tpu_custom_call" | custom-call | flops 15728640 | bytes 16000000 | tf_op jit(solution)/shard_map/pallas_call | solution.py:459
  46.3 0.9 collective-permute-done.8.refs_6_
  47.4 9.2 %shard_map.159 = (f32[128,512]{1,0:T(8,128)S(1)}, f32[128,256]{1,0:T(8,128)S(1)}, f32[128,512]{1,0:T(8,128)S(1)}, f32[128,256]{1,0:T(8,128)S(1)}, f32[8,512]{1,0:T(8,128)S(1)}) custom-call(bf16[128,512]{1,0:T(8,128)(2,1)S(1)} %get-tuple-element.56.after.refs_0_, bf16[128,512]{1,0:T(8,128)(2,1)} %collective-permute-done.2.refs_1_, ...), custom_call_target="tpu_custom_call" | custom-call | flops 3221225472 | bytes 14000000 | tf_op jit(solution)/shard_map/pallas_call | solution.py:475
  56.7 0.5 collective-permute-start.11
  57.2 1.2 collective-permute-done.11.got
  58.4 4.8 %collective-permute-start.12 = (f32[128,128]{1,0:T(8,128)S(1)}, f32[128,128]{1,0:T(8,128)S(1)}, u32[]{:S(2)}, u32[]{:S(2)}) collective-permute-start(f32[128,128]{1,0:T(8,128)S(1)} %get-tuple-element.66), channel_id=1, source_target_pairs={{0,7},{1,0},{2,1},{3,2},{4,3},{5,4},{6,5},{7,6},{8,15},{9,8},{10,9... | collective-permute-start | bytes 196616 | tf_op jit(solution)/shard_map/ppermute | solution.py:331
  63.1 1.9 %collective-permute-done.12.from_next = f32[128,128]{1,0:T(8,128)S(1)} collective-permute-done((f32[128,128]{1,0:T(8,128)S(1)}, f32[128,128]{1,0:T(8,128)S(1)}, u32[]{:S(2)}, u32[]{:S(2)}) %collective-permute-start.12) | collective-permute-done | bytes 65568 | tf_op jit(solution)/shard_map/ppermute | solution.py:331
  65.0 5.1 %collective-permute-done.13.from_prev = f32[128,128]{1,0:T(8,128)S(1)} collective-permute-done((f32[128,128]{1,0:T(8,128)S(1)}, f32[128,128]{1,0:T(8,128)S(1)}, u32[]{:S(2)}, u32[]{:S(2)}) %collective-permute-start.13) | collective-permute-done | bytes 65568 | tf_op jit(solution)/shard_map/ppermute | solution.py:331
  70.2 3.6 %shard_map.161 = (f32[256,1792]{1,0:T(8,128)S(1)}, bf16[128,1792]{1,0:T(8,128)(2,1)S(1)}, bf16[128,1792]{1,0:T(8,128)(2,1)S(1)}) custom-call(f32[128,512]{1,0:T(8,128)S(1)} %get-tuple-element.62.own_mid, f32[128,512]{1,0:T(8,128)S(1)} %collective-permute-done.10.pair_mid, f32[128,128]{1,0:T(8,128)S(1)} %collective-permute-done.12.from_next, ...), custom_call_target="tpu_custom_call" | custom-call | flops 2415919104 | bytes 14042112 | tf_op jit(solution)/shard_map/pallas_call | solution.py:345
  73.9 0.5 collective-permute-start.14
  74.4 1.3 %collective-permute-done.15.got = bf16[128,1792]{1,0:T(8,128)(2,1)S(1)} collective-permute-done((bf16[128,1792]{1,0:T(8,128)(2,1)S(1)}, bf16[128,1792]{1,0:T(8,128)(2,1)S(1)}, u32[]{:S(2)}, u32[]{:S(2)}) %collective-permute-start.15) | collective-permute-done | bytes 458784 | tf_op jit(solution)/shard_map/ppermute | solution.py:336
  75.8 0.9 collective-permute-start.16
  76.7 1.2 collective-permute-start.20
  77.9 6.4 %collective-permute-done.16.far = bf16[64,1792]{1,0:T(8,128)(2,1)S(1)} collective-permute-done((bf16[64,1792]{1,0:T(8,128)(2,1)S(1)}, bf16[64,1792]{1,0:T(8,128)(2,1)S(1)}, u32[]{:S(2)}, u32[]{:S(2)}) %collective-permute-start.16) | collective-permute-done | bytes 229408 | tf_op jit(solution)/shard_map/ppermute | solution.py:336
  84.7 3.8 %collective-permute-done.20.far = bf16[64,1792]{1,0:T(8,128)(2,1)S(1)} collective-permute-done((bf16[64,1792]{1,0:T(8,128)(2,1)S(1)}, bf16[64,1792]{1,0:T(8,128)(2,1)S(1)}, u32[]{:S(2)}, u32[]{:S(2)}) %collective-permute-start.20) | collective-permute-done | bytes 229408 | tf_op jit(solution)/shard_map/ppermute | solution.py:336
  88.6 0.5 collective-permute-start.21
  89.2 1.9 %collective-permute-start.23 = (bf16[16,1792]{1,0:T(8,128)(2,1)S(1)}, bf16[16,1792]{1,0:T(8,128)(2,1)S(1)}, u32[]{:S(2)}, u32[]{:S(2)}) collective-permute-start(bf16[16,1792]{1,0:T(8,128)(2,1)S(1)} %get-tuple-element.86), channel_id=1, source_target_pairs={{0,2},{1,3},{2,4},{3,5},{4,6},{5,7},{6,0},{7,1},{8,10},{9,11},{10,... | collective-permute-start | bytes 172040 | tf_op jit(solution)/shard_map/ppermute | solution.py:331
  91.1 2.0 %collective-permute-start.24 = (bf16[16,1792]{1,0:T(8,128)(2,1)S(1)}, bf16[16,1792]{1,0:T(8,128)(2,1)S(1)}, u32[]{:S(2)}, u32[]{:S(2)}) collective-permute-start(bf16[16,1792]{1,0:T(8,128)(2,1)S(1)} %get-tuple-element.87), channel_id=1, source_target_pairs={{0,1},{1,2},{2,3},{3,4},{4,5},{5,6},{6,7},{7,0},{8,9},{9,10},{10,1... | collective-permute-start | bytes 172040 | tf_op jit(solution)/shard_map/ppermute | solution.py:331
  93.1 3.0 %collective-permute-done.21.refs_4_ = bf16[16,1792]{1,0:T(8,128)(2,1)S(1)} collective-permute-done((bf16[16,1792]{1,0:T(8,128)(2,1)S(1)}, bf16[16,1792]{1,0:T(8,128)(2,1)S(1)}, u32[]{:S(2)}, u32[]{:S(2)}) %collective-permute-start.21) | collective-permute-done | bytes 57376 | tf_op jit(solution)/shard_map/ppermute | solution.py:331
  96.1 2.9 %collective-permute-done.24.refs_7_ = bf16[16,1792]{1,0:T(8,128)(2,1)S(1)} collective-permute-done((bf16[16,1792]{1,0:T(8,128)(2,1)S(1)}, bf16[16,1792]{1,0:T(8,128)(2,1)S(1)}, u32[]{:S(2)}, u32[]{:S(2)}) %collective-permute-start.24) | collective-permute-done | bytes 57376 | tf_op jit(solution)/shard_map/ppermute | solution.py:331
  99.2 0.6 collective-permute-start.26
  99.8 1.5 %collective-permute-start.25 = (bf16[16,1792]{1,0:T(8,128)(2,1)S(1)}, bf16[16,1792]{1,0:T(8,128)(2,1)S(1)}, u32[]{:S(2)}, u32[]{:S(2)}) collective-permute-start(bf16[16,1792]{1,0:T(8,128)(2,1)S(1)} %shard_map.165.refs_0_), channel_id=1, source_target_pairs={{0,1},{1,2},{2,3},{3,4},{4,5},{5,6},{6,7},{7,0},{8,9},{9,10},{10,1... | collective-permute-start | bytes 172040 | tf_op jit(solution)/shard_map/ppermute | solution.py:331
  101.3 3.2 %collective-permute-start.31 = (bf16[16,1792]{1,0:T(8,128)(2,1)S(1)}, bf16[16,1792]{1,0:T(8,128)(2,1)S(1)}, u32[]{:S(2)}, u32[]{:S(2)}) collective-permute-start(bf16[16,1792]{1,0:T(8,128)(2,1)S(1)} %shard_map.165.refs_0_), channel_id=1, source_target_pairs={{0,7},{1,0},{2,1},{3,2},{4,3},{5,4},{6,5},{7,6},{8,15},{9,8},{10,9... | collective-permute-start | bytes 172040 | tf_op jit(solution)/shard_map/ppermute | solution.py:331
  104.5 1.5 %collective-permute-start.30 = (bf16[16,1792]{1,0:T(8,128)(2,1)S(1)}, bf16[16,1792]{1,0:T(8,128)(2,1)S(1)}, u32[]{:S(2)}, u32[]{:S(2)}) collective-permute-start(bf16[16,1792]{1,0:T(8,128)(2,1)S(1)} %shard_map.165.refs_0_), channel_id=1, source_target_pairs={{0,6},{1,7},{2,0},{3,1},{4,2},{5,3},{6,4},{7,5},{8,14},{9,15},{10,... | collective-permute-start | bytes 172040 | tf_op jit(solution)/shard_map/ppermute | solution.py:331
  106.0 1.0 collective-permute-done.27.refs_3_
  107.1 1.8 %collective-permute-start.28 = (bf16[16,1792]{1,0:T(8,128)(2,1)S(1)}, bf16[16,1792]{1,0:T(8,128)(2,1)S(1)}, u32[]{:S(2)}, u32[]{:S(2)}) collective-permute-start(bf16[16,1792]{1,0:T(8,128)(2,1)S(1)} %shard_map.165.refs_0_), channel_id=1, source_target_pairs={{0,4},{1,5},{2,6},{3,7},{4,0},{5,1},{6,2},{7,3},{8,12},{9,13},{10,... | collective-permute-start | bytes 172040 | tf_op jit(solution)/shard_map/ppermute | solution.py:331
  108.9 0.9 collective-permute-start.34
  109.8 2.3 %collective-permute-done.29.refs_1_ = bf16[16,1792]{1,0:T(8,128)(2,1)S(1)} collective-permute-done((bf16[16,1792]{1,0:T(8,128)(2,1)S(1)}, bf16[16,1792]{1,0:T(8,128)(2,1)S(1)}, u32[]{:S(2)}, u32[]{:S(2)}) %collective-permute-start.29) | collective-permute-done | bytes 57376 | tf_op jit(solution)/shard_map/ppermute | solution.py:331
  112.0 0.5 collective-permute-done.28.refs_0_
  112.5 0.9 collective-permute-start.35
  113.4 0.5 collective-permute-start.33
  113.9 2.9 %collective-permute-done.34.refs_4_ = bf16[64,1792]{1,0:T(8,128)(2,1)S(1)} collective-permute-done((bf16[64,1792]{1,0:T(8,128)(2,1)S(1)}, bf16[64,1792]{1,0:T(8,128)(2,1)S(1)}, u32[]{:S(2)}, u32[]{:S(2)}) %collective-permute-start.34) | collective-permute-done | bytes 229408 | tf_op jit(solution)/shard_map/ppermute | solution.py:336
  116.8 3.1 %collective-permute-done.35.refs_5_ = bf16[64,1792]{1,0:T(8,128)(2,1)S(1)} collective-permute-done((bf16[64,1792]{1,0:T(8,128)(2,1)S(1)}, bf16[64,1792]{1,0:T(8,128)(2,1)S(1)}, u32[]{:S(2)}, u32[]{:S(2)}) %collective-permute-start.35) | collective-permute-done | bytes 229408 | tf_op jit(solution)/shard_map/ppermute | solution.py:336
  119.9 1.5 %collective-permute-done.37.refs_7_ = bf16[64,1792]{1,0:T(8,128)(2,1)S(1)} collective-permute-done((bf16[64,1792]{1,0:T(8,128)(2,1)S(1)}, bf16[64,1792]{1,0:T(8,128)(2,1)S(1)}, u32[]{:S(2)}, u32[]{:S(2)}) %collective-permute-start.37) | collective-permute-done | bytes 229408 | tf_op jit(solution)/shard_map/ppermute | solution.py:336
  121.4 2.0 %shard_map.168 = (f32[512,512]{1,0:T(8,128)}, f32[512,512]{1,0:T(8,128)}, f32[512,512]{1,0:T(8,128)}, f32[512,128]{1,0:T(8,128)}, f32[1,1]{1,0:T(1,128)}) custom-call(bf16[64,1792]{1,0:T(8,128)(2,1)S(1)} %shard_map.166.refs_0_, bf16[64,1792]{1,0:T(8,128)(2,1)S(1)} %shard_map.167.refs_1_, bf16[64,1792]{1,0:T(8,128)(2,1)S(1)} %collective-permute-done.32.refs_2_, ...), custom_call_target="tpu_custom_call" | custom-call | bytes 5505024 | tf_op jit(solution)/shard_map/pallas_call | solution.py:516
  (88 shorter events, 1.7 us)
Async XLA Ops:
  0.6 1.0 copy-start.20
  3.5 20.3 %copy-start.4 = (bf16[512,512]{1,0:T(8,128)(2,1)}, bf16[512,512]{1,0:T(8,128)(2,1)S(1)}, u32[]{:S(2)}) copy-start(bf16[512,512]{1,0:T(8,128)(2,1)S(1)} %get-tuple-element.49.nodes_t) | copy-start | bytes 1572868
  3.5 10.7 %collective-permute-start = (bf16[512,128]{1,0:T(8,128)(2,1)S(1)}, bf16[512,128]{1,0:T(8,128)(2,1)S(1)}, u32[]{:S(2)}, u32[]{:S(2)}) collective-permute-start(bf16[512,128]{1,0:T(8,128)(2,1)S(1)} %get-tuple-element.50), channel_id=1, source_target_pairs={{0,1},{1,2},{2,3},{3,4},{4,5},{5,6},{6,7},{7,0},{8,9},{9,10},{10,1... | collective-permute-start | bytes 393224 | tf_op jit(solution)/shard_map/ppermute | solution.py:331
  6.5 7.8 %collective-permute-start.1 = (bf16[512,128]{1,0:T(8,128)(2,1)S(1)}, bf16[512,128]{1,0:T(8,128)(2,1)S(1)}, u32[]{:S(2)}, u32[]{:S(2)}) collective-permute-start(bf16[512,128]{1,0:T(8,128)(2,1)S(1)} %get-tuple-element.51), channel_id=1, source_target_pairs={{0,7},{1,0},{2,1},{3,2},{4,3},{5,4},{6,5},{7,6},{8,15},{9,8},{10,9... | collective-permute-start | bytes 393224 | tf_op jit(solution)/shard_map/ppermute | solution.py:331
  9.6 1.0 copy-start.2
  10.6 0.9 copy-start.12
  11.5 1.0 copy-start.14
  12.6 1.0 copy-start.15
  15.6 0.7 copy-start.29
  16.3 24.1 %copy-start.21 = (s32[3,4096]{1,0:T(4,128)S(1)}, s32[3,4096]{1,0:T(4,128)}, u32[]{:S(2)}) copy-start(s32[3,4096]{1,0:T(4,128)} %vertices.1) | copy-start | bytes 147460
  16.3 24.1 %copy-start.22 = (f32[3,4096]{1,0:T(4,128)S(1)}, f32[3,4096]{1,0:T(4,128)}, u32[]{:S(2)}) copy-start(f32[3,4096]{1,0:T(4,128)} %weights.1) | copy-start | bytes 147460
  23.8 1.6 %copy-start = (bf16[512,3072]{1,0:T(8,128)(2,1)}, bf16[512,3072]{1,0:T(8,128)(2,1)S(1)}, u32[]{:S(2)}) copy-start(bf16[512,3072]{1,0:T(8,128)(2,1)S(1)} %get-tuple-element.70.slope_t) | copy-start | bytes 9437188
  25.5 1.0 copy-start.6
  26.4 1.0 copy-start.8
  27.4 0.8 copy-start.16
  28.2 0.8 copy-start.18
  29.0 6.6 %collective-permute-start.5 = (bf16[128,128]{1,0:T(8,128)(2,1)S(1)}, bf16[128,128]{1,0:T(8,128)(2,1)S(1)}, u32[]{:S(2)}, u32[]{:S(2)}) collective-permute-start(bf16[128,128]{1,0:T(8,128)(2,1)S(1)} %get-tuple-element.57), channel_id=1, source_target_pairs={{0,1},{1,2},{2,3},{3,4},{4,5},{5,6},{6,7},{7,0},{8,9},{9,10},{10,1... | collective-permute-start | bytes 98312 | tf_op jit(solution)/shard_map/ppermute | solution.py:331
  29.3 6.4 %collective-permute-start.6 = (bf16[128,128]{1,0:T(8,128)(2,1)S(1)}, bf16[128,128]{1,0:T(8,128)(2,1)S(1)}, u32[]{:S(2)}, u32[]{:S(2)}) collective-permute-start(bf16[128,128]{1,0:T(8,128)(2,1)S(1)} %get-tuple-element.58), channel_id=1, source_target_pairs={{0,7},{1,0},{2,1},{3,2},{4,3},{5,4},{6,5},{7,6},{8,15},{9,8},{10,9... | collective-permute-start | bytes 98312 | tf_op jit(solution)/shard_map/ppermute | solution.py:331
  35.6 4.4 %collective-permute-start.9 = (bf16[128,256]{1,0:T(8,128)(2,1)S(1)}, bf16[128,256]{1,0:T(8,128)(2,1)S(1)}, u32[]{:S(2)}, u32[]{:S(2)}) collective-permute-start(bf16[128,256]{1,0:T(8,128)(2,1)S(1)} %constant_dynamic-update-slice_fusion.refs_4_), channel_id=1, source_target_pairs={{0,24},{8,16},{16,8},{24,0},{1,25},{9,17},{17,9},{25,1},{2,26},{10... | collective-permute-start | bytes 196616 | tf_op jit(solution)/shard_map/ppermute | solution.py:336
  35.7 11.5 %collective-permute-start.4 = (bf16[128,512]{1,0:T(8,128)(2,1)S(1)}, bf16[128,512]{1,0:T(8,128)(2,1)}, u32[]{:S(2)}, u32[]{:S(2)}) collective-permute-start(bf16[128,512]{1,0:T(8,128)(2,1)S(1)} %get-tuple-element.56.after.refs_0_), channel_id=1, source_target_pairs={{0,24},{8,16},{16,8},{24,0},{1,25},{9,17},{17,9},{25,1},{2,26},{10... | collective-permute-start | bytes 393224 | tf_op jit(solution)/shard_map/ppermute | solution.py:336
  37.5 9.8 %collective-permute-start.3 = (bf16[128,512]{1,0:T(8,128)(2,1)S(1)}, bf16[128,512]{1,0:T(8,128)(2,1)}, u32[]{:S(2)}, u32[]{:S(2)}) collective-permute-start(bf16[128,512]{1,0:T(8,128)(2,1)S(1)} %get-tuple-element.56.after.refs_0_), channel_id=1, source_target_pairs={{0,16},{8,24},{16,0},{24,8},{1,17},{9,25},{17,1},{25,9},{2,18},{10... | collective-permute-start | bytes 393224 | tf_op jit(solution)/shard_map/ppermute | solution.py:336
  39.0 8.3 %collective-permute-start.2 = (bf16[128,512]{1,0:T(8,128)(2,1)S(1)}, bf16[128,512]{1,0:T(8,128)(2,1)}, u32[]{:S(2)}, u32[]{:S(2)}) collective-permute-start(bf16[128,512]{1,0:T(8,128)(2,1)S(1)} %get-tuple-element.56.after.refs_0_), channel_id=1, source_target_pairs={{0,8},{8,0},{16,24},{24,16},{1,9},{9,1},{17,25},{25,17},{2,10},{10... | collective-permute-start | bytes 393224 | tf_op jit(solution)/shard_map/ppermute | solution.py:336
  39.0 8.3 %collective-permute-start.8 = (bf16[128,256]{1,0:T(8,128)(2,1)S(1)}, bf16[128,256]{1,0:T(8,128)(2,1)}, u32[]{:S(2)}, u32[]{:S(2)}) collective-permute-start(bf16[128,256]{1,0:T(8,128)(2,1)S(1)} %constant_dynamic-update-slice_fusion.refs_4_), channel_id=1, source_target_pairs={{0,16},{8,24},{16,0},{24,8},{1,17},{9,25},{17,1},{25,9},{2,18},{10... | collective-permute-start | bytes 196616 | tf_op jit(solution)/shard_map/ppermute | solution.py:336
  40.0 7.2 %collective-permute-start.7 = (bf16[128,256]{1,0:T(8,128)(2,1)S(1)}, bf16[128,256]{1,0:T(8,128)(2,1)}, u32[]{:S(2)}, u32[]{:S(2)}) collective-permute-start(bf16[128,256]{1,0:T(8,128)(2,1)S(1)} %constant_dynamic-update-slice_fusion.refs_4_), channel_id=1, source_target_pairs={{0,8},{8,0},{16,24},{24,16},{1,9},{9,1},{17,25},{25,17},{2,10},{10... | collective-permute-start | bytes 196616 | tf_op jit(solution)/shard_map/ppermute | solution.py:336
  40.4 1.2 copy-start.10
  41.6 1.2 copy-start.11
  47.2 22.9 %copy-start.1 = (bf16[512,3072]{1,0:T(8,128)(2,1)S(1)}, bf16[512,3072]{1,0:T(8,128)(2,1)}, u32[]{:S(2)}) copy-start(bf16[512,3072]{1,0:T(8,128)(2,1)} %copy-done) | copy-start | bytes 9437188
  47.3 22.9 %copy-start.3 = (bf16[512,512]{1,0:T(8,128)(2,1)S(1)}, bf16[512,512]{1,0:T(8,128)(2,1)}, u32[]{:S(2)}) copy-start(bf16[512,512]{1,0:T(8,128)(2,1)} %vertex.3) | copy-start | bytes 1572868
  47.3 22.8 %copy-start.5 = (bf16[512,512]{1,0:T(8,128)(2,1)S(1)}, bf16[512,512]{1,0:T(8,128)(2,1)}, u32[]{:S(2)}) copy-start(bf16[512,512]{1,0:T(8,128)(2,1)} %copy-done.4) | copy-start | bytes 1572868
  47.3 22.8 %copy-start.7 = (f32[512,512]{1,0:T(8,128)S(1)}, f32[512,512]{1,0:T(8,128)}, u32[]{:S(2)}) copy-start(f32[512,512]{1,0:T(8,128)} %copy-done.6) | copy-start | bytes 3145732
  47.3 22.8 %copy-start.9 = (f32[512,512]{1,0:T(8,128)S(1)}, f32[512,512]{1,0:T(8,128)}, u32[]{:S(2)}) copy-start(f32[512,512]{1,0:T(8,128)} %copy-done.8) | copy-start | bytes 3145732
  47.3 22.8 %copy-start.13 = (bf16[512,128]{1,0:T(8,128)(2,1)S(1)}, bf16[512,128]{1,0:T(8,128)(2,1)}, u32[]{:S(2)}) copy-start(bf16[512,128]{1,0:T(8,128)(2,1)} %w_decode.3) | copy-start | bytes 393220
  47.3 22.8 %copy-start.17 = (bf16[512,512]{1,0:T(8,128)(2,1)S(1)}, bf16[512,512]{1,0:T(8,128)(2,1)}, u32[]{:S(2)}) copy-start(bf16[512,512]{1,0:T(8,128)(2,1)} %copy-done.16) | copy-start | bytes 1572868
  47.3 22.8 %copy-start.19 = (bf16[512,512]{1,0:T(8,128)(2,1)S(1)}, bf16[512,512]{1,0:T(8,128)(2,1)}, u32[]{:S(2)}) copy-start(bf16[512,512]{1,0:T(8,128)(2,1)} %copy-done.18) | copy-start | bytes 1572868
  47.3 22.8 %copy-start.25 = (s32[128]{0:T(128)S(1)}, s32[128]{0:T(128)}, u32[]{:S(2)}) copy-start(s32[128]{0:T(128)} %param.14) | copy-start | bytes 1540
  47.4 22.8 %copy-start.28 = (s32[128]{0:T(128)S(1)}, s32[128]{0:T(128)}, u32[]{:S(2)}) copy-start(s32[128]{0:T(128)} %param.15) | copy-start | bytes 1540
  56.6 13.5 %collective-permute-start.10 = (f32[128,512]{1,0:T(8,128)S(1)}, f32[128,512]{1,0:T(8,128)S(1)}, u32[]{:S(2)}, u32[]{:S(2)}) collective-permute-start(f32[128,512]{1,0:T(8,128)S(1)} %get-tuple-element.63), channel_id=1, source_target_pairs={{0,8},{8,0},{16,24},{24,16},{1,9},{9,1},{17,25},{25,17},{2,10},{10... | collective-permute-start | bytes 786440 | tf_op jit(solution)/shard_map/ppermute | solution.py:336
  56.7 1.7 %collective-permute-start.11 = (f32[128,256]{1,0:T(8,128)S(1)}, f32[128,256]{1,0:T(8,128)S(1)}, u32[]{:S(2)}, u32[]{:S(2)}) collective-permute-start(f32[128,256]{1,0:T(8,128)S(1)} %get-tuple-element.65), channel_id=1, source_target_pairs={{0,8},{8,0},{16,24},{24,16},{1,9},{9,1},{17,25},{25,17},{2,10},{10... | collective-permute-start | bytes 393224 | tf_op jit(solution)/shard_map/ppermute | solution.py:336
  58.4 6.7 %collective-permute-start.12 = (f32[128,128]{1,0:T(8,128)S(1)}, f32[128,128]{1,0:T(8,128)S(1)}, u32[]{:S(2)}, u32[]{:S(2)}) collective-permute-start(f32[128,128]{1,0:T(8,128)S(1)} %get-tuple-element.66), channel_id=1, source_target_pairs={{0,7},{1,0},{2,1},{3,2},{4,3},{5,4},{6,5},{7,6},{8,15},{9,8},{10,9... | collective-permute-start | bytes 196616 | tf_op jit(solution)/shard_map/ppermute | solution.py:331
  63.1 7.0 %collective-permute-start.13 = (f32[128,128]{1,0:T(8,128)S(1)}, f32[128,128]{1,0:T(8,128)S(1)}, u32[]{:S(2)}, u32[]{:S(2)}) collective-permute-start(f32[128,128]{1,0:T(8,128)S(1)} %get-tuple-element.67), channel_id=1, source_target_pairs={{0,1},{1,2},{2,3},{3,4},{4,5},{5,6},{6,7},{7,0},{8,9},{9,10},{10,1... | collective-permute-start | bytes 196616 | tf_op jit(solution)/shard_map/ppermute | solution.py:331
  73.8 1.9 %collective-permute-start.15 = (bf16[128,1792]{1,0:T(8,128)(2,1)S(1)}, bf16[128,1792]{1,0:T(8,128)(2,1)S(1)}, u32[]{:S(2)}, u32[]{:S(2)}) collective-permute-start(bf16[128,1792]{1,0:T(8,128)(2,1)S(1)} %get-tuple-element.77), channel_id=1, source_target_pairs={{0,8},{8,0},{16,24},{24,16},{1,9},{9,1},{17,25},{25,17},{2,10},{10... | collective-permute-start | bytes 1376264 | tf_op jit(solution)/shard_map/ppermute | solution.py:336
  73.9 4.0 %collective-permute-start.14 = (bf16[128,1792]{1,0:T(8,128)(2,1)S(1)}, bf16[128,1792]{1,0:T(8,128)(2,1)S(1)}, u32[]{:S(2)}, u32[]{:S(2)}) collective-permute-start(bf16[128,1792]{1,0:T(8,128)(2,1)S(1)} %get-tuple-element.76), channel_id=1, source_target_pairs={{0,8},{8,0},{16,24},{24,16},{1,9},{9,1},{17,25},{25,17},{2,10},{10... | collective-permute-start | bytes 1376264 | tf_op jit(solution)/shard_map/ppermute | solution.py:336
  75.8 8.5 %collective-permute-start.16 = (bf16[64,1792]{1,0:T(8,128)(2,1)S(1)}, bf16[64,1792]{1,0:T(8,128)(2,1)S(1)}, u32[]{:S(2)}, u32[]{:S(2)}) collective-permute-start(bf16[64,1792]{1,0:T(8,128)(2,1)S(1)} %get-tuple-element.78), channel_id=1, source_target_pairs={{0,16},{8,24},{16,0},{24,8},{1,17},{9,25},{17,1},{25,9},{2,18},{10... | collective-permute-start | bytes 688136 | tf_op jit(solution)/shard_map/ppermute | solution.py:336
  76.7 11.8 %collective-permute-start.20 = (bf16[64,1792]{1,0:T(8,128)(2,1)S(1)}, bf16[64,1792]{1,0:T(8,128)(2,1)S(1)}, u32[]{:S(2)}, u32[]{:S(2)}) collective-permute-start(bf16[64,1792]{1,0:T(8,128)(2,1)S(1)} %get-tuple-element.83), channel_id=1, source_target_pairs={{0,16},{8,24},{16,0},{24,8},{1,17},{9,25},{17,1},{25,9},{2,18},{10... | collective-permute-start | bytes 688136 | tf_op jit(solution)/shard_map/ppermute | solution.py:336
  84.5 4.7 %collective-permute-start.17 = (bf16[16,1792]{1,0:T(8,128)(2,1)S(1)}, bf16[16,1792]{1,0:T(8,128)(2,1)S(1)}, u32[]{:S(2)}, u32[]{:S(2)}) collective-permute-start(bf16[16,1792]{1,0:T(8,128)(2,1)S(1)} %get-tuple-element.80), channel_id=1, source_target_pairs={{0,7},{1,0},{2,1},{3,2},{4,3},{5,4},{6,5},{7,6},{8,15},{9,8},{10,9... | collective-permute-start | bytes 172040 | tf_op jit(solution)/shard_map/ppermute | solution.py:331
  84.5 6.6 %collective-permute-start.18 = (bf16[16,1792]{1,0:T(8,128)(2,1)S(1)}, bf16[16,1792]{1,0:T(8,128)(2,1)S(1)}, u32[]{:S(2)}, u32[]{:S(2)}) collective-permute-start(bf16[16,1792]{1,0:T(8,128)(2,1)S(1)} %get-tuple-element.81), channel_id=1, source_target_pairs={{0,6},{1,7},{2,0},{3,1},{4,2},{5,3},{6,4},{7,5},{8,14},{9,15},{10,... | collective-permute-start | bytes 172040 | tf_op jit(solution)/shard_map/ppermute | solution.py:331
  84.6 8.5 %collective-permute-start.19 = (bf16[16,1792]{1,0:T(8,128)(2,1)S(1)}, bf16[16,1792]{1,0:T(8,128)(2,1)S(1)}, u32[]{:S(2)}, u32[]{:S(2)}) collective-permute-start(bf16[16,1792]{1,0:T(8,128)(2,1)S(1)} %get-tuple-element.82), channel_id=1, source_target_pairs={{0,5},{1,6},{2,7},{3,0},{4,1},{5,2},{6,3},{7,4},{8,13},{9,14},{10,... | collective-permute-start | bytes 172040 | tf_op jit(solution)/shard_map/ppermute | solution.py:331
  88.6 7.5 %collective-permute-start.21 = (bf16[16,1792]{1,0:T(8,128)(2,1)S(1)}, bf16[16,1792]{1,0:T(8,128)(2,1)S(1)}, u32[]{:S(2)}, u32[]{:S(2)}) collective-permute-start(bf16[16,1792]{1,0:T(8,128)(2,1)S(1)} %get-tuple-element.84), channel_id=1, source_target_pairs={{0,4},{1,5},{2,6},{3,7},{4,0},{5,1},{6,2},{7,3},{8,12},{9,13},{10,... | collective-permute-start | bytes 172040 | tf_op jit(solution)/shard_map/ppermute | solution.py:331
  89.1 7.0 %collective-permute-start.22 = (bf16[16,1792]{1,0:T(8,128)(2,1)S(1)}, bf16[16,1792]{1,0:T(8,128)(2,1)S(1)}, u32[]{:S(2)}, u32[]{:S(2)}) collective-permute-start(bf16[16,1792]{1,0:T(8,128)(2,1)S(1)} %get-tuple-element.85), channel_id=1, source_target_pairs={{0,3},{1,4},{2,5},{3,6},{4,7},{5,0},{6,1},{7,2},{8,11},{9,12},{10,... | collective-permute-start | bytes 172040 | tf_op jit(solution)/shard_map/ppermute | solution.py:331
  89.2 6.9 %collective-permute-start.23 = (bf16[16,1792]{1,0:T(8,128)(2,1)S(1)}, bf16[16,1792]{1,0:T(8,128)(2,1)S(1)}, u32[]{:S(2)}, u32[]{:S(2)}) collective-permute-start(bf16[16,1792]{1,0:T(8,128)(2,1)S(1)} %get-tuple-element.86), channel_id=1, source_target_pairs={{0,2},{1,3},{2,4},{3,5},{4,6},{5,7},{6,0},{7,1},{8,10},{9,11},{10,... | collective-permute-start | bytes 172040 | tf_op jit(solution)/shard_map/ppermute | solution.py:331
  91.1 7.9 %collective-permute-start.24 = (bf16[16,1792]{1,0:T(8,128)(2,1)S(1)}, bf16[16,1792]{1,0:T(8,128)(2,1)S(1)}, u32[]{:S(2)}, u32[]{:S(2)}) collective-permute-start(bf16[16,1792]{1,0:T(8,128)(2,1)S(1)} %get-tuple-element.87), channel_id=1, source_target_pairs={{0,1},{1,2},{2,3},{3,4},{4,5},{5,6},{6,7},{7,0},{8,9},{9,10},{10,1... | collective-permute-start | bytes 172040 | tf_op jit(solution)/shard_map/ppermute | solution.py:331
  99.1 7.8 %collective-permute-start.27 = (bf16[16,1792]{1,0:T(8,128)(2,1)S(1)}, bf16[16,1792]{1,0:T(8,128)(2,1)S(1)}, u32[]{:S(2)}, u32[]{:S(2)}) collective-permute-start(bf16[16,1792]{1,0:T(8,128)(2,1)S(1)} %shard_map.165.refs_0_), channel_id=1, source_target_pairs={{0,3},{1,4},{2,5},{3,6},{4,7},{5,0},{6,1},{7,2},{8,11},{9,12},{10,... | collective-permute-start | bytes 172040 | tf_op jit(solution)/shard_map/ppermute | solution.py:331
  99.2 7.9 %collective-permute-start.26 = (bf16[16,1792]{1,0:T(8,128)(2,1)S(1)}, bf16[16,1792]{1,0:T(8,128)(2,1)S(1)}, u32[]{:S(2)}, u32[]{:S(2)}) collective-permute-start(bf16[16,1792]{1,0:T(8,128)(2,1)S(1)} %shard_map.165.refs_0_), channel_id=1, source_target_pairs={{0,2},{1,3},{2,4},{3,5},{4,6},{5,7},{6,0},{7,1},{8,10},{9,11},{10,... | collective-permute-start | bytes 172040 | tf_op jit(solution)/shard_map/ppermute | solution.py:331
  99.8 9.1 %collective-permute-start.25 = (bf16[16,1792]{1,0:T(8,128)(2,1)S(1)}, bf16[16,1792]{1,0:T(8,128)(2,1)S(1)}, u32[]{:S(2)}, u32[]{:S(2)}) collective-permute-start(bf16[16,1792]{1,0:T(8,128)(2,1)S(1)} %shard_map.165.refs_0_), channel_id=1, source_target_pairs={{0,1},{1,2},{2,3},{3,4},{4,5},{5,6},{6,7},{7,0},{8,9},{9,10},{10,1... | collective-permute-start | bytes 172040 | tf_op jit(solution)/shard_map/ppermute | solution.py:331
  101.3 8.4 %collective-permute-start.31 = (bf16[16,1792]{1,0:T(8,128)(2,1)S(1)}, bf16[16,1792]{1,0:T(8,128)(2,1)S(1)}, u32[]{:S(2)}, u32[]{:S(2)}) collective-permute-start(bf16[16,1792]{1,0:T(8,128)(2,1)S(1)} %shard_map.165.refs_0_), channel_id=1, source_target_pairs={{0,7},{1,0},{2,1},{3,2},{4,3},{5,4},{6,5},{7,6},{8,15},{9,8},{10,9... | collective-permute-start | bytes 172040 | tf_op jit(solution)/shard_map/ppermute | solution.py:331
  104.5 5.2 %collective-permute-start.30 = (bf16[16,1792]{1,0:T(8,128)(2,1)S(1)}, bf16[16,1792]{1,0:T(8,128)(2,1)S(1)}, u32[]{:S(2)}, u32[]{:S(2)}) collective-permute-start(bf16[16,1792]{1,0:T(8,128)(2,1)S(1)} %shard_map.165.refs_0_), channel_id=1, source_target_pairs={{0,6},{1,7},{2,0},{3,1},{4,2},{5,3},{6,4},{7,5},{8,14},{9,15},{10,... | collective-permute-start | bytes 172040 | tf_op jit(solution)/shard_map/ppermute | solution.py:331
  107.0 5.1 %collective-permute-start.29 = (bf16[16,1792]{1,0:T(8,128)(2,1)S(1)}, bf16[16,1792]{1,0:T(8,128)(2,1)S(1)}, u32[]{:S(2)}, u32[]{:S(2)}) collective-permute-start(bf16[16,1792]{1,0:T(8,128)(2,1)S(1)} %shard_map.165.refs_0_), channel_id=1, source_target_pairs={{0,5},{1,6},{2,7},{3,0},{4,1},{5,2},{6,3},{7,4},{8,13},{9,14},{10,... | collective-permute-start | bytes 172040 | tf_op jit(solution)/shard_map/ppermute | solution.py:331
  107.1 5.5 %collective-permute-start.28 = (bf16[16,1792]{1,0:T(8,128)(2,1)S(1)}, bf16[16,1792]{1,0:T(8,128)(2,1)S(1)}, u32[]{:S(2)}, u32[]{:S(2)}) collective-permute-start(bf16[16,1792]{1,0:T(8,128)(2,1)S(1)} %shard_map.165.refs_0_), channel_id=1, source_target_pairs={{0,4},{1,5},{2,6},{3,7},{4,0},{5,1},{6,2},{7,3},{8,12},{9,13},{10,... | collective-permute-start | bytes 172040 | tf_op jit(solution)/shard_map/ppermute | solution.py:331
  108.9 7.9 %collective-permute-start.34 = (bf16[64,1792]{1,0:T(8,128)(2,1)S(1)}, bf16[64,1792]{1,0:T(8,128)(2,1)S(1)}, u32[]{:S(2)}, u32[]{:S(2)}) collective-permute-start(bf16[64,1792]{1,0:T(8,128)(2,1)S(1)} %shard_map.166.refs_0_), channel_id=1, source_target_pairs={{0,16},{8,24},{16,0},{24,8},{1,17},{9,25},{17,1},{25,9},{2,18},{10... | collective-permute-start | bytes 688136 | tf_op jit(solution)/shard_map/ppermute | solution.py:336
  112.5 7.3 %collective-permute-start.35 = (bf16[64,1792]{1,0:T(8,128)(2,1)S(1)}, bf16[64,1792]{1,0:T(8,128)(2,1)S(1)}, u32[]{:S(2)}, u32[]{:S(2)}) collective-permute-start(bf16[64,1792]{1,0:T(8,128)(2,1)S(1)} %shard_map.167.refs_1_), channel_id=1, source_target_pairs={{0,16},{8,24},{16,0},{24,8},{1,17},{9,25},{17,1},{25,9},{2,18},{10... | collective-permute-start | bytes 688136 | tf_op jit(solution)/shard_map/ppermute | solution.py:336
  113.4 6.5 %collective-permute-start.32 = (bf16[64,1792]{1,0:T(8,128)(2,1)S(1)}, bf16[64,1792]{1,0:T(8,128)(2,1)S(1)}, u32[]{:S(2)}, u32[]{:S(2)}) collective-permute-start(bf16[64,1792]{1,0:T(8,128)(2,1)S(1)} %shard_map.166.refs_0_), channel_id=1, source_target_pairs={{0,8},{8,0},{16,24},{24,16},{1,9},{9,1},{17,25},{25,17},{2,10},{10... | collective-permute-start | bytes 688136 | tf_op jit(solution)/shard_map/ppermute | solution.py:336
  113.4 6.5 %collective-permute-start.33 = (bf16[64,1792]{1,0:T(8,128)(2,1)S(1)}, bf16[64,1792]{1,0:T(8,128)(2,1)S(1)}, u32[]{:S(2)}, u32[]{:S(2)}) collective-permute-start(bf16[64,1792]{1,0:T(8,128)(2,1)S(1)} %shard_map.167.refs_1_), channel_id=1, source_target_pairs={{0,8},{8,0},{16,24},{24,16},{1,9},{9,1},{17,25},{25,17},{2,10},{10... | collective-permute-start | bytes 688136 | tf_op jit(solution)/shard_map/ppermute | solution.py:336
  116.8 3.1 %collective-permute-start.36 = (bf16[64,1792]{1,0:T(8,128)(2,1)S(1)}, bf16[64,1792]{1,0:T(8,128)(2,1)S(1)}, u32[]{:S(2)}, u32[]{:S(2)}) collective-permute-start(bf16[64,1792]{1,0:T(8,128)(2,1)S(1)} %collective-permute-done.34.refs_4_), channel_id=1, source_target_pairs={{0,8},{8,0},{16,24},{24,16},{1,9},{9,1},{17,25},{25,17},{2,10},{10... | collective-permute-start | bytes 688136 | tf_op jit(solution)/shard_map/ppermute | solution.py:336
  119.9 1.5 %collective-permute-start.37 = (bf16[64,1792]{1,0:T(8,128)(2,1)S(1)}, bf16[64,1792]{1,0:T(8,128)(2,1)S(1)}, u32[]{:S(2)}, u32[]{:S(2)}) collective-permute-start(bf16[64,1792]{1,0:T(8,128)(2,1)S(1)} %collective-permute-done.35.refs_5_), channel_id=1, source_target_pairs={{0,8},{8,0},{16,24},{24,16},{1,9},{9,1},{17,25},{25,17},{2,10},{10... | collective-permute-start | bytes 688136 | tf_op jit(solution)/shard_map/ppermute | solution.py:336
  (4 other events, 2.6 us)

commit v5 on v4

--- a/solution.py
+++ b/solution.py
@@ -43,23 +43,40 @@
     return jax.ShapeDtypeStruct(shape, dtype)
 
 
-def lend_kernel(nodes, to_next, to_prev, nodes_t, next_t, prev_t):
-    table = nodes[...].T
+HBM = pl.BlockSpec(memory_space=pltpu.HBM)
+
+
+def fetched(sources, targets, sems):
+    copies = [pltpu.make_async_copy(a, b, sems.at[i]) for i, (a, b) in enumerate(zip(sources, targets))]
+    for copy in copies:
+        copy.start()
+    return copies
+
+
+def lend_kernel(nodes, to_next, to_prev, nodes_t, next_t, prev_t, held, rows_next, rows_prev, sems):
+    for copy in fetched((nodes, to_next, to_prev), (held, rows_next, rows_prev), sems):
+        copy.wait()
+    table = held[...].T
     nodes_t[...] = table
     count = table.shape[1]
-    next_t[...] = dot(table, one_hot(count, to_next[...])).astype(BF16)
-    prev_t[...] = dot(table, one_hot(count, to_prev[...])).astype(BF16)
-
-
-def weights_kernel(w_send, w_recv, vertex, w_decode, nodes_t, w_send_t, vertex_t, w_decode_t, recv_t):
-    w_send_t[...] = w_send[...].T * 0.5
-    vertex_t[...] = vertex[...].T * 0.5
-    w_decode_t[...] = w_decode[...].T
-    recv_t[...] = dot(w_recv[...].T, nodes_t[...]) * 0.5
-
-
-def decoder_kernel(core, vertices, weights, base, truth, after, mat, base_t, truth_t):
-    del core, after
+    next_t[...] = dot(table, one_hot(count, rows_next[...])).astype(BF16)
+    prev_t[...] = dot(table, one_hot(count, rows_prev[...])).astype(BF16)
+
+
+def decoder_kernel(core, vertices, weights, base, truth, after, mat, base_t, truth_t, base_rows, truth_rows, sems):
+    del after
+    span = base_rows.shape[0]
+    half = pl.ds(pl.multiple_of(core[0] * span, span), span)
+    copies = [
+        pltpu.make_async_copy(base.at[half, :], base_rows, sems.at[0]),
+        pltpu.make_async_copy(truth.at[half, :], truth_rows, sems.at[1]),
+    ]
+
+    @pl.when(pl.program_id(0) == 0)
+    def _():
+        for copy in copies:
+            copy.start()
+
     rows, tile = mat.shape[0] // 2, 16
     shape = (tile, mat.shape[1])
     spread = lambda ref, k: jnp.broadcast_to(ref[k : k + 1, :], shape)
@@ -75,8 +92,13 @@
         hi, lo = split(total)
         mat[start : start + tile, :] = hi
         mat[rows + start : rows + start + tile, :] = lo
-    base_t[...] = base[...].T
-    truth_t[...] = truth[...].T
+
+    @pl.when(pl.program_id(0) == pl.num_programs(0) - 1)
+    def _():
+        for copy in copies:
+            copy.wait()
+        base_t[...] = base_rows[...].T
+        truth_t[...] = truth_rows[...].T
 
 
 TILE = 16
@@ -89,18 +111,35 @@
 
 
 def forward_kernel(
-    nodes_t, from_prev, from_next, senders, w_send_t, recv_t, vertex_t, w_decode_t, to_next, to_prev,
-    picked_t, slope_t, slope_sum_t, agg_t, upd_slope_t, hidden_t, field_t, next_t, prev_t,
-    pre,
+    nodes_t, from_prev, from_next, senders_in, to_next_in, to_prev_in, w_send_in, w_recv_in, vertex_in, w_decode_in,
+    picked_t, field_t, next_t, prev_t, slope_out, slope_sum_out, agg_out, upd_slope_out, hidden_out,
+    pre, senders, to_next, to_prev, w_send, w_recv, vertex, w_decode, recv_t,
+    slope_t, slope_sum_t, agg_t, upd_slope_t, hidden_t, in_sems, out_sems,
 ):
+    fetch = fetched(
+        (senders_in, to_next_in, to_prev_in, w_send_in, w_recv_in, vertex_in, w_decode_in),
+        (senders, to_next, to_prev, w_send, w_recv, vertex, w_decode),
+        in_sems,
+    )
+    stored = []
+
+    def store(source, target):
+        copy = pltpu.make_async_copy(source, target, out_sems.at[len(stored)])
+        copy.start()
+        stored.append(copy)
+
     degree, count = senders.shape
     halo = from_prev.shape[1]
     width = nodes_t.shape[0]
     ext = jnp.concatenate([nodes_t[...], from_prev[...], from_next[...]], axis=1)
+    for copy in fetch:
+        copy.wait()
+    w_send_t = w_send[...].T * 0.5
+    recv_t[...] = dot(w_recv[...].T, nodes_t[...]) * 0.5
     for k in range(degree):
         here = slice(k * count, (k + 1) * count)
         picked_t[:, here] = dot(ext, one_hot(count + 2 * halo, senders[k : k + 1, :])).astype(BF16)
-        pre[:, here] = dot(w_send_t[...], picked_t[:, here])
+        pre[:, here] = dot(w_send_t, picked_t[:, here])
     for start in range(0, width, TILE):
         rows = slice(start, start + TILE)
         recv = recv_t[rows, :]
@@ -113,16 +152,25 @@
             slopes = slope if k == 0 else slopes + slope
         slope_sum_t[rows, :] = slopes
         agg_t[rows, :] = (total * (1.0 / degree)).astype(BF16)
-    pre[:, :count] = dot(vertex_t[...], agg_t[...])
+        if (start + TILE) % 128 == 0:
+            group = slice(start + TILE - 128, start + TILE)
+            store(slope_t.at[group, :], slope_out.at[group, :])
+    store(slope_sum_t, slope_sum_out)
+    store(agg_t, agg_out)
+    pre[:, :count] = dot(vertex[...].T * 0.5, agg_t[...])
     for start in range(0, width, TILE):
         rows = slice(start, start + TILE)
         value, slope = bent(pre[rows, :count])
         upd_slope_t[rows, :] = slope * 0.5
         hidden_t[rows, :] = (nodes_t[rows, :].astype(F32) + value).astype(BF16)
-    field = dot(w_decode_t[...], hidden_t[...]).astype(BF16)
+    store(upd_slope_t, upd_slope_out)
+    store(hidden_t, hidden_out)
+    field = dot(w_decode[...].T, hidden_t[...]).astype(BF16)
     field_t[...] = field
     next_t[...] = dot(field, one_hot(count, to_next[...])).astype(BF16)
     prev_t[...] = dot(field, one_hot(count, to_prev[...])).astype(BF16)
+    for copy in stored:
+        copy.wait()
 
 
 def readout_kernel(line_span, *refs):
@@ -219,10 +267,11 @@
 
 
 def backward_kernel(
-    parts, own_mid, pair_mid, from_next, from_prev, to_next, to_prev, term, w_decode, vertex, nodes_t,
+    own_mid, pair_mid, from_next, from_prev, to_next, to_prev, term, w_decode, vertex, nodes_t,
     picked_t, slope_t, slope_sum_t, agg_t, upd_slope_t, hidden_t,
-    keep, send_far, send_near, whole, back, grad_pre,
+    *refs,
 ):
+    whole, back, grad_pre = refs[-3:]
     count = nodes_t.shape[1]
     width = nodes_t.shape[0]
     grad_z = own_mid[...] + pair_mid[...]
@@ -249,37 +298,55 @@
     whole[:, main:] = jnp.zeros((width, LANES), F32)
     spot = (lax.broadcasted_iota(jnp.int32, (8, LANES), 0) == 0) & (lax.broadcasted_iota(jnp.int32, (8, LANES), 1) == 0)
     whole[0:8, main:] = jnp.where(spot, jnp.sum(term[...]), 0.0)
-    ens, dom = lax.axis_index("ens"), lax.axis_index("dom")
-    core, chip = lax.rem(ens, 2), lax.div(ens, 2)
-    rows = send_far.shape[0]
-    share = rows // parts
-
-    def block(c, x, k):
-        start = ((2 * c + x) * parts + lax.rem(dom + k, parts)) * share
+    if len(refs) == 3:
+        return
+    keep, send_first, send_rest = refs[:3]
+    core, x, z, y = position()
+    share = width // 32
+
+    def block(c, xr, yr, k):
+        quarter = 2 * c + lax.bitwise_xor(x, xr)
+        start = (8 * quarter + 2 * lax.rem(z + k, 4) + lax.bitwise_xor(y, yr)) * share
         return whole[pl.ds(pl.multiple_of(start, share), share), :]
 
-    for place, k in enumerate(list(range(1, parts)) + [0]):
-        here = slice(place * share, (place + 1) * share)
-        there = slice(rows + place * share, rows + (place + 1) * share)
-        keep[here, :] = block(core, chip, k)
-        keep[there, :] = block(core, 1 - chip, k)
-        send_far[here, :] = encoded(block(1 - core, 1 - chip, k))
-        send_near[here, :] = encoded(block(1 - core, chip, k))
-
-
-def chip_kernel(mine, got, first, second):
-    total = encoded(mine[...] + got[...].astype(F32))
-    rows = first.shape[0]
-    first[...] = total[:rows]
-    second[...] = total[rows:]
-
-
-def shares_kernel(mine, near, far, *outs):
-    total = mine[...] + near[...].astype(F32) + far[...].astype(F32)
+    at = 0
+    for xr, yr in ((1, 1), (1, 0), (0, 1), (0, 0)):
+        for k in (1, 2, 3, 0):
+            keep[at : at + share, :] = block(core, xr, yr, k)
+            value = encoded(block(1 - core, xr, yr, k))
+            if at < 4 * share:
+                send_first[at : at + share, :] = value
+            else:
+                send_rest[at - 4 * share : at - 3 * share, :] = value
+            at += share
+
+
+def corner_kernel(keep, first, by_x, by_y):
+    block = 2 * by_x.shape[0]
+    total = encoded(keep[:block, :] + first[...].astype(F32))
+    by_x[...] = total[: block // 2]
+    by_y[...] = total[block // 2 :]
+
+
+def sides_kernel(keep, rest, from_x, from_y, to_x, to_y):
+    block = to_x.shape[0]
+    half = block // 2
+    for rows, source, target in ((slice(half, block), from_y, to_x), (slice(0, half), from_x, to_y)):
+        base = 0 if target is to_x else block
+        total = keep[block + base : 2 * block + base, :] + rest[base : base + block, :].astype(F32)
+        extra = source[...].astype(F32)
+        zeros = jnp.zeros_like(extra)
+        extra = jnp.concatenate([zeros, extra] if rows.start else [extra, zeros], axis=0)
+        target[...] = encoded(total + extra)
+
+
+def shares_kernel(keep, rest, from_x, from_y, *outs):
     rows = outs[0].shape[0]
+    block = from_x.shape[0]
+    total = keep[3 * block :, :] + rest[2 * block :, :].astype(F32) + from_x[...].astype(F32) + from_y[...].astype(F32)
     for k, out in enumerate(outs):
-        block = total[k * rows : (k + 1) * rows]
-        out[...] = encoded(block) if out.dtype == BF16 else block
+        value = total[k * rows : (k + 1) * rows]
+        out[...] = encoded(value) if out.dtype == BF16 else value
 
 
 def sum_kernel(*refs):
@@ -295,32 +362,37 @@
         refs[-1][k * rows : (k + 1) * rows, :] = ref[...]
 
 
-def finish_kernel(scale, parts, *refs):
+def half_kernel(at, source, target):
+    rows = target.shape[0]
+    target[...] = source[at * rows : (at + 1) * rows, :]
+
+
+def finish_kernel(scale, *refs):
     g_send, g_recv, g_update, g_decode, loss = refs[-5:]
     pieces = refs[:-5]
     width = g_send.shape[1]
-    turn = parts if parts > 1 else 2
-    share = width // 4 // turn
+    share = width // 32
+    core, x, z, y = position()
+    total = jnp.zeros((share, LANES), F32)
+    layout = ((0, 0, 0), (1, 0, 0), (0, 1, 0), (1, 1, 0), (1, 1, 2))
+    for i, piece in enumerate(pieces):
+        xr, yr, first = layout[i % 5]
+        quarter = 2 * (core if i < 5 else 1 - core) + lax.bitwise_xor(x, xr)
+        for j in range(piece.shape[0] // share):
+            start = (8 * quarter + 2 * lax.rem(z + 4 - first - j, 4) + lax.bitwise_xor(y, yr)) * share
+            place = pl.ds(pl.multiple_of(start, share), share)
+            value = piece[j * share : (j + 1) * share, :].astype(F32)
+            g_send[place, :] = value[:, :width]
+            g_recv[place, :] = value[:, width : 2 * width]
+            g_update[place, :] = value[:, 2 * width : 3 * width]
+            g_decode[place, :] = value[:, 3 * width : -LANES]
+            total += value[:, -LANES:]
+    loss[0, 0] = jnp.sum(total) * scale
+
+
+def position():
     ens, dom = lax.axis_index("ens"), lax.axis_index("dom")
-    spot = 2 * lax.rem(ens, 2) + lax.div(ens, 2)
-    total = jnp.zeros((share, LANES), F32)
-    each = len(pieces) // 4
-    for q, other in enumerate((0, 2, 1, 3)):
-        quarter = lax.bitwise_xor(spot, other)
-        step = 0
-        for piece in pieces[q * each : (q + 1) * each]:
-            for j in range(piece.shape[0] // share):
-                spin = lax.rem(dom + parts - step, parts) if parts > 1 else step
-                start = (quarter * turn + spin) * share
-                place = pl.ds(pl.multiple_of(start, share), share)
-                block = piece[j * share : (j + 1) * share, :].astype(F32)
-                g_send[place, :] = block[:, :width]
-                g_recv[place, :] = block[:, width : 2 * width]
-                g_update[place, :] = block[:, 2 * width : 3 * width]
-                g_decode[place, :] = block[:, 3 * width : -LANES]
-                total += block[:, -LANES:]
-                step += 1
-    loss[0, 0] = jnp.sum(total) * scale
+    return lax.rem(ens, 2), lax.div(ens, 2), lax.div(dom, 2), lax.rem(dom, 2)
 
 
 SCALAR = pl.BlockSpec(memory_space=pltpu.SMEM)
@@ -340,13 +412,13 @@
     return sum(x.size * x.dtype.itemsize for x in arrays)
 
 
-def call(kernel, ins, outs, scratch=(), flops=0, room=4):
+def call(kernel, ins, outs, scratch=(), flops=0, room=4, in_hbm=0, out_hbm=0):
     size = nbytes(list(ins) + list(outs))
     return pl.pallas_call(
         kernel,
         out_shape=outs,
-        in_specs=vmem(len(ins)),
-        out_specs=vmem(len(outs)),
+        in_specs=vmem(len(ins) - in_hbm) + [HBM] * in_hbm,
+        out_specs=vmem(len(outs) - out_hbm) + [HBM] * out_hbm,
         scratch_shapes=list(scratch),
         compiler_params=params(1.1 * size / MIB + room),
         cost_estimate=cost(flops, size),
@@ -357,49 +429,27 @@
     return jnp.reshape(value, (1,)).astype(jnp.int32)
 
 
-def reduced(keep, send_far, send_near, parts):
-    quarter, cols = send_far.shape
-    half, share = quarter // 2, quarter // parts
-    got_far, got_near = flip(send_far, "ens", 1), flip(send_near, "ens", 1)
-    whole = lambda x: pl.BlockSpec(x.shape, lambda i: (0, 0))
-    rows = lambda size, at: pl.BlockSpec((size, cols), lambda i: (at, 0))
-    piece = sds((half, cols), BF16)
-    first, second = pl.pallas_call(
-        chip_kernel,
-        grid=(1,),
-        out_shape=[piece, piece],
-        in_specs=[rows(quarter, 1), whole(got_far)],
-        out_specs=[whole(piece)] * 2,
-        compiler_params=params(12),
-        cost_estimate=cost(0, 8 * keep.size),
-    )(keep, got_far)
-    first, second = flip(first, "ens", 2), flip(second, "ens", 2)
-
-    def shares(at, far, outs):
-        return pl.pallas_call(
-            shares_kernel,
-            grid=(1,),
-            out_shape=outs,
-            in_specs=[rows(half, at), rows(half, at), whole(far)],
-            out_specs=[whole(x) for x in outs],
-            compiler_params=params(12),
-            cost_estimate=cost(0, 8 * keep.size),
-        )(keep, got_near, far)
-
-    if parts == 1:
-        sums = [shares(at, far, [sds((half, cols), F32)])[0] for at, far in enumerate((first, second))]
-        return [call(sum_kernel, [lax.psum(x, "dom")], [piece])[0] for x in sums]
-    terms = []
-    count = half // share
-    for at, far in enumerate((first, second)):
-        outs = [sds((share, cols), BF16)] * count
-        if at == 1:
-            outs[-1] = sds((share, cols), F32)
-        steps = range(at * count + 1, at * count + 1 + count)
-        terms += [along(x, "dom", k) if k < parts else x for k, x in zip(steps, shares(at, far, outs))]
-    (own,) = call(sum_kernel, terms[::-1], [sds((share, cols), BF16)])
-    pieces = [own] + [along(own, "dom", k) for k in range(1, parts)]
-    return [call(join_kernel, pieces[at * count : (at + 1) * count], [piece])[0] for at in range(2)]
+def summed(keep, send_first, send_rest):
+    block, cols = send_first.shape
+    half, share = block // 2, block // 4
+    core = lambda v: flip(v, "ens", 1)
+    over_x = lambda v: flip(v, "ens", 2)
+    over_y = lambda v: flip(v, "dom", 1)
+    piece = lambda rows: sds((rows, cols), BF16)
+    first, rest = core(send_first), core(send_rest)
+    by_x, by_y = call(corner_kernel, [keep, first], [piece(half)] * 2)
+    by_x, by_y = over_x(by_x), over_y(by_y)
+    to_x, to_y = call(sides_kernel, [keep, rest, by_x, by_y], [piece(block)] * 2)
+    to_x, to_y = over_x(to_x), over_y(to_y)
+    shares = call(shares_kernel, [keep, rest, to_x, to_y], [piece(share)] * 3 + [sds((share, cols), F32)])
+    terms = [shares[3]] + [along(shares[k - 1], "dom", 2 * k) for k in (1, 2, 3)]
+    (own,) = call(sum_kernel, terms, [piece(share)])
+    (mine,) = call(join_kernel, [own] + [along(own, "dom", 2 * k) for k in (1, 2, 3)], [piece(block)])
+    x, y = over_x(mine), over_y(mine)
+    (low,) = call(functools.partial(half_kernel, 0), [y], [piece(half)])
+    (high,) = call(functools.partial(half_kernel, 1), [x], [piece(half)])
+    here = [mine, x, y, over_x(low), over_y(high)]
+    return here + [core(v) for v in here]
 
 
 def per_device(
@@ -417,34 +467,38 @@
     ens, dom = lax.axis_index("ens"), lax.axis_index("dom")
     to_next, to_prev = send_next.reshape(1, halo), send_prev.reshape(1, halo)
 
+    held = lambda shape, dtype=BF16: pltpu.VMEM(shape, dtype)
+    indices = lambda: [held((1, halo), jnp.int32)] * 2
     nodes_t, next_t, prev_t = call(
         lend_kernel,
         [latent, to_next, to_prev],
         [sds((width, count), BF16), sds((width, halo), BF16), sds((width, halo), BF16)],
+        [held((count, width))] + indices() + [pltpu.SemaphoreType.DMA((3,))],
         flops=4 * width * count * halo,
+        in_hbm=3,
     )
     lat_prev = along(next_t, "dom", 1)
     lat_next = along(prev_t, "dom", -1)
 
     core = scalar(lax.rem(ens, 2))
-    w_send_t, vertex_t, w_decode_t, recv_t = call(
-        weights_kernel,
-        [w_send, w_recv, vertex_refresh_matrix, w_decode, nodes_t],
-        [sds((width, width), BF16), sds((width, width), BF16), sds((variables, width), BF16), sds((width, count), F32)],
-        flops=2 * width * width * count,
-    )
-
-    picked_t, slope_t, slope_sum_t, agg_t, upd_slope_t, hidden_t, field_t, next_t, prev_t = call(
+    picked_t, field_t, next_t, prev_t, slope_t, slope_sum_t, agg_t, upd_slope_t, hidden_t = call(
         forward_kernel,
-        [nodes_t, lat_prev, lat_next, senders, w_send_t, recv_t, vertex_t, w_decode_t, to_next, to_prev],
+        [nodes_t, lat_prev, lat_next, senders, to_next, to_prev, w_send, w_recv, vertex_refresh_matrix, w_decode],
         [
-            sds((width, degree * count), BF16), sds((width, degree * count), BF16), sds((width, count), F32),
+            sds((width, degree * count), BF16), sds((variables, count), BF16), sds((variables, halo), BF16),
+            sds((variables, halo), BF16), sds((width, degree * count), BF16), sds((width, count), F32),
             sds((width, count), BF16), sds((width, count), F32), sds((width, count), BF16),
-            sds((variables, count), BF16), sds((variables, halo), BF16), sds((variables, halo), BF16),
         ],
-        [pltpu.VMEM((width, degree * count), F32)],
+        [held((width, degree * count), F32), held((degree, count), jnp.int32)] + indices() + [
+            held((width, width)), held((width, width)), held((width, width)), held((width, variables)),
+            held((width, count), F32), held((width, degree * count)), held((width, count), F32),
+            held((width, count)), held((width, count), F32), held((width, count)),
+            pltpu.SemaphoreType.DMA((7,)), pltpu.SemaphoreType.DMA((width // 128 + 4,)),
+        ],
         flops=2 * degree * width * count * (ext_rows + width),
         room=14,
+        in_hbm=7,
+        out_hbm=5,
     )
     lent = (along(next_t, "dom", 1), along(prev_t, "dom", -1))
     mids = [field_t] + [flip(field_t, "ens", m) for m in range(1, members)]
@@ -454,15 +508,15 @@
     fixed = lambda shape: pl.BlockSpec(shape, lambda i, *at: (0,) * len(shape))
     tall = lambda rows: pl.BlockSpec((rows, block), lambda i, *at: (0, i))
     tall_half = lambda rows: pl.BlockSpec((rows, block), lambda i, at: (0, i + at[0] * steps))
-    flat_half = pl.BlockSpec((block, variables), lambda i, at: (i + at[0] * steps, 0))
     half_span = line_span // 2
     mat, base_t, truth_t = pl.pallas_call(
         decoder_kernel,
         grid_spec=pltpu.PrefetchScalarGridSpec(
             num_scalar_prefetch=1,
             grid=(steps,),
-            in_specs=[tall_half(fan), tall_half(fan), flat_half, flat_half, pl.BlockSpec(memory_space=pl.ANY)],
-            out_specs=[tall(2 * ext_rows), tall(variables), tall(variables)],
+            in_specs=[tall_half(fan), tall_half(fan), HBM, HBM, pl.BlockSpec(memory_space=pl.ANY)],
+            out_specs=[tall(2 * ext_rows), fixed((variables, half_span)), fixed((variables, half_span))],
+            scratch_shapes=[held((half_span, variables)), held((half_span, variables)), pltpu.SemaphoreType.DMA((2,))],
         ),
         out_shape=[sds((2 * ext_rows, half_span), BF16)] + [sds((variables, half_span), BF16)] * 2,
         compiler_params=params(12),
@@ -494,33 +548,37 @@
     from_next, from_prev = along(to_before, "dom", -1), along(to_after, "dom", 1)
 
     cols = 3 * width + variables + LANES
-    quarter = width // 4
-    parts = lax.axis_size("dom")
-    if quarter % (16 * parts):
-        parts = 1
-    keep, send_far, send_near = call(
-        functools.partial(backward_kernel, parts),
-        [
-            own_mid, got_mid, from_next, from_prev, to_next, to_prev, term, w_decode,
-            vertex_refresh_matrix, nodes_t, picked_t, slope_t, slope_sum_t, agg_t, upd_slope_t, hidden_t,
-        ],
-        [sds((2 * quarter, cols), F32), sds((quarter, cols), BF16), sds((quarter, cols), BF16)],
-        [pltpu.VMEM((width, cols), F32), pltpu.VMEM((width, count), F32), pltpu.VMEM((width, (degree + 1) * count), BF16)],
-        flops=2 * (degree + 3) * width * width * count,
+    operands = [
+        own_mid, got_mid, from_next, from_prev, to_next, to_prev, term, w_decode,
+        vertex_refresh_matrix, nodes_t, picked_t, slope_t, slope_sum_t, agg_t, upd_slope_t, hidden_t,
+    ]
+    whole = sds((width, cols), F32)
+    scratch = [held((width, count), F32), held((width, (degree + 1) * count))]
+    flops = 2 * (degree + 3) * width * width * count
+    scale = 1.0 / line_span
+    if lax.axis_size("dom") != 8 or members != 4 or width % 512:
+        (total,) = call(backward_kernel, operands, [whole], scratch, flops, room=16)
+        total = lax.psum(total, ("ens", "dom"))
+        cuts = [total[:, i * width : (i + 1) * width] for i in range(3)]
+        return *cuts, total[:, 3 * width : -LANES], jnp.sum(total[:, -LANES:]) * scale
+    block = width // 8
+    parts = call(
+        backward_kernel,
+        operands,
+        [sds((4 * block, cols), F32), sds((block, cols), BF16), sds((3 * block, cols), BF16)],
+        [held(whole.shape, F32)] + scratch,
+        flops,
         room=16,
     )
-    mine = reduced(keep, send_far, send_near, parts)
-    across = [flip(x, "ens", 2) for x in mine]
-    beside = [flip(x, "ens", 1) for x in mine]
-    corner = [flip(x, "ens", 1) for x in across]
+    pieces = summed(*parts)
     g_send, g_recv, g_update, g_decode, loss = pl.pallas_call(
-        functools.partial(finish_kernel, 1.0 / line_span, parts),
+        functools.partial(finish_kernel, scale),
         out_shape=[sds((width, width), F32)] * 3 + [sds((width, variables), F32), sds((1, 1), F32)],
-        in_specs=vmem(8),
+        in_specs=vmem(len(pieces)),
         out_specs=vmem(4) + [SCALAR],
         compiler_params=params(14),
         cost_estimate=cost(0, 6 * width * cols),
-    )(*mine, *beside, *across, *corner)
+    )(*pieces)
     return g_send, g_recv, g_update, g_decode, loss[0, 0]
 
 

time: 124 us -> 130 us (1.048)
  waiting for transfers between devices: 40.4 us -> 49.4 us
  starting transfers between devices: 38.7 us -> 34.4 us
    ppermute x20 -> x12, starting transfers between devices: 29 us -> 22.7 us  [along(): lax.ppermute(value, axis, [(i, (i + steps) % size) for i in range(size)])]
    ppermute x18 -> x23, waiting for transfers between devices: 21.7 us -> 26.9 us  [flip(): return lax.ppermute(value, axis, [(i, i ^ bit) for i in range(size)])]
    ppermute x20 -> x12, waiting for transfers between devices: 18.7 us -> 22.5 us  [along(): lax.ppermute(value, axis, [(i, (i + steps) % size) for i in range(size)])]
    ppermute x18 -> x23, starting transfers between devices: 9.66 us -> 11.7 us  [flip(): return lax.ppermute(value, axis, [(i, i ^ bit) for i in range(size)])]
  transfers between devices with their start and end apart: 38 -> 35, of which waited for: 18 -> 23; matrix products, arithmetic and copies ran while one was open for 0% -> 0% of each run, Pallas kernels for 4% -> 3%
where the time goes in v5:
time: 130 us; the launch traced here: 129 us
  waiting for transfers between devices  49.4 us (38%)
  starting transfers between devices  34.4 us (26%)
  Pallas kernels  28.1 us (22%)
  local copies, waits for them, and re-layouts  16.1 us (12%)
    ppermute x23, waiting for transfers between devices, flip(): return lax.ppermute(value, axis, [(i, i ^ bit) for i in range(size)])  26.9 us
    ppermute x12, starting transfers between devices, along(): lax.ppermute(value, axis, [(i, (i + steps) % size) for i in range(size)])  22.7 us
    ppermute x12, waiting for transfers between devices, along(): lax.ppermute(value, axis, [(i, (i + steps) % size) for i in range(size)])  22.5 us
    unnamed x61, local copies, waits for them, and re-layouts  16.1 us
    pallas_call x11, Pallas kernels, call(): pl.pallas_call(kernel, out_shape=outs, in_specs=vmem(len(ins) - in_hbm) +...  13.5 us
    ppermute x23, starting transfers between devices, flip(): return lax.ppermute(value, axis, [(i, i ^ bit) for i in range(size)])  11.7 us
    pallas_call x1, Pallas kernels, per_device(): pl.pallas_call(functools.partial(readout_kernel, line_span), grid=(steps,...  9.21 us
    pallas_call x1, Pallas kernels, per_device(): pl.pallas_call(decoder_kernel, grid_spec=pltpu.PrefetchScalarGridSpec(num...  3.35 us
  transfers between devices with their start and end apart: 35, of which 23 were waited for; matrix products, arithmetic and copies ran while one was open for 0% of the time, Pallas kernels for 3%

profile of v5, /device:TPU:0, one launch (start us, length us, event | category | flops | bytes accessed | tf_op | source)
XLA Modules:
  0.0 129.1 jit_solution(13183039210914170005)
XLA Ops:
  0.6 1.0 copy-done.16
  1.7 0.7 copy-done.21
  2.3 0.7 copy-done.24
  3.0 0.5 shard_map.155
  3.5 3.0 %collective-permute-start = (bf16[512,128]{1,0:T(8,128)(2,1)S(1)}, bf16[512,128]{1,0:T(8,128)(2,1)S(1)}, u32[]{:S(2)}, u32[]{:S(2)}) collective-permute-start(bf16[512,128]{1,0:T(8,128)(2,1)S(1)} %get-tuple-element.44), channel_id=1, source_target_pairs={{0,1},{1,2},{2,3},{3,4},{4,5},{5,6},{6,7},{7,0},{8,9},{9,10},{10,1... | collective-permute-start | bytes 393224 | tf_op jit(solution)/shard_map/ppermute | solution.py:403
  6.6 3.1 %collective-permute-start.1 = (bf16[512,128]{1,0:T(8,128)(2,1)S(1)}, bf16[512,128]{1,0:T(8,128)(2,1)S(1)}, u32[]{:S(2)}, u32[]{:S(2)}) collective-permute-start(bf16[512,128]{1,0:T(8,128)(2,1)S(1)} %get-tuple-element.45), channel_id=1, source_target_pairs={{0,7},{1,0},{2,1},{3,2},{4,3},{5,4},{6,5},{7,6},{8,15},{9,8},{10,9... | collective-permute-start | bytes 393224 | tf_op jit(solution)/shard_map/ppermute | solution.py:403
  9.7 3.5 %collective-permute-done.from_prev = bf16[512,128]{1,0:T(8,128)(2,1)S(1)} collective-permute-done((bf16[512,128]{1,0:T(8,128)(2,1)S(1)}, bf16[512,128]{1,0:T(8,128)(2,1)S(1)}, u32[]{:S(2)}, u32[]{:S(2)}) %collective-permute-start) | collective-permute-done | bytes 131104 | tf_op jit(solution)/shard_map/ppermute | solution.py:403
  13.2 1.1 collective-permute-done.1.from_next
  14.3 1.0 copy-done.8
  15.4 0.9 copy-done.17
  16.3 0.7 copy-done.22
  16.9 0.7 copy-done.25
  17.6 1.0 copy-done.27
  18.6 1.0 copy-done.28
  19.7 0.7 copy-done.29
  20.4 8.8 %shard_map.156 = (bf16[512,3072]{1,0:T(8,128)(2,1)S(1)}, bf16[128,512]{1,0:T(8,128)(2,1)S(1)}, bf16[128,128]{1,0:T(8,128)(2,1)S(1)}, bf16[128,128]{1,0:T(8,128)(...) custom-call(bf16[512,512]{1,0:T(8,128)(2,1)S(1)} %get-tuple-element., ...), custom_call_target="tpu_custom_call" | custom-call | flops 4026531840 | bytes 12137472 | tf_op jit(solution)/shard_map/pallas_call | solution.py:417
  29.3 1.6 %copy-done = bf16[512,3072]{1,0:T(8,128)(2,1)} copy-done((bf16[512,3072]{1,0:T(8,128)(2,1)}, bf16[512,3072]{1,0:T(8,128)(2,1)S(1)}, u32[]{:S(2)}) %copy-start) | copy-done | bytes 3145752
  30.9 1.0 copy-done.2
  31.9 1.0 copy-done.4
  32.8 0.8 copy-done.12
  33.6 0.8 copy-done.14
  34.7 4.4 %collective-permute-start.6 = (bf16[128,128]{1,0:T(8,128)(2,1)S(1)}, bf16[128,128]{1,0:T(8,128)(2,1)S(1)}, u32[]{:S(2)}, u32[]{:S(2)}) collective-permute-start(bf16[128,128]{1,0:T(8,128)(2,1)S(1)} %get-tuple-element.48), channel_id=1, source_target_pairs={{0,7},{1,0},{2,1},{3,2},{4,3},{5,4},{6,5},{7,6},{8,15},{9,8},{10,9... | collective-permute-start | bytes 98312 | tf_op jit(solution)/shard_map/ppermute | solution.py:403
  39.2 1.9 %collective-permute-done.5 = bf16[128,128]{1,0:T(8,128)(2,1)S(1)} collective-permute-done((bf16[128,128]{1,0:T(8,128)(2,1)S(1)}, bf16[128,128]{1,0:T(8,128)(2,1)S(1)}, u32[]{:S(2)}, u32[]{:S(2)}) %collective-permute-start.5) | collective-permute-done | bytes 32800 | tf_op jit(solution)/shard_map/ppermute | solution.py:403
  41.2 1.7 %collective-permute-start.4 = (bf16[128,512]{1,0:T(8,128)(2,1)S(1)}, bf16[128,512]{1,0:T(8,128)(2,1)}, u32[]{:S(2)}, u32[]{:S(2)}) collective-permute-start(bf16[128,512]{1,0:T(8,128)(2,1)S(1)} %get-tuple-element.46.after.refs_0_), channel_id=1, source_target_pairs={{0,24},{8,16},{16,8},{24,0},{1,25},{9,17},{17,9},{25,1},{2,26},{10... | collective-permute-start | bytes 393224 | tf_op jit(solution)/shard_map/ppermute | solution.py:408
  42.9 1.5 %collective-permute-start.3 = (bf16[128,512]{1,0:T(8,128)(2,1)S(1)}, bf16[128,512]{1,0:T(8,128)(2,1)}, u32[]{:S(2)}, u32[]{:S(2)}) collective-permute-start(bf16[128,512]{1,0:T(8,128)(2,1)S(1)} %get-tuple-element.46.after.refs_0_), channel_id=1, source_target_pairs={{0,16},{8,24},{16,0},{24,8},{1,17},{9,25},{17,1},{25,9},{2,18},{10... | collective-permute-start | bytes 393224 | tf_op jit(solution)/shard_map/ppermute | solution.py:408
  44.4 0.5 collective-permute-start.8
  44.9 0.6 collective-permute-done.9.refs_7_
  45.8 1.2 copy-done.6
  47.0 1.2 copy-done.7
  48.3 3.4 %shard_map.157 = (bf16[1536,2048]{1,0:T(8,128)(2,1)S(1)}, bf16[128,2048]{1,0:T(8,128)(2,1)S(1)}, bf16[128,2048]{1,0:T(8,128)(2,1)S(1)}) custom-call(s32[1]{0:T(128)} %bitcast.3.core, s32[3,4096]{1,0:T(4,128)S(1)} %copy-done.19, f32[3,4096]{1,0:T(4,128)S(1)} %copy-done.20, bf16[4096,128]{1,0:T(8,128)(2,1)S(1)} %copy-done.6, bf16[4096,128]{1,0:T(8,128)(2,1)S(1)} %copy-done.7, ...), custom_call_target="tpu_custom_call" | custom-call | flops 15728640 | bytes 16000000 | tf_op jit(solution)/shard_map/pallas_call | solution.py:512
  51.6 1.0 collective-permute-done.8.refs_6_
  52.8 9.2 %shard_map.158 = (f32[128,512]{1,0:T(8,128)S(1)}, f32[128,256]{1,0:T(8,128)S(1)}, f32[128,512]{1,0:T(8,128)S(1)}, f32[128,256]{1,0:T(8,128)S(1)}, f32[8,512]{1,0:T(8,128)S(1)}) custom-call(bf16[128,512]{1,0:T(8,128)(2,1)S(1)} %get-tuple-element.46.after.refs_0_, bf16[128,512]{1,0:T(8,128)(2,1)} %collective-permute-done.2.refs_1_, ...), custom_call_target="tpu_custom_call" | custom-call | flops 3221225472 | bytes 14000000 | tf_op jit(solution)/shard_map/pallas_call | solution.py:529
  62.1 0.5 collective-permute-start.11
  62.6 1.2 collective-permute-done.11.got
  63.8 4.8 %collective-permute-start.12 = (f32[128,128]{1,0:T(8,128)S(1)}, f32[128,128]{1,0:T(8,128)S(1)}, u32[]{:S(2)}, u32[]{:S(2)}) collective-permute-start(f32[128,128]{1,0:T(8,128)S(1)} %get-tuple-element.56), channel_id=1, source_target_pairs={{0,7},{1,0},{2,1},{3,2},{4,3},{5,4},{6,5},{7,6},{8,15},{9,8},{10,9... | collective-permute-start | bytes 196616 | tf_op jit(solution)/shard_map/ppermute | solution.py:403
  68.6 1.9 %collective-permute-done.12.from_next = f32[128,128]{1,0:T(8,128)S(1)} collective-permute-done((f32[128,128]{1,0:T(8,128)S(1)}, f32[128,128]{1,0:T(8,128)S(1)}, u32[]{:S(2)}, u32[]{:S(2)}) %collective-permute-start.12) | collective-permute-done | bytes 65568 | tf_op jit(solution)/shard_map/ppermute | solution.py:403
  70.5 5.1 %collective-permute-done.13.from_prev = f32[128,128]{1,0:T(8,128)S(1)} collective-permute-done((f32[128,128]{1,0:T(8,128)S(1)}, f32[128,128]{1,0:T(8,128)S(1)}, u32[]{:S(2)}, u32[]{:S(2)}) %collective-permute-start.13) | collective-permute-done | bytes 65568 | tf_op jit(solution)/shard_map/ppermute | solution.py:403
  75.6 3.6 %shard_map.160 = (f32[256,1792]{1,0:T(8,128)S(1)}, bf16[64,1792]{1,0:T(8,128)(2,1)S(1)}, bf16[192,1792]{1,0:T(8,128)(2,1)S(1)}) custom-call(f32[128,512]{1,0:T(8,128)S(1)} %get-tuple-element.52.own_mid, f32[128,512]{1,0:T(8,128)S(1)} %collective-permute-done.10.pair_mid, f32[128,128]{1,0:T(8,128)S(1)} %collective-permute-done.12.from_next, ...), custom_call_target="tpu_custom_call" | custom-call | flops 2415919104 | bytes 14042112 | tf_op jit(solution)/shard_map/pallas_call | solution.py:417
  79.3 0.5 collective-permute-start.15
  79.8 2.0 %collective-permute-done.15.first = bf16[64,1792]{1,0:T(8,128)(2,1)S(1)} collective-permute-done((bf16[64,1792]{1,0:T(8,128)(2,1)S(1)}, bf16[64,1792]{1,0:T(8,128)(2,1)S(1)}, u32[]{:S(2)}, u32[]{:S(2)}) %collective-permute-start.15) | collective-permute-done | bytes 229408 | tf_op jit(solution)/shard_map/ppermute | solution.py:408
  81.9 0.9 collective-permute-start.16
  82.8 4.4 %collective-permute-done.16.from_x = bf16[32,1792]{1,0:T(8,128)(2,1)S(1)} collective-permute-done((bf16[32,1792]{1,0:T(8,128)(2,1)S(1)}, bf16[32,1792]{1,0:T(8,128)(2,1)S(1)}, u32[]{:S(2)}, u32[]{:S(2)}) %collective-permute-start.16) | collective-permute-done | bytes 114720 | tf_op jit(solution)/shard_map/ppermute | solution.py:408
  87.1 0.5 collective-permute-done.17.from_y
  87.8 1.3 collective-permute-start.18
  89.4 5.0 %collective-permute-done.18.from_x = bf16[64,1792]{1,0:T(8,128)(2,1)S(1)} collective-permute-done((bf16[64,1792]{1,0:T(8,128)(2,1)S(1)}, bf16[64,1792]{1,0:T(8,128)(2,1)S(1)}, u32[]{:S(2)}, u32[]{:S(2)}) %collective-permute-start.18) | collective-permute-done | bytes 229408 | tf_op jit(solution)/shard_map/ppermute | solution.py:408
  94.4 0.9 collective-permute-done.19.from_y
  95.6 3.7 %collective-permute-start.22 = (bf16[16,1792]{1,0:T(8,128)(2,1)S(1)}, bf16[16,1792]{1,0:T(8,128)(2,1)S(1)}, u32[]{:S(2)}, u32[]{:S(2)}) collective-permute-start(bf16[16,1792]{1,0:T(8,128)(2,1)S(1)} %get-tuple-element.75), channel_id=1, source_target_pairs={{0,6},{1,7},{2,0},{3,1},{4,2},{5,3},{6,4},{7,5},{8,14},{9,15},{10,... | collective-permute-start | bytes 172040 | tf_op jit(solution)/shard_map/ppermute | solution.py:403
  99.4 2.2 %collective-permute-done.20.refs_1_ = bf16[16,1792]{1,0:T(8,128)(2,1)S(1)} collective-permute-done((bf16[16,1792]{1,0:T(8,128)(2,1)S(1)}, bf16[16,1792]{1,0:T(8,128)(2,1)S(1)}, u32[]{:S(2)}, u32[]{:S(2)}) %collective-permute-start.20) | collective-permute-done | bytes 57376 | tf_op jit(solution)/shard_map/ppermute | solution.py:403
  101.5 1.2 collective-permute-done.22.refs_3_
  102.8 2.6 %collective-permute-start.25 = (bf16[16,1792]{1,0:T(8,128)(2,1)S(1)}, bf16[16,1792]{1,0:T(8,128)(2,1)S(1)}, u32[]{:S(2)}, u32[]{:S(2)}) collective-permute-start(bf16[16,1792]{1,0:T(8,128)(2,1)S(1)} %shard_map.164.refs_0_), channel_id=1, source_target_pairs={{0,6},{1,7},{2,0},{3,1},{4,2},{5,3},{6,4},{7,5},{8,14},{9,15},{10,... | collective-permute-start | bytes 172040 | tf_op jit(solution)/shard_map/ppermute | solution.py:403
  105.7 0.4 collective-permute-start.23
  106.1 1.5 %collective-permute-done.25.refs_3_ = bf16[16,1792]{1,0:T(8,128)(2,1)S(1)} collective-permute-done((bf16[16,1792]{1,0:T(8,128)(2,1)S(1)}, bf16[16,1792]{1,0:T(8,128)(2,1)S(1)}, u32[]{:S(2)}, u32[]{:S(2)}) %collective-permute-start.25) | collective-permute-done | bytes 57376 | tf_op jit(solution)/shard_map/ppermute | solution.py:403
  107.6 2.9 %collective-permute-done.24.refs_2_ = bf16[16,1792]{1,0:T(8,128)(2,1)S(1)} collective-permute-done((bf16[16,1792]{1,0:T(8,128)(2,1)S(1)}, bf16[16,1792]{1,0:T(8,128)(2,1)S(1)}, u32[]{:S(2)}, u32[]{:S(2)}) %collective-permute-start.24) | collective-permute-done | bytes 57376 | tf_op jit(solution)/shard_map/ppermute | solution.py:403
  110.5 1.1 collective-permute-done.23.refs_1_
  111.7 1.1 collective-permute-start.27
  112.7 0.8 collective-permute-start.26
  113.6 4.2 %collective-permute-done.27.source.refs_2_ = bf16[64,1792]{1,0:T(8,128)(2,1)S(1)} collective-permute-done((bf16[64,1792]{1,0:T(8,128)(2,1)S(1)}, bf16[64,1792]{1,0:T(8,128)(2,1)S(1)}, u32[]{:S(2)}, u32[]{:S(2)}) %collective-permute-start.27) | collective-permute-done | bytes 229408 | tf_op jit(solution)/shard_map/ppermute | solution.py:408
  117.8 0.9 collective-permute-start.28
  118.6 1.4 %collective-permute-done.26.source.refs_1_ = bf16[64,1792]{1,0:T(8,128)(2,1)S(1)} collective-permute-done((bf16[64,1792]{1,0:T(8,128)(2,1)S(1)}, bf16[64,1792]{1,0:T(8,128)(2,1)S(1)}, u32[]{:S(2)}, u32[]{:S(2)}) %collective-permute-start.26) | collective-permute-done | bytes 229408 | tf_op jit(solution)/shard_map/ppermute | solution.py:408
  120.1 1.1 collective-permute-start.29
  121.2 1.5 %collective-permute-done.28.refs_3_ = bf16[32,1792]{1,0:T(8,128)(2,1)S(1)} collective-permute-done((bf16[32,1792]{1,0:T(8,128)(2,1)S(1)}, bf16[32,1792]{1,0:T(8,128)(2,1)S(1)}, u32[]{:S(2)}, u32[]{:S(2)}) %collective-permute-start.28) | collective-permute-done | bytes 114720 | tf_op jit(solution)/shard_map/ppermute | solution.py:408
  122.6 3.0 %collective-permute-done.29.refs_4_ = bf16[32,1792]{1,0:T(8,128)(2,1)S(1)} collective-permute-done((bf16[32,1792]{1,0:T(8,128)(2,1)S(1)}, bf16[32,1792]{1,0:T(8,128)(2,1)S(1)}, u32[]{:S(2)}, u32[]{:S(2)}) %collective-permute-start.29) | collective-permute-done | bytes 114720 | tf_op jit(solution)/shard_map/ppermute | solution.py:408
  125.7 1.3 collective-permute-done.34.refs_9_
  127.0 2.0 %shard_map.168 = (f32[512,512]{1,0:T(8,128)}, f32[512,512]{1,0:T(8,128)}, f32[512,512]{1,0:T(8,128)}, f32[512,128]{1,0:T(8,128)}, f32[1,1]{1,0:T(1,128)}) custom-call(bf16[64,1792]{1,0:T(8,128)(2,1)S(1)} %shard_map.165.refs_0_, bf16[64,1792]{1,0:T(8,128)(2,1)S(1)} %collective-permute-done.26.source.refs_1_, ...), custom_call_target="tpu_custom_call" | custom-call | bytes 5505024 | tf_op jit(solution)/shard_map/pallas_call | solution.py:574
  (82 shorter events, 2.3 us)
Async XLA Ops:
  0.6 1.0 copy-start.16
  1.7 0.7 copy-start.21
  2.3 0.7 copy-start.24
  3.5 25.7 %copy-start.10 = (bf16[512,512]{1,0:T(8,128)(2,1)}, bf16[512,512]{1,0:T(8,128)(2,1)S(1)}, u32[]{:S(2)}) copy-start(bf16[512,512]{1,0:T(8,128)(2,1)S(1)} %get-tuple-element.43.nodes_t) | copy-start | bytes 1572868
  3.5 9.7 %collective-permute-start = (bf16[512,128]{1,0:T(8,128)(2,1)S(1)}, bf16[512,128]{1,0:T(8,128)(2,1)S(1)}, u32[]{:S(2)}, u32[]{:S(2)}) collective-permute-start(bf16[512,128]{1,0:T(8,128)(2,1)S(1)} %get-tuple-element.44), channel_id=1, source_target_pairs={{0,1},{1,2},{2,3},{3,4},{4,5},{5,6},{6,7},{7,0},{8,9},{9,10},{10,1... | collective-permute-start | bytes 393224 | tf_op jit(solution)/shard_map/ppermute | solution.py:403
  6.6 7.8 %collective-permute-start.1 = (bf16[512,128]{1,0:T(8,128)(2,1)S(1)}, bf16[512,128]{1,0:T(8,128)(2,1)S(1)}, u32[]{:S(2)}, u32[]{:S(2)}) collective-permute-start(bf16[512,128]{1,0:T(8,128)(2,1)S(1)} %get-tuple-element.45), channel_id=1, source_target_pairs={{0,7},{1,0},{2,1},{3,2},{4,3},{5,4},{6,5},{7,6},{8,15},{9,8},{10,9... | collective-permute-start | bytes 393224 | tf_op jit(solution)/shard_map/ppermute | solution.py:403
  14.3 1.0 copy-start.8
  15.4 0.9 copy-start.17
  16.3 0.7 copy-start.22
  17.6 1.0 copy-start.27
  18.6 1.0 copy-start.28
  19.7 0.7 copy-start.29
  20.4 25.4 %copy-start.19 = (s32[3,4096]{1,0:T(4,128)S(1)}, s32[3,4096]{1,0:T(4,128)}, u32[]{:S(2)}) copy-start(s32[3,4096]{1,0:T(4,128)} %vertices.1) | copy-start | bytes 147460
  20.4 25.4 %copy-start.20 = (f32[3,4096]{1,0:T(4,128)S(1)}, f32[3,4096]{1,0:T(4,128)}, u32[]{:S(2)}) copy-start(f32[3,4096]{1,0:T(4,128)} %weights.1) | copy-start | bytes 147460
  29.3 1.6 %copy-start = (bf16[512,3072]{1,0:T(8,128)(2,1)}, bf16[512,3072]{1,0:T(8,128)(2,1)S(1)}, u32[]{:S(2)}) copy-start(bf16[512,3072]{1,0:T(8,128)(2,1)S(1)} %get-tuple-element.60.slope_t) | copy-start | bytes 9437188
  30.9 1.0 copy-start.2
  31.9 1.0 copy-start.4
  32.8 0.8 copy-start.12
  33.6 0.8 copy-start.14
  34.4 6.6 %collective-permute-start.5 = (bf16[128,128]{1,0:T(8,128)(2,1)S(1)}, bf16[128,128]{1,0:T(8,128)(2,1)S(1)}, u32[]{:S(2)}, u32[]{:S(2)}) collective-permute-start(bf16[128,128]{1,0:T(8,128)(2,1)S(1)} %get-tuple-element.47), channel_id=1, source_target_pairs={{0,1},{1,2},{2,3},{3,4},{4,5},{5,6},{6,7},{7,0},{8,9},{9,10},{10,1... | collective-permute-start | bytes 98312 | tf_op jit(solution)/shard_map/ppermute | solution.py:403
  34.7 6.3 %collective-permute-start.6 = (bf16[128,128]{1,0:T(8,128)(2,1)S(1)}, bf16[128,128]{1,0:T(8,128)(2,1)S(1)}, u32[]{:S(2)}, u32[]{:S(2)}) collective-permute-start(bf16[128,128]{1,0:T(8,128)(2,1)S(1)} %get-tuple-element.48), channel_id=1, source_target_pairs={{0,7},{1,0},{2,1},{3,2},{4,3},{5,4},{6,5},{7,6},{8,15},{9,8},{10,9... | collective-permute-start | bytes 98312 | tf_op jit(solution)/shard_map/ppermute | solution.py:403
  41.1 4.4 %collective-permute-start.9 = (bf16[128,256]{1,0:T(8,128)(2,1)S(1)}, bf16[128,256]{1,0:T(8,128)(2,1)S(1)}, u32[]{:S(2)}, u32[]{:S(2)}) collective-permute-start(bf16[128,256]{1,0:T(8,128)(2,1)S(1)} %constant_dynamic-update-slice_fusion.refs_4_), channel_id=1, source_target_pairs={{0,24},{8,16},{16,8},{24,0},{1,25},{9,17},{17,9},{25,1},{2,26},{10... | collective-permute-start | bytes 196616 | tf_op jit(solution)/shard_map/ppermute | solution.py:408
  41.2 11.5 %collective-permute-start.4 = (bf16[128,512]{1,0:T(8,128)(2,1)S(1)}, bf16[128,512]{1,0:T(8,128)(2,1)}, u32[]{:S(2)}, u32[]{:S(2)}) collective-permute-start(bf16[128,512]{1,0:T(8,128)(2,1)S(1)} %get-tuple-element.46.after.refs_0_), channel_id=1, source_target_pairs={{0,24},{8,16},{16,8},{24,0},{1,25},{9,17},{17,9},{25,1},{2,26},{10... | collective-permute-start | bytes 393224 | tf_op jit(solution)/shard_map/ppermute | solution.py:408
  42.9 9.8 %collective-permute-start.3 = (bf16[128,512]{1,0:T(8,128)(2,1)S(1)}, bf16[128,512]{1,0:T(8,128)(2,1)}, u32[]{:S(2)}, u32[]{:S(2)}) collective-permute-start(bf16[128,512]{1,0:T(8,128)(2,1)S(1)} %get-tuple-element.46.after.refs_0_), channel_id=1, source_target_pairs={{0,16},{8,24},{16,0},{24,8},{1,17},{9,25},{17,1},{25,9},{2,18},{10... | collective-permute-start | bytes 393224 | tf_op jit(solution)/shard_map/ppermute | solution.py:408
  44.4 8.3 %collective-permute-start.2 = (bf16[128,512]{1,0:T(8,128)(2,1)S(1)}, bf16[128,512]{1,0:T(8,128)(2,1)}, u32[]{:S(2)}, u32[]{:S(2)}) collective-permute-start(bf16[128,512]{1,0:T(8,128)(2,1)S(1)} %get-tuple-element.46.after.refs_0_), channel_id=1, source_target_pairs={{0,8},{8,0},{16,24},{24,16},{1,9},{9,1},{17,25},{25,17},{2,10},{10... | collective-permute-start | bytes 393224 | tf_op jit(solution)/shard_map/ppermute | solution.py:408
  44.4 8.3 %collective-permute-start.8 = (bf16[128,256]{1,0:T(8,128)(2,1)S(1)}, bf16[128,256]{1,0:T(8,128)(2,1)}, u32[]{:S(2)}, u32[]{:S(2)}) collective-permute-start(bf16[128,256]{1,0:T(8,128)(2,1)S(1)} %constant_dynamic-update-slice_fusion.refs_4_), channel_id=1, source_target_pairs={{0,16},{8,24},{16,0},{24,8},{1,17},{9,25},{17,1},{25,9},{2,18},{10... | collective-permute-start | bytes 196616 | tf_op jit(solution)/shard_map/ppermute | solution.py:408
  45.5 7.2 %collective-permute-start.7 = (bf16[128,256]{1,0:T(8,128)(2,1)S(1)}, bf16[128,256]{1,0:T(8,128)(2,1)}, u32[]{:S(2)}, u32[]{:S(2)}) collective-permute-start(bf16[128,256]{1,0:T(8,128)(2,1)S(1)} %constant_dynamic-update-slice_fusion.refs_4_), channel_id=1, source_target_pairs={{0,8},{8,0},{16,24},{24,16},{1,9},{9,1},{17,25},{25,17},{2,10},{10... | collective-permute-start | bytes 196616 | tf_op jit(solution)/shard_map/ppermute | solution.py:408
  45.8 1.2 copy-start.6
  47.0 1.2 copy-start.7
  52.7 22.9 %copy-start.1 = (bf16[512,3072]{1,0:T(8,128)(2,1)S(1)}, bf16[512,3072]{1,0:T(8,128)(2,1)}, u32[]{:S(2)}) copy-start(bf16[512,3072]{1,0:T(8,128)(2,1)} %copy-done) | copy-start | bytes 9437188
  52.7 22.9 %copy-start.3 = (f32[512,512]{1,0:T(8,128)S(1)}, f32[512,512]{1,0:T(8,128)}, u32[]{:S(2)}) copy-start(f32[512,512]{1,0:T(8,128)} %copy-done.2) | copy-start | bytes 3145732
  52.7 22.8 %copy-start.5 = (f32[512,512]{1,0:T(8,128)S(1)}, f32[512,512]{1,0:T(8,128)}, u32[]{:S(2)}) copy-start(f32[512,512]{1,0:T(8,128)} %copy-done.4) | copy-start | bytes 3145732
  52.7 22.8 %copy-start.9 = (bf16[512,512]{1,0:T(8,128)(2,1)S(1)}, bf16[512,512]{1,0:T(8,128)(2,1)}, u32[]{:S(2)}) copy-start(bf16[512,512]{1,0:T(8,128)(2,1)} %vertex.1) | copy-start | bytes 1572868
  52.7 22.8 %copy-start.11 = (bf16[512,512]{1,0:T(8,128)(2,1)S(1)}, bf16[512,512]{1,0:T(8,128)(2,1)}, u32[]{:S(2)}) copy-start(bf16[512,512]{1,0:T(8,128)(2,1)} %copy-done.10) | copy-start | bytes 1572868
  52.7 22.8 %copy-start.13 = (bf16[512,512]{1,0:T(8,128)(2,1)S(1)}, bf16[512,512]{1,0:T(8,128)(2,1)}, u32[]{:S(2)}) copy-start(bf16[512,512]{1,0:T(8,128)(2,1)} %copy-done.12) | copy-start | bytes 1572868
  52.8 22.8 %copy-start.15 = (bf16[512,512]{1,0:T(8,128)(2,1)S(1)}, bf16[512,512]{1,0:T(8,128)(2,1)}, u32[]{:S(2)}) copy-start(bf16[512,512]{1,0:T(8,128)(2,1)} %copy-done.14) | copy-start | bytes 1572868
  52.8 22.8 %copy-start.18 = (bf16[512,128]{1,0:T(8,128)(2,1)S(1)}, bf16[512,128]{1,0:T(8,128)(2,1)}, u32[]{:S(2)}) copy-start(bf16[512,128]{1,0:T(8,128)(2,1)} %w_decode.1) | copy-start | bytes 393220
  52.8 22.8 %copy-start.23 = (s32[128]{0:T(128)S(1)}, s32[128]{0:T(128)}, u32[]{:S(2)}) copy-start(s32[128]{0:T(128)} %param.14) | copy-start | bytes 1540
  52.8 22.8 %copy-start.26 = (s32[128]{0:T(128)S(1)}, s32[128]{0:T(128)}, u32[]{:S(2)}) copy-start(s32[128]{0:T(128)} %param.15) | copy-start | bytes 1540
  62.0 13.5 %collective-permute-start.10 = (f32[128,512]{1,0:T(8,128)S(1)}, f32[128,512]{1,0:T(8,128)S(1)}, u32[]{:S(2)}, u32[]{:S(2)}) collective-permute-start(f32[128,512]{1,0:T(8,128)S(1)} %get-tuple-element.53), channel_id=1, source_target_pairs={{0,8},{8,0},{16,24},{24,16},{1,9},{9,1},{17,25},{25,17},{2,10},{10... | collective-permute-start | bytes 786440 | tf_op jit(solution)/shard_map/ppermute | solution.py:408
  62.1 1.7 %collective-permute-start.11 = (f32[128,256]{1,0:T(8,128)S(1)}, f32[128,256]{1,0:T(8,128)S(1)}, u32[]{:S(2)}, u32[]{:S(2)}) collective-permute-start(f32[128,256]{1,0:T(8,128)S(1)} %get-tuple-element.55), channel_id=1, source_target_pairs={{0,8},{8,0},{16,24},{24,16},{1,9},{9,1},{17,25},{25,17},{2,10},{10... | collective-permute-start | bytes 393224 | tf_op jit(solution)/shard_map/ppermute | solution.py:408
  63.8 6.7 %collective-permute-start.12 = (f32[128,128]{1,0:T(8,128)S(1)}, f32[128,128]{1,0:T(8,128)S(1)}, u32[]{:S(2)}, u32[]{:S(2)}) collective-permute-start(f32[128,128]{1,0:T(8,128)S(1)} %get-tuple-element.56), channel_id=1, source_target_pairs={{0,7},{1,0},{2,1},{3,2},{4,3},{5,4},{6,5},{7,6},{8,15},{9,8},{10,9... | collective-permute-start | bytes 196616 | tf_op jit(solution)/shard_map/ppermute | solution.py:403
  68.6 7.0 %collective-permute-start.13 = (f32[128,128]{1,0:T(8,128)S(1)}, f32[128,128]{1,0:T(8,128)S(1)}, u32[]{:S(2)}, u32[]{:S(2)}) collective-permute-start(f32[128,128]{1,0:T(8,128)S(1)} %get-tuple-element.57), channel_id=1, source_target_pairs={{0,1},{1,2},{2,3},{3,4},{4,5},{5,6},{6,7},{7,0},{8,9},{9,10},{10,1... | collective-permute-start | bytes 196616 | tf_op jit(solution)/shard_map/ppermute | solution.py:403
  79.3 8.4 %collective-permute-start.14 = (bf16[192,1792]{1,0:T(8,128)(2,1)S(1)}, bf16[192,1792]{1,0:T(8,128)(2,1)S(1)}, u32[]{:S(2)}, u32[]{:S(2)}) collective-permute-start(bf16[192,1792]{1,0:T(8,128)(2,1)S(1)} %get-tuple-element.66), channel_id=1, source_target_pairs={{0,8},{8,0},{16,24},{24,16},{1,9},{9,1},{17,25},{25,17},{2,10},{10... | collective-permute-start | bytes 2064392 | tf_op jit(solution)/shard_map/ppermute | solution.py:408
  79.3 2.5 %collective-permute-start.15 = (bf16[64,1792]{1,0:T(8,128)(2,1)S(1)}, bf16[64,1792]{1,0:T(8,128)(2,1)S(1)}, u32[]{:S(2)}, u32[]{:S(2)}) collective-permute-start(bf16[64,1792]{1,0:T(8,128)(2,1)S(1)} %get-tuple-element.67), channel_id=1, source_target_pairs={{0,8},{8,0},{16,24},{24,16},{1,9},{9,1},{17,25},{25,17},{2,10},{10... | collective-permute-start | bytes 688136 | tf_op jit(solution)/shard_map/ppermute | solution.py:408
  81.9 5.3 %collective-permute-start.16 = (bf16[32,1792]{1,0:T(8,128)(2,1)S(1)}, bf16[32,1792]{1,0:T(8,128)(2,1)S(1)}, u32[]{:S(2)}, u32[]{:S(2)}) collective-permute-start(bf16[32,1792]{1,0:T(8,128)(2,1)S(1)} %get-tuple-element.68), channel_id=1, source_target_pairs={{0,16},{8,24},{16,0},{24,8},{1,17},{9,25},{17,1},{25,9},{2,18},{10... | collective-permute-start | bytes 344072 | tf_op jit(solution)/shard_map/ppermute | solution.py:408
  82.8 4.9 %collective-permute-start.17 = (bf16[32,1792]{1,0:T(8,128)(2,1)S(1)}, bf16[32,1792]{1,0:T(8,128)(2,1)S(1)}, u32[]{:S(2)}, u32[]{:S(2)}) collective-permute-start(bf16[32,1792]{1,0:T(8,128)(2,1)S(1)} %get-tuple-element.69), channel_id=1, source_target_pairs={{0,1},{1,0},{2,3},{3,2},{4,5},{5,4},{6,7},{7,6},{8,9},{9,8},{10,11... | collective-permute-start | bytes 344072 | tf_op jit(solution)/shard_map/ppermute | solution.py:408
  87.8 6.6 %collective-permute-start.18 = (bf16[64,1792]{1,0:T(8,128)(2,1)S(1)}, bf16[64,1792]{1,0:T(8,128)(2,1)S(1)}, u32[]{:S(2)}, u32[]{:S(2)}) collective-permute-start(bf16[64,1792]{1,0:T(8,128)(2,1)S(1)} %get-tuple-element.70), channel_id=1, source_target_pairs={{0,16},{8,24},{16,0},{24,8},{1,17},{9,25},{17,1},{25,9},{2,18},{10... | collective-permute-start | bytes 688136 | tf_op jit(solution)/shard_map/ppermute | solution.py:408
  89.1 6.2 %collective-permute-start.19 = (bf16[64,1792]{1,0:T(8,128)(2,1)S(1)}, bf16[64,1792]{1,0:T(8,128)(2,1)S(1)}, u32[]{:S(2)}, u32[]{:S(2)}) collective-permute-start(bf16[64,1792]{1,0:T(8,128)(2,1)S(1)} %get-tuple-element.71), channel_id=1, source_target_pairs={{0,1},{1,0},{2,3},{3,2},{4,5},{5,4},{6,7},{7,6},{8,9},{9,8},{10,11... | collective-permute-start | bytes 688136 | tf_op jit(solution)/shard_map/ppermute | solution.py:408
  95.5 6.0 %collective-permute-start.20 = (bf16[16,1792]{1,0:T(8,128)(2,1)S(1)}, bf16[16,1792]{1,0:T(8,128)(2,1)S(1)}, u32[]{:S(2)}, u32[]{:S(2)}) collective-permute-start(bf16[16,1792]{1,0:T(8,128)(2,1)S(1)} %get-tuple-element.73), channel_id=1, source_target_pairs={{0,2},{1,3},{2,4},{3,5},{4,6},{5,7},{6,0},{7,1},{8,10},{9,11},{10,... | collective-permute-start | bytes 172040 | tf_op jit(solution)/shard_map/ppermute | solution.py:403
  95.6 6.0 %collective-permute-start.21 = (bf16[16,1792]{1,0:T(8,128)(2,1)S(1)}, bf16[16,1792]{1,0:T(8,128)(2,1)S(1)}, u32[]{:S(2)}, u32[]{:S(2)}) collective-permute-start(bf16[16,1792]{1,0:T(8,128)(2,1)S(1)} %get-tuple-element.74), channel_id=1, source_target_pairs={{0,4},{1,5},{2,6},{3,7},{4,0},{5,1},{6,2},{7,3},{8,12},{9,13},{10,... | collective-permute-start | bytes 172040 | tf_op jit(solution)/shard_map/ppermute | solution.py:403
  95.6 7.1 %collective-permute-start.22 = (bf16[16,1792]{1,0:T(8,128)(2,1)S(1)}, bf16[16,1792]{1,0:T(8,128)(2,1)S(1)}, u32[]{:S(2)}, u32[]{:S(2)}) collective-permute-start(bf16[16,1792]{1,0:T(8,128)(2,1)S(1)} %get-tuple-element.75), channel_id=1, source_target_pairs={{0,6},{1,7},{2,0},{3,1},{4,2},{5,3},{6,4},{7,5},{8,14},{9,15},{10,... | collective-permute-start | bytes 172040 | tf_op jit(solution)/shard_map/ppermute | solution.py:403
  102.8 4.8 %collective-permute-start.25 = (bf16[16,1792]{1,0:T(8,128)(2,1)S(1)}, bf16[16,1792]{1,0:T(8,128)(2,1)S(1)}, u32[]{:S(2)}, u32[]{:S(2)}) collective-permute-start(bf16[16,1792]{1,0:T(8,128)(2,1)S(1)} %shard_map.164.refs_0_), channel_id=1, source_target_pairs={{0,6},{1,7},{2,0},{3,1},{4,2},{5,3},{6,4},{7,5},{8,14},{9,15},{10,... | collective-permute-start | bytes 172040 | tf_op jit(solution)/shard_map/ppermute | solution.py:403
  105.4 5.1 %collective-permute-start.24 = (bf16[16,1792]{1,0:T(8,128)(2,1)S(1)}, bf16[16,1792]{1,0:T(8,128)(2,1)S(1)}, u32[]{:S(2)}, u32[]{:S(2)}) collective-permute-start(bf16[16,1792]{1,0:T(8,128)(2,1)S(1)} %shard_map.164.refs_0_), channel_id=1, source_target_pairs={{0,4},{1,5},{2,6},{3,7},{4,0},{5,1},{6,2},{7,3},{8,12},{9,13},{10,... | collective-permute-start | bytes 172040 | tf_op jit(solution)/shard_map/ppermute | solution.py:403
  105.7 6.0 %collective-permute-start.23 = (bf16[16,1792]{1,0:T(8,128)(2,1)S(1)}, bf16[16,1792]{1,0:T(8,128)(2,1)S(1)}, u32[]{:S(2)}, u32[]{:S(2)}) collective-permute-start(bf16[16,1792]{1,0:T(8,128)(2,1)S(1)} %shard_map.164.refs_0_), channel_id=1, source_target_pairs={{0,2},{1,3},{2,4},{3,5},{4,6},{5,7},{6,0},{7,1},{8,10},{9,11},{10,... | collective-permute-start | bytes 172040 | tf_op jit(solution)/shard_map/ppermute | solution.py:403
  111.7 6.1 %collective-permute-start.27 = (bf16[64,1792]{1,0:T(8,128)(2,1)S(1)}, bf16[64,1792]{1,0:T(8,128)(2,1)S(1)}, u32[]{:S(2)}, u32[]{:S(2)}) collective-permute-start(bf16[64,1792]{1,0:T(8,128)(2,1)S(1)} %shard_map.165.refs_0_), channel_id=1, source_target_pairs={{0,1},{1,0},{2,3},{3,2},{4,5},{5,4},{6,7},{7,6},{8,9},{9,8},{10,11... | collective-permute-start | bytes 688136 | tf_op jit(solution)/shard_map/ppermute | solution.py:408
  112.7 7.2 %collective-permute-start.26 = (bf16[64,1792]{1,0:T(8,128)(2,1)S(1)}, bf16[64,1792]{1,0:T(8,128)(2,1)S(1)}, u32[]{:S(2)}, u32[]{:S(2)}) collective-permute-start(bf16[64,1792]{1,0:T(8,128)(2,1)S(1)} %shard_map.165.refs_0_), channel_id=1, source_target_pairs={{0,16},{8,24},{16,0},{24,8},{1,17},{9,25},{17,1},{25,9},{2,18},{10... | collective-permute-start | bytes 688136 | tf_op jit(solution)/shard_map/ppermute | solution.py:408
  113.6 12.1 %collective-permute-start.30 = (bf16[64,1792]{1,0:T(8,128)(2,1)S(1)}, bf16[64,1792]{1,0:T(8,128)(2,1)S(1)}, u32[]{:S(2)}, u32[]{:S(2)}) collective-permute-start(bf16[64,1792]{1,0:T(8,128)(2,1)S(1)} %shard_map.165.refs_0_), channel_id=1, source_target_pairs={{0,8},{8,0},{16,24},{24,16},{1,9},{9,1},{17,25},{25,17},{2,10},{10... | collective-permute-start | bytes 688136 | tf_op jit(solution)/shard_map/ppermute | solution.py:408
  117.8 4.9 %collective-permute-start.28 = (bf16[32,1792]{1,0:T(8,128)(2,1)S(1)}, bf16[32,1792]{1,0:T(8,128)(2,1)S(1)}, u32[]{:S(2)}, u32[]{:S(2)}) collective-permute-start(bf16[32,1792]{1,0:T(8,128)(2,1)S(1)} %shard_map.166), channel_id=1, source_target_pairs={{0,16},{8,24},{16,0},{24,8},{1,17},{9,25},{17,1},{25,9},{2,18},{10... | collective-permute-start | bytes 344072 | tf_op jit(solution)/shard_map/ppermute | solution.py:408
  118.6 7.0 %collective-permute-start.32 = (bf16[64,1792]{1,0:T(8,128)(2,1)S(1)}, bf16[64,1792]{1,0:T(8,128)(2,1)S(1)}, u32[]{:S(2)}, u32[]{:S(2)}) collective-permute-start(bf16[64,1792]{1,0:T(8,128)(2,1)S(1)} %collective-permute-done.27.source.refs_2_), channel_id=1, source_target_pairs={{0,8},{8,0},{16,24},{24,16},{1,9},{9,1},{17,25},{25,17},{2,10},{10... | collective-permute-start | bytes 688136 | tf_op jit(solution)/shard_map/ppermute | solution.py:408
  120.0 5.7 %collective-permute-start.31 = (bf16[64,1792]{1,0:T(8,128)(2,1)S(1)}, bf16[64,1792]{1,0:T(8,128)(2,1)S(1)}, u32[]{:S(2)}, u32[]{:S(2)}) collective-permute-start(bf16[64,1792]{1,0:T(8,128)(2,1)S(1)} %collective-permute-done.26.source.refs_1_), channel_id=1, source_target_pairs={{0,8},{8,0},{16,24},{24,16},{1,9},{9,1},{17,25},{25,17},{2,10},{10... | collective-permute-start | bytes 688136 | tf_op jit(solution)/shard_map/ppermute | solution.py:408
  120.1 5.6 %collective-permute-start.29 = (bf16[32,1792]{1,0:T(8,128)(2,1)S(1)}, bf16[32,1792]{1,0:T(8,128)(2,1)S(1)}, u32[]{:S(2)}, u32[]{:S(2)}) collective-permute-start(bf16[32,1792]{1,0:T(8,128)(2,1)S(1)} %shard_map.167), channel_id=1, source_target_pairs={{0,1},{1,0},{2,3},{3,2},{4,5},{5,4},{6,7},{7,6},{8,9},{9,8},{10,11... | collective-permute-start | bytes 344072 | tf_op jit(solution)/shard_map/ppermute | solution.py:408
  122.6 3.1 %collective-permute-start.33 = (bf16[32,1792]{1,0:T(8,128)(2,1)S(1)}, bf16[32,1792]{1,0:T(8,128)(2,1)S(1)}, u32[]{:S(2)}, u32[]{:S(2)}) collective-permute-start(bf16[32,1792]{1,0:T(8,128)(2,1)S(1)} %collective-permute-done.28.refs_3_), channel_id=1, source_target_pairs={{0,8},{8,0},{16,24},{24,16},{1,9},{9,1},{17,25},{25,17},{2,10},{10... | collective-permute-start | bytes 344072 | tf_op jit(solution)/shard_map/ppermute | solution.py:408
  125.7 1.3 %collective-permute-start.34 = (bf16[32,1792]{1,0:T(8,128)(2,1)S(1)}, bf16[32,1792]{1,0:T(8,128)(2,1)S(1)}, u32[]{:S(2)}, u32[]{:S(2)}) collective-permute-start(bf16[32,1792]{1,0:T(8,128)(2,1)S(1)} %collective-permute-done.29.refs_4_), channel_id=1, source_target_pairs={{0,8},{8,0},{16,24},{24,16},{1,9},{9,1},{17,25},{25,17},{2,10},{10... | collective-permute-start | bytes 344072 | tf_op jit(solution)/shard_map/ppermute | solution.py:408
  (1 other events, 0.7 us)

commit v6 on v5

--- a/solution.py
+++ b/solution.py
@@ -53,14 +53,20 @@
     return copies
 
 
-def lend_kernel(nodes, to_next, to_prev, nodes_t, next_t, prev_t, held, rows_next, rows_prev, sems):
+def sides(next_side, prev_side):
+    even = lax.rem(lax.axis_index("dom"), 2) == 0
+    return jnp.where(even, next_side, prev_side), jnp.where(even, prev_side, next_side)
+
+
+def lend_kernel(nodes, to_next, to_prev, nodes_t, first_t, second_t, held, rows_next, rows_prev, sems):
     for copy in fetched((nodes, to_next, to_prev), (held, rows_next, rows_prev), sems):
         copy.wait()
     table = held[...].T
     nodes_t[...] = table
     count = table.shape[1]
-    next_t[...] = dot(table, one_hot(count, rows_next[...])).astype(BF16)
-    prev_t[...] = dot(table, one_hot(count, rows_prev[...])).astype(BF16)
+    first, second = sides(rows_next[...], rows_prev[...])
+    first_t[...] = dot(table, one_hot(count, first)).astype(BF16)
+    second_t[...] = dot(table, one_hot(count, second)).astype(BF16)
 
 
 def decoder_kernel(core, vertices, weights, base, truth, after, mat, base_t, truth_t, base_rows, truth_rows, sems):
@@ -111,8 +117,8 @@
 
 
 def forward_kernel(
-    nodes_t, from_prev, from_next, senders_in, to_next_in, to_prev_in, w_send_in, w_recv_in, vertex_in, w_decode_in,
-    picked_t, field_t, next_t, prev_t, slope_out, slope_sum_out, agg_out, upd_slope_out, hidden_out,
+    nodes_t, from_first, from_second, senders_in, to_next_in, to_prev_in, w_send_in, w_recv_in, vertex_in, w_decode_in,
+    picked_t, field_t, first_t, second_t, slope_out, slope_sum_out, agg_out, upd_slope_out, hidden_out,
     pre, senders, to_next, to_prev, w_send, w_recv, vertex, w_decode, recv_t,
     slope_t, slope_sum_t, agg_t, upd_slope_t, hidden_t, in_sems, out_sems,
 ):
@@ -129,10 +135,11 @@
         stored.append(copy)
 
     degree, count = senders.shape
-    halo = from_prev.shape[1]
+    halo = from_first.shape[1]
     width = nodes_t.shape[0]
-    ext = jnp.concatenate([nodes_t[...], from_prev[...], from_next[...]], axis=1)
-    for copy in fetch:
+    from_next, from_prev = sides(from_first[...], from_second[...])
+    ext = jnp.concatenate([nodes_t[...], from_prev, from_next], axis=1)
+    for copy in fetch[:5]:
         copy.wait()
     w_send_t = w_send[...].T * 0.5
     recv_t[...] = dot(w_recv[...].T, nodes_t[...]) * 0.5
@@ -157,6 +164,8 @@
             store(slope_t.at[group, :], slope_out.at[group, :])
     store(slope_sum_t, slope_sum_out)
     store(agg_t, agg_out)
+    for copy in fetch[5:]:
+        copy.wait()
     pre[:, :count] = dot(vertex[...].T * 0.5, agg_t[...])
     for start in range(0, width, TILE):
         rows = slice(start, start + TILE)
@@ -167,8 +176,9 @@
     store(hidden_t, hidden_out)
     field = dot(w_decode[...].T, hidden_t[...]).astype(BF16)
     field_t[...] = field
-    next_t[...] = dot(field, one_hot(count, to_next[...])).astype(BF16)
-    prev_t[...] = dot(field, one_hot(count, to_prev[...])).astype(BF16)
+    first, second = sides(to_next[...], to_prev[...])
+    first_t[...] = dot(field, one_hot(count, first)).astype(BF16)
+    second_t[...] = dot(field, one_hot(count, second)).astype(BF16)
     for copy in stored:
         copy.wait()
 
@@ -242,11 +252,19 @@
             end[...] = grad[rows, count:]
 
 
-def ends_kernel(mine, got, after, before):
-    halo = after.shape[1]
+def borrowed_kernel(first, second, end):
+    halo = first.shape[1]
+    from_next, from_prev = sides(first[...], second[...])
+    end[:, :halo] = from_prev
+    end[:, halo:] = from_next
+
+
+def ends_kernel(mine, got, first, second):
+    halo = first.shape[1]
     total = mine[...] + got[...]
-    after[...] = total[:, :halo]
-    before[...] = total[:, halo:]
+    to_first, to_second = sides(total[:, halo:], total[:, :halo])
+    first[...] = to_first.astype(BF16)
+    second[...] = to_second.astype(BF16)
 
 
 def split(value):
@@ -267,7 +285,7 @@
 
 
 def backward_kernel(
-    own_mid, pair_mid, from_next, from_prev, to_next, to_prev, term, w_decode, vertex, nodes_t,
+    own_mid, pair_mid, from_first, from_second, to_next, to_prev, term, w_decode, vertex, nodes_t,
     picked_t, slope_t, slope_sum_t, agg_t, upd_slope_t, hidden_t,
     *refs,
 ):
@@ -275,10 +293,8 @@
     count = nodes_t.shape[1]
     width = nodes_t.shape[0]
     grad_z = own_mid[...] + pair_mid[...]
-    for got, rows in ((from_next[...], to_next), (from_prev[...], to_prev)):
-        place = one_hot(count, rows[...])
-        hi, lo = split(got)
-        grad_z += dot_nt(hi, place) + dot_nt(lo, place)
+    for got, rows in zip((from_first, from_second), sides(to_next[...], to_prev[...])):
+        grad_z += dot_nt(got[...], one_hot(count, rows))
     grad_z = grad_z.astype(BF16)
     main = whole.shape[1] - LANES
     whole[:, 3 * width : main] = dot_nt(hidden_t[...], grad_z)
@@ -306,7 +322,7 @@
 
     def block(c, xr, yr, k):
         quarter = 2 * c + lax.bitwise_xor(x, xr)
-        start = (8 * quarter + 2 * lax.rem(z + k, 4) + lax.bitwise_xor(y, yr)) * share
+        start = (8 * quarter + 2 * lax.bitwise_xor(z, k) + lax.bitwise_xor(y, yr)) * share
         return whole[pl.ds(pl.multiple_of(start, share), share), :]
 
     at = 0
@@ -362,11 +378,6 @@
         refs[-1][k * rows : (k + 1) * rows, :] = ref[...]
 
 
-def half_kernel(at, source, target):
-    rows = target.shape[0]
-    target[...] = source[at * rows : (at + 1) * rows, :]
-
-
 def finish_kernel(scale, *refs):
     g_send, g_recv, g_update, g_decode, loss = refs[-5:]
     pieces = refs[:-5]
@@ -374,12 +385,10 @@
     share = width // 32
     core, x, z, y = position()
     total = jnp.zeros((share, LANES), F32)
-    layout = ((0, 0, 0), (1, 0, 0), (0, 1, 0), (1, 1, 0), (1, 1, 2))
     for i, piece in enumerate(pieces):
-        xr, yr, first = layout[i % 5]
-        quarter = 2 * (core if i < 5 else 1 - core) + lax.bitwise_xor(x, xr)
+        quarter = 2 * (core if i < 4 else 1 - core) + (x if i % 4 < 2 else 1 - x)
         for j in range(piece.shape[0] // share):
-            start = (8 * quarter + 2 * lax.rem(z + 4 - first - j, 4) + lax.bitwise_xor(y, yr)) * share
+            start = (8 * quarter + lax.bitwise_xor(2 * z + y, 4 * (i % 2) + j)) * share
             place = pl.ds(pl.multiple_of(start, share), share)
             value = piece[j * share : (j + 1) * share, :].astype(F32)
             g_send[place, :] = value[:, :width]
@@ -398,9 +407,10 @@
 SCALAR = pl.BlockSpec(memory_space=pltpu.SMEM)
 
 
-def along(value, axis, steps):
-    size = lax.axis_size(axis)
-    return lax.ppermute(value, axis, [(i, (i + steps) % size) for i in range(size)])
+def meet(first, second):
+    size = lax.axis_size("dom")
+    second = lax.ppermute(second, "dom", [(i, (i + (1 if i % 2 else size - 1)) % size) for i in range(size)])
+    return flip(first, "dom", 1), second
 
 
 def flip(value, axis, bit):
@@ -412,7 +422,7 @@
     return sum(x.size * x.dtype.itemsize for x in arrays)
 
 
-def call(kernel, ins, outs, scratch=(), flops=0, room=4, in_hbm=0, out_hbm=0):
+def call(kernel, ins, outs, scratch=(), flops=0, room=4, in_hbm=0, out_hbm=0, limit=0):
     size = nbytes(list(ins) + list(outs))
     return pl.pallas_call(
         kernel,
@@ -420,13 +430,22 @@
         in_specs=vmem(len(ins) - in_hbm) + [HBM] * in_hbm,
         out_specs=vmem(len(outs) - out_hbm) + [HBM] * out_hbm,
         scratch_shapes=list(scratch),
-        compiler_params=params(1.1 * size / MIB + room),
+        compiler_params=params(limit or 1.1 * size / MIB + room),
         cost_estimate=cost(flops, size),
     )(*ins)
 
 
 def scalar(value):
     return jnp.reshape(value, (1,)).astype(jnp.int32)
+
+
+def gathered(value):
+    found = [value]
+    bit = lax.axis_size("ens") // 2
+    while bit:
+        found = [x for v in found for x in (v, flip(v, "ens", bit))]
+        bit //= 2
+    return found
 
 
 def summed(keep, send_first, send_rest):
@@ -442,13 +461,11 @@
     to_x, to_y = call(sides_kernel, [keep, rest, by_x, by_y], [piece(block)] * 2)
     to_x, to_y = over_x(to_x), over_y(to_y)
     shares = call(shares_kernel, [keep, rest, to_x, to_y], [piece(share)] * 3 + [sds((share, cols), F32)])
-    terms = [shares[3]] + [along(shares[k - 1], "dom", 2 * k) for k in (1, 2, 3)]
+    terms = [shares[3]] + [flip(shares[k - 1], "dom", 2 * k) for k in (1, 2, 3)]
     (own,) = call(sum_kernel, terms, [piece(share)])
-    (mine,) = call(join_kernel, [own] + [along(own, "dom", 2 * k) for k in (1, 2, 3)], [piece(block)])
-    x, y = over_x(mine), over_y(mine)
-    (low,) = call(functools.partial(half_kernel, 0), [y], [piece(half)])
-    (high,) = call(functools.partial(half_kernel, 1), [x], [piece(half)])
-    here = [mine, x, y, over_x(low), over_y(high)]
+    pieces = [own] + [flip(own, "dom", k) for k in range(1, 8)]
+    here = [call(join_kernel, pieces[i : i + 4], [piece(block)])[0] for i in (0, 4)]
+    here += [over_x(v) for v in here]
     return here + [core(v) for v in here]
 
 
@@ -469,21 +486,21 @@
 
     held = lambda shape, dtype=BF16: pltpu.VMEM(shape, dtype)
     indices = lambda: [held((1, halo), jnp.int32)] * 2
-    nodes_t, next_t, prev_t = call(
+    nodes_t, first_t, second_t = call(
         lend_kernel,
         [latent, to_next, to_prev],
         [sds((width, count), BF16), sds((width, halo), BF16), sds((width, halo), BF16)],
         [held((count, width))] + indices() + [pltpu.SemaphoreType.DMA((3,))],
         flops=4 * width * count * halo,
         in_hbm=3,
+        limit=56,
     )
-    lat_prev = along(next_t, "dom", 1)
-    lat_next = along(prev_t, "dom", -1)
+    from_first, from_second = meet(first_t, second_t)
 
     core = scalar(lax.rem(ens, 2))
-    picked_t, field_t, next_t, prev_t, slope_t, slope_sum_t, agg_t, upd_slope_t, hidden_t = call(
+    picked_t, field_t, first_t, second_t, slope_t, slope_sum_t, agg_t, upd_slope_t, hidden_t = call(
         forward_kernel,
-        [nodes_t, lat_prev, lat_next, senders, to_next, to_prev, w_send, w_recv, vertex_refresh_matrix, w_decode],
+        [nodes_t, from_first, from_second, senders, to_next, to_prev, w_send, w_recv, vertex_refresh_matrix, w_decode],
         [
             sds((width, degree * count), BF16), sds((variables, count), BF16), sds((variables, halo), BF16),
             sds((variables, halo), BF16), sds((width, degree * count), BF16), sds((width, count), F32),
@@ -496,12 +513,12 @@
             pltpu.SemaphoreType.DMA((7,)), pltpu.SemaphoreType.DMA((width // 128 + 4,)),
         ],
         flops=2 * degree * width * count * (ext_rows + width),
-        room=14,
         in_hbm=7,
         out_hbm=5,
+        limit=56,
     )
-    lent = (along(next_t, "dom", 1), along(prev_t, "dom", -1))
-    mids = [field_t] + [flip(field_t, "ens", m) for m in range(1, members)]
+    lent = meet(first_t, second_t)
+    mids = gathered(field_t)
 
     block = 512
     steps = line_span // 2 // block
@@ -521,10 +538,10 @@
         out_shape=[sds((2 * ext_rows, half_span), BF16)] + [sds((variables, half_span), BF16)] * 2,
         compiler_params=params(12),
         cost_estimate=cost(10 * ext_rows * half_span, 16e6),
-    )(core, readout_vertex_list, dec_weights, base, observed_analysis, field_t)
-
-    end = jnp.concatenate(lent, axis=1)
-    ends = [end] + [flip(end, "ens", m) for m in range(1, members)]
+    )(core, readout_vertex_list, dec_weights, base, observed_analysis, nodes_t)
+
+    (end,) = call(borrowed_kernel, list(lent), [sds((variables, 2 * halo), BF16)])
+    ends = gathered(end)
 
     grads = pl.pallas_call(
         functools.partial(readout_kernel, line_span),
@@ -544,12 +561,12 @@
     own_mid, own_end, pair_mid, pair_end, term = grads
     got_end = flip(pair_end, "ens", 1)
     got_mid = flip(pair_mid, "ens", 1)
-    to_before, to_after = call(ends_kernel, [own_end, got_end], [sds((variables, halo), F32)] * 2)
-    from_next, from_prev = along(to_before, "dom", -1), along(to_after, "dom", 1)
+    to_first, to_second = call(ends_kernel, [own_end, got_end], [sds((variables, halo), BF16)] * 2)
+    from_first, from_second = meet(to_first, to_second)
 
     cols = 3 * width + variables + LANES
     operands = [
-        own_mid, got_mid, from_next, from_prev, to_next, to_prev, term, w_decode,
+        own_mid, got_mid, from_first, from_second, to_next, to_prev, term, w_decode,
         vertex_refresh_matrix, nodes_t, picked_t, slope_t, slope_sum_t, agg_t, upd_slope_t, hidden_t,
     ]
     whole = sds((width, cols), F32)

time: 130 us -> 117 us (0.900)
  local copies, waits for them, and re-layouts: 16.1 us -> 1.62 us
  waiting for transfers between devices: 49.4 us -> 42.8 us
  Pallas kernels: 28.1 us -> 33.4 us
  starting transfers between devices: 34.4 us -> 37.5 us
    ppermute x23 -> x33, starting transfers between devices: 11.7 us -> 26.8 us  [flip(): return lax.ppermute(value, axis, [(i, i ^ bit) for i in range(size)])]
    ppermute x12 -> x3, waiting for transfers between devices: 22.5 us -> 7.89 us  [meet(): lax.ppermute(second, 'dom', [(i, (i + (1 if i % 2 else size - 1)) % size)...]
    unnamed x61 -> x36, local copies, waits for them, and re-layouts: 16.1 us -> 1.62 us
    ppermute x12 -> x3, starting transfers between devices: 22.7 us -> 10.7 us  [meet(): lax.ppermute(second, 'dom', [(i, (i + (1 if i % 2 else size - 1)) % size)...]
    ppermute x23 -> x33, waiting for transfers between devices: 26.9 us -> 34.9 us  [flip(): return lax.ppermute(value, axis, [(i, i ^ bit) for i in range(size)])]
    pallas_call x11, Pallas kernels: 13.5 us -> 19.8 us  [call(): pl.pallas_call(kernel, out_shape=outs, in_specs=vmem(len(ins) - in_hbm) +...]
  transfers between devices with their start and end apart: 35 -> 36, of which waited for: 23 -> 20; matrix products, arithmetic and copies ran while one was open for 0% -> 0% of each run, Pallas kernels for 3% -> 3%
where the time goes in v6:
time: 117 us; the launch traced here: 116 us
  waiting for transfers between devices  42.8 us (37%)
  starting transfers between devices  37.5 us (32%)
  Pallas kernels  33.4 us (29%)
  local copies, waits for them, and re-layouts  1.62 us (1%)
    ppermute x33, waiting for transfers between devices, flip(): return lax.ppermute(value, axis, [(i, i ^ bit) for i in range(size)])  34.9 us
    ppermute x33, starting transfers between devices, flip(): return lax.ppermute(value, axis, [(i, i ^ bit) for i in range(size)])  26.8 us
    pallas_call x11, Pallas kernels, call(): pl.pallas_call(kernel, out_shape=outs, in_specs=vmem(len(ins) - in_hbm) +...  19.8 us
    ppermute x3, starting transfers between devices, meet(): lax.ppermute(second, 'dom', [(i, (i + (1 if i % 2 else size - 1)) % size)...  10.7 us
    pallas_call x1, Pallas kernels, per_device(): pl.pallas_call(functools.partial(readout_kernel, line_span), grid=(steps,...  8.07 us
    ppermute x3, waiting for transfers between devices, meet(): lax.ppermute(second, 'dom', [(i, (i + (1 if i % 2 else size - 1)) % size)...  7.89 us
    pallas_call x1, Pallas kernels, per_device(): pl.pallas_call(decoder_kernel, grid_spec=pltpu.PrefetchScalarGridSpec(num...  3.56 us
  transfers between devices with their start and end apart: 36, of which 20 were waited for; matrix products, arithmetic and copies ran while one was open for 0% of the time, Pallas kernels for 3%

profile of v6, /device:TPU:0, one launch (start us, length us, event | category | flops | bytes accessed | tf_op | source)
XLA Modules:
  0.0 116.4 jit_solution(17483603798326427717)
XLA Ops:
  0.6 2.2 %shard_map.155 = (bf16[512,512]{1,0:T(8,128)(2,1)}, bf16[512,128]{1,0:T(8,128)(2,1)}, bf16[512,128]{1,0:T(8,128)(2,1)}) custom-call(bf16[512,512]{1,0:T(8,128)(2,1)} %bitcast.11, s32[1,128]{1,0:T(1,128)} %bitcast.5, s32[1,128]{1,0:T(1,128)} %bitcast.8), custom_call_target="tpu_custom_call" | custom-call | flops 134217728 | bytes 1311744 | tf_op jit(solution)/shard_map/pallas_call | solution.py:427
  2.9 3.0 %collective-permute-start = (bf16[512,128]{1,0:T(8,128)(2,1)}, bf16[512,128]{1,0:T(8,128)(2,1)S(1)}, u32[]{:S(2)}, u32[]{:S(2)}) collective-permute-start(bf16[512,128]{1,0:T(8,128)(2,1)} %get-tuple-element.44), channel_id=1, source_target_pairs={{0,1},{1,0},{2,3},{3,2},{4,5},{5,4},{6,7},{7,6},{8,9},{9,8},{10,11... | collective-permute-start | bytes 393224 | tf_op jit(solution)/shard_map/ppermute | solution.py:418
  5.9 3.5 %collective-permute-start.1 = (bf16[512,128]{1,0:T(8,128)(2,1)}, bf16[512,128]{1,0:T(8,128)(2,1)S(1)}, u32[]{:S(2)}, u32[]{:S(2)}) collective-permute-start(bf16[512,128]{1,0:T(8,128)(2,1)} %get-tuple-element.45), channel_id=1, source_target_pairs={{0,7},{1,2},{2,1},{3,4},{4,3},{5,6},{6,5},{7,0},{8,15},{9,10},{10,... | collective-permute-start | bytes 393224 | tf_op jit(solution)/shard_map/ppermute | solution.py:412
  9.5 2.3 %collective-permute-done.from_first = bf16[512,128]{1,0:T(8,128)(2,1)S(1)} collective-permute-done((bf16[512,128]{1,0:T(8,128)(2,1)}, bf16[512,128]{1,0:T(8,128)(2,1)S(1)}, u32[]{:S(2)}, u32[]{:S(2)}) %collective-permute-start) | collective-permute-done | bytes 131104 | tf_op jit(solution)/shard_map/ppermute | solution.py:418
  11.8 2.0 %collective-permute-done.1.from_second = bf16[512,128]{1,0:T(8,128)(2,1)S(1)} collective-permute-done((bf16[512,128]{1,0:T(8,128)(2,1)}, bf16[512,128]{1,0:T(8,128)(2,1)S(1)}, u32[]{:S(2)}, u32[]{:S(2)}) %collective-permute-start.1) | collective-permute-done | bytes 131104 | tf_op jit(solution)/shard_map/ppermute | solution.py:412
  13.8 0.6 copy-done.17
  14.5 13.5 %shard_map.156 = (bf16[512,3072]{1,0:T(8,128)(2,1)}, bf16[128,512]{1,0:T(8,128)(2,1)}, bf16[128,128]{1,0:T(8,128)(2,1)}, bf16[128,128]{1,0:T(8,128)(2,1)}, bf16[...) custom-call(bf16[512,512]{1,0:T(8,128)(2,1)} %get-tuple-element.43.n, ...), custom_call_target="tpu_custom_call" | custom-call | flops 4026531840 | bytes 12137472 | tf_op jit(solution)/shard_map/pallas_call | solution.py:427
  28.0 1.6 %collective-permute-start.3 = (bf16[128,512]{1,0:T(8,128)(2,1)}, bf16[128,512]{1,0:T(8,128)(2,1)S(1)}, u32[]{:S(2)}, u32[]{:S(2)}) collective-permute-start(bf16[128,512]{1,0:T(8,128)(2,1)} %get-tuple-element.46.refs_0_), channel_id=1, source_target_pairs={{0,16},{8,24},{16,0},{24,8},{1,17},{9,25},{17,1},{25,9},{2,18},{10... | collective-permute-start | bytes 393224 | tf_op jit(solution)/shard_map/ppermute | solution.py:418
  29.6 0.4 collective-permute-start.5
  30.0 3.5 %collective-permute-start.6 = (bf16[128,128]{1,0:T(8,128)(2,1)}, bf16[128,128]{1,0:T(8,128)(2,1)S(1)}, u32[]{:S(2)}, u32[]{:S(2)}) collective-permute-start(bf16[128,128]{1,0:T(8,128)(2,1)} %get-tuple-element.48), channel_id=1, source_target_pairs={{0,7},{1,2},{2,1},{3,4},{4,3},{5,6},{6,5},{7,0},{8,15},{9,10},{10,... | collective-permute-start | bytes 98312 | tf_op jit(solution)/shard_map/ppermute | solution.py:412
  33.5 0.2 collective-permute-done.5.first
  33.7 3.1 %collective-permute-done.6.second = bf16[128,128]{1,0:T(8,128)(2,1)S(1)} collective-permute-done((bf16[128,128]{1,0:T(8,128)(2,1)}, bf16[128,128]{1,0:T(8,128)(2,1)S(1)}, u32[]{:S(2)}, u32[]{:S(2)}) %collective-permute-start.6) | collective-permute-done | bytes 32800 | tf_op jit(solution)/shard_map/ppermute | solution.py:412
  36.8 0.6 collective-permute-start.8
  37.4 0.5 collective-permute-start.7
  37.9 3.2 %collective-permute-done.8.refs_6_ = bf16[128,256]{1,0:T(8,128)(2,1)S(1)} collective-permute-done((bf16[128,256]{1,0:T(8,128)(2,1)S(1)}, bf16[128,256]{1,0:T(8,128)(2,1)S(1)}, u32[]{:S(2)}, u32[]{:S(2)}) %collective-permute-start.8) | collective-permute-done | bytes 65568 | tf_op jit(solution)/shard_map/ppermute | solution.py:418
  41.2 3.6 %shard_map.158 = (bf16[1536,2048]{1,0:T(8,128)(2,1)S(1)}, bf16[128,2048]{1,0:T(8,128)(2,1)S(1)}, bf16[128,2048]{1,0:T(8,128)(2,1)S(1)}) custom-call(s32[1]{0:T(128)} %bitcast.3.core, s32[3,4096]{1,0:T(4,128)S(1)} %copy-done.11, f32[3,4096]{1,0:T(4,128)S(1)} %copy-done.12, bf16[4096,128]{1,0:T(8,128)(2,1)S(1)} %copy-done.5, bf16[4096,128]{1,0:T(8,128)(2,1)S(1)} %copy-done.6, ...), custom_call_target="tpu_custom_call" | custom-call | flops 15728640 | bytes 16000000 | tf_op jit(solution)/shard_map/pallas_call | solution.py:529
  44.8 0.9 copy-done.15
  45.7 0.0 copy-start.7
  45.8 0.0 copy-start.10
  45.8 8.1 %shard_map.159 = (f32[128,512]{1,0:T(8,128)S(1)}, f32[128,256]{1,0:T(8,128)S(1)}, f32[128,512]{1,0:T(8,128)S(1)}, f32[128,256]{1,0:T(8,128)S(1)}, f32[8,512]{1,0:T(8,128)S(1)}) custom-call(bf16[128,512]{1,0:T(8,128)(2,1)S(1)} %copy-done.15, bf16[128,512]{1,0:T(8,128)(2,1)S(1)} %collective-permute-done.2.refs_1_, ...), custom_call_target="tpu_custom_call" | custom-call | flops 3221225472 | bytes 14000000 | tf_op jit(solution)/shard_map/pallas_call | solution.py:546
  53.9 0.6 collective-permute-start.10
  54.4 0.1 collective-permute-start.11
  54.5 1.3 %collective-permute-done.11.got = f32[128,256]{1,0:T(8,128)S(1)} collective-permute-done((f32[128,256]{1,0:T(8,128)S(1)}, f32[128,256]{1,0:T(8,128)S(1)}, u32[]{:S(2)}, u32[]{:S(2)}) %collective-permute-start.11) | collective-permute-done | bytes 131104 | tf_op jit(solution)/shard_map/ppermute | solution.py:418
  55.8 0.1 collective-permute-start.12
  55.9 3.6 %collective-permute-start.13 = (bf16[128,128]{1,0:T(8,128)(2,1)S(1)}, bf16[128,128]{1,0:T(8,128)(2,1)S(1)}, u32[]{:S(2)}, u32[]{:S(2)}) collective-permute-start(bf16[128,128]{1,0:T(8,128)(2,1)S(1)} %get-tuple-element.57), channel_id=1, source_target_pairs={{0,7},{1,2},{2,1},{3,4},{4,3},{5,6},{6,5},{7,0},{8,15},{9,10},{10,... | collective-permute-start | bytes 98312 | tf_op jit(solution)/shard_map/ppermute | solution.py:412
  59.5 0.3 collective-permute-done.12.from_first
  59.8 2.8 %collective-permute-done.13.from_second = bf16[128,128]{1,0:T(8,128)(2,1)S(1)} collective-permute-done((bf16[128,128]{1,0:T(8,128)(2,1)S(1)}, bf16[128,128]{1,0:T(8,128)(2,1)S(1)}, u32[]{:S(2)}, u32[]{:S(2)}) %collective-permute-start.13) | collective-permute-done | bytes 32800 | tf_op jit(solution)/shard_map/ppermute | solution.py:412
  62.7 3.5 %shard_map.161 = (f32[256,1792]{1,0:T(8,128)S(1)}, bf16[64,1792]{1,0:T(8,128)(2,1)S(1)}, bf16[192,1792]{1,0:T(8,128)(2,1)S(1)}) custom-call(f32[128,512]{1,0:T(8,128)S(1)} %get-tuple-element.52.own_mid, f32[128,512]{1,0:T(8,128)S(1)} %collective-permute-done.10.pair_mid, bf16[128,128]{1,0:T(8,128)(2,1)S(1)} %collective-permute-done.12.from_first, ...), custom_call_target="tpu_custom_call" | custom-call | flops 2415919104 | bytes 13976576 | tf_op jit(solution)/shard_map/pallas_call | solution.py:427
  66.1 0.1 collective-permute-start.14
  66.2 0.5 collective-permute-start.15
  66.7 2.0 %collective-permute-done.15.first = bf16[64,1792]{1,0:T(8,128)(2,1)S(1)} collective-permute-done((bf16[64,1792]{1,0:T(8,128)(2,1)S(1)}, bf16[64,1792]{1,0:T(8,128)(2,1)S(1)}, u32[]{:S(2)}, u32[]{:S(2)}) %collective-permute-start.15) | collective-permute-done | bytes 229408 | tf_op jit(solution)/shard_map/ppermute | solution.py:418
  68.7 0.1 shard_map.162
  68.7 0.6 collective-permute-start.16
  69.3 0.1 collective-permute-start.17
  69.5 4.5 %collective-permute-done.16.from_x = bf16[32,1792]{1,0:T(8,128)(2,1)S(1)} collective-permute-done((bf16[32,1792]{1,0:T(8,128)(2,1)S(1)}, bf16[32,1792]{1,0:T(8,128)(2,1)S(1)}, u32[]{:S(2)}, u32[]{:S(2)}) %collective-permute-start.16) | collective-permute-done | bytes 114720 | tf_op jit(solution)/shard_map/ppermute | solution.py:418
  74.0 0.2 collective-permute-done.17.from_y
  74.2 0.2 shard_map.163
  74.4 1.6 %collective-permute-start.18 = (bf16[64,1792]{1,0:T(8,128)(2,1)S(1)}, bf16[64,1792]{1,0:T(8,128)(2,1)S(1)}, u32[]{:S(2)}, u32[]{:S(2)}) collective-permute-start(bf16[64,1792]{1,0:T(8,128)(2,1)S(1)} %get-tuple-element.70), channel_id=1, source_target_pairs={{0,16},{8,24},{16,0},{24,8},{1,17},{9,25},{17,1},{25,9},{2,18},{10... | collective-permute-start | bytes 688136 | tf_op jit(solution)/shard_map/ppermute | solution.py:418
  76.0 0.3 collective-permute-start.19
  76.3 4.8 %collective-permute-done.18.from_x = bf16[64,1792]{1,0:T(8,128)(2,1)S(1)} collective-permute-done((bf16[64,1792]{1,0:T(8,128)(2,1)S(1)}, bf16[64,1792]{1,0:T(8,128)(2,1)S(1)}, u32[]{:S(2)}, u32[]{:S(2)}) %collective-permute-start.18) | collective-permute-done | bytes 229408 | tf_op jit(solution)/shard_map/ppermute | solution.py:418
  81.1 1.1 collective-permute-done.19.from_y
  82.2 0.2 shard_map.164
  82.4 0.1 collective-permute-start.20
  82.4 3.1 %collective-permute-start.21 = (bf16[16,1792]{1,0:T(8,128)(2,1)S(1)}, bf16[16,1792]{1,0:T(8,128)(2,1)S(1)}, u32[]{:S(2)}, u32[]{:S(2)}) collective-permute-start(bf16[16,1792]{1,0:T(8,128)(2,1)S(1)} %get-tuple-element.74), channel_id=1, source_target_pairs={{0,4},{1,5},{2,6},{3,7},{4,0},{5,1},{6,2},{7,3},{8,12},{9,13},{10,... | collective-permute-start | bytes 172040 | tf_op jit(solution)/shard_map/ppermute | solution.py:418
  85.5 1.3 %collective-permute-start.22 = (bf16[16,1792]{1,0:T(8,128)(2,1)S(1)}, bf16[16,1792]{1,0:T(8,128)(2,1)S(1)}, u32[]{:S(2)}, u32[]{:S(2)}) collective-permute-start(bf16[16,1792]{1,0:T(8,128)(2,1)S(1)} %get-tuple-element.75), channel_id=1, source_target_pairs={{0,6},{1,7},{2,4},{3,5},{4,2},{5,3},{6,0},{7,1},{8,14},{9,15},{10,... | collective-permute-start | bytes 172040 | tf_op jit(solution)/shard_map/ppermute | solution.py:418
  86.8 1.5 %collective-permute-done.21.refs_2_ = bf16[16,1792]{1,0:T(8,128)(2,1)S(1)} collective-permute-done((bf16[16,1792]{1,0:T(8,128)(2,1)S(1)}, bf16[16,1792]{1,0:T(8,128)(2,1)S(1)}, u32[]{:S(2)}, u32[]{:S(2)}) %collective-permute-start.21) | collective-permute-done | bytes 57376 | tf_op jit(solution)/shard_map/ppermute | solution.py:418
  88.3 3.8 %collective-permute-done.22.refs_3_ = bf16[16,1792]{1,0:T(8,128)(2,1)S(1)} collective-permute-done((bf16[16,1792]{1,0:T(8,128)(2,1)S(1)}, bf16[16,1792]{1,0:T(8,128)(2,1)S(1)}, u32[]{:S(2)}, u32[]{:S(2)}) %collective-permute-start.22) | collective-permute-done | bytes 57376 | tf_op jit(solution)/shard_map/ppermute | solution.py:418
  92.0 0.1 shard_map.165.refs_0_
  92.1 0.0 collective-permute-start.25
  92.1 2.6 %collective-permute-start.24 = (bf16[16,1792]{1,0:T(8,128)(2,1)S(1)}, bf16[16,1792]{1,0:T(8,128)(2,1)S(1)}, u32[]{:S(2)}, u32[]{:S(2)}) collective-permute-start(bf16[16,1792]{1,0:T(8,128)(2,1)S(1)} %shard_map.165.refs_0_), channel_id=1, source_target_pairs={{0,2},{1,3},{2,0},{3,1},{4,6},{5,7},{6,4},{7,5},{8,10},{9,11},{10,... | collective-permute-start | bytes 172040 | tf_op jit(solution)/shard_map/ppermute | solution.py:418
  94.7 0.9 collective-permute-start.23
  95.6 1.1 collective-permute-start.29
  96.7 3.3 %collective-permute-start.28 = (bf16[16,1792]{1,0:T(8,128)(2,1)S(1)}, bf16[16,1792]{1,0:T(8,128)(2,1)S(1)}, u32[]{:S(2)}, u32[]{:S(2)}) collective-permute-start(bf16[16,1792]{1,0:T(8,128)(2,1)S(1)} %shard_map.165.refs_0_), channel_id=1, source_target_pairs={{0,6},{1,7},{2,4},{3,5},{4,2},{5,3},{6,0},{7,1},{8,14},{9,15},{10,... | collective-permute-start | bytes 172040 | tf_op jit(solution)/shard_map/ppermute | solution.py:418
  100.0 3.2 %collective-permute-start.26 = (bf16[16,1792]{1,0:T(8,128)(2,1)S(1)}, bf16[16,1792]{1,0:T(8,128)(2,1)S(1)}, u32[]{:S(2)}, u32[]{:S(2)}) collective-permute-start(bf16[16,1792]{1,0:T(8,128)(2,1)S(1)} %shard_map.165.refs_0_), channel_id=1, source_target_pairs={{0,4},{1,5},{2,6},{3,7},{4,0},{5,1},{6,2},{7,3},{8,12},{9,13},{10,... | collective-permute-start | bytes 172040 | tf_op jit(solution)/shard_map/ppermute | solution.py:418
  103.3 0.5 collective-permute-start.30
  103.8 2.2 %collective-permute-done.27.refs_1_ = bf16[16,1792]{1,0:T(8,128)(2,1)S(1)} collective-permute-done((bf16[16,1792]{1,0:T(8,128)(2,1)S(1)}, bf16[16,1792]{1,0:T(8,128)(2,1)S(1)}, u32[]{:S(2)}, u32[]{:S(2)}) %collective-permute-start.27) | collective-permute-done | bytes 57376 | tf_op jit(solution)/shard_map/ppermute | solution.py:418
  106.0 0.6 collective-permute-done.26.refs_0_
  106.7 0.1 collective-permute-start.31
  106.8 0.1 collective-permute-start.32
  106.8 0.5 collective-permute-start.33
  107.3 2.1 %collective-permute-done.30.refs_2_ = bf16[64,1792]{1,0:T(8,128)(2,1)S(1)} collective-permute-done((bf16[64,1792]{1,0:T(8,128)(2,1)S(1)}, bf16[64,1792]{1,0:T(8,128)(2,1)S(1)}, u32[]{:S(2)}, u32[]{:S(2)}) %collective-permute-start.30) | collective-permute-done | bytes 229408 | tf_op jit(solution)/shard_map/ppermute | solution.py:418
  109.4 3.4 %collective-permute-done.31.refs_3_ = bf16[64,1792]{1,0:T(8,128)(2,1)S(1)} collective-permute-done((bf16[64,1792]{1,0:T(8,128)(2,1)S(1)}, bf16[64,1792]{1,0:T(8,128)(2,1)S(1)}, u32[]{:S(2)}, u32[]{:S(2)}) %collective-permute-start.31) | collective-permute-done | bytes 229408 | tf_op jit(solution)/shard_map/ppermute | solution.py:418
  112.8 1.5 %collective-permute-done.35.refs_7_ = bf16[64,1792]{1,0:T(8,128)(2,1)S(1)} collective-permute-done((bf16[64,1792]{1,0:T(8,128)(2,1)S(1)}, bf16[64,1792]{1,0:T(8,128)(2,1)S(1)}, u32[]{:S(2)}, u32[]{:S(2)}) %collective-permute-start.35) | collective-permute-done | bytes 229408 | tf_op jit(solution)/shard_map/ppermute | solution.py:418
  114.2 2.0 %shard_map.168 = (f32[512,512]{1,0:T(8,128)}, f32[512,512]{1,0:T(8,128)}, f32[512,512]{1,0:T(8,128)}, f32[512,128]{1,0:T(8,128)}, f32[1,1]{1,0:T(1,128)}) custom-call(bf16[64,1792]{1,0:T(8,128)(2,1)S(1)} %shard_map.166.refs_0_, bf16[64,1792]{1,0:T(8,128)(2,1)S(1)} %shard_map.167.refs_1_, bf16[64,1792]{1,0:T(8,128)(2,1)S(1)} %collective-permute-done.30.refs_2_, ...), custom_call_target="tpu_custom_call" | custom-call | bytes 5505024 | tf_op jit(solution)/shard_map/pallas_call | solution.py:591
  (58 shorter events, 0.2 us)
Async XLA Ops:
  2.9 8.9 %collective-permute-start = (bf16[512,128]{1,0:T(8,128)(2,1)}, bf16[512,128]{1,0:T(8,128)(2,1)S(1)}, u32[]{:S(2)}, u32[]{:S(2)}) collective-permute-start(bf16[512,128]{1,0:T(8,128)(2,1)} %get-tuple-element.44), channel_id=1, source_target_pairs={{0,1},{1,0},{2,3},{3,2},{4,5},{5,4},{6,7},{7,6},{8,9},{9,8},{10,11... | collective-permute-start | bytes 393224 | tf_op jit(solution)/shard_map/ppermute | solution.py:418
  5.9 7.9 %collective-permute-start.1 = (bf16[512,128]{1,0:T(8,128)(2,1)}, bf16[512,128]{1,0:T(8,128)(2,1)S(1)}, u32[]{:S(2)}, u32[]{:S(2)}) collective-permute-start(bf16[512,128]{1,0:T(8,128)(2,1)} %get-tuple-element.45), channel_id=1, source_target_pairs={{0,7},{1,2},{2,1},{3,4},{4,3},{5,6},{6,5},{7,0},{8,15},{9,10},{10,... | collective-permute-start | bytes 393224 | tf_op jit(solution)/shard_map/ppermute | solution.py:412
  11.8 2.0 %copy-start.16 = (bf16[512,128]{1,0:T(8,128)(2,1)}, bf16[512,128]{1,0:T(8,128)(2,1)S(1)}, u32[]{:S(2)}) copy-start(bf16[512,128]{1,0:T(8,128)(2,1)S(1)} %collective-permute-done.from_first) | copy-start | bytes 393220
  13.8 0.7 copy-start.17
  14.4 26.7 %copy-start.2 = (bf16[512,512]{1,0:T(8,128)(2,1)S(1)}, bf16[512,512]{1,0:T(8,128)(2,1)}, u32[]{:S(2)}) copy-start(bf16[512,512]{1,0:T(8,128)(2,1)} %get-tuple-element.43.nodes_t.after) | copy-start | bytes 1572868
  14.4 26.7 %copy-start.5 = (bf16[4096,128]{1,0:T(8,128)(2,1)S(1)}, bf16[4096,128]{1,0:T(8,128)(2,1)}, u32[]{:S(2)}) copy-start(bf16[4096,128]{1,0:T(8,128)(2,1)} %base.1) | copy-start | bytes 3145732
  14.4 26.7 %copy-start.6 = (bf16[4096,128]{1,0:T(8,128)(2,1)S(1)}, bf16[4096,128]{1,0:T(8,128)(2,1)}, u32[]{:S(2)}) copy-start(bf16[4096,128]{1,0:T(8,128)(2,1)} %truth.1) | copy-start | bytes 3145732
  14.4 26.7 %copy-start.11 = (s32[3,4096]{1,0:T(4,128)S(1)}, s32[3,4096]{1,0:T(4,128)}, u32[]{:S(2)}) copy-start(s32[3,4096]{1,0:T(4,128)} %vertices.1) | copy-start | bytes 147460
  14.5 26.7 %copy-start.12 = (f32[3,4096]{1,0:T(4,128)S(1)}, f32[3,4096]{1,0:T(4,128)}, u32[]{:S(2)}) copy-start(f32[3,4096]{1,0:T(4,128)} %weights.1) | copy-start | bytes 147460
  28.0 9.4 %collective-permute-start.3 = (bf16[128,512]{1,0:T(8,128)(2,1)}, bf16[128,512]{1,0:T(8,128)(2,1)S(1)}, u32[]{:S(2)}, u32[]{:S(2)}) collective-permute-start(bf16[128,512]{1,0:T(8,128)(2,1)} %get-tuple-element.46.refs_0_), channel_id=1, source_target_pairs={{0,16},{8,24},{16,0},{24,8},{1,17},{9,25},{17,1},{25,9},{2,18},{10... | collective-permute-start | bytes 393224 | tf_op jit(solution)/shard_map/ppermute | solution.py:418
  29.6 4.1 %collective-permute-start.5 = (bf16[128,128]{1,0:T(8,128)(2,1)}, bf16[128,128]{1,0:T(8,128)(2,1)S(1)}, u32[]{:S(2)}, u32[]{:S(2)}) collective-permute-start(bf16[128,128]{1,0:T(8,128)(2,1)} %get-tuple-element.47), channel_id=1, source_target_pairs={{0,1},{1,0},{2,3},{3,2},{4,5},{5,4},{6,7},{7,6},{8,9},{9,8},{10,11... | collective-permute-start | bytes 98312 | tf_op jit(solution)/shard_map/ppermute | solution.py:418
  30.0 6.8 %collective-permute-start.6 = (bf16[128,128]{1,0:T(8,128)(2,1)}, bf16[128,128]{1,0:T(8,128)(2,1)S(1)}, u32[]{:S(2)}, u32[]{:S(2)}) collective-permute-start(bf16[128,128]{1,0:T(8,128)(2,1)} %get-tuple-element.48), channel_id=1, source_target_pairs={{0,7},{1,2},{2,1},{3,4},{4,3},{5,6},{6,5},{7,0},{8,15},{9,10},{10,... | collective-permute-start | bytes 98312 | tf_op jit(solution)/shard_map/ppermute | solution.py:412
  33.5 11.3 %collective-permute-start.2 = (bf16[128,512]{1,0:T(8,128)(2,1)}, bf16[128,512]{1,0:T(8,128)(2,1)S(1)}, u32[]{:S(2)}, u32[]{:S(2)}) collective-permute-start(bf16[128,512]{1,0:T(8,128)(2,1)} %get-tuple-element.46.refs_0_), channel_id=1, source_target_pairs={{0,8},{8,0},{16,24},{24,16},{1,9},{9,1},{17,25},{25,17},{2,10},{10... | collective-permute-start | bytes 393224 | tf_op jit(solution)/shard_map/ppermute | solution.py:418
  36.8 4.3 %collective-permute-start.8 = (bf16[128,256]{1,0:T(8,128)(2,1)S(1)}, bf16[128,256]{1,0:T(8,128)(2,1)S(1)}, u32[]{:S(2)}, u32[]{:S(2)}) collective-permute-start(bf16[128,256]{1,0:T(8,128)(2,1)S(1)} %shard_map.157.refs_4_), channel_id=1, source_target_pairs={{0,16},{8,24},{16,0},{24,8},{1,17},{9,25},{17,1},{25,9},{2,18},{10... | collective-permute-start | bytes 196616 | tf_op jit(solution)/shard_map/ppermute | solution.py:418
  37.4 7.4 %collective-permute-start.4 = (bf16[128,512]{1,0:T(8,128)(2,1)S(1)}, bf16[128,512]{1,0:T(8,128)(2,1)S(1)}, u32[]{:S(2)}, u32[]{:S(2)}) collective-permute-start(bf16[128,512]{1,0:T(8,128)(2,1)S(1)} %collective-permute-done.3.refs_2_), channel_id=1, source_target_pairs={{0,8},{8,0},{16,24},{24,16},{1,9},{9,1},{17,25},{25,17},{2,10},{10... | collective-permute-start | bytes 393224 | tf_op jit(solution)/shard_map/ppermute | solution.py:418
  37.4 7.3 %collective-permute-start.7 = (bf16[128,256]{1,0:T(8,128)(2,1)S(1)}, bf16[128,256]{1,0:T(8,128)(2,1)S(1)}, u32[]{:S(2)}, u32[]{:S(2)}) collective-permute-start(bf16[128,256]{1,0:T(8,128)(2,1)S(1)} %shard_map.157.refs_4_), channel_id=1, source_target_pairs={{0,8},{8,0},{16,24},{24,16},{1,9},{9,1},{17,25},{25,17},{2,10},{10... | collective-permute-start | bytes 196616 | tf_op jit(solution)/shard_map/ppermute | solution.py:418
  41.2 3.6 %collective-permute-start.9 = (bf16[128,256]{1,0:T(8,128)(2,1)S(1)}, bf16[128,256]{1,0:T(8,128)(2,1)S(1)}, u32[]{:S(2)}, u32[]{:S(2)}) collective-permute-start(bf16[128,256]{1,0:T(8,128)(2,1)S(1)} %collective-permute-done.8.refs_6_), channel_id=1, source_target_pairs={{0,8},{8,0},{16,24},{24,16},{1,9},{9,1},{17,25},{25,17},{2,10},{10... | collective-permute-start | bytes 196616 | tf_op jit(solution)/shard_map/ppermute | solution.py:418
  44.8 0.9 copy-start.15
  45.7 16.9 %copy-start = (bf16[512,3072]{1,0:T(8,128)(2,1)S(1)}, bf16[512,3072]{1,0:T(8,128)(2,1)}, u32[]{:S(2)}) copy-start(bf16[512,3072]{1,0:T(8,128)(2,1)} %get-tuple-element.59.picked_t) | copy-start | bytes 9437188
  45.7 16.9 %copy-start.1 = (bf16[512,3072]{1,0:T(8,128)(2,1)S(1)}, bf16[512,3072]{1,0:T(8,128)(2,1)}, u32[]{:S(2)}) copy-start(bf16[512,3072]{1,0:T(8,128)(2,1)} %get-tuple-element.60.slope_t) | copy-start | bytes 9437188
  45.7 16.9 %copy-start.3 = (f32[512,512]{1,0:T(8,128)S(1)}, f32[512,512]{1,0:T(8,128)}, u32[]{:S(2)}) copy-start(f32[512,512]{1,0:T(8,128)} %get-tuple-element.61.slope_sum_t) | copy-start | bytes 3145732
  45.7 16.9 %copy-start.4 = (f32[512,512]{1,0:T(8,128)S(1)}, f32[512,512]{1,0:T(8,128)}, u32[]{:S(2)}) copy-start(f32[512,512]{1,0:T(8,128)} %get-tuple-element.63.upd_slope_t) | copy-start | bytes 3145732
  45.7 16.9 %copy-start.7 = (bf16[512,512]{1,0:T(8,128)(2,1)S(1)}, bf16[512,512]{1,0:T(8,128)(2,1)}, u32[]{:S(2)}) copy-start(bf16[512,512]{1,0:T(8,128)(2,1)} %vertex.1) | copy-start | bytes 1572868
  45.7 16.9 %copy-start.8 = (bf16[512,512]{1,0:T(8,128)(2,1)S(1)}, bf16[512,512]{1,0:T(8,128)(2,1)}, u32[]{:S(2)}) copy-start(bf16[512,512]{1,0:T(8,128)(2,1)} %get-tuple-element.62.agg_t) | copy-start | bytes 1572868
  45.7 16.9 %copy-start.9 = (bf16[512,512]{1,0:T(8,128)(2,1)S(1)}, bf16[512,512]{1,0:T(8,128)(2,1)}, u32[]{:S(2)}) copy-start(bf16[512,512]{1,0:T(8,128)(2,1)} %get-tuple-element.64.hidden_t) | copy-start | bytes 1572868
  45.8 16.9 %copy-start.10 = (bf16[512,128]{1,0:T(8,128)(2,1)S(1)}, bf16[512,128]{1,0:T(8,128)(2,1)}, u32[]{:S(2)}) copy-start(bf16[512,128]{1,0:T(8,128)(2,1)} %w_decode.1) | copy-start | bytes 393220
  45.8 16.9 %copy-start.13 = (s32[128]{0:T(128)S(1)}, s32[128]{0:T(128)}, u32[]{:S(2)}) copy-start(s32[128]{0:T(128)} %param.14) | copy-start | bytes 1540
  45.8 16.9 %copy-start.14 = (s32[128]{0:T(128)S(1)}, s32[128]{0:T(128)}, u32[]{:S(2)}) copy-start(s32[128]{0:T(128)} %param.15) | copy-start | bytes 1540
  53.9 8.7 %collective-permute-start.10 = (f32[128,512]{1,0:T(8,128)S(1)}, f32[128,512]{1,0:T(8,128)S(1)}, u32[]{:S(2)}, u32[]{:S(2)}) collective-permute-start(f32[128,512]{1,0:T(8,128)S(1)} %get-tuple-element.53), channel_id=1, source_target_pairs={{0,8},{8,0},{16,24},{24,16},{1,9},{9,1},{17,25},{25,17},{2,10},{10... | collective-permute-start | bytes 786440 | tf_op jit(solution)/shard_map/ppermute | solution.py:418
  54.4 1.3 %collective-permute-start.11 = (f32[128,256]{1,0:T(8,128)S(1)}, f32[128,256]{1,0:T(8,128)S(1)}, u32[]{:S(2)}, u32[]{:S(2)}) collective-permute-start(f32[128,256]{1,0:T(8,128)S(1)} %get-tuple-element.55), channel_id=1, source_target_pairs={{0,8},{8,0},{16,24},{24,16},{1,9},{9,1},{17,25},{25,17},{2,10},{10... | collective-permute-start | bytes 393224 | tf_op jit(solution)/shard_map/ppermute | solution.py:418
  55.8 4.0 %collective-permute-start.12 = (bf16[128,128]{1,0:T(8,128)(2,1)S(1)}, bf16[128,128]{1,0:T(8,128)(2,1)S(1)}, u32[]{:S(2)}, u32[]{:S(2)}) collective-permute-start(bf16[128,128]{1,0:T(8,128)(2,1)S(1)} %get-tuple-element.56), channel_id=1, source_target_pairs={{0,1},{1,0},{2,3},{3,2},{4,5},{5,4},{6,7},{7,6},{8,9},{9,8},{10,11... | collective-permute-start | bytes 98312 | tf_op jit(solution)/shard_map/ppermute | solution.py:418
  55.9 6.7 %collective-permute-start.13 = (bf16[128,128]{1,0:T(8,128)(2,1)S(1)}, bf16[128,128]{1,0:T(8,128)(2,1)S(1)}, u32[]{:S(2)}, u32[]{:S(2)}) collective-permute-start(bf16[128,128]{1,0:T(8,128)(2,1)S(1)} %get-tuple-element.57), channel_id=1, source_target_pairs={{0,7},{1,2},{2,1},{3,4},{4,3},{5,6},{6,5},{7,0},{8,15},{9,10},{10,... | collective-permute-start | bytes 98312 | tf_op jit(solution)/shard_map/ppermute | solution.py:412
  66.1 8.1 %collective-permute-start.14 = (bf16[192,1792]{1,0:T(8,128)(2,1)S(1)}, bf16[192,1792]{1,0:T(8,128)(2,1)S(1)}, u32[]{:S(2)}, u32[]{:S(2)}) collective-permute-start(bf16[192,1792]{1,0:T(8,128)(2,1)S(1)} %get-tuple-element.66), channel_id=1, source_target_pairs={{0,8},{8,0},{16,24},{24,16},{1,9},{9,1},{17,25},{25,17},{2,10},{10... | collective-permute-start | bytes 2064392 | tf_op jit(solution)/shard_map/ppermute | solution.py:418
  66.2 2.5 %collective-permute-start.15 = (bf16[64,1792]{1,0:T(8,128)(2,1)S(1)}, bf16[64,1792]{1,0:T(8,128)(2,1)S(1)}, u32[]{:S(2)}, u32[]{:S(2)}) collective-permute-start(bf16[64,1792]{1,0:T(8,128)(2,1)S(1)} %get-tuple-element.67), channel_id=1, source_target_pairs={{0,8},{8,0},{16,24},{24,16},{1,9},{9,1},{17,25},{25,17},{2,10},{10... | collective-permute-start | bytes 688136 | tf_op jit(solution)/shard_map/ppermute | solution.py:418
  68.7 5.3 %collective-permute-start.16 = (bf16[32,1792]{1,0:T(8,128)(2,1)S(1)}, bf16[32,1792]{1,0:T(8,128)(2,1)S(1)}, u32[]{:S(2)}, u32[]{:S(2)}) collective-permute-start(bf16[32,1792]{1,0:T(8,128)(2,1)S(1)} %get-tuple-element.68), channel_id=1, source_target_pairs={{0,16},{8,24},{16,0},{24,8},{1,17},{9,25},{17,1},{25,9},{2,18},{10... | collective-permute-start | bytes 344072 | tf_op jit(solution)/shard_map/ppermute | solution.py:418
  69.3 4.9 %collective-permute-start.17 = (bf16[32,1792]{1,0:T(8,128)(2,1)S(1)}, bf16[32,1792]{1,0:T(8,128)(2,1)S(1)}, u32[]{:S(2)}, u32[]{:S(2)}) collective-permute-start(bf16[32,1792]{1,0:T(8,128)(2,1)S(1)} %get-tuple-element.69), channel_id=1, source_target_pairs={{0,1},{1,0},{2,3},{3,2},{4,5},{5,4},{6,7},{7,6},{8,9},{9,8},{10,11... | collective-permute-start | bytes 344072 | tf_op jit(solution)/shard_map/ppermute | solution.py:418
  74.4 6.6 %collective-permute-start.18 = (bf16[64,1792]{1,0:T(8,128)(2,1)S(1)}, bf16[64,1792]{1,0:T(8,128)(2,1)S(1)}, u32[]{:S(2)}, u32[]{:S(2)}) collective-permute-start(bf16[64,1792]{1,0:T(8,128)(2,1)S(1)} %get-tuple-element.70), channel_id=1, source_target_pairs={{0,16},{8,24},{16,0},{24,8},{1,17},{9,25},{17,1},{25,9},{2,18},{10... | collective-permute-start | bytes 688136 | tf_op jit(solution)/shard_map/ppermute | solution.py:418
  76.0 6.2 %collective-permute-start.19 = (bf16[64,1792]{1,0:T(8,128)(2,1)S(1)}, bf16[64,1792]{1,0:T(8,128)(2,1)S(1)}, u32[]{:S(2)}, u32[]{:S(2)}) collective-permute-start(bf16[64,1792]{1,0:T(8,128)(2,1)S(1)} %get-tuple-element.71), channel_id=1, source_target_pairs={{0,1},{1,0},{2,3},{3,2},{4,5},{5,4},{6,7},{7,6},{8,9},{9,8},{10,11... | collective-permute-start | bytes 688136 | tf_op jit(solution)/shard_map/ppermute | solution.py:418
  82.4 4.5 %collective-permute-start.20 = (bf16[16,1792]{1,0:T(8,128)(2,1)S(1)}, bf16[16,1792]{1,0:T(8,128)(2,1)S(1)}, u32[]{:S(2)}, u32[]{:S(2)}) collective-permute-start(bf16[16,1792]{1,0:T(8,128)(2,1)S(1)} %get-tuple-element.73), channel_id=1, source_target_pairs={{0,2},{1,3},{2,0},{3,1},{4,6},{5,7},{6,4},{7,5},{8,10},{9,11},{10,... | collective-permute-start | bytes 172040 | tf_op jit(solution)/shard_map/ppermute | solution.py:418
  82.4 5.8 %collective-permute-start.21 = (bf16[16,1792]{1,0:T(8,128)(2,1)S(1)}, bf16[16,1792]{1,0:T(8,128)(2,1)S(1)}, u32[]{:S(2)}, u32[]{:S(2)}) collective-permute-start(bf16[16,1792]{1,0:T(8,128)(2,1)S(1)} %get-tuple-element.74), channel_id=1, source_target_pairs={{0,4},{1,5},{2,6},{3,7},{4,0},{5,1},{6,2},{7,3},{8,12},{9,13},{10,... | collective-permute-start | bytes 172040 | tf_op jit(solution)/shard_map/ppermute | solution.py:418
  85.5 6.5 %collective-permute-start.22 = (bf16[16,1792]{1,0:T(8,128)(2,1)S(1)}, bf16[16,1792]{1,0:T(8,128)(2,1)S(1)}, u32[]{:S(2)}, u32[]{:S(2)}) collective-permute-start(bf16[16,1792]{1,0:T(8,128)(2,1)S(1)} %get-tuple-element.75), channel_id=1, source_target_pairs={{0,6},{1,7},{2,4},{3,5},{4,2},{5,3},{6,0},{7,1},{8,14},{9,15},{10,... | collective-permute-start | bytes 172040 | tf_op jit(solution)/shard_map/ppermute | solution.py:418
  92.1 7.9 %collective-permute-start.25 = (bf16[16,1792]{1,0:T(8,128)(2,1)S(1)}, bf16[16,1792]{1,0:T(8,128)(2,1)S(1)}, u32[]{:S(2)}, u32[]{:S(2)}) collective-permute-start(bf16[16,1792]{1,0:T(8,128)(2,1)S(1)} %shard_map.165.refs_0_), channel_id=1, source_target_pairs={{0,3},{1,2},{2,1},{3,0},{4,7},{5,6},{6,5},{7,4},{8,11},{9,10},{10,... | collective-permute-start | bytes 172040 | tf_op jit(solution)/shard_map/ppermute | solution.py:418
  92.1 7.9 %collective-permute-start.24 = (bf16[16,1792]{1,0:T(8,128)(2,1)S(1)}, bf16[16,1792]{1,0:T(8,128)(2,1)S(1)}, u32[]{:S(2)}, u32[]{:S(2)}) collective-permute-start(bf16[16,1792]{1,0:T(8,128)(2,1)S(1)} %shard_map.165.refs_0_), channel_id=1, source_target_pairs={{0,2},{1,3},{2,0},{3,1},{4,6},{5,7},{6,4},{7,5},{8,10},{9,11},{10,... | collective-permute-start | bytes 172040 | tf_op jit(solution)/shard_map/ppermute | solution.py:418
  94.7 8.5 %collective-permute-start.23 = (bf16[16,1792]{1,0:T(8,128)(2,1)S(1)}, bf16[16,1792]{1,0:T(8,128)(2,1)S(1)}, u32[]{:S(2)}, u32[]{:S(2)}) collective-permute-start(bf16[16,1792]{1,0:T(8,128)(2,1)S(1)} %shard_map.165.refs_0_), channel_id=1, source_target_pairs={{0,1},{1,0},{2,3},{3,2},{4,5},{5,4},{6,7},{7,6},{8,9},{9,8},{10,11... | collective-permute-start | bytes 172040 | tf_op jit(solution)/shard_map/ppermute | solution.py:418
  95.6 8.2 %collective-permute-start.29 = (bf16[16,1792]{1,0:T(8,128)(2,1)S(1)}, bf16[16,1792]{1,0:T(8,128)(2,1)S(1)}, u32[]{:S(2)}, u32[]{:S(2)}) collective-permute-start(bf16[16,1792]{1,0:T(8,128)(2,1)S(1)} %shard_map.165.refs_0_), channel_id=1, source_target_pairs={{0,7},{1,6},{2,5},{3,4},{4,3},{5,2},{6,1},{7,0},{8,15},{9,14},{10,... | collective-permute-start | bytes 172040 | tf_op jit(solution)/shard_map/ppermute | solution.py:418
  96.7 7.1 %collective-permute-start.28 = (bf16[16,1792]{1,0:T(8,128)(2,1)S(1)}, bf16[16,1792]{1,0:T(8,128)(2,1)S(1)}, u32[]{:S(2)}, u32[]{:S(2)}) collective-permute-start(bf16[16,1792]{1,0:T(8,128)(2,1)S(1)} %shard_map.165.refs_0_), channel_id=1, source_target_pairs={{0,6},{1,7},{2,4},{3,5},{4,2},{5,3},{6,0},{7,1},{8,14},{9,15},{10,... | collective-permute-start | bytes 172040 | tf_op jit(solution)/shard_map/ppermute | solution.py:418
  100.0 6.0 %collective-permute-start.27 = (bf16[16,1792]{1,0:T(8,128)(2,1)S(1)}, bf16[16,1792]{1,0:T(8,128)(2,1)S(1)}, u32[]{:S(2)}, u32[]{:S(2)}) collective-permute-start(bf16[16,1792]{1,0:T(8,128)(2,1)S(1)} %shard_map.165.refs_0_), channel_id=1, source_target_pairs={{0,5},{1,4},{2,7},{3,6},{4,1},{5,0},{6,3},{7,2},{8,13},{9,12},{10,... | collective-permute-start | bytes 172040 | tf_op jit(solution)/shard_map/ppermute | solution.py:418
  100.0 6.6 %collective-permute-start.26 = (bf16[16,1792]{1,0:T(8,128)(2,1)S(1)}, bf16[16,1792]{1,0:T(8,128)(2,1)S(1)}, u32[]{:S(2)}, u32[]{:S(2)}) collective-permute-start(bf16[16,1792]{1,0:T(8,128)(2,1)S(1)} %shard_map.165.refs_0_), channel_id=1, source_target_pairs={{0,4},{1,5},{2,6},{3,7},{4,0},{5,1},{6,2},{7,3},{8,12},{9,13},{10,... | collective-permute-start | bytes 172040 | tf_op jit(solution)/shard_map/ppermute | solution.py:418
  103.3 6.1 %collective-permute-start.30 = (bf16[64,1792]{1,0:T(8,128)(2,1)S(1)}, bf16[64,1792]{1,0:T(8,128)(2,1)S(1)}, u32[]{:S(2)}, u32[]{:S(2)}) collective-permute-start(bf16[64,1792]{1,0:T(8,128)(2,1)S(1)} %shard_map.166.refs_0_), channel_id=1, source_target_pairs={{0,16},{8,24},{16,0},{24,8},{1,17},{9,25},{17,1},{25,9},{2,18},{10... | collective-permute-start | bytes 688136 | tf_op jit(solution)/shard_map/ppermute | solution.py:418
  106.7 6.1 %collective-permute-start.31 = (bf16[64,1792]{1,0:T(8,128)(2,1)S(1)}, bf16[64,1792]{1,0:T(8,128)(2,1)S(1)}, u32[]{:S(2)}, u32[]{:S(2)}) collective-permute-start(bf16[64,1792]{1,0:T(8,128)(2,1)S(1)} %shard_map.167.refs_1_), channel_id=1, source_target_pairs={{0,16},{8,24},{16,0},{24,8},{1,17},{9,25},{17,1},{25,9},{2,18},{10... | collective-permute-start | bytes 688136 | tf_op jit(solution)/shard_map/ppermute | solution.py:418
  106.8 6.0 %collective-permute-start.32 = (bf16[64,1792]{1,0:T(8,128)(2,1)S(1)}, bf16[64,1792]{1,0:T(8,128)(2,1)S(1)}, u32[]{:S(2)}, u32[]{:S(2)}) collective-permute-start(bf16[64,1792]{1,0:T(8,128)(2,1)S(1)} %shard_map.166.refs_0_), channel_id=1, source_target_pairs={{0,8},{8,0},{16,24},{24,16},{1,9},{9,1},{17,25},{25,17},{2,10},{10... | collective-permute-start | bytes 688136 | tf_op jit(solution)/shard_map/ppermute | solution.py:418
  106.8 5.9 %collective-permute-start.33 = (bf16[64,1792]{1,0:T(8,128)(2,1)S(1)}, bf16[64,1792]{1,0:T(8,128)(2,1)S(1)}, u32[]{:S(2)}, u32[]{:S(2)}) collective-permute-start(bf16[64,1792]{1,0:T(8,128)(2,1)S(1)} %shard_map.167.refs_1_), channel_id=1, source_target_pairs={{0,8},{8,0},{16,24},{24,16},{1,9},{9,1},{17,25},{25,17},{2,10},{10... | collective-permute-start | bytes 688136 | tf_op jit(solution)/shard_map/ppermute | solution.py:418
  109.4 3.4 %collective-permute-start.34 = (bf16[64,1792]{1,0:T(8,128)(2,1)S(1)}, bf16[64,1792]{1,0:T(8,128)(2,1)S(1)}, u32[]{:S(2)}, u32[]{:S(2)}) collective-permute-start(bf16[64,1792]{1,0:T(8,128)(2,1)S(1)} %collective-permute-done.30.refs_2_), channel_id=1, source_target_pairs={{0,8},{8,0},{16,24},{24,16},{1,9},{9,1},{17,25},{25,17},{2,10},{10... | collective-permute-start | bytes 688136 | tf_op jit(solution)/shard_map/ppermute | solution.py:418
  112.8 1.5 %collective-permute-start.35 = (bf16[64,1792]{1,0:T(8,128)(2,1)S(1)}, bf16[64,1792]{1,0:T(8,128)(2,1)S(1)}, u32[]{:S(2)}, u32[]{:S(2)}) collective-permute-start(bf16[64,1792]{1,0:T(8,128)(2,1)S(1)} %collective-permute-done.31.refs_3_), channel_id=1, source_target_pairs={{0,8},{8,0},{16,24},{24,16},{1,9},{9,1},{17,25},{25,17},{2,10},{10... | collective-permute-start | bytes 688136 | tf_op jit(solution)/shard_map/ppermute | solution.py:418

commit v7 on v6

--- a/solution.py
+++ b/solution.py
@@ -69,8 +69,9 @@
     second_t[...] = dot(table, one_hot(count, second)).astype(BF16)
 
 
-def decoder_kernel(core, vertices, weights, base, truth, after, mat, base_t, truth_t, base_rows, truth_rows, sems):
+def decoder_kernel(core, vertices, weights, base, truth, after, mat, base_t, truth_t, done, base_rows, truth_rows, sems):
     del after
+    done[...] = jnp.zeros_like(done)
     span = base_rows.shape[0]
     half = pl.ds(pl.multiple_of(core[0] * span, span), span)
     copies = [
@@ -117,14 +118,23 @@
 
 
 def forward_kernel(
-    nodes_t, from_first, from_second, senders_in, to_next_in, to_prev_in, w_send_in, w_recv_in, vertex_in, w_decode_in,
-    picked_t, field_t, first_t, second_t, slope_out, slope_sum_out, agg_out, upd_slope_out, hidden_out,
-    pre, senders, to_next, to_prev, w_send, w_recv, vertex, w_decode, recv_t,
-    slope_t, slope_sum_t, agg_t, upd_slope_t, hidden_t, in_sems, out_sems,
+    nodes_in, from_first, from_second, senders_in, w_send_in, w_recv_in, to_next_in, to_prev_in, vertex_in, w_decode_in, after,
+    field_t, first_t, second_t, picked_out, slope_out, slope_sum_out, agg_out, upd_slope_out, hidden_out,
+    ext, senders, w_send, w_recv, to_next, to_prev, vertex, w_decode, picked_t, recv_t,
+    slope_t, slope_sum_t, agg_t, upd_slope_t, hidden_t, pre, in_sems, out_sems,
 ):
+    del after
+    degree, count = senders.shape
+    width, ext_rows = ext.shape
+    halo = from_first.shape[1]
+    swap = lax.rem(lax.axis_index("dom"), 2) * halo
+    column = lambda start: ext.at[:, pl.ds(pl.multiple_of(start, 128), halo)]
     fetch = fetched(
-        (senders_in, to_next_in, to_prev_in, w_send_in, w_recv_in, vertex_in, w_decode_in),
-        (senders, to_next, to_prev, w_send, w_recv, vertex, w_decode),
+        (nodes_in, from_first, from_second, senders_in, w_recv_in, w_send_in, vertex_in, to_next_in, to_prev_in, w_decode_in),
+        (
+            ext.at[:, :count], column(count + halo - swap), column(count + swap),
+            senders, w_recv, w_send, vertex, to_next, to_prev, w_decode,
+        ),
         in_sems,
     )
     stored = []
@@ -134,19 +144,17 @@
         copy.start()
         stored.append(copy)
 
-    degree, count = senders.shape
-    halo = from_first.shape[1]
-    width = nodes_t.shape[0]
-    from_next, from_prev = sides(from_first[...], from_second[...])
-    ext = jnp.concatenate([nodes_t[...], from_prev, from_next], axis=1)
-    for copy in fetch[:5]:
+    for copy in fetch[:6]:
         copy.wait()
+    recv_t[...] = dot(w_recv[...].T, ext[:, :count]) * 0.5
     w_send_t = w_send[...].T * 0.5
-    recv_t[...] = dot(w_recv[...].T, nodes_t[...]) * 0.5
     for k in range(degree):
         here = slice(k * count, (k + 1) * count)
-        picked_t[:, here] = dot(ext, one_hot(count + 2 * halo, senders[k : k + 1, :])).astype(BF16)
+        picked_t[:, here] = dot(ext[...], one_hot(ext_rows, senders[k : k + 1, :])).astype(BF16)
         pre[:, here] = dot(w_send_t, picked_t[:, here])
+    store(picked_t, picked_out)
+    for copy in fetch[6:]:
+        copy.wait()
     for start in range(0, width, TILE):
         rows = slice(start, start + TILE)
         recv = recv_t[rows, :]
@@ -164,14 +172,12 @@
             store(slope_t.at[group, :], slope_out.at[group, :])
     store(slope_sum_t, slope_sum_out)
     store(agg_t, agg_out)
-    for copy in fetch[5:]:
-        copy.wait()
     pre[:, :count] = dot(vertex[...].T * 0.5, agg_t[...])
     for start in range(0, width, TILE):
         rows = slice(start, start + TILE)
         value, slope = bent(pre[rows, :count])
         upd_slope_t[rows, :] = slope * 0.5
-        hidden_t[rows, :] = (nodes_t[rows, :].astype(F32) + value).astype(BF16)
+        hidden_t[rows, :] = (ext[rows, :count].astype(F32) + value).astype(BF16)
     store(upd_slope_t, upd_slope_out)
     store(hidden_t, hidden_out)
     field = dot(w_decode[...].T, hidden_t[...]).astype(BF16)
@@ -187,7 +193,8 @@
     mids, ends = refs[0:4], refs[4:8]
     mat, base_t, truth_t = refs[8:11]
     own_mid, own_end, pair_mid, pair_end, loss = refs[11:16]
-    table, grad, states, slopes = refs[16:20]
+    table, grad = refs[16:18]
+    states, slopes = refs[18:20], refs[20:22]
     step = pl.program_id(0)
     members = len(mids)
     variables, count = own_mid.shape
@@ -202,7 +209,9 @@
                 table[m * variables : (m + 1) * variables, base : base + count] = mids[m][...]
                 table[m * variables : (m + 1) * variables, base + count : base + ext_rows] = ends[m][...]
 
-    states[...] = dot(table[...], mat[...])
+    wide = states[0].shape[1]
+    for i, state in enumerate(states):
+        state[...] = dot(table[...], mat[:, i * wide : (i + 1) * wide])
 
     def bend(diff):
         square = diff * diff + EPS
@@ -210,39 +219,37 @@
         return square * inverse, diff * inverse
 
     alone = EPS**0.5
-    across = states.shape[1]
-    wide = min(256, across)
-    for left in range(0, across, wide):
-        cols = slice(left, left + wide)
+    for i, (state, slope_out) in enumerate(zip(states, slopes)):
+        cols = slice(i * wide, (i + 1) * wide)
         summed = jnp.zeros((8, wide), F32)
         for start in range(0, variables, TILE):
             rows = slice(start, start + TILE)
             ready = base_t[rows, cols].astype(F32)
             truth = truth_t[rows, cols].astype(F32)
             x = [
-                (states[m * variables + start : m * variables + start + TILE, cols] + ready).astype(BF16).astype(F32)
+                (state[m * variables + start : m * variables + start + TILE, :] + ready).astype(BF16).astype(F32)
                 for m in range(members)
             ]
             apart = [alone, alone]
             pull = [0.0, 0.0]
-            for i in range(2):
-                for j in range(i + 1, members):
-                    size, slope = bend(x[i] - x[j])
-                    apart[i] = apart[i] + size
-                    pull[i] = pull[i] + slope
+            for m in range(2):
+                for j in range(m + 1, members):
+                    size, slope = bend(x[m] - x[j])
+                    apart[m] = apart[m] + size
+                    pull[m] = pull[m] + slope
                     if j < 2:
                         apart[j] = apart[j] + size
                         pull[j] = pull[j] - slope
             near = 0.0
-            for i in range(2):
-                size, push = bend(x[i] - truth)
+            for m in range(2):
+                size, push = bend(x[m] - truth)
                 near = near + size
-                slope = push * (1.0 / members / line_span) - pull[i] * (1.0 / (members * (members - 1.0)) / line_span)
-                slopes[i * variables + start : i * variables + start + TILE, cols] = slope.astype(BF16)
+                slope = push * (1.0 / members / line_span) - pull[m] * (1.0 / (members * (members - 1.0)) / line_span)
+                slope_out[m * variables + start : m * variables + start + TILE, :] = slope.astype(BF16)
             term = near * (1.0 / members) - (apart[0] + apart[1]) * (1.0 / (2.0 * members * (members - 1)))
             summed += term[:8] + term[8:]
         loss[:, cols] += summed
-    grad[...] += dot_nt(slopes[...], mat[:ext_rows, :])
+        grad[...] += dot_nt(slope_out[...], mat[:ext_rows, cols])
 
     @pl.when(step == pl.num_programs(0) - 1)
     def _():
@@ -317,65 +324,73 @@
     if len(refs) == 3:
         return
     keep, send_first, send_rest = refs[:3]
-    core, x, z, y = position()
+    core, x, dom = position()
     share = width // 32
 
-    def block(c, xr, yr, k):
-        quarter = 2 * c + lax.bitwise_xor(x, xr)
-        start = (8 * quarter + 2 * lax.bitwise_xor(z, k) + lax.bitwise_xor(y, yr)) * share
+    def block(c, other, k):
+        quarter = 2 * c + (1 - x if other else x)
+        start = (8 * quarter + lax.bitwise_xor(dom, k)) * share
         return whole[pl.ds(pl.multiple_of(start, share), share), :]
 
-    at = 0
-    for xr, yr in ((1, 1), (1, 0), (0, 1), (0, 0)):
-        for k in (1, 2, 3, 0):
-            keep[at : at + share, :] = block(core, xr, yr, k)
-            value = encoded(block(1 - core, xr, yr, k))
-            if at < 4 * share:
-                send_first[at : at + share, :] = value
-            else:
-                send_rest[at - 4 * share : at - 3 * share, :] = value
-            at += share
-
-
-def corner_kernel(keep, first, by_x, by_y):
-    block = 2 * by_x.shape[0]
-    total = encoded(keep[:block, :] + first[...].astype(F32))
-    by_x[...] = total[: block // 2]
-    by_y[...] = total[block // 2 :]
-
-
-def sides_kernel(keep, rest, from_x, from_y, to_x, to_y):
-    block = to_x.shape[0]
-    half = block // 2
-    for rows, source, target in ((slice(half, block), from_y, to_x), (slice(0, half), from_x, to_y)):
-        base = 0 if target is to_x else block
-        total = keep[block + base : 2 * block + base, :] + rest[base : base + block, :].astype(F32)
-        extra = source[...].astype(F32)
-        zeros = jnp.zeros_like(extra)
-        extra = jnp.concatenate([zeros, extra] if rows.start else [extra, zeros], axis=0)
-        target[...] = encoded(total + extra)
-
-
-def shares_kernel(keep, rest, from_x, from_y, *outs):
+    order = [(1, k) for k in (4, 5, 6, 7)]
+    order += [(other, k) for k in (1, 2, 3) for other in (1, 0)]
+    order += [(0, k) for k in (4, 5, 6, 7)] + [(1, 0), (0, 0)]
+    for i, (other, k) in enumerate(order):
+        keep[i * share : (i + 1) * share, :] = block(core, other, k)
+        value = encoded(block(1 - core, other, k))
+        if i < 4:
+            send_first[i * share : (i + 1) * share, :] = value
+        else:
+            send_rest[(i - 4) * share : (i - 3) * share, :] = value
+
+
+def far_kernel(keep, first, out):
+    out[...] = encoded(keep[: out.shape[0], :] + first[...].astype(F32))
+
+
+def pairs_kernel(keep, rest, *outs):
     rows = outs[0].shape[0]
-    block = from_x.shape[0]
-    total = keep[3 * block :, :] + rest[2 * block :, :].astype(F32) + from_x[...].astype(F32) + from_y[...].astype(F32)
     for k, out in enumerate(outs):
-        value = total[k * rows : (k + 1) * rows]
-        out[...] = encoded(value) if out.dtype == BF16 else value
-
-
-def sum_kernel(*refs):
-    total = refs[0][...]
-    for ref in refs[1:-1]:
-        total += ref[...].astype(F32)
-    refs[-1][...] = encoded(total)
+        out[...] = encoded(keep[(k + 2) * rows : (k + 3) * rows, :] + rest[k * rows : (k + 1) * rows, :].astype(F32))
+
+
+def quads_kernel(keep, rest, far, *outs):
+    rows = outs[0].shape[0]
+    for k, out in enumerate(outs):
+        total = keep[(k + 10) * rows : (k + 11) * rows, :] + rest[(k + 6) * rows : (k + 7) * rows, :].astype(F32)
+        out[...] = encoded(total + far[k * rows : (k + 1) * rows, :].astype(F32))
+
+
+def across_kernel(keep, rest, *refs):
+    out = refs[-1]
+    rows = out.shape[0]
+    total = keep[14 * rows : 15 * rows, :] + rest[10 * rows : 11 * rows, :].astype(F32)
+    for ref in refs[:-1]:
+        total += ref[:rows, :].astype(F32)
+    out[...] = encoded(total)
+
+
+def own_kernel(keep, rest, *refs):
+    out = refs[-1]
+    rows = out.shape[0]
+    total = keep[15 * rows :, :] + rest[11 * rows :, :].astype(F32)
+    for ref in refs[:-1]:
+        total += ref[ref.shape[0] - rows :, :].astype(F32)
+    out[...] = encoded(total)
 
 
 def join_kernel(*refs):
-    rows = refs[0].shape[0]
-    for k, ref in enumerate(refs[:-1]):
-        refs[-1][k * rows : (k + 1) * rows, :] = ref[...]
+    start = 0
+    for ref in refs[:-1]:
+        refs[-1][start : start + ref.shape[0], :] = ref[...]
+        start += ref.shape[0]
+
+
+def pair_kernel(mine, other, after, out):
+    del after
+    rows = mine.shape[0]
+    out[:rows, :] = mine[...]
+    out[rows:, :] = other[...]
 
 
 def finish_kernel(scale, *refs):
@@ -383,12 +398,16 @@
     pieces = refs[:-5]
     width = g_send.shape[1]
     share = width // 32
-    core, x, z, y = position()
+    core, x, dom = position()
     total = jnp.zeros((share, LANES), F32)
     for i, piece in enumerate(pieces):
-        quarter = 2 * (core if i < 4 else 1 - core) + (x if i % 4 < 2 else 1 - x)
         for j in range(piece.shape[0] // share):
-            start = (8 * quarter + lax.bitwise_xor(2 * z + y, 4 * (i % 2) + j)) * share
+            if i % 3 == 0:
+                other, k = j % 2, j // 2
+            else:
+                other, k = i % 3 - 1, 4 + j
+            quarter = 2 * (core if i < 3 else 1 - core) + (1 - x if other else x)
+            start = (8 * quarter + lax.bitwise_xor(dom, k)) * share
             place = pl.ds(pl.multiple_of(start, share), share)
             value = piece[j * share : (j + 1) * share, :].astype(F32)
             g_send[place, :] = value[:, :width]
@@ -400,8 +419,8 @@
 
 
 def position():
-    ens, dom = lax.axis_index("ens"), lax.axis_index("dom")
-    return lax.rem(ens, 2), lax.div(ens, 2), lax.div(dom, 2), lax.rem(dom, 2)
+    ens = lax.axis_index("ens")
+    return lax.rem(ens, 2), lax.div(ens, 2), lax.axis_index("dom")
 
 
 SCALAR = pl.BlockSpec(memory_space=pltpu.SMEM)
@@ -449,23 +468,27 @@
 
 
 def summed(keep, send_first, send_rest):
-    block, cols = send_first.shape
-    half, share = block // 2, block // 4
+    cols = keep.shape[1]
+    share = keep.shape[0] // 16
     core = lambda v: flip(v, "ens", 1)
     over_x = lambda v: flip(v, "ens", 2)
-    over_y = lambda v: flip(v, "dom", 1)
-    piece = lambda rows: sds((rows, cols), BF16)
+    piece = lambda shares: sds((shares * share, cols), BF16)
+    near, far = (1, 2, 3), (4, 5, 6, 7)
     first, rest = core(send_first), core(send_rest)
-    by_x, by_y = call(corner_kernel, [keep, first], [piece(half)] * 2)
-    by_x, by_y = over_x(by_x), over_y(by_y)
-    to_x, to_y = call(sides_kernel, [keep, rest, by_x, by_y], [piece(block)] * 2)
-    to_x, to_y = over_x(to_x), over_y(to_y)
-    shares = call(shares_kernel, [keep, rest, to_x, to_y], [piece(share)] * 3 + [sds((share, cols), F32)])
-    terms = [shares[3]] + [flip(shares[k - 1], "dom", 2 * k) for k in (1, 2, 3)]
-    (own,) = call(sum_kernel, terms, [piece(share)])
-    pieces = [own] + [flip(own, "dom", k) for k in range(1, 8)]
-    here = [call(join_kernel, pieces[i : i + 4], [piece(block)])[0] for i in (0, 4)]
-    here += [over_x(v) for v in here]
+    (out,) = call(far_kernel, [keep, first], [piece(4)])
+    from_x = over_x(out)
+    outs = call(pairs_kernel, [keep, rest], [piece(2)] * 3)
+    pairs = [flip(v, "dom", k) for k, v in zip(near, outs)]
+    outs = call(quads_kernel, [keep, rest, from_x], [piece(1)] * 4)
+    quads = [flip(v, "dom", k) for k, v in zip(far, outs)]
+    (out,) = call(across_kernel, [keep, rest] + pairs, [piece(1)])
+    got = over_x(out)
+    (own,) = call(own_kernel, [keep, rest] + pairs + quads + [got], [piece(1)])
+
+    (far_own,) = call(join_kernel, [flip(own, "dom", k) for k in far], [piece(4)])
+    (pair,) = call(pair_kernel, [own, over_x(own), far_own], [piece(2)])
+    (close,) = call(join_kernel, [pair] + [flip(pair, "dom", k) for k in near], [piece(8)])
+    here = [close, far_own, over_x(far_own)]
     return here + [core(v) for v in here]
 
 
@@ -498,47 +521,47 @@
     from_first, from_second = meet(first_t, second_t)
 
     core = scalar(lax.rem(ens, 2))
-    picked_t, field_t, first_t, second_t, slope_t, slope_sum_t, agg_t, upd_slope_t, hidden_t = call(
-        forward_kernel,
-        [nodes_t, from_first, from_second, senders, to_next, to_prev, w_send, w_recv, vertex_refresh_matrix, w_decode],
-        [
-            sds((width, degree * count), BF16), sds((variables, count), BF16), sds((variables, halo), BF16),
-            sds((variables, halo), BF16), sds((width, degree * count), BF16), sds((width, count), F32),
-            sds((width, count), BF16), sds((width, count), F32), sds((width, count), BF16),
-        ],
-        [held((width, degree * count), F32), held((degree, count), jnp.int32)] + indices() + [
-            held((width, width)), held((width, width)), held((width, width)), held((width, variables)),
-            held((width, count), F32), held((width, degree * count)), held((width, count), F32),
-            held((width, count)), held((width, count), F32), held((width, count)),
-            pltpu.SemaphoreType.DMA((7,)), pltpu.SemaphoreType.DMA((width // 128 + 4,)),
-        ],
-        flops=2 * degree * width * count * (ext_rows + width),
-        in_hbm=7,
-        out_hbm=5,
-        limit=56,
-    )
-    lent = meet(first_t, second_t)
-    mids = gathered(field_t)
-
     block = 512
     steps = line_span // 2 // block
     fixed = lambda shape: pl.BlockSpec(shape, lambda i, *at: (0,) * len(shape))
     tall = lambda rows: pl.BlockSpec((rows, block), lambda i, *at: (0, i))
     tall_half = lambda rows: pl.BlockSpec((rows, block), lambda i, at: (0, i + at[0] * steps))
     half_span = line_span // 2
-    mat, base_t, truth_t = pl.pallas_call(
+    mat, base_t, truth_t, done = pl.pallas_call(
         decoder_kernel,
         grid_spec=pltpu.PrefetchScalarGridSpec(
             num_scalar_prefetch=1,
             grid=(steps,),
             in_specs=[tall_half(fan), tall_half(fan), HBM, HBM, pl.BlockSpec(memory_space=pl.ANY)],
-            out_specs=[tall(2 * ext_rows), fixed((variables, half_span)), fixed((variables, half_span))],
+            out_specs=[tall(2 * ext_rows), fixed((variables, half_span)), fixed((variables, half_span)), fixed((8, 128))],
             scratch_shapes=[held((half_span, variables)), held((half_span, variables)), pltpu.SemaphoreType.DMA((2,))],
         ),
-        out_shape=[sds((2 * ext_rows, half_span), BF16)] + [sds((variables, half_span), BF16)] * 2,
-        compiler_params=params(12),
+        out_shape=[sds((2 * ext_rows, half_span), BF16)] + [sds((variables, half_span), BF16)] * 2 + [sds((8, 128), F32)],
+        compiler_params=params(56),
         cost_estimate=cost(10 * ext_rows * half_span, 16e6),
     )(core, readout_vertex_list, dec_weights, base, observed_analysis, nodes_t)
+
+    field_t, first_t, second_t, picked_t, slope_t, slope_sum_t, agg_t, upd_slope_t, hidden_t = call(
+        forward_kernel,
+        [nodes_t, from_first, from_second, senders, w_send, w_recv, to_next, to_prev, vertex_refresh_matrix, w_decode, done],
+        [
+            sds((variables, count), BF16), sds((variables, halo), BF16), sds((variables, halo), BF16),
+            sds((width, degree * count), BF16), sds((width, degree * count), BF16), sds((width, count), F32),
+            sds((width, count), BF16), sds((width, count), F32), sds((width, count), BF16),
+        ],
+        [held((width, ext_rows)), held((degree, count), jnp.int32), held((width, width)), held((width, width))] + indices() + [
+            held((width, width)), held((width, variables)), held((width, degree * count)), held((width, count), F32),
+            held((width, degree * count)), held((width, count), F32), held((width, count)), held((width, count), F32),
+            held((width, count)), held((width, degree * count), F32),
+            pltpu.SemaphoreType.DMA((10,)), pltpu.SemaphoreType.DMA((width // 128 + 5,)),
+        ],
+        flops=2 * degree * width * count * (ext_rows + width),
+        in_hbm=11,
+        out_hbm=6,
+        limit=56,
+    )
+    lent = meet(first_t, second_t)
+    mids = gathered(field_t)
 
     (end,) = call(borrowed_kernel, list(lent), [sds((variables, 2 * halo), BF16)])
     ends = gathered(end)
@@ -553,7 +576,8 @@
         out_specs=[fixed((variables, count)), fixed((variables, 2 * halo))] * 2 + [fixed((8, block))],
         scratch_shapes=[
             pltpu.VMEM((members * variables, 2 * ext_rows), BF16), pltpu.VMEM((2 * variables, ext_rows), F32),
-            pltpu.VMEM((members * variables, block), F32), pltpu.VMEM((2 * variables, block), BF16),
+            *[pltpu.VMEM((members * variables, 256), F32)] * (block // 256),
+            *[pltpu.VMEM((2 * variables, 256), BF16)] * (block // 256),
         ],
         compiler_params=params(20),
         cost_estimate=cost(4 * members * variables * ext_rows * half_span, 14e6),

time: 117 us -> 113 us (0.966)
  waiting for transfers between devices: 42.8 us -> 33.7 us
  starting transfers between devices: 37.5 us -> 40.9 us
  Pallas kernels: 33.4 us -> 35.1 us
    ppermute x33 -> x34, waiting for transfers between devices: 34.9 us -> 28.1 us  [flip(): return lax.ppermute(value, axis, [(i, i ^ bit) for i in range(size)])]
    ppermute x33 -> x34, starting transfers between devices: 26.8 us -> 32.6 us  [flip(): return lax.ppermute(value, axis, [(i, i ^ bit) for i in range(size)])]
    ppermute x3, starting transfers between devices: 10.7 us -> 8.28 us  [meet(): lax.ppermute(second, 'dom', [(i, (i + (1 if i % 2 else size - 1)) % size)...]
    ppermute x3, waiting for transfers between devices: 7.89 us -> 5.62 us  [meet(): lax.ppermute(second, 'dom', [(i, (i + (1 if i % 2 else size - 1)) % size)...]
    pallas_call x1, Pallas kernels: 3.56 us -> 5.79 us  [per_device(): pl.pallas_call(decoder_kernel, grid_spec=pltpu.PrefetchScalarGridSpec(num...]
    pallas_call x11 -> x13, Pallas kernels: 19.8 us -> 19.4 us  [call(): pl.pallas_call(kernel, out_shape=outs, in_specs=vmem(len(ins) - in_hbm) +...]
  transfers between devices with their start and end apart: 36 -> 37, of which waited for: 20 -> 21; matrix products, arithmetic and copies ran while one was open for 0% -> 0% of each run, Pallas kernels for 3% -> 6%
where the time goes in v7:
time: 113 us; the launch traced here: 112 us
  starting transfers between devices  40.9 us (36%)
  Pallas kernels  35.1 us (31%)
  waiting for transfers between devices  33.7 us (30%)
  local copies, waits for them, and re-layouts  1.63 us (1%)
    ppermute x34, starting transfers between devices, flip(): return lax.ppermute(value, axis, [(i, i ^ bit) for i in range(size)])  32.6 us
    ppermute x34, waiting for transfers between devices, flip(): return lax.ppermute(value, axis, [(i, i ^ bit) for i in range(size)])  28.1 us
    pallas_call x13, Pallas kernels, call(): pl.pallas_call(kernel, out_shape=outs, in_specs=vmem(len(ins) - in_hbm) +...  19.4 us
    ppermute x3, starting transfers between devices, meet(): lax.ppermute(second, 'dom', [(i, (i + (1 if i % 2 else size - 1)) % size)...  8.28 us
    pallas_call x1, Pallas kernels, per_device(): pl.pallas_call(functools.partial(readout_kernel, line_span), grid=(steps,...  8 us
    pallas_call x1, Pallas kernels, per_device(): pl.pallas_call(decoder_kernel, grid_spec=pltpu.PrefetchScalarGridSpec(num...  5.79 us
    ppermute x3, waiting for transfers between devices, meet(): lax.ppermute(second, 'dom', [(i, (i + (1 if i % 2 else size - 1)) % size)...  5.62 us
  transfers between devices with their start and end apart: 37, of which 21 were waited for; matrix products, arithmetic and copies ran while one was open for 0% of the time, Pallas kernels for 6%

profile of v7, /device:TPU:0, one launch (start us, length us, event | category | flops | bytes accessed | tf_op | source)
XLA Modules:
  0.0 112.5 jit_solution(16708430555518073360)
XLA Ops:
  0.6 2.2 %shard_map.155 = (bf16[512,512]{1,0:T(8,128)(2,1)}, bf16[512,128]{1,0:T(8,128)(2,1)}, bf16[512,128]{1,0:T(8,128)(2,1)}) custom-call(bf16[512,512]{1,0:T(8,128)(2,1)} %bitcast.11, s32[1,128]{1,0:T(1,128)} %bitcast.5, s32[1,128]{1,0:T(1,128)} %bitcast.8), custom_call_target="tpu_custom_call" | custom-call | flops 134217728 | bytes 1311744 | tf_op jit(solution)/shard_map/pallas_call | solution.py:446
  2.9 3.0 %collective-permute-start = (bf16[512,128]{1,0:T(8,128)(2,1)}, bf16[512,128]{1,0:T(8,128)(2,1)S(1)}, u32[]{:S(2)}, u32[]{:S(2)}) collective-permute-start(bf16[512,128]{1,0:T(8,128)(2,1)} %get-tuple-element.44), channel_id=1, source_target_pairs={{0,1},{1,0},{2,3},{3,2},{4,5},{5,4},{6,7},{7,6},{8,9},{9,8},{10,11... | collective-permute-start | bytes 393224 | tf_op jit(solution)/shard_map/ppermute | solution.py:437
  5.9 3.5 %collective-permute-start.1 = (bf16[512,128]{1,0:T(8,128)(2,1)}, bf16[512,128]{1,0:T(8,128)(2,1)S(1)}, u32[]{:S(2)}, u32[]{:S(2)}) collective-permute-start(bf16[512,128]{1,0:T(8,128)(2,1)} %get-tuple-element.45), channel_id=1, source_target_pairs={{0,7},{1,2},{2,1},{3,4},{4,3},{5,6},{6,5},{7,0},{8,15},{9,10},{10,... | collective-permute-start | bytes 393224 | tf_op jit(solution)/shard_map/ppermute | solution.py:431
  9.5 5.8 %shard_map.156 = (bf16[1536,2048]{1,0:T(8,128)(2,1)}, bf16[128,2048]{1,0:T(8,128)(2,1)}, bf16[128,2048]{1,0:T(8,128)(2,1)}, f32[8,128]{1,0:T(8,128)}) custom-call(s32[1]{0:T(128)} %bitcast.3.core, s32[3,4096]{1,0:T(4,128)} %vertices.1, f32[3,4096]{1,0:T(4,128)} %weights.1, bf16[4096,128]{1,0:T(8,128)(2,1)} %base.1, bf16[4096,128]{1,0:T(8,128)(2,1)} %truth.1, ...), custom_call_target="tpu_custom_call" | custom-call | flops 15728640 | bytes 16000000 | tf_op jit(solution)/shard_map/pallas_call | solution.py:530
  15.3 0.6 copy-done.15
  16.0 13.1 %shard_map.157 = (bf16[128,512]{1,0:T(8,128)(2,1)}, bf16[128,128]{1,0:T(8,128)(2,1)}, bf16[128,128]{1,0:T(8,128)(2,1)}, bf16[512,3072]{1,0:T(8,128)(2,1)}, bf16[...) custom-call(bf16[512,512]{1,0:T(8,128)(2,1)} %get-tuple-element.43.a, ...), custom_call_target="tpu_custom_call" | custom-call | flops 4026531840 | bytes 12141568 | tf_op jit(solution)/shard_map/pallas_call | solution.py:446
  29.1 1.5 %collective-permute-start.3 = (bf16[128,512]{1,0:T(8,128)(2,1)}, bf16[128,512]{1,0:T(8,128)(2,1)S(1)}, u32[]{:S(2)}, u32[]{:S(2)}) collective-permute-start(bf16[128,512]{1,0:T(8,128)(2,1)} %get-tuple-element.47.refs_0_), channel_id=1, source_target_pairs={{0,16},{8,24},{16,0},{24,8},{1,17},{9,25},{17,1},{25,9},{2,18},{10... | collective-permute-start | bytes 393224 | tf_op jit(solution)/shard_map/ppermute | solution.py:437
  30.6 2.4 %collective-permute-start.6 = (bf16[128,128]{1,0:T(8,128)(2,1)}, bf16[128,128]{1,0:T(8,128)(2,1)S(1)}, u32[]{:S(2)}, u32[]{:S(2)}) collective-permute-start(bf16[128,128]{1,0:T(8,128)(2,1)} %get-tuple-element.49), channel_id=1, source_target_pairs={{0,7},{1,2},{2,1},{3,4},{4,3},{5,6},{6,5},{7,0},{8,15},{9,10},{10,... | collective-permute-start | bytes 98312 | tf_op jit(solution)/shard_map/ppermute | solution.py:431
  33.0 1.7 %collective-permute-done.5.first = bf16[128,128]{1,0:T(8,128)(2,1)S(1)} collective-permute-done((bf16[128,128]{1,0:T(8,128)(2,1)}, bf16[128,128]{1,0:T(8,128)(2,1)S(1)}, u32[]{:S(2)}, u32[]{:S(2)}) %collective-permute-start.5) | collective-permute-done | bytes 32800 | tf_op jit(solution)/shard_map/ppermute | solution.py:437
  34.7 2.7 %collective-permute-done.6.second = bf16[128,128]{1,0:T(8,128)(2,1)S(1)} collective-permute-done((bf16[128,128]{1,0:T(8,128)(2,1)}, bf16[128,128]{1,0:T(8,128)(2,1)S(1)}, u32[]{:S(2)}, u32[]{:S(2)}) %collective-permute-start.6) | collective-permute-done | bytes 32800 | tf_op jit(solution)/shard_map/ppermute | solution.py:431
  37.4 0.6 collective-permute-start.8
  38.1 0.5 collective-permute-start.7
  38.6 3.2 %collective-permute-done.8.refs_6_ = bf16[128,256]{1,0:T(8,128)(2,1)S(1)} collective-permute-done((bf16[128,256]{1,0:T(8,128)(2,1)S(1)}, bf16[128,256]{1,0:T(8,128)(2,1)S(1)}, u32[]{:S(2)}, u32[]{:S(2)}) %collective-permute-start.8) | collective-permute-done | bytes 65568 | tf_op jit(solution)/shard_map/ppermute | solution.py:437
  41.8 1.2 %collective-permute-done.9.refs_7_ = bf16[128,256]{1,0:T(8,128)(2,1)S(1)} collective-permute-done((bf16[128,256]{1,0:T(8,128)(2,1)S(1)}, bf16[128,256]{1,0:T(8,128)(2,1)S(1)}, u32[]{:S(2)}, u32[]{:S(2)}) %collective-permute-start.9) | collective-permute-done | bytes 65568 | tf_op jit(solution)/shard_map/ppermute | solution.py:437
  43.1 0.9 copy-done.14
  44.0 8.0 %shard_map.159 = (f32[128,512]{1,0:T(8,128)S(1)}, f32[128,256]{1,0:T(8,128)S(1)}, f32[128,512]{1,0:T(8,128)S(1)}, f32[128,256]{1,0:T(8,128)S(1)}, f32[8,512]{1,0:T(8,128)S(1)}) custom-call(bf16[128,512]{1,0:T(8,128)(2,1)S(1)} %copy-done.14, bf16[128,512]{1,0:T(8,128)(2,1)S(1)} %collective-permute-done.2.refs_1_, ...), custom_call_target="tpu_custom_call" | custom-call | flops 3221225472 | bytes 14000000 | tf_op jit(solution)/shard_map/pallas_call | solution.py:569
  52.1 0.2 collective-permute-start.10
  52.3 0.4 collective-permute-start.11
  52.6 1.2 %collective-permute-done.11.got = f32[128,256]{1,0:T(8,128)S(1)} collective-permute-done((f32[128,256]{1,0:T(8,128)S(1)}, f32[128,256]{1,0:T(8,128)S(1)}, u32[]{:S(2)}, u32[]{:S(2)}) %collective-permute-start.11) | collective-permute-done | bytes 131104 | tf_op jit(solution)/shard_map/ppermute | solution.py:437
  53.9 0.3 collective-permute-start.12
  54.2 2.3 %collective-permute-start.13 = (bf16[128,128]{1,0:T(8,128)(2,1)S(1)}, bf16[128,128]{1,0:T(8,128)(2,1)S(1)}, u32[]{:S(2)}, u32[]{:S(2)}) collective-permute-start(bf16[128,128]{1,0:T(8,128)(2,1)S(1)} %get-tuple-element.58), channel_id=1, source_target_pairs={{0,7},{1,2},{2,1},{3,4},{4,3},{5,6},{6,5},{7,0},{8,15},{9,10},{10,... | collective-permute-start | bytes 98312 | tf_op jit(solution)/shard_map/ppermute | solution.py:431
  56.5 1.4 %collective-permute-done.12.from_first = bf16[128,128]{1,0:T(8,128)(2,1)S(1)} collective-permute-done((bf16[128,128]{1,0:T(8,128)(2,1)S(1)}, bf16[128,128]{1,0:T(8,128)(2,1)S(1)}, u32[]{:S(2)}, u32[]{:S(2)}) %collective-permute-start.12) | collective-permute-done | bytes 32800 | tf_op jit(solution)/shard_map/ppermute | solution.py:437
  57.8 2.9 %collective-permute-done.13.from_second = bf16[128,128]{1,0:T(8,128)(2,1)S(1)} collective-permute-done((bf16[128,128]{1,0:T(8,128)(2,1)S(1)}, bf16[128,128]{1,0:T(8,128)(2,1)S(1)}, u32[]{:S(2)}, u32[]{:S(2)}) %collective-permute-start.13) | collective-permute-done | bytes 32800 | tf_op jit(solution)/shard_map/ppermute | solution.py:431
  60.9 3.5 %shard_map.161 = (f32[256,1792]{1,0:T(8,128)S(1)}, bf16[64,1792]{1,0:T(8,128)(2,1)S(1)}, bf16[192,1792]{1,0:T(8,128)(2,1)S(1)}) custom-call(f32[128,512]{1,0:T(8,128)S(1)} %get-tuple-element.53.own_mid, f32[128,512]{1,0:T(8,128)S(1)} %collective-permute-done.10.pair_mid, bf16[128,128]{1,0:T(8,128)(2,1)S(1)} %collective-permute-done.12.from_first, ...), custom_call_target="tpu_custom_call" | custom-call | flops 2415919104 | bytes 13976576 | tf_op jit(solution)/shard_map/pallas_call | solution.py:446
  64.3 0.1 collective-permute-start.14
  64.4 0.5 collective-permute-start.18
  64.9 2.0 %collective-permute-done.18.first = bf16[64,1792]{1,0:T(8,128)(2,1)S(1)} collective-permute-done((bf16[64,1792]{1,0:T(8,128)(2,1)S(1)}, bf16[64,1792]{1,0:T(8,128)(2,1)S(1)}, u32[]{:S(2)}, u32[]{:S(2)}) %collective-permute-start.18) | collective-permute-done | bytes 229408 | tf_op jit(solution)/shard_map/ppermute | solution.py:437
  66.9 0.1 shard_map.163
  67.0 0.6 collective-permute-start.19
  67.6 0.1 shard_map.162
  67.7 0.1 collective-permute-start.15
  67.9 3.4 %collective-permute-start.17 = (bf16[32,1792]{1,0:T(8,128)(2,1)S(1)}, bf16[32,1792]{1,0:T(8,128)(2,1)S(1)}, u32[]{:S(2)}, u32[]{:S(2)}) collective-permute-start(bf16[32,1792]{1,0:T(8,128)(2,1)S(1)} %get-tuple-element.70), channel_id=1, source_target_pairs={{0,3},{1,2},{2,1},{3,0},{4,7},{5,6},{6,5},{7,4},{8,11},{9,10},{10,... | collective-permute-start | bytes 344072 | tf_op jit(solution)/shard_map/ppermute | solution.py:437
  71.3 3.4 %collective-permute-done.19.far = bf16[64,1792]{1,0:T(8,128)(2,1)S(1)} collective-permute-done((bf16[64,1792]{1,0:T(8,128)(2,1)S(1)}, bf16[64,1792]{1,0:T(8,128)(2,1)S(1)}, u32[]{:S(2)}, u32[]{:S(2)}) %collective-permute-start.19) | collective-permute-done | bytes 229408 | tf_op jit(solution)/shard_map/ppermute | solution.py:437
  74.7 0.1 shard_map.164
  74.9 2.4 %collective-permute-start.21 = (bf16[16,1792]{1,0:T(8,128)(2,1)S(1)}, bf16[16,1792]{1,0:T(8,128)(2,1)S(1)}, u32[]{:S(2)}, u32[]{:S(2)}) collective-permute-start(bf16[16,1792]{1,0:T(8,128)(2,1)S(1)} %get-tuple-element.73), channel_id=1, source_target_pairs={{0,5},{1,4},{2,7},{3,6},{4,1},{5,0},{6,3},{7,2},{8,13},{9,12},{10,... | collective-permute-start | bytes 172040 | tf_op jit(solution)/shard_map/ppermute | solution.py:437
  77.2 2.9 %collective-permute-start.22 = (bf16[16,1792]{1,0:T(8,128)(2,1)S(1)}, bf16[16,1792]{1,0:T(8,128)(2,1)S(1)}, u32[]{:S(2)}, u32[]{:S(2)}) collective-permute-start(bf16[16,1792]{1,0:T(8,128)(2,1)S(1)} %get-tuple-element.74), channel_id=1, source_target_pairs={{0,6},{1,7},{2,4},{3,5},{4,2},{5,3},{6,0},{7,1},{8,14},{9,15},{10,... | collective-permute-start | bytes 172040 | tf_op jit(solution)/shard_map/ppermute | solution.py:437
  80.1 2.4 %collective-permute-start.23 = (bf16[16,1792]{1,0:T(8,128)(2,1)S(1)}, bf16[16,1792]{1,0:T(8,128)(2,1)S(1)}, u32[]{:S(2)}, u32[]{:S(2)}) collective-permute-start(bf16[16,1792]{1,0:T(8,128)(2,1)S(1)} %get-tuple-element.75), channel_id=1, source_target_pairs={{0,7},{1,6},{2,5},{3,4},{4,3},{5,2},{6,1},{7,0},{8,15},{9,14},{10,... | collective-permute-start | bytes 172040 | tf_op jit(solution)/shard_map/ppermute | solution.py:437
  82.5 0.1 shard_map.165
  82.6 0.6 collective-permute-start.24
  83.2 0.5 collective-permute-done.21.refs_4_
  83.7 0.1 collective-permute-done.22.refs_5_
  83.8 3.3 %collective-permute-done.23.refs_6_ = bf16[16,1792]{1,0:T(8,128)(2,1)S(1)} collective-permute-done((bf16[16,1792]{1,0:T(8,128)(2,1)S(1)}, bf16[16,1792]{1,0:T(8,128)(2,1)S(1)}, u32[]{:S(2)}, u32[]{:S(2)}) %collective-permute-start.23) | collective-permute-done | bytes 57376 | tf_op jit(solution)/shard_map/ppermute | solution.py:437
  87.1 0.1 shard_map.166.mine
  87.2 2.5 %collective-permute-start.29 = (bf16[16,1792]{1,0:T(8,128)(2,1)S(1)}, bf16[16,1792]{1,0:T(8,128)(2,1)S(1)}, u32[]{:S(2)}, u32[]{:S(2)}) collective-permute-start(bf16[16,1792]{1,0:T(8,128)(2,1)S(1)} %shard_map.166.mine), channel_id=1, source_target_pairs={{0,7},{1,6},{2,5},{3,4},{4,3},{5,2},{6,1},{7,0},{8,15},{9,14},{10,... | collective-permute-start | bytes 172040 | tf_op jit(solution)/shard_map/ppermute | solution.py:437
  89.7 1.0 collective-permute-start.28
  90.6 0.7 collective-permute-start.27
  91.4 3.5 %collective-permute-start.26 = (bf16[16,1792]{1,0:T(8,128)(2,1)S(1)}, bf16[16,1792]{1,0:T(8,128)(2,1)S(1)}, u32[]{:S(2)}, u32[]{:S(2)}) collective-permute-start(bf16[16,1792]{1,0:T(8,128)(2,1)S(1)} %shard_map.166.mine), channel_id=1, source_target_pairs={{0,4},{1,5},{2,6},{3,7},{4,0},{5,1},{6,2},{7,3},{8,12},{9,13},{10,... | collective-permute-start | bytes 172040 | tf_op jit(solution)/shard_map/ppermute | solution.py:437
  94.9 0.5 collective-permute-start.25
  95.4 0.3 collective-permute-done.28.refs_2_
  95.7 2.5 %collective-permute-done.27.refs_1_ = bf16[16,1792]{1,0:T(8,128)(2,1)S(1)} collective-permute-done((bf16[16,1792]{1,0:T(8,128)(2,1)S(1)}, bf16[16,1792]{1,0:T(8,128)(2,1)S(1)}, u32[]{:S(2)}, u32[]{:S(2)}) %collective-permute-start.27) | collective-permute-done | bytes 57376 | tf_op jit(solution)/shard_map/ppermute | solution.py:437
  98.2 1.0 collective-permute-done.26.refs_0_
  99.3 0.9 collective-permute-start.32
  100.2 1.5 %collective-permute-start.31 = (bf16[32,1792]{1,0:T(8,128)(2,1)S(1)}, bf16[32,1792]{1,0:T(8,128)(2,1)S(1)}, u32[]{:S(2)}, u32[]{:S(2)}) collective-permute-start(bf16[32,1792]{1,0:T(8,128)(2,1)S(1)} %shard_map.168.refs_0_), channel_id=1, source_target_pairs={{0,2},{1,3},{2,0},{3,1},{4,6},{5,7},{6,4},{7,5},{8,10},{9,11},{10,... | collective-permute-start | bytes 344072 | tf_op jit(solution)/shard_map/ppermute | solution.py:437
  101.6 1.2 %collective-permute-start.30 = (bf16[32,1792]{1,0:T(8,128)(2,1)S(1)}, bf16[32,1792]{1,0:T(8,128)(2,1)S(1)}, u32[]{:S(2)}, u32[]{:S(2)}) collective-permute-start(bf16[32,1792]{1,0:T(8,128)(2,1)S(1)} %shard_map.168.refs_0_), channel_id=1, source_target_pairs={{0,1},{1,0},{2,3},{3,2},{4,5},{5,4},{6,7},{7,6},{8,9},{9,8},{10,11... | collective-permute-start | bytes 344072 | tf_op jit(solution)/shard_map/ppermute | solution.py:437
  102.8 0.7 collective-permute-start.33
  103.5 2.2 %collective-permute-done.32.refs_3_ = bf16[32,1792]{1,0:T(8,128)(2,1)S(1)} collective-permute-done((bf16[32,1792]{1,0:T(8,128)(2,1)S(1)}, bf16[32,1792]{1,0:T(8,128)(2,1)S(1)}, u32[]{:S(2)}, u32[]{:S(2)}) %collective-permute-start.32) | collective-permute-done | bytes 114720 | tf_op jit(solution)/shard_map/ppermute | solution.py:437
  105.7 0.2 collective-permute-done.31.refs_2_
  105.9 1.0 collective-permute-done.30.refs_1_
  106.9 0.1 collective-permute-start.34
  107.0 0.5 collective-permute-start.35
  107.5 1.4 %collective-permute-done.33.refs_2_ = bf16[64,1792]{1,0:T(8,128)(2,1)S(1)} collective-permute-done((bf16[64,1792]{1,0:T(8,128)(2,1)S(1)}, bf16[64,1792]{1,0:T(8,128)(2,1)S(1)}, u32[]{:S(2)}, u32[]{:S(2)}) %collective-permute-start.33) | collective-permute-done | bytes 229408 | tf_op jit(solution)/shard_map/ppermute | solution.py:437
  108.8 0.3 collective-permute-done.35.refs_4_
  109.1 1.2 %collective-permute-done.36.refs_5_ = bf16[64,1792]{1,0:T(8,128)(2,1)S(1)} collective-permute-done((bf16[64,1792]{1,0:T(8,128)(2,1)S(1)}, bf16[64,1792]{1,0:T(8,128)(2,1)S(1)}, u32[]{:S(2)}, u32[]{:S(2)}) %collective-permute-start.36) | collective-permute-done | bytes 229408 | tf_op jit(solution)/shard_map/ppermute | solution.py:437
  110.3 2.0 %shard_map.170 = (f32[512,512]{1,0:T(8,128)}, f32[512,512]{1,0:T(8,128)}, f32[512,512]{1,0:T(8,128)}, f32[512,128]{1,0:T(8,128)}, f32[1,1]{1,0:T(1,128)}) custom-call(bf16[128,1792]{1,0:T(8,128)(2,1)S(1)} %shard_map.169.refs_0_, bf16[64,1792]{1,0:T(8,128)(2,1)S(1)} %shard_map.167.after.refs_1_, bf16[64,1792]{1,0:T(8,128)(2,1)S(1)} %collective-permute-done.33.refs_2_, ...), custom_call_target="tpu_custom_call" | custom-call | bytes 5505024 | tf_op jit(solution)/shard_map/pallas_call | solution.py:615
  (60 shorter events, 0.4 us)
Async XLA Ops:
  2.9 12.4 %collective-permute-start = (bf16[512,128]{1,0:T(8,128)(2,1)}, bf16[512,128]{1,0:T(8,128)(2,1)S(1)}, u32[]{:S(2)}, u32[]{:S(2)}) collective-permute-start(bf16[512,128]{1,0:T(8,128)(2,1)} %get-tuple-element.44), channel_id=1, source_target_pairs={{0,1},{1,0},{2,3},{3,2},{4,5},{5,4},{6,7},{7,6},{8,9},{9,8},{10,11... | collective-permute-start | bytes 393224 | tf_op jit(solution)/shard_map/ppermute | solution.py:437
  5.9 9.4 %collective-permute-start.1 = (bf16[512,128]{1,0:T(8,128)(2,1)}, bf16[512,128]{1,0:T(8,128)(2,1)S(1)}, u32[]{:S(2)}, u32[]{:S(2)}) collective-permute-start(bf16[512,128]{1,0:T(8,128)(2,1)} %get-tuple-element.45), channel_id=1, source_target_pairs={{0,7},{1,2},{2,1},{3,4},{4,3},{5,6},{6,5},{7,0},{8,15},{9,10},{10,... | collective-permute-start | bytes 393224 | tf_op jit(solution)/shard_map/ppermute | solution.py:431
  15.3 0.7 copy-start.15
  15.3 0.7 copy-start.16
  16.0 27.1 %copy-start.11 = (bf16[1536,2048]{1,0:T(8,128)(2,1)S(1)}, bf16[1536,2048]{1,0:T(8,128)(2,1)}, u32[]{:S(2)}) copy-start(bf16[1536,2048]{1,0:T(8,128)(2,1)} %get-tuple-element.50.refs_8_) | copy-start | bytes 18874372
  16.0 27.1 %copy-start.12 = (bf16[128,2048]{1,0:T(8,128)(2,1)S(1)}, bf16[128,2048]{1,0:T(8,128)(2,1)}, u32[]{:S(2)}) copy-start(bf16[128,2048]{1,0:T(8,128)(2,1)} %get-tuple-element.51.refs_9_) | copy-start | bytes 1572868
  16.0 27.1 %copy-start.13 = (bf16[128,2048]{1,0:T(8,128)(2,1)S(1)}, bf16[128,2048]{1,0:T(8,128)(2,1)}, u32[]{:S(2)}) copy-start(bf16[128,2048]{1,0:T(8,128)(2,1)} %get-tuple-element.52.refs_10_) | copy-start | bytes 1572868
  29.1 9.0 %collective-permute-start.3 = (bf16[128,512]{1,0:T(8,128)(2,1)}, bf16[128,512]{1,0:T(8,128)(2,1)S(1)}, u32[]{:S(2)}, u32[]{:S(2)}) collective-permute-start(bf16[128,512]{1,0:T(8,128)(2,1)} %get-tuple-element.47.refs_0_), channel_id=1, source_target_pairs={{0,16},{8,24},{16,0},{24,8},{1,17},{9,25},{17,1},{25,9},{2,18},{10... | collective-permute-start | bytes 393224 | tf_op jit(solution)/shard_map/ppermute | solution.py:437
  30.6 4.1 %collective-permute-start.5 = (bf16[128,128]{1,0:T(8,128)(2,1)}, bf16[128,128]{1,0:T(8,128)(2,1)S(1)}, u32[]{:S(2)}, u32[]{:S(2)}) collective-permute-start(bf16[128,128]{1,0:T(8,128)(2,1)} %get-tuple-element.48), channel_id=1, source_target_pairs={{0,1},{1,0},{2,3},{3,2},{4,5},{5,4},{6,7},{7,6},{8,9},{9,8},{10,11... | collective-permute-start | bytes 98312 | tf_op jit(solution)/shard_map/ppermute | solution.py:437
  30.6 6.8 %collective-permute-start.6 = (bf16[128,128]{1,0:T(8,128)(2,1)}, bf16[128,128]{1,0:T(8,128)(2,1)S(1)}, u32[]{:S(2)}, u32[]{:S(2)}) collective-permute-start(bf16[128,128]{1,0:T(8,128)(2,1)} %get-tuple-element.49), channel_id=1, source_target_pairs={{0,7},{1,2},{2,1},{3,4},{4,3},{5,6},{6,5},{7,0},{8,15},{9,10},{10,... | collective-permute-start | bytes 98312 | tf_op jit(solution)/shard_map/ppermute | solution.py:431
  33.0 8.7 %collective-permute-start.2 = (bf16[128,512]{1,0:T(8,128)(2,1)}, bf16[128,512]{1,0:T(8,128)(2,1)S(1)}, u32[]{:S(2)}, u32[]{:S(2)}) collective-permute-start(bf16[128,512]{1,0:T(8,128)(2,1)} %get-tuple-element.47.refs_0_), channel_id=1, source_target_pairs={{0,8},{8,0},{16,24},{24,16},{1,9},{9,1},{17,25},{25,17},{2,10},{10... | collective-permute-start | bytes 393224 | tf_op jit(solution)/shard_map/ppermute | solution.py:437
  37.4 4.3 %collective-permute-start.8 = (bf16[128,256]{1,0:T(8,128)(2,1)S(1)}, bf16[128,256]{1,0:T(8,128)(2,1)S(1)}, u32[]{:S(2)}, u32[]{:S(2)}) collective-permute-start(bf16[128,256]{1,0:T(8,128)(2,1)S(1)} %shard_map.158.refs_4_), channel_id=1, source_target_pairs={{0,16},{8,24},{16,0},{24,8},{1,17},{9,25},{17,1},{25,9},{2,18},{10... | collective-permute-start | bytes 196616 | tf_op jit(solution)/shard_map/ppermute | solution.py:437
  38.1 5.0 %collective-permute-start.4 = (bf16[128,512]{1,0:T(8,128)(2,1)S(1)}, bf16[128,512]{1,0:T(8,128)(2,1)S(1)}, u32[]{:S(2)}, u32[]{:S(2)}) collective-permute-start(bf16[128,512]{1,0:T(8,128)(2,1)S(1)} %collective-permute-done.3.refs_2_), channel_id=1, source_target_pairs={{0,8},{8,0},{16,24},{24,16},{1,9},{9,1},{17,25},{25,17},{2,10},{10... | collective-permute-start | bytes 393224 | tf_op jit(solution)/shard_map/ppermute | solution.py:437
  38.1 3.7 %collective-permute-start.7 = (bf16[128,256]{1,0:T(8,128)(2,1)S(1)}, bf16[128,256]{1,0:T(8,128)(2,1)S(1)}, u32[]{:S(2)}, u32[]{:S(2)}) collective-permute-start(bf16[128,256]{1,0:T(8,128)(2,1)S(1)} %shard_map.158.refs_4_), channel_id=1, source_target_pairs={{0,8},{8,0},{16,24},{24,16},{1,9},{9,1},{17,25},{25,17},{2,10},{10... | collective-permute-start | bytes 196616 | tf_op jit(solution)/shard_map/ppermute | solution.py:437
  41.8 1.3 %collective-permute-start.9 = (bf16[128,256]{1,0:T(8,128)(2,1)S(1)}, bf16[128,256]{1,0:T(8,128)(2,1)S(1)}, u32[]{:S(2)}, u32[]{:S(2)}) collective-permute-start(bf16[128,256]{1,0:T(8,128)(2,1)S(1)} %collective-permute-done.8.refs_6_), channel_id=1, source_target_pairs={{0,8},{8,0},{16,24},{24,16},{1,9},{9,1},{17,25},{25,17},{2,10},{10... | collective-permute-start | bytes 196616 | tf_op jit(solution)/shard_map/ppermute | solution.py:437
  43.1 0.9 copy-start.14
  44.0 16.8 %copy-start = (bf16[512,3072]{1,0:T(8,128)(2,1)S(1)}, bf16[512,3072]{1,0:T(8,128)(2,1)}, u32[]{:S(2)}) copy-start(bf16[512,3072]{1,0:T(8,128)(2,1)} %get-tuple-element.60.picked_t) | copy-start | bytes 9437188
  44.0 16.8 %copy-start.1 = (bf16[512,3072]{1,0:T(8,128)(2,1)S(1)}, bf16[512,3072]{1,0:T(8,128)(2,1)}, u32[]{:S(2)}) copy-start(bf16[512,3072]{1,0:T(8,128)(2,1)} %get-tuple-element.61.slope_t) | copy-start | bytes 9437188
  44.0 16.8 %copy-start.2 = (bf16[512,512]{1,0:T(8,128)(2,1)S(1)}, bf16[512,512]{1,0:T(8,128)(2,1)}, u32[]{:S(2)}) copy-start(bf16[512,512]{1,0:T(8,128)(2,1)} %get-tuple-element.43.after.nodes_in.nodes_t) | copy-start | bytes 1572868
  44.0 16.8 %copy-start.3 = (f32[512,512]{1,0:T(8,128)S(1)}, f32[512,512]{1,0:T(8,128)}, u32[]{:S(2)}) copy-start(f32[512,512]{1,0:T(8,128)} %get-tuple-element.62.slope_sum_t) | copy-start | bytes 3145732
  44.0 16.8 %copy-start.4 = (f32[512,512]{1,0:T(8,128)S(1)}, f32[512,512]{1,0:T(8,128)}, u32[]{:S(2)}) copy-start(f32[512,512]{1,0:T(8,128)} %get-tuple-element.64.upd_slope_t) | copy-start | bytes 3145732
  44.0 16.8 %copy-start.5 = (bf16[512,512]{1,0:T(8,128)(2,1)S(1)}, bf16[512,512]{1,0:T(8,128)(2,1)}, u32[]{:S(2)}) copy-start(bf16[512,512]{1,0:T(8,128)(2,1)} %vertex.1) | copy-start | bytes 1572868
  44.0 16.8 %copy-start.6 = (bf16[512,512]{1,0:T(8,128)(2,1)S(1)}, bf16[512,512]{1,0:T(8,128)(2,1)}, u32[]{:S(2)}) copy-start(bf16[512,512]{1,0:T(8,128)(2,1)} %get-tuple-element.63.agg_t) | copy-start | bytes 1572868
  44.0 16.8 %copy-start.7 = (bf16[512,512]{1,0:T(8,128)(2,1)S(1)}, bf16[512,512]{1,0:T(8,128)(2,1)}, u32[]{:S(2)}) copy-start(bf16[512,512]{1,0:T(8,128)(2,1)} %get-tuple-element.65.hidden_t) | copy-start | bytes 1572868
  44.0 16.8 %copy-start.8 = (bf16[512,128]{1,0:T(8,128)(2,1)S(1)}, bf16[512,128]{1,0:T(8,128)(2,1)}, u32[]{:S(2)}) copy-start(bf16[512,128]{1,0:T(8,128)(2,1)} %w_decode.1) | copy-start | bytes 393220
  44.0 16.8 %copy-start.9 = (s32[128]{0:T(128)S(1)}, s32[128]{0:T(128)}, u32[]{:S(2)}) copy-start(s32[128]{0:T(128)} %param.14) | copy-start | bytes 1540
  44.0 16.8 %copy-start.10 = (s32[128]{0:T(128)S(1)}, s32[128]{0:T(128)}, u32[]{:S(2)}) copy-start(s32[128]{0:T(128)} %param.15) | copy-start | bytes 1540
  52.1 8.7 %collective-permute-start.10 = (f32[128,512]{1,0:T(8,128)S(1)}, f32[128,512]{1,0:T(8,128)S(1)}, u32[]{:S(2)}, u32[]{:S(2)}) collective-permute-start(f32[128,512]{1,0:T(8,128)S(1)} %get-tuple-element.54), channel_id=1, source_target_pairs={{0,8},{8,0},{16,24},{24,16},{1,9},{9,1},{17,25},{25,17},{2,10},{10... | collective-permute-start | bytes 786440 | tf_op jit(solution)/shard_map/ppermute | solution.py:437
  52.3 1.6 %collective-permute-start.11 = (f32[128,256]{1,0:T(8,128)S(1)}, f32[128,256]{1,0:T(8,128)S(1)}, u32[]{:S(2)}, u32[]{:S(2)}) collective-permute-start(f32[128,256]{1,0:T(8,128)S(1)} %get-tuple-element.56), channel_id=1, source_target_pairs={{0,8},{8,0},{16,24},{24,16},{1,9},{9,1},{17,25},{25,17},{2,10},{10... | collective-permute-start | bytes 393224 | tf_op jit(solution)/shard_map/ppermute | solution.py:437
  53.9 4.0 %collective-permute-start.12 = (bf16[128,128]{1,0:T(8,128)(2,1)S(1)}, bf16[128,128]{1,0:T(8,128)(2,1)S(1)}, u32[]{:S(2)}, u32[]{:S(2)}) collective-permute-start(bf16[128,128]{1,0:T(8,128)(2,1)S(1)} %get-tuple-element.57), channel_id=1, source_target_pairs={{0,1},{1,0},{2,3},{3,2},{4,5},{5,4},{6,7},{7,6},{8,9},{9,8},{10,11... | collective-permute-start | bytes 98312 | tf_op jit(solution)/shard_map/ppermute | solution.py:437
  54.2 6.6 %collective-permute-start.13 = (bf16[128,128]{1,0:T(8,128)(2,1)S(1)}, bf16[128,128]{1,0:T(8,128)(2,1)S(1)}, u32[]{:S(2)}, u32[]{:S(2)}) collective-permute-start(bf16[128,128]{1,0:T(8,128)(2,1)S(1)} %get-tuple-element.58), channel_id=1, source_target_pairs={{0,7},{1,2},{2,1},{3,4},{4,3},{5,6},{6,5},{7,0},{8,15},{9,10},{10,... | collective-permute-start | bytes 98312 | tf_op jit(solution)/shard_map/ppermute | solution.py:431
  64.3 3.3 %collective-permute-start.14 = (bf16[192,1792]{1,0:T(8,128)(2,1)S(1)}, bf16[192,1792]{1,0:T(8,128)(2,1)S(1)}, u32[]{:S(2)}, u32[]{:S(2)}) collective-permute-start(bf16[192,1792]{1,0:T(8,128)(2,1)S(1)} %get-tuple-element.67), channel_id=1, source_target_pairs={{0,8},{8,0},{16,24},{24,16},{1,9},{9,1},{17,25},{25,17},{2,10},{10... | collective-permute-start | bytes 2064392 | tf_op jit(solution)/shard_map/ppermute | solution.py:437
  64.4 2.5 %collective-permute-start.18 = (bf16[64,1792]{1,0:T(8,128)(2,1)S(1)}, bf16[64,1792]{1,0:T(8,128)(2,1)S(1)}, u32[]{:S(2)}, u32[]{:S(2)}) collective-permute-start(bf16[64,1792]{1,0:T(8,128)(2,1)S(1)} %get-tuple-element.71), channel_id=1, source_target_pairs={{0,8},{8,0},{16,24},{24,16},{1,9},{9,1},{17,25},{25,17},{2,10},{10... | collective-permute-start | bytes 688136 | tf_op jit(solution)/shard_map/ppermute | solution.py:437
  67.0 7.7 %collective-permute-start.19 = (bf16[64,1792]{1,0:T(8,128)(2,1)S(1)}, bf16[64,1792]{1,0:T(8,128)(2,1)S(1)}, u32[]{:S(2)}, u32[]{:S(2)}) collective-permute-start(bf16[64,1792]{1,0:T(8,128)(2,1)S(1)} %shard_map.163), channel_id=1, source_target_pairs={{0,16},{8,24},{16,0},{24,8},{1,17},{9,25},{17,1},{25,9},{2,18},{10... | collective-permute-start | bytes 688136 | tf_op jit(solution)/shard_map/ppermute | solution.py:437
  67.7 9.5 %collective-permute-start.15 = (bf16[32,1792]{1,0:T(8,128)(2,1)S(1)}, bf16[32,1792]{1,0:T(8,128)(2,1)S(1)}, u32[]{:S(2)}, u32[]{:S(2)}) collective-permute-start(bf16[32,1792]{1,0:T(8,128)(2,1)S(1)} %get-tuple-element.68), channel_id=1, source_target_pairs={{0,1},{1,0},{2,3},{3,2},{4,5},{5,4},{6,7},{7,6},{8,9},{9,8},{10,11... | collective-permute-start | bytes 344072 | tf_op jit(solution)/shard_map/ppermute | solution.py:437
  67.8 12.3 %collective-permute-start.16 = (bf16[32,1792]{1,0:T(8,128)(2,1)S(1)}, bf16[32,1792]{1,0:T(8,128)(2,1)S(1)}, u32[]{:S(2)}, u32[]{:S(2)}) collective-permute-start(bf16[32,1792]{1,0:T(8,128)(2,1)S(1)} %get-tuple-element.69), channel_id=1, source_target_pairs={{0,2},{1,3},{2,0},{3,1},{4,6},{5,7},{6,4},{7,5},{8,10},{9,11},{10,... | collective-permute-start | bytes 344072 | tf_op jit(solution)/shard_map/ppermute | solution.py:437
  67.9 14.7 %collective-permute-start.17 = (bf16[32,1792]{1,0:T(8,128)(2,1)S(1)}, bf16[32,1792]{1,0:T(8,128)(2,1)S(1)}, u32[]{:S(2)}, u32[]{:S(2)}) collective-permute-start(bf16[32,1792]{1,0:T(8,128)(2,1)S(1)} %get-tuple-element.70), channel_id=1, source_target_pairs={{0,3},{1,2},{2,1},{3,0},{4,7},{5,6},{6,5},{7,4},{8,11},{9,10},{10,... | collective-permute-start | bytes 344072 | tf_op jit(solution)/shard_map/ppermute | solution.py:437
  74.8 8.4 %collective-permute-start.20 = (bf16[16,1792]{1,0:T(8,128)(2,1)S(1)}, bf16[16,1792]{1,0:T(8,128)(2,1)S(1)}, u32[]{:S(2)}, u32[]{:S(2)}) collective-permute-start(bf16[16,1792]{1,0:T(8,128)(2,1)S(1)} %get-tuple-element.72), channel_id=1, source_target_pairs={{0,4},{1,5},{2,6},{3,7},{4,0},{5,1},{6,2},{7,3},{8,12},{9,13},{10,... | collective-permute-start | bytes 172040 | tf_op jit(solution)/shard_map/ppermute | solution.py:437
  74.9 8.8 %collective-permute-start.21 = (bf16[16,1792]{1,0:T(8,128)(2,1)S(1)}, bf16[16,1792]{1,0:T(8,128)(2,1)S(1)}, u32[]{:S(2)}, u32[]{:S(2)}) collective-permute-start(bf16[16,1792]{1,0:T(8,128)(2,1)S(1)} %get-tuple-element.73), channel_id=1, source_target_pairs={{0,5},{1,4},{2,7},{3,6},{4,1},{5,0},{6,3},{7,2},{8,13},{9,12},{10,... | collective-permute-start | bytes 172040 | tf_op jit(solution)/shard_map/ppermute | solution.py:437
  77.2 6.5 %collective-permute-start.22 = (bf16[16,1792]{1,0:T(8,128)(2,1)S(1)}, bf16[16,1792]{1,0:T(8,128)(2,1)S(1)}, u32[]{:S(2)}, u32[]{:S(2)}) collective-permute-start(bf16[16,1792]{1,0:T(8,128)(2,1)S(1)} %get-tuple-element.74), channel_id=1, source_target_pairs={{0,6},{1,7},{2,4},{3,5},{4,2},{5,3},{6,0},{7,1},{8,14},{9,15},{10,... | collective-permute-start | bytes 172040 | tf_op jit(solution)/shard_map/ppermute | solution.py:437
  80.1 7.0 %collective-permute-start.23 = (bf16[16,1792]{1,0:T(8,128)(2,1)S(1)}, bf16[16,1792]{1,0:T(8,128)(2,1)S(1)}, u32[]{:S(2)}, u32[]{:S(2)}) collective-permute-start(bf16[16,1792]{1,0:T(8,128)(2,1)S(1)} %get-tuple-element.75), channel_id=1, source_target_pairs={{0,7},{1,6},{2,5},{3,4},{4,3},{5,2},{6,1},{7,0},{8,15},{9,14},{10,... | collective-permute-start | bytes 172040 | tf_op jit(solution)/shard_map/ppermute | solution.py:437
  82.6 4.5 %collective-permute-start.24 = (bf16[16,1792]{1,0:T(8,128)(2,1)S(1)}, bf16[16,1792]{1,0:T(8,128)(2,1)S(1)}, u32[]{:S(2)}, u32[]{:S(2)}) collective-permute-start(bf16[16,1792]{1,0:T(8,128)(2,1)S(1)} %shard_map.165), channel_id=1, source_target_pairs={{0,16},{8,24},{16,0},{24,8},{1,17},{9,25},{17,1},{25,9},{2,18},{10... | collective-permute-start | bytes 172040 | tf_op jit(solution)/shard_map/ppermute | solution.py:437
  87.2 8.2 %collective-permute-start.29 = (bf16[16,1792]{1,0:T(8,128)(2,1)S(1)}, bf16[16,1792]{1,0:T(8,128)(2,1)S(1)}, u32[]{:S(2)}, u32[]{:S(2)}) collective-permute-start(bf16[16,1792]{1,0:T(8,128)(2,1)S(1)} %shard_map.166.mine), channel_id=1, source_target_pairs={{0,7},{1,6},{2,5},{3,4},{4,3},{5,2},{6,1},{7,0},{8,15},{9,14},{10,... | collective-permute-start | bytes 172040 | tf_op jit(solution)/shard_map/ppermute | solution.py:437
  89.7 6.1 %collective-permute-start.28 = (bf16[16,1792]{1,0:T(8,128)(2,1)S(1)}, bf16[16,1792]{1,0:T(8,128)(2,1)S(1)}, u32[]{:S(2)}, u32[]{:S(2)}) collective-permute-start(bf16[16,1792]{1,0:T(8,128)(2,1)S(1)} %shard_map.166.mine), channel_id=1, source_target_pairs={{0,6},{1,7},{2,4},{3,5},{4,2},{5,3},{6,0},{7,1},{8,14},{9,15},{10,... | collective-permute-start | bytes 172040 | tf_op jit(solution)/shard_map/ppermute | solution.py:437
  90.6 7.6 %collective-permute-start.27 = (bf16[16,1792]{1,0:T(8,128)(2,1)S(1)}, bf16[16,1792]{1,0:T(8,128)(2,1)S(1)}, u32[]{:S(2)}, u32[]{:S(2)}) collective-permute-start(bf16[16,1792]{1,0:T(8,128)(2,1)S(1)} %shard_map.166.mine), channel_id=1, source_target_pairs={{0,5},{1,4},{2,7},{3,6},{4,1},{5,0},{6,3},{7,2},{8,13},{9,12},{10,... | collective-permute-start | bytes 172040 | tf_op jit(solution)/shard_map/ppermute | solution.py:437
  91.4 7.9 %collective-permute-start.26 = (bf16[16,1792]{1,0:T(8,128)(2,1)S(1)}, bf16[16,1792]{1,0:T(8,128)(2,1)S(1)}, u32[]{:S(2)}, u32[]{:S(2)}) collective-permute-start(bf16[16,1792]{1,0:T(8,128)(2,1)S(1)} %shard_map.166.mine), channel_id=1, source_target_pairs={{0,4},{1,5},{2,6},{3,7},{4,0},{5,1},{6,2},{7,3},{8,12},{9,13},{10,... | collective-permute-start | bytes 172040 | tf_op jit(solution)/shard_map/ppermute | solution.py:437
  94.9 4.4 %collective-permute-start.25 = (bf16[16,1792]{1,0:T(8,128)(2,1)S(1)}, bf16[16,1792]{1,0:T(8,128)(2,1)S(1)}, u32[]{:S(2)}, u32[]{:S(2)}) collective-permute-start(bf16[16,1792]{1,0:T(8,128)(2,1)S(1)} %shard_map.166.mine), channel_id=1, source_target_pairs={{0,16},{8,24},{16,0},{24,8},{1,17},{9,25},{17,1},{25,9},{2,18},{10... | collective-permute-start | bytes 172040 | tf_op jit(solution)/shard_map/ppermute | solution.py:437
  99.3 6.4 %collective-permute-start.32 = (bf16[32,1792]{1,0:T(8,128)(2,1)S(1)}, bf16[32,1792]{1,0:T(8,128)(2,1)S(1)}, u32[]{:S(2)}, u32[]{:S(2)}) collective-permute-start(bf16[32,1792]{1,0:T(8,128)(2,1)S(1)} %shard_map.168.refs_0_), channel_id=1, source_target_pairs={{0,3},{1,2},{2,1},{3,0},{4,7},{5,6},{6,5},{7,4},{8,11},{9,10},{10,... | collective-permute-start | bytes 344072 | tf_op jit(solution)/shard_map/ppermute | solution.py:437
  100.2 5.8 %collective-permute-start.31 = (bf16[32,1792]{1,0:T(8,128)(2,1)S(1)}, bf16[32,1792]{1,0:T(8,128)(2,1)S(1)}, u32[]{:S(2)}, u32[]{:S(2)}) collective-permute-start(bf16[32,1792]{1,0:T(8,128)(2,1)S(1)} %shard_map.168.refs_0_), channel_id=1, source_target_pairs={{0,2},{1,3},{2,0},{3,1},{4,6},{5,7},{6,4},{7,5},{8,10},{9,11},{10,... | collective-permute-start | bytes 344072 | tf_op jit(solution)/shard_map/ppermute | solution.py:437
  101.6 5.2 %collective-permute-start.30 = (bf16[32,1792]{1,0:T(8,128)(2,1)S(1)}, bf16[32,1792]{1,0:T(8,128)(2,1)S(1)}, u32[]{:S(2)}, u32[]{:S(2)}) collective-permute-start(bf16[32,1792]{1,0:T(8,128)(2,1)S(1)} %shard_map.168.refs_0_), channel_id=1, source_target_pairs={{0,1},{1,0},{2,3},{3,2},{4,5},{5,4},{6,7},{7,6},{8,9},{9,8},{10,11... | collective-permute-start | bytes 344072 | tf_op jit(solution)/shard_map/ppermute | solution.py:437
  102.8 6.0 %collective-permute-start.33 = (bf16[64,1792]{1,0:T(8,128)(2,1)S(1)}, bf16[64,1792]{1,0:T(8,128)(2,1)S(1)}, u32[]{:S(2)}, u32[]{:S(2)}) collective-permute-start(bf16[64,1792]{1,0:T(8,128)(2,1)S(1)} %shard_map.167.after.refs_1_), channel_id=1, source_target_pairs={{0,16},{8,24},{16,0},{24,8},{1,17},{9,25},{17,1},{25,9},{2,18},{10... | collective-permute-start | bytes 688136 | tf_op jit(solution)/shard_map/ppermute | solution.py:437
  106.9 3.4 %collective-permute-start.34 = (bf16[128,1792]{1,0:T(8,128)(2,1)S(1)}, bf16[128,1792]{1,0:T(8,128)(2,1)S(1)}, u32[]{:S(2)}, u32[]{:S(2)}) collective-permute-start(bf16[128,1792]{1,0:T(8,128)(2,1)S(1)} %shard_map.169.refs_0_), channel_id=1, source_target_pairs={{0,8},{8,0},{16,24},{24,16},{1,9},{9,1},{17,25},{25,17},{2,10},{10... | collective-permute-start | bytes 1376264 | tf_op jit(solution)/shard_map/ppermute | solution.py:437
  107.0 2.1 %collective-permute-start.35 = (bf16[64,1792]{1,0:T(8,128)(2,1)S(1)}, bf16[64,1792]{1,0:T(8,128)(2,1)S(1)}, u32[]{:S(2)}, u32[]{:S(2)}) collective-permute-start(bf16[64,1792]{1,0:T(8,128)(2,1)S(1)} %shard_map.167.after.refs_1_), channel_id=1, source_target_pairs={{0,8},{8,0},{16,24},{24,16},{1,9},{9,1},{17,25},{25,17},{2,10},{10... | collective-permute-start | bytes 688136 | tf_op jit(solution)/shard_map/ppermute | solution.py:437
  108.8 1.5 %collective-permute-start.36 = (bf16[64,1792]{1,0:T(8,128)(2,1)S(1)}, bf16[64,1792]{1,0:T(8,128)(2,1)S(1)}, u32[]{:S(2)}, u32[]{:S(2)}) collective-permute-start(bf16[64,1792]{1,0:T(8,128)(2,1)S(1)} %collective-permute-done.33.refs_2_), channel_id=1, source_target_pairs={{0,8},{8,0},{16,24},{24,16},{1,9},{9,1},{17,25},{25,17},{2,10},{10... | collective-permute-start | bytes 688136 | tf_op jit(solution)/shard_map/ppermute | solution.py:437

commit v8 on v7

--- a/solution.py
+++ b/solution.py
@@ -84,28 +84,35 @@
         for copy in copies:
             copy.start()
 
-    rows, tile = mat.shape[0] // 2, 16
-    shape = (tile, mat.shape[1])
-    spread = lambda ref, k: jnp.broadcast_to(ref[k : k + 1, :], shape)
-    vertex = [spread(vertices, k) for k in range(vertices.shape[0])]
-    weight = [spread(weights, k) for k in range(vertices.shape[0])]
-    row = lax.broadcasted_iota(jnp.int32, shape, 0)
-
-    for start in range(0, rows, tile):
-        here = row + start
-        total = jnp.where(here == vertex[0], weight[0], 0.0)
-        for k in range(1, len(vertex)):
-            total += jnp.where(here == vertex[k], weight[k], 0.0)
-        hi, lo = split(total)
-        mat[start : start + tile, :] = hi
-        mat[rows + start : rows + start + tile, :] = lo
-
-    @pl.when(pl.program_id(0) == pl.num_programs(0) - 1)
+    rows, lanes = mat.shape[0] // 2, 256
+    row = lax.broadcasted_iota(jnp.int32, (8, lanes), 0)
+    for left in range(0, mat.shape[1], lanes):
+        cols = slice(left, left + lanes)
+        spread = lambda ref, k: jnp.broadcast_to(ref[k : k + 1, cols], (8, lanes))
+        ahead = [spread(vertices, k) - row for k in range(vertices.shape[0])]
+        weight = [spread(weights, k) for k in range(vertices.shape[0])]
+
+        def weighted(start):
+            total = jnp.where(ahead[0] == start, weight[0], 0.0)
+            for k in range(1, len(ahead)):
+                total += jnp.where(ahead[k] == start, weight[k], 0.0)
+            return total
+
+        for start in range(0, rows, 16):
+            hi, lo = split(jnp.concatenate([weighted(start), weighted(start + 8)], axis=0))
+            mat[start : start + 16, cols] = hi
+            mat[rows + start : rows + start + 16, cols] = lo
+
+    step, block = pl.program_id(0), mat.shape[1]
+
+    @pl.when(step == 0)
     def _():
         for copy in copies:
             copy.wait()
-        base_t[...] = base_rows[...].T
-        truth_t[...] = truth_rows[...].T
+
+    some = pl.ds(pl.multiple_of(step * block, block), block)
+    base_t[...] = base_rows[some, :].T
+    truth_t[...] = truth_rows[some, :].T
 
 
 TILE = 16
@@ -119,9 +126,9 @@
 
 def forward_kernel(
     nodes_in, from_first, from_second, senders_in, w_send_in, w_recv_in, to_next_in, to_prev_in, vertex_in, w_decode_in, after,
-    field_t, first_t, second_t, picked_out, slope_out, slope_sum_out, agg_out, upd_slope_out, hidden_out,
+    field_out, first_out, second_out, picked_out, slope_out, slope_sum_out, agg_out, upd_slope_out, hidden_out,
     ext, senders, w_send, w_recv, to_next, to_prev, vertex, w_decode, picked_t, recv_t,
-    slope_t, slope_sum_t, agg_t, upd_slope_t, hidden_t, pre, in_sems, out_sems,
+    slope_t, slope_sum_t, agg_t, upd_slope_t, hidden_t, pre, field_t, first_t, second_t, in_sems, out_sems,
 ):
     del after
     degree, count = senders.shape
@@ -144,17 +151,18 @@
         copy.start()
         stored.append(copy)
 
-    for copy in fetch[:6]:
+    for copy in fetch[:4]:
         copy.wait()
-    recv_t[...] = dot(w_recv[...].T, ext[:, :count]) * 0.5
-    w_send_t = w_send[...].T * 0.5
     for k in range(degree):
         here = slice(k * count, (k + 1) * count)
         picked_t[:, here] = dot(ext[...], one_hot(ext_rows, senders[k : k + 1, :])).astype(BF16)
+        store(picked_t.at[:, here], picked_out.at[:, here])
+        if k == 0:
+            for copy in fetch[4:]:
+                copy.wait()
+            w_send_t = w_send[...].T * 0.5
         pre[:, here] = dot(w_send_t, picked_t[:, here])
-    store(picked_t, picked_out)
-    for copy in fetch[6:]:
-        copy.wait()
+    recv_t[...] = dot(w_recv[...].T, ext[:, :count]) * 0.5
     for start in range(0, width, TILE):
         rows = slice(start, start + TILE)
         recv = recv_t[rows, :]
@@ -178,13 +186,16 @@
         value, slope = bent(pre[rows, :count])
         upd_slope_t[rows, :] = slope * 0.5
         hidden_t[rows, :] = (ext[rows, :count].astype(F32) + value).astype(BF16)
+    store(hidden_t, hidden_out)
     store(upd_slope_t, upd_slope_out)
-    store(hidden_t, hidden_out)
     field = dot(w_decode[...].T, hidden_t[...]).astype(BF16)
     field_t[...] = field
     first, second = sides(to_next[...], to_prev[...])
     first_t[...] = dot(field, one_hot(count, first)).astype(BF16)
     second_t[...] = dot(field, one_hot(count, second)).astype(BF16)
+    store(field_t, field_out)
+    store(first_t, first_out)
+    store(second_t, second_out)
     for copy in stored:
         copy.wait()
 
@@ -194,7 +205,8 @@
     mat, base_t, truth_t = refs[8:11]
     own_mid, own_end, pair_mid, pair_end, loss = refs[11:16]
     table, grad = refs[16:18]
-    states, slopes = refs[18:20], refs[20:22]
+    subs = (len(refs) - 18) // 2
+    states, slopes = refs[18 : 18 + subs], refs[18 + subs :]
     step = pl.program_id(0)
     members = len(mids)
     variables, count = own_mid.shape
@@ -521,7 +533,7 @@
     from_first, from_second = meet(first_t, second_t)
 
     core = scalar(lax.rem(ens, 2))
-    block = 512
+    block = 1024
     steps = line_span // 2 // block
     fixed = lambda shape: pl.BlockSpec(shape, lambda i, *at: (0,) * len(shape))
     tall = lambda rows: pl.BlockSpec((rows, block), lambda i, *at: (0, i))
@@ -533,7 +545,7 @@
             num_scalar_prefetch=1,
             grid=(steps,),
             in_specs=[tall_half(fan), tall_half(fan), HBM, HBM, pl.BlockSpec(memory_space=pl.ANY)],
-            out_specs=[tall(2 * ext_rows), fixed((variables, half_span)), fixed((variables, half_span)), fixed((8, 128))],
+            out_specs=[tall(2 * ext_rows), tall(variables), tall(variables), fixed((8, 128))],
             scratch_shapes=[held((half_span, variables)), held((half_span, variables)), pltpu.SemaphoreType.DMA((2,))],
         ),
         out_shape=[sds((2 * ext_rows, half_span), BF16)] + [sds((variables, half_span), BF16)] * 2 + [sds((8, 128), F32)],
@@ -553,11 +565,12 @@
             held((width, width)), held((width, variables)), held((width, degree * count)), held((width, count), F32),
             held((width, degree * count)), held((width, count), F32), held((width, count)), held((width, count), F32),
             held((width, count)), held((width, degree * count), F32),
-            pltpu.SemaphoreType.DMA((10,)), pltpu.SemaphoreType.DMA((width // 128 + 5,)),
+            held((variables, count)), held((variables, halo)), held((variables, halo)),
+            pltpu.SemaphoreType.DMA((10,)), pltpu.SemaphoreType.DMA((width // 128 + 7 + degree,)),
         ],
         flops=2 * degree * width * count * (ext_rows + width),
         in_hbm=11,
-        out_hbm=6,
+        out_hbm=9,
         limit=56,
     )
     lent = meet(first_t, second_t)
@@ -566,6 +579,7 @@
     (end,) = call(borrowed_kernel, list(lent), [sds((variables, 2 * halo), BF16)])
     ends = gathered(end)
 
+    wide = lambda rows: pl.BlockSpec((rows, 2 * block), lambda i, *at: (0, i))
     grads = pl.pallas_call(
         functools.partial(readout_kernel, line_span),
         grid=(steps,),

time: 113 us -> 109 us (0.965)
  Pallas kernels: 35.1 us -> 31 us
    pallas_call x13, Pallas kernels: 19.4 us -> 17 us  [call(): pl.pallas_call(kernel, out_shape=outs, in_specs=vmem(len(ins) - in_hbm) +...]
    pallas_call x1, Pallas kernels: 8 us -> 6.8 us  [per_device(): pl.pallas_call(functools.partial(readout_kernel, line_span), grid=(steps,...]
  transfers between devices with their start and end apart: 37 -> 37, of which waited for: 21 -> 20; matrix products, arithmetic and copies ran while one was open for 0% -> 0% of each run, Pallas kernels for 6% -> 5%
where the time goes in v8:
time: 109 us
  starting transfers between devices  41.8 us (38%)
  waiting for transfers between devices  33 us (30%)
  Pallas kernels  31 us (28%)
  local copies, waits for them, and re-layouts  1.63 us (1%)
  between operations  1.11 us (1%)
    ppermute x34, starting transfers between devices, flip(): return lax.ppermute(value, axis, [(i, i ^ bit) for i in range(size)])  32.4 us
    ppermute x34, waiting for transfers between devices, flip(): return lax.ppermute(value, axis, [(i, i ^ bit) for i in range(size)])  27.4 us
    pallas_call x13, Pallas kernels, call(): pl.pallas_call(kernel, out_shape=outs, in_specs=vmem(len(ins) - in_hbm) +...  17 us
    ppermute x3, starting transfers between devices, meet(): lax.ppermute(second, 'dom', [(i, (i + (1 if i % 2 else size - 1)) % size)...  9.39 us
    pallas_call x1, Pallas kernels, per_device(): pl.pallas_call(functools.partial(readout_kernel, line_span), grid=(steps,...  6.8 us
    ppermute x3, waiting for transfers between devices, meet(): lax.ppermute(second, 'dom', [(i, (i + (1 if i % 2 else size - 1)) % size)...  5.62 us
    pallas_call x1, Pallas kernels, per_device(): pl.pallas_call(decoder_kernel, grid_spec=pltpu.PrefetchScalarGridSpec(num...  5.23 us
  transfers between devices with their start and end apart: 37, of which 20 were waited for; matrix products, arithmetic and copies ran while one was open for 0% of the time, Pallas kernels for 5%

profile of v8, /device:TPU:0, one launch (start us, length us, event | category | flops | bytes accessed | tf_op | source)
XLA Modules:
  0.0 108.6 jit_solution(3029598794829098613)
XLA Ops:
  0.6 2.2 %shard_map.155 = (bf16[512,512]{1,0:T(8,128)(2,1)}, bf16[512,128]{1,0:T(8,128)(2,1)}, bf16[512,128]{1,0:T(8,128)(2,1)}) custom-call(bf16[512,512]{1,0:T(8,128)(2,1)} %bitcast.11, s32[1,128]{1,0:T(1,128)} %bitcast.5, s32[1,128]{1,0:T(1,128)} %bitcast.8), custom_call_target="tpu_custom_call" | custom-call | flops 134217728 | bytes 1311744 | tf_op jit(solution)/shard_map/pallas_call | solution.py:458
  2.9 3.0 %collective-permute-start = (bf16[512,128]{1,0:T(8,128)(2,1)}, bf16[512,128]{1,0:T(8,128)(2,1)S(1)}, u32[]{:S(2)}, u32[]{:S(2)}) collective-permute-start(bf16[512,128]{1,0:T(8,128)(2,1)} %get-tuple-element.44), channel_id=1, source_target_pairs={{0,1},{1,0},{2,3},{3,2},{4,5},{5,4},{6,7},{7,6},{8,9},{9,8},{10,11... | collective-permute-start | bytes 393224 | tf_op jit(solution)/shard_map/ppermute | solution.py:449
  5.9 3.5 %collective-permute-start.1 = (bf16[512,128]{1,0:T(8,128)(2,1)}, bf16[512,128]{1,0:T(8,128)(2,1)S(1)}, u32[]{:S(2)}, u32[]{:S(2)}) collective-permute-start(bf16[512,128]{1,0:T(8,128)(2,1)} %get-tuple-element.45), channel_id=1, source_target_pairs={{0,7},{1,2},{2,1},{3,4},{4,3},{5,6},{6,5},{7,0},{8,15},{9,10},{10,... | collective-permute-start | bytes 393224 | tf_op jit(solution)/shard_map/ppermute | solution.py:443
  9.5 5.2 %shard_map.156 = (bf16[1536,2048]{1,0:T(8,128)(2,1)}, bf16[128,2048]{1,0:T(8,128)(2,1)}, bf16[128,2048]{1,0:T(8,128)(2,1)}, f32[8,128]{1,0:T(8,128)}) custom-call(s32[1]{0:T(128)} %bitcast.3.core, s32[3,4096]{1,0:T(4,128)} %vertices.1, f32[3,4096]{1,0:T(4,128)} %weights.1, bf16[4096,128]{1,0:T(8,128)(2,1)} %base.1, bf16[4096,128]{1,0:T(8,128)(2,1)} %truth.1, ...), custom_call_target="tpu_custom_call" | custom-call | flops 15728640 | bytes 16000000 | tf_op jit(solution)/shard_map/pallas_call | solution.py:542
  14.7 0.6 copy-done.15
  15.4 10.7 %shard_map.157 = (bf16[128,512]{1,0:T(8,128)(2,1)}, bf16[128,128]{1,0:T(8,128)(2,1)}, bf16[128,128]{1,0:T(8,128)(2,1)}, bf16[512,3072]{1,0:T(8,128)(2,1)}, bf16[...) custom-call(bf16[512,512]{1,0:T(8,128)(2,1)} %get-tuple-element.43.a, ...), custom_call_target="tpu_custom_call" | custom-call | flops 4026531840 | bytes 12141568 | tf_op jit(solution)/shard_map/pallas_call | solution.py:458
  26.1 1.6 %collective-permute-start.3 = (bf16[128,512]{1,0:T(8,128)(2,1)}, bf16[128,512]{1,0:T(8,128)(2,1)S(1)}, u32[]{:S(2)}, u32[]{:S(2)}) collective-permute-start(bf16[128,512]{1,0:T(8,128)(2,1)} %get-tuple-element.47.refs_0_), channel_id=1, source_target_pairs={{0,16},{8,24},{16,0},{24,8},{1,17},{9,25},{17,1},{25,9},{2,18},{10... | collective-permute-start | bytes 393224 | tf_op jit(solution)/shard_map/ppermute | solution.py:449
  27.7 3.0 %collective-permute-start.6 = (bf16[128,128]{1,0:T(8,128)(2,1)}, bf16[128,128]{1,0:T(8,128)(2,1)S(1)}, u32[]{:S(2)}, u32[]{:S(2)}) collective-permute-start(bf16[128,128]{1,0:T(8,128)(2,1)} %get-tuple-element.49), channel_id=1, source_target_pairs={{0,7},{1,2},{2,1},{3,4},{4,3},{5,6},{6,5},{7,0},{8,15},{9,10},{10,... | collective-permute-start | bytes 98312 | tf_op jit(solution)/shard_map/ppermute | solution.py:443
  30.7 1.1 %collective-permute-done.5.first = bf16[128,128]{1,0:T(8,128)(2,1)S(1)} collective-permute-done((bf16[128,128]{1,0:T(8,128)(2,1)}, bf16[128,128]{1,0:T(8,128)(2,1)S(1)}, u32[]{:S(2)}, u32[]{:S(2)}) %collective-permute-start.5) | collective-permute-done | bytes 32800 | tf_op jit(solution)/shard_map/ppermute | solution.py:449
  31.8 2.7 %collective-permute-done.6.second = bf16[128,128]{1,0:T(8,128)(2,1)S(1)} collective-permute-done((bf16[128,128]{1,0:T(8,128)(2,1)}, bf16[128,128]{1,0:T(8,128)(2,1)S(1)}, u32[]{:S(2)}, u32[]{:S(2)}) %collective-permute-start.6) | collective-permute-done | bytes 32800 | tf_op jit(solution)/shard_map/ppermute | solution.py:443
  34.5 0.6 collective-permute-start.8
  35.1 0.5 collective-permute-start.7
  35.6 3.2 %collective-permute-done.8.refs_6_ = bf16[128,256]{1,0:T(8,128)(2,1)S(1)} collective-permute-done((bf16[128,256]{1,0:T(8,128)(2,1)S(1)}, bf16[128,256]{1,0:T(8,128)(2,1)S(1)}, u32[]{:S(2)}, u32[]{:S(2)}) %collective-permute-start.8) | collective-permute-done | bytes 65568 | tf_op jit(solution)/shard_map/ppermute | solution.py:449
  38.9 1.2 %collective-permute-done.9.refs_7_ = bf16[128,256]{1,0:T(8,128)(2,1)S(1)} collective-permute-done((bf16[128,256]{1,0:T(8,128)(2,1)S(1)}, bf16[128,256]{1,0:T(8,128)(2,1)S(1)}, u32[]{:S(2)}, u32[]{:S(2)}) %collective-permute-start.9) | collective-permute-done | bytes 65568 | tf_op jit(solution)/shard_map/ppermute | solution.py:449
  40.1 0.9 copy-done.14
  41.1 6.8 %shard_map.159 = (f32[128,512]{1,0:T(8,128)S(1)}, f32[128,256]{1,0:T(8,128)S(1)}, f32[128,512]{1,0:T(8,128)S(1)}, f32[128,256]{1,0:T(8,128)S(1)}, f32[8,1024]{1,0:T(8,128)S(1)}) custom-call(bf16[128,512]{1,0:T(8,128)(2,1)S(1)} %copy-done.14, bf16[128,512]{1,0:T(8,128)(2,1)S(1)} %collective-permute-done.2.refs_1_, ...), custom_call_target="tpu_custom_call" | custom-call | flops 3221225472 | bytes 14000000 | tf_op jit(solution)/shard_map/pallas_call | solution.py:583
  47.9 0.2 collective-permute-start.10
  48.1 0.4 collective-permute-start.11
  48.5 1.2 %collective-permute-done.11.got = f32[128,256]{1,0:T(8,128)S(1)} collective-permute-done((f32[128,256]{1,0:T(8,128)S(1)}, f32[128,256]{1,0:T(8,128)S(1)}, u32[]{:S(2)}, u32[]{:S(2)}) %collective-permute-start.11) | collective-permute-done | bytes 131104 | tf_op jit(solution)/shard_map/ppermute | solution.py:449
  49.8 0.3 collective-permute-start.12
  50.0 2.8 %collective-permute-start.13 = (bf16[128,128]{1,0:T(8,128)(2,1)S(1)}, bf16[128,128]{1,0:T(8,128)(2,1)S(1)}, u32[]{:S(2)}, u32[]{:S(2)}) collective-permute-start(bf16[128,128]{1,0:T(8,128)(2,1)S(1)} %get-tuple-element.58), channel_id=1, source_target_pairs={{0,7},{1,2},{2,1},{3,4},{4,3},{5,6},{6,5},{7,0},{8,15},{9,10},{10,... | collective-permute-start | bytes 98312 | tf_op jit(solution)/shard_map/ppermute | solution.py:443
  52.9 0.8 collective-permute-done.12.from_first
  53.7 2.9 %collective-permute-done.13.from_second = bf16[128,128]{1,0:T(8,128)(2,1)S(1)} collective-permute-done((bf16[128,128]{1,0:T(8,128)(2,1)S(1)}, bf16[128,128]{1,0:T(8,128)(2,1)S(1)}, u32[]{:S(2)}, u32[]{:S(2)}) %collective-permute-start.13) | collective-permute-done | bytes 32800 | tf_op jit(solution)/shard_map/ppermute | solution.py:443
  56.8 3.5 %shard_map.161 = (f32[256,1792]{1,0:T(8,128)S(1)}, bf16[64,1792]{1,0:T(8,128)(2,1)S(1)}, bf16[192,1792]{1,0:T(8,128)(2,1)S(1)}) custom-call(f32[128,512]{1,0:T(8,128)S(1)} %get-tuple-element.53.own_mid, f32[128,512]{1,0:T(8,128)S(1)} %collective-permute-done.10.pair_mid, bf16[128,128]{1,0:T(8,128)(2,1)S(1)} %collective-permute-done.12.from_first, ...), custom_call_target="tpu_custom_call" | custom-call | flops 2415919104 | bytes 13992960 | tf_op jit(solution)/shard_map/pallas_call | solution.py:458
  60.2 0.1 collective-permute-start.14
  60.3 0.5 collective-permute-start.18
  60.8 2.0 %collective-permute-done.18.first = bf16[64,1792]{1,0:T(8,128)(2,1)S(1)} collective-permute-done((bf16[64,1792]{1,0:T(8,128)(2,1)S(1)}, bf16[64,1792]{1,0:T(8,128)(2,1)S(1)}, u32[]{:S(2)}, u32[]{:S(2)}) %collective-permute-start.18) | collective-permute-done | bytes 229408 | tf_op jit(solution)/shard_map/ppermute | solution.py:449
  62.7 0.1 shard_map.163
  62.9 0.6 collective-permute-start.19
  63.5 0.1 shard_map.162
  63.6 0.1 collective-permute-start.15
  63.6 0.1 collective-permute-start.16
  63.7 3.4 %collective-permute-start.17 = (bf16[32,1792]{1,0:T(8,128)(2,1)S(1)}, bf16[32,1792]{1,0:T(8,128)(2,1)S(1)}, u32[]{:S(2)}, u32[]{:S(2)}) collective-permute-start(bf16[32,1792]{1,0:T(8,128)(2,1)S(1)} %get-tuple-element.70), channel_id=1, source_target_pairs={{0,3},{1,2},{2,1},{3,0},{4,7},{5,6},{6,5},{7,4},{8,11},{9,10},{10,... | collective-permute-start | bytes 344072 | tf_op jit(solution)/shard_map/ppermute | solution.py:449
  67.1 3.5 %collective-permute-done.19.far = bf16[64,1792]{1,0:T(8,128)(2,1)S(1)} collective-permute-done((bf16[64,1792]{1,0:T(8,128)(2,1)S(1)}, bf16[64,1792]{1,0:T(8,128)(2,1)S(1)}, u32[]{:S(2)}, u32[]{:S(2)}) %collective-permute-start.19) | collective-permute-done | bytes 229408 | tf_op jit(solution)/shard_map/ppermute | solution.py:449
  70.6 0.1 shard_map.164
  70.7 0.1 collective-permute-start.20
  70.8 2.4 %collective-permute-start.21 = (bf16[16,1792]{1,0:T(8,128)(2,1)S(1)}, bf16[16,1792]{1,0:T(8,128)(2,1)S(1)}, u32[]{:S(2)}, u32[]{:S(2)}) collective-permute-start(bf16[16,1792]{1,0:T(8,128)(2,1)S(1)} %get-tuple-element.73), channel_id=1, source_target_pairs={{0,5},{1,4},{2,7},{3,6},{4,1},{5,0},{6,3},{7,2},{8,13},{9,12},{10,... | collective-permute-start | bytes 172040 | tf_op jit(solution)/shard_map/ppermute | solution.py:449
  73.1 3.4 %collective-permute-start.22 = (bf16[16,1792]{1,0:T(8,128)(2,1)S(1)}, bf16[16,1792]{1,0:T(8,128)(2,1)S(1)}, u32[]{:S(2)}, u32[]{:S(2)}) collective-permute-start(bf16[16,1792]{1,0:T(8,128)(2,1)S(1)} %get-tuple-element.74), channel_id=1, source_target_pairs={{0,6},{1,7},{2,4},{3,5},{4,2},{5,3},{6,0},{7,1},{8,14},{9,15},{10,... | collective-permute-start | bytes 172040 | tf_op jit(solution)/shard_map/ppermute | solution.py:449
  76.5 1.9 %collective-permute-start.23 = (bf16[16,1792]{1,0:T(8,128)(2,1)S(1)}, bf16[16,1792]{1,0:T(8,128)(2,1)S(1)}, u32[]{:S(2)}, u32[]{:S(2)}) collective-permute-start(bf16[16,1792]{1,0:T(8,128)(2,1)S(1)} %get-tuple-element.75), channel_id=1, source_target_pairs={{0,7},{1,6},{2,5},{3,4},{4,3},{5,2},{6,1},{7,0},{8,15},{9,14},{10,... | collective-permute-start | bytes 172040 | tf_op jit(solution)/shard_map/ppermute | solution.py:449
  78.4 0.1 shard_map.165
  78.5 0.6 collective-permute-start.24
  79.1 0.5 collective-permute-done.21.refs_4_
  79.6 0.2 collective-permute-done.22.refs_5_
  79.7 3.7 %collective-permute-done.23.refs_6_ = bf16[16,1792]{1,0:T(8,128)(2,1)S(1)} collective-permute-done((bf16[16,1792]{1,0:T(8,128)(2,1)S(1)}, bf16[16,1792]{1,0:T(8,128)(2,1)S(1)}, u32[]{:S(2)}, u32[]{:S(2)}) %collective-permute-start.23) | collective-permute-done | bytes 57376 | tf_op jit(solution)/shard_map/ppermute | solution.py:449
  83.4 0.1 shard_map.166.mine
  83.5 2.2 %collective-permute-start.29 = (bf16[16,1792]{1,0:T(8,128)(2,1)S(1)}, bf16[16,1792]{1,0:T(8,128)(2,1)S(1)}, u32[]{:S(2)}, u32[]{:S(2)}) collective-permute-start(bf16[16,1792]{1,0:T(8,128)(2,1)S(1)} %shard_map.166.mine), channel_id=1, source_target_pairs={{0,7},{1,6},{2,5},{3,4},{4,3},{5,2},{6,1},{7,0},{8,15},{9,14},{10,... | collective-permute-start | bytes 172040 | tf_op jit(solution)/shard_map/ppermute | solution.py:449
  85.7 1.4 %collective-permute-start.28 = (bf16[16,1792]{1,0:T(8,128)(2,1)S(1)}, bf16[16,1792]{1,0:T(8,128)(2,1)S(1)}, u32[]{:S(2)}, u32[]{:S(2)}) collective-permute-start(bf16[16,1792]{1,0:T(8,128)(2,1)S(1)} %shard_map.166.mine), channel_id=1, source_target_pairs={{0,6},{1,7},{2,4},{3,5},{4,2},{5,3},{6,0},{7,1},{8,14},{9,15},{10,... | collective-permute-start | bytes 172040 | tf_op jit(solution)/shard_map/ppermute | solution.py:449
  87.1 0.5 collective-permute-start.27
  87.6 3.6 %collective-permute-start.26 = (bf16[16,1792]{1,0:T(8,128)(2,1)S(1)}, bf16[16,1792]{1,0:T(8,128)(2,1)S(1)}, u32[]{:S(2)}, u32[]{:S(2)}) collective-permute-start(bf16[16,1792]{1,0:T(8,128)(2,1)S(1)} %shard_map.166.mine), channel_id=1, source_target_pairs={{0,4},{1,5},{2,6},{3,7},{4,0},{5,1},{6,2},{7,3},{8,12},{9,13},{10,... | collective-permute-start | bytes 172040 | tf_op jit(solution)/shard_map/ppermute | solution.py:449
  91.2 0.5 collective-permute-start.25
  91.8 2.6 %collective-permute-done.27.refs_1_ = bf16[16,1792]{1,0:T(8,128)(2,1)S(1)} collective-permute-done((bf16[16,1792]{1,0:T(8,128)(2,1)S(1)}, bf16[16,1792]{1,0:T(8,128)(2,1)S(1)}, u32[]{:S(2)}, u32[]{:S(2)}) %collective-permute-start.27) | collective-permute-done | bytes 57376 | tf_op jit(solution)/shard_map/ppermute | solution.py:449
  94.4 0.6 collective-permute-done.26.refs_0_
  95.0 0.4 collective-permute-done.25.other
  95.4 0.9 collective-permute-start.32
  96.3 1.1 %collective-permute-start.31 = (bf16[32,1792]{1,0:T(8,128)(2,1)S(1)}, bf16[32,1792]{1,0:T(8,128)(2,1)S(1)}, u32[]{:S(2)}, u32[]{:S(2)}) collective-permute-start(bf16[32,1792]{1,0:T(8,128)(2,1)S(1)} %shard_map.168.refs_0_), channel_id=1, source_target_pairs={{0,2},{1,3},{2,0},{3,1},{4,6},{5,7},{6,4},{7,5},{8,10},{9,11},{10,... | collective-permute-start | bytes 344072 | tf_op jit(solution)/shard_map/ppermute | solution.py:449
  97.4 1.6 %collective-permute-start.30 = (bf16[32,1792]{1,0:T(8,128)(2,1)S(1)}, bf16[32,1792]{1,0:T(8,128)(2,1)S(1)}, u32[]{:S(2)}, u32[]{:S(2)}) collective-permute-start(bf16[32,1792]{1,0:T(8,128)(2,1)S(1)} %shard_map.168.refs_0_), channel_id=1, source_target_pairs={{0,1},{1,0},{2,3},{3,2},{4,5},{5,4},{6,7},{7,6},{8,9},{9,8},{10,11... | collective-permute-start | bytes 344072 | tf_op jit(solution)/shard_map/ppermute | solution.py:449
  99.0 0.5 collective-permute-start.33
  99.5 1.7 %collective-permute-done.32.refs_3_ = bf16[32,1792]{1,0:T(8,128)(2,1)S(1)} collective-permute-done((bf16[32,1792]{1,0:T(8,128)(2,1)S(1)}, bf16[32,1792]{1,0:T(8,128)(2,1)S(1)}, u32[]{:S(2)}, u32[]{:S(2)}) %collective-permute-start.32) | collective-permute-done | bytes 114720 | tf_op jit(solution)/shard_map/ppermute | solution.py:449
  101.2 0.7 collective-permute-done.31.refs_2_
  101.8 0.5 collective-permute-done.30.refs_1_
  102.5 0.5 collective-permute-start.35
  103.0 2.0 %collective-permute-done.33.refs_2_ = bf16[64,1792]{1,0:T(8,128)(2,1)S(1)} collective-permute-done((bf16[64,1792]{1,0:T(8,128)(2,1)S(1)}, bf16[64,1792]{1,0:T(8,128)(2,1)S(1)}, u32[]{:S(2)}, u32[]{:S(2)}) %collective-permute-start.33) | collective-permute-done | bytes 229408 | tf_op jit(solution)/shard_map/ppermute | solution.py:449
  105.0 1.5 %collective-permute-done.36.refs_5_ = bf16[64,1792]{1,0:T(8,128)(2,1)S(1)} collective-permute-done((bf16[64,1792]{1,0:T(8,128)(2,1)S(1)}, bf16[64,1792]{1,0:T(8,128)(2,1)S(1)}, u32[]{:S(2)}, u32[]{:S(2)}) %collective-permute-start.36) | collective-permute-done | bytes 229408 | tf_op jit(solution)/shard_map/ppermute | solution.py:449
  106.5 2.0 %shard_map.170 = (f32[512,512]{1,0:T(8,128)}, f32[512,512]{1,0:T(8,128)}, f32[512,512]{1,0:T(8,128)}, f32[512,128]{1,0:T(8,128)}, f32[1,1]{1,0:T(1,128)}) custom-call(bf16[128,1792]{1,0:T(8,128)(2,1)S(1)} %shard_map.169.refs_0_, bf16[64,1792]{1,0:T(8,128)(2,1)S(1)} %shard_map.167.after.refs_1_, bf16[64,1792]{1,0:T(8,128)(2,1)S(1)} %collective-permute-done.33.refs_2_, ...), custom_call_target="tpu_custom_call" | custom-call | bytes 5505024 | tf_op jit(solution)/shard_map/pallas_call | solution.py:629
  (60 shorter events, 0.4 us)
Async XLA Ops:
  2.9 11.8 %collective-permute-start = (bf16[512,128]{1,0:T(8,128)(2,1)}, bf16[512,128]{1,0:T(8,128)(2,1)S(1)}, u32[]{:S(2)}, u32[]{:S(2)}) collective-permute-start(bf16[512,128]{1,0:T(8,128)(2,1)} %get-tuple-element.44), channel_id=1, source_target_pairs={{0,1},{1,0},{2,3},{3,2},{4,5},{5,4},{6,7},{7,6},{8,9},{9,8},{10,11... | collective-permute-start | bytes 393224 | tf_op jit(solution)/shard_map/ppermute | solution.py:449
  5.9 8.8 %collective-permute-start.1 = (bf16[512,128]{1,0:T(8,128)(2,1)}, bf16[512,128]{1,0:T(8,128)(2,1)S(1)}, u32[]{:S(2)}, u32[]{:S(2)}) collective-permute-start(bf16[512,128]{1,0:T(8,128)(2,1)} %get-tuple-element.45), channel_id=1, source_target_pairs={{0,7},{1,2},{2,1},{3,4},{4,3},{5,6},{6,5},{7,0},{8,15},{9,10},{10,... | collective-permute-start | bytes 393224 | tf_op jit(solution)/shard_map/ppermute | solution.py:443
  14.7 0.7 copy-start.15
  14.7 0.7 copy-start.16
  15.4 24.7 %copy-start.11 = (bf16[1536,2048]{1,0:T(8,128)(2,1)S(1)}, bf16[1536,2048]{1,0:T(8,128)(2,1)}, u32[]{:S(2)}) copy-start(bf16[1536,2048]{1,0:T(8,128)(2,1)} %get-tuple-element.50.refs_8_) | copy-start | bytes 18874372
  15.4 24.7 %copy-start.12 = (bf16[128,2048]{1,0:T(8,128)(2,1)S(1)}, bf16[128,2048]{1,0:T(8,128)(2,1)}, u32[]{:S(2)}) copy-start(bf16[128,2048]{1,0:T(8,128)(2,1)} %get-tuple-element.51.refs_9_) | copy-start | bytes 1572868
  15.4 24.7 %copy-start.13 = (bf16[128,2048]{1,0:T(8,128)(2,1)S(1)}, bf16[128,2048]{1,0:T(8,128)(2,1)}, u32[]{:S(2)}) copy-start(bf16[128,2048]{1,0:T(8,128)(2,1)} %get-tuple-element.52.refs_10_) | copy-start | bytes 1572868
  26.1 9.0 %collective-permute-start.3 = (bf16[128,512]{1,0:T(8,128)(2,1)}, bf16[128,512]{1,0:T(8,128)(2,1)S(1)}, u32[]{:S(2)}, u32[]{:S(2)}) collective-permute-start(bf16[128,512]{1,0:T(8,128)(2,1)} %get-tuple-element.47.refs_0_), channel_id=1, source_target_pairs={{0,16},{8,24},{16,0},{24,8},{1,17},{9,25},{17,1},{25,9},{2,18},{10... | collective-permute-start | bytes 393224 | tf_op jit(solution)/shard_map/ppermute | solution.py:449
  27.7 4.1 %collective-permute-start.5 = (bf16[128,128]{1,0:T(8,128)(2,1)}, bf16[128,128]{1,0:T(8,128)(2,1)S(1)}, u32[]{:S(2)}, u32[]{:S(2)}) collective-permute-start(bf16[128,128]{1,0:T(8,128)(2,1)} %get-tuple-element.48), channel_id=1, source_target_pairs={{0,1},{1,0},{2,3},{3,2},{4,5},{5,4},{6,7},{7,6},{8,9},{9,8},{10,11... | collective-permute-start | bytes 98312 | tf_op jit(solution)/shard_map/ppermute | solution.py:449
  27.7 6.8 %collective-permute-start.6 = (bf16[128,128]{1,0:T(8,128)(2,1)}, bf16[128,128]{1,0:T(8,128)(2,1)S(1)}, u32[]{:S(2)}, u32[]{:S(2)}) collective-permute-start(bf16[128,128]{1,0:T(8,128)(2,1)} %get-tuple-element.49), channel_id=1, source_target_pairs={{0,7},{1,2},{2,1},{3,4},{4,3},{5,6},{6,5},{7,0},{8,15},{9,10},{10,... | collective-permute-start | bytes 98312 | tf_op jit(solution)/shard_map/ppermute | solution.py:443
  30.7 8.2 %collective-permute-start.2 = (bf16[128,512]{1,0:T(8,128)(2,1)}, bf16[128,512]{1,0:T(8,128)(2,1)S(1)}, u32[]{:S(2)}, u32[]{:S(2)}) collective-permute-start(bf16[128,512]{1,0:T(8,128)(2,1)} %get-tuple-element.47.refs_0_), channel_id=1, source_target_pairs={{0,8},{8,0},{16,24},{24,16},{1,9},{9,1},{17,25},{25,17},{2,10},{10... | collective-permute-start | bytes 393224 | tf_op jit(solution)/shard_map/ppermute | solution.py:449
  34.5 4.3 %collective-permute-start.8 = (bf16[128,256]{1,0:T(8,128)(2,1)S(1)}, bf16[128,256]{1,0:T(8,128)(2,1)S(1)}, u32[]{:S(2)}, u32[]{:S(2)}) collective-permute-start(bf16[128,256]{1,0:T(8,128)(2,1)S(1)} %shard_map.158.refs_4_), channel_id=1, source_target_pairs={{0,16},{8,24},{16,0},{24,8},{1,17},{9,25},{17,1},{25,9},{2,18},{10... | collective-permute-start | bytes 196616 | tf_op jit(solution)/shard_map/ppermute | solution.py:449
  35.1 5.0 %collective-permute-start.4 = (bf16[128,512]{1,0:T(8,128)(2,1)S(1)}, bf16[128,512]{1,0:T(8,128)(2,1)S(1)}, u32[]{:S(2)}, u32[]{:S(2)}) collective-permute-start(bf16[128,512]{1,0:T(8,128)(2,1)S(1)} %collective-permute-done.3.refs_2_), channel_id=1, source_target_pairs={{0,8},{8,0},{16,24},{24,16},{1,9},{9,1},{17,25},{25,17},{2,10},{10... | collective-permute-start | bytes 393224 | tf_op jit(solution)/shard_map/ppermute | solution.py:449
  35.1 3.7 %collective-permute-start.7 = (bf16[128,256]{1,0:T(8,128)(2,1)S(1)}, bf16[128,256]{1,0:T(8,128)(2,1)S(1)}, u32[]{:S(2)}, u32[]{:S(2)}) collective-permute-start(bf16[128,256]{1,0:T(8,128)(2,1)S(1)} %shard_map.158.refs_4_), channel_id=1, source_target_pairs={{0,8},{8,0},{16,24},{24,16},{1,9},{9,1},{17,25},{25,17},{2,10},{10... | collective-permute-start | bytes 196616 | tf_op jit(solution)/shard_map/ppermute | solution.py:449
  38.9 1.3 %collective-permute-start.9 = (bf16[128,256]{1,0:T(8,128)(2,1)S(1)}, bf16[128,256]{1,0:T(8,128)(2,1)S(1)}, u32[]{:S(2)}, u32[]{:S(2)}) collective-permute-start(bf16[128,256]{1,0:T(8,128)(2,1)S(1)} %collective-permute-done.8.refs_6_), channel_id=1, source_target_pairs={{0,8},{8,0},{16,24},{24,16},{1,9},{9,1},{17,25},{25,17},{2,10},{10... | collective-permute-start | bytes 196616 | tf_op jit(solution)/shard_map/ppermute | solution.py:449
  40.1 0.9 copy-start.14
  41.0 15.6 %copy-start = (bf16[512,3072]{1,0:T(8,128)(2,1)S(1)}, bf16[512,3072]{1,0:T(8,128)(2,1)}, u32[]{:S(2)}) copy-start(bf16[512,3072]{1,0:T(8,128)(2,1)} %get-tuple-element.60.picked_t) | copy-start | bytes 9437188
  41.0 15.6 %copy-start.1 = (bf16[512,3072]{1,0:T(8,128)(2,1)S(1)}, bf16[512,3072]{1,0:T(8,128)(2,1)}, u32[]{:S(2)}) copy-start(bf16[512,3072]{1,0:T(8,128)(2,1)} %get-tuple-element.61.slope_t) | copy-start | bytes 9437188
  41.0 15.6 %copy-start.2 = (bf16[512,512]{1,0:T(8,128)(2,1)S(1)}, bf16[512,512]{1,0:T(8,128)(2,1)}, u32[]{:S(2)}) copy-start(bf16[512,512]{1,0:T(8,128)(2,1)} %get-tuple-element.43.after.nodes_in.nodes_t) | copy-start | bytes 1572868
  41.0 15.6 %copy-start.3 = (f32[512,512]{1,0:T(8,128)S(1)}, f32[512,512]{1,0:T(8,128)}, u32[]{:S(2)}) copy-start(f32[512,512]{1,0:T(8,128)} %get-tuple-element.62.slope_sum_t) | copy-start | bytes 3145732
  41.0 15.6 %copy-start.4 = (f32[512,512]{1,0:T(8,128)S(1)}, f32[512,512]{1,0:T(8,128)}, u32[]{:S(2)}) copy-start(f32[512,512]{1,0:T(8,128)} %get-tuple-element.64.upd_slope_t) | copy-start | bytes 3145732
  41.1 15.6 %copy-start.5 = (bf16[512,512]{1,0:T(8,128)(2,1)S(1)}, bf16[512,512]{1,0:T(8,128)(2,1)}, u32[]{:S(2)}) copy-start(bf16[512,512]{1,0:T(8,128)(2,1)} %vertex.1) | copy-start | bytes 1572868
  41.1 15.6 %copy-start.6 = (bf16[512,512]{1,0:T(8,128)(2,1)S(1)}, bf16[512,512]{1,0:T(8,128)(2,1)}, u32[]{:S(2)}) copy-start(bf16[512,512]{1,0:T(8,128)(2,1)} %get-tuple-element.63.agg_t) | copy-start | bytes 1572868
  41.1 15.6 %copy-start.7 = (bf16[512,512]{1,0:T(8,128)(2,1)S(1)}, bf16[512,512]{1,0:T(8,128)(2,1)}, u32[]{:S(2)}) copy-start(bf16[512,512]{1,0:T(8,128)(2,1)} %get-tuple-element.65.hidden_t) | copy-start | bytes 1572868
  41.1 15.6 %copy-start.8 = (bf16[512,128]{1,0:T(8,128)(2,1)S(1)}, bf16[512,128]{1,0:T(8,128)(2,1)}, u32[]{:S(2)}) copy-start(bf16[512,128]{1,0:T(8,128)(2,1)} %w_decode.1) | copy-start | bytes 393220
  41.1 15.6 %copy-start.9 = (s32[128]{0:T(128)S(1)}, s32[128]{0:T(128)}, u32[]{:S(2)}) copy-start(s32[128]{0:T(128)} %param.14) | copy-start | bytes 1540
  41.1 15.6 %copy-start.10 = (s32[128]{0:T(128)S(1)}, s32[128]{0:T(128)}, u32[]{:S(2)}) copy-start(s32[128]{0:T(128)} %param.15) | copy-start | bytes 1540
  47.9 8.7 %collective-permute-start.10 = (f32[128,512]{1,0:T(8,128)S(1)}, f32[128,512]{1,0:T(8,128)S(1)}, u32[]{:S(2)}, u32[]{:S(2)}) collective-permute-start(f32[128,512]{1,0:T(8,128)S(1)} %get-tuple-element.54), channel_id=1, source_target_pairs={{0,8},{8,0},{16,24},{24,16},{1,9},{9,1},{17,25},{25,17},{2,10},{10... | collective-permute-start | bytes 786440 | tf_op jit(solution)/shard_map/ppermute | solution.py:449
  48.1 1.6 %collective-permute-start.11 = (f32[128,256]{1,0:T(8,128)S(1)}, f32[128,256]{1,0:T(8,128)S(1)}, u32[]{:S(2)}, u32[]{:S(2)}) collective-permute-start(f32[128,256]{1,0:T(8,128)S(1)} %get-tuple-element.56), channel_id=1, source_target_pairs={{0,8},{8,0},{16,24},{24,16},{1,9},{9,1},{17,25},{25,17},{2,10},{10... | collective-permute-start | bytes 393224 | tf_op jit(solution)/shard_map/ppermute | solution.py:449
  49.8 4.0 %collective-permute-start.12 = (bf16[128,128]{1,0:T(8,128)(2,1)S(1)}, bf16[128,128]{1,0:T(8,128)(2,1)S(1)}, u32[]{:S(2)}, u32[]{:S(2)}) collective-permute-start(bf16[128,128]{1,0:T(8,128)(2,1)S(1)} %get-tuple-element.57), channel_id=1, source_target_pairs={{0,1},{1,0},{2,3},{3,2},{4,5},{5,4},{6,7},{7,6},{8,9},{9,8},{10,11... | collective-permute-start | bytes 98312 | tf_op jit(solution)/shard_map/ppermute | solution.py:449
  50.0 6.6 %collective-permute-start.13 = (bf16[128,128]{1,0:T(8,128)(2,1)S(1)}, bf16[128,128]{1,0:T(8,128)(2,1)S(1)}, u32[]{:S(2)}, u32[]{:S(2)}) collective-permute-start(bf16[128,128]{1,0:T(8,128)(2,1)S(1)} %get-tuple-element.58), channel_id=1, source_target_pairs={{0,7},{1,2},{2,1},{3,4},{4,3},{5,6},{6,5},{7,0},{8,15},{9,10},{10,... | collective-permute-start | bytes 98312 | tf_op jit(solution)/shard_map/ppermute | solution.py:443
  60.2 3.3 %collective-permute-start.14 = (bf16[192,1792]{1,0:T(8,128)(2,1)S(1)}, bf16[192,1792]{1,0:T(8,128)(2,1)S(1)}, u32[]{:S(2)}, u32[]{:S(2)}) collective-permute-start(bf16[192,1792]{1,0:T(8,128)(2,1)S(1)} %get-tuple-element.67), channel_id=1, source_target_pairs={{0,8},{8,0},{16,24},{24,16},{1,9},{9,1},{17,25},{25,17},{2,10},{10... | collective-permute-start | bytes 2064392 | tf_op jit(solution)/shard_map/ppermute | solution.py:449
  60.3 2.5 %collective-permute-start.18 = (bf16[64,1792]{1,0:T(8,128)(2,1)S(1)}, bf16[64,1792]{1,0:T(8,128)(2,1)S(1)}, u32[]{:S(2)}, u32[]{:S(2)}) collective-permute-start(bf16[64,1792]{1,0:T(8,128)(2,1)S(1)} %get-tuple-element.71), channel_id=1, source_target_pairs={{0,8},{8,0},{16,24},{24,16},{1,9},{9,1},{17,25},{25,17},{2,10},{10... | collective-permute-start | bytes 688136 | tf_op jit(solution)/shard_map/ppermute | solution.py:449
  62.9 7.7 %collective-permute-start.19 = (bf16[64,1792]{1,0:T(8,128)(2,1)S(1)}, bf16[64,1792]{1,0:T(8,128)(2,1)S(1)}, u32[]{:S(2)}, u32[]{:S(2)}) collective-permute-start(bf16[64,1792]{1,0:T(8,128)(2,1)S(1)} %shard_map.163), channel_id=1, source_target_pairs={{0,16},{8,24},{16,0},{24,8},{1,17},{9,25},{17,1},{25,9},{2,18},{10... | collective-permute-start | bytes 688136 | tf_op jit(solution)/shard_map/ppermute | solution.py:449
  63.6 9.5 %collective-permute-start.15 = (bf16[32,1792]{1,0:T(8,128)(2,1)S(1)}, bf16[32,1792]{1,0:T(8,128)(2,1)S(1)}, u32[]{:S(2)}, u32[]{:S(2)}) collective-permute-start(bf16[32,1792]{1,0:T(8,128)(2,1)S(1)} %get-tuple-element.68), channel_id=1, source_target_pairs={{0,1},{1,0},{2,3},{3,2},{4,5},{5,4},{6,7},{7,6},{8,9},{9,8},{10,11... | collective-permute-start | bytes 344072 | tf_op jit(solution)/shard_map/ppermute | solution.py:449
  63.6 12.9 %collective-permute-start.16 = (bf16[32,1792]{1,0:T(8,128)(2,1)S(1)}, bf16[32,1792]{1,0:T(8,128)(2,1)S(1)}, u32[]{:S(2)}, u32[]{:S(2)}) collective-permute-start(bf16[32,1792]{1,0:T(8,128)(2,1)S(1)} %get-tuple-element.69), channel_id=1, source_target_pairs={{0,2},{1,3},{2,0},{3,1},{4,6},{5,7},{6,4},{7,5},{8,10},{9,11},{10,... | collective-permute-start | bytes 344072 | tf_op jit(solution)/shard_map/ppermute | solution.py:449
  63.7 14.7 %collective-permute-start.17 = (bf16[32,1792]{1,0:T(8,128)(2,1)S(1)}, bf16[32,1792]{1,0:T(8,128)(2,1)S(1)}, u32[]{:S(2)}, u32[]{:S(2)}) collective-permute-start(bf16[32,1792]{1,0:T(8,128)(2,1)S(1)} %get-tuple-element.70), channel_id=1, source_target_pairs={{0,3},{1,2},{2,1},{3,0},{4,7},{5,6},{6,5},{7,4},{8,11},{9,10},{10,... | collective-permute-start | bytes 344072 | tf_op jit(solution)/shard_map/ppermute | solution.py:449
  70.7 8.4 %collective-permute-start.20 = (bf16[16,1792]{1,0:T(8,128)(2,1)S(1)}, bf16[16,1792]{1,0:T(8,128)(2,1)S(1)}, u32[]{:S(2)}, u32[]{:S(2)}) collective-permute-start(bf16[16,1792]{1,0:T(8,128)(2,1)S(1)} %get-tuple-element.72), channel_id=1, source_target_pairs={{0,4},{1,5},{2,6},{3,7},{4,0},{5,1},{6,2},{7,3},{8,12},{9,13},{10,... | collective-permute-start | bytes 172040 | tf_op jit(solution)/shard_map/ppermute | solution.py:449
  70.8 8.8 %collective-permute-start.21 = (bf16[16,1792]{1,0:T(8,128)(2,1)S(1)}, bf16[16,1792]{1,0:T(8,128)(2,1)S(1)}, u32[]{:S(2)}, u32[]{:S(2)}) collective-permute-start(bf16[16,1792]{1,0:T(8,128)(2,1)S(1)} %get-tuple-element.73), channel_id=1, source_target_pairs={{0,5},{1,4},{2,7},{3,6},{4,1},{5,0},{6,3},{7,2},{8,13},{9,12},{10,... | collective-permute-start | bytes 172040 | tf_op jit(solution)/shard_map/ppermute | solution.py:449
  73.1 6.6 %collective-permute-start.22 = (bf16[16,1792]{1,0:T(8,128)(2,1)S(1)}, bf16[16,1792]{1,0:T(8,128)(2,1)S(1)}, u32[]{:S(2)}, u32[]{:S(2)}) collective-permute-start(bf16[16,1792]{1,0:T(8,128)(2,1)S(1)} %get-tuple-element.74), channel_id=1, source_target_pairs={{0,6},{1,7},{2,4},{3,5},{4,2},{5,3},{6,0},{7,1},{8,14},{9,15},{10,... | collective-permute-start | bytes 172040 | tf_op jit(solution)/shard_map/ppermute | solution.py:449
  76.5 6.9 %collective-permute-start.23 = (bf16[16,1792]{1,0:T(8,128)(2,1)S(1)}, bf16[16,1792]{1,0:T(8,128)(2,1)S(1)}, u32[]{:S(2)}, u32[]{:S(2)}) collective-permute-start(bf16[16,1792]{1,0:T(8,128)(2,1)S(1)} %get-tuple-element.75), channel_id=1, source_target_pairs={{0,7},{1,6},{2,5},{3,4},{4,3},{5,2},{6,1},{7,0},{8,15},{9,14},{10,... | collective-permute-start | bytes 172040 | tf_op jit(solution)/shard_map/ppermute | solution.py:449
  78.5 4.9 %collective-permute-start.24 = (bf16[16,1792]{1,0:T(8,128)(2,1)S(1)}, bf16[16,1792]{1,0:T(8,128)(2,1)S(1)}, u32[]{:S(2)}, u32[]{:S(2)}) collective-permute-start(bf16[16,1792]{1,0:T(8,128)(2,1)S(1)} %shard_map.165), channel_id=1, source_target_pairs={{0,16},{8,24},{16,0},{24,8},{1,17},{9,25},{17,1},{25,9},{2,18},{10... | collective-permute-start | bytes 172040 | tf_op jit(solution)/shard_map/ppermute | solution.py:449
  83.5 8.3 %collective-permute-start.29 = (bf16[16,1792]{1,0:T(8,128)(2,1)S(1)}, bf16[16,1792]{1,0:T(8,128)(2,1)S(1)}, u32[]{:S(2)}, u32[]{:S(2)}) collective-permute-start(bf16[16,1792]{1,0:T(8,128)(2,1)S(1)} %shard_map.166.mine), channel_id=1, source_target_pairs={{0,7},{1,6},{2,5},{3,4},{4,3},{5,2},{6,1},{7,0},{8,15},{9,14},{10,... | collective-permute-start | bytes 172040 | tf_op jit(solution)/shard_map/ppermute | solution.py:449
  85.7 6.1 %collective-permute-start.28 = (bf16[16,1792]{1,0:T(8,128)(2,1)S(1)}, bf16[16,1792]{1,0:T(8,128)(2,1)S(1)}, u32[]{:S(2)}, u32[]{:S(2)}) collective-permute-start(bf16[16,1792]{1,0:T(8,128)(2,1)S(1)} %shard_map.166.mine), channel_id=1, source_target_pairs={{0,6},{1,7},{2,4},{3,5},{4,2},{5,3},{6,0},{7,1},{8,14},{9,15},{10,... | collective-permute-start | bytes 172040 | tf_op jit(solution)/shard_map/ppermute | solution.py:449
  87.1 7.3 %collective-permute-start.27 = (bf16[16,1792]{1,0:T(8,128)(2,1)S(1)}, bf16[16,1792]{1,0:T(8,128)(2,1)S(1)}, u32[]{:S(2)}, u32[]{:S(2)}) collective-permute-start(bf16[16,1792]{1,0:T(8,128)(2,1)S(1)} %shard_map.166.mine), channel_id=1, source_target_pairs={{0,5},{1,4},{2,7},{3,6},{4,1},{5,0},{6,3},{7,2},{8,13},{9,12},{10,... | collective-permute-start | bytes 172040 | tf_op jit(solution)/shard_map/ppermute | solution.py:449
  87.6 7.4 %collective-permute-start.26 = (bf16[16,1792]{1,0:T(8,128)(2,1)S(1)}, bf16[16,1792]{1,0:T(8,128)(2,1)S(1)}, u32[]{:S(2)}, u32[]{:S(2)}) collective-permute-start(bf16[16,1792]{1,0:T(8,128)(2,1)S(1)} %shard_map.166.mine), channel_id=1, source_target_pairs={{0,4},{1,5},{2,6},{3,7},{4,0},{5,1},{6,2},{7,3},{8,12},{9,13},{10,... | collective-permute-start | bytes 172040 | tf_op jit(solution)/shard_map/ppermute | solution.py:449
  91.2 4.2 %collective-permute-start.25 = (bf16[16,1792]{1,0:T(8,128)(2,1)S(1)}, bf16[16,1792]{1,0:T(8,128)(2,1)S(1)}, u32[]{:S(2)}, u32[]{:S(2)}) collective-permute-start(bf16[16,1792]{1,0:T(8,128)(2,1)S(1)} %shard_map.166.mine), channel_id=1, source_target_pairs={{0,16},{8,24},{16,0},{24,8},{1,17},{9,25},{17,1},{25,9},{2,18},{10... | collective-permute-start | bytes 172040 | tf_op jit(solution)/shard_map/ppermute | solution.py:449
  95.4 5.8 %collective-permute-start.32 = (bf16[32,1792]{1,0:T(8,128)(2,1)S(1)}, bf16[32,1792]{1,0:T(8,128)(2,1)S(1)}, u32[]{:S(2)}, u32[]{:S(2)}) collective-permute-start(bf16[32,1792]{1,0:T(8,128)(2,1)S(1)} %shard_map.168.refs_0_), channel_id=1, source_target_pairs={{0,3},{1,2},{2,1},{3,0},{4,7},{5,6},{6,5},{7,4},{8,11},{9,10},{10,... | collective-permute-start | bytes 344072 | tf_op jit(solution)/shard_map/ppermute | solution.py:449
  96.3 5.6 %collective-permute-start.31 = (bf16[32,1792]{1,0:T(8,128)(2,1)S(1)}, bf16[32,1792]{1,0:T(8,128)(2,1)S(1)}, u32[]{:S(2)}, u32[]{:S(2)}) collective-permute-start(bf16[32,1792]{1,0:T(8,128)(2,1)S(1)} %shard_map.168.refs_0_), channel_id=1, source_target_pairs={{0,2},{1,3},{2,0},{3,1},{4,6},{5,7},{6,4},{7,5},{8,10},{9,11},{10,... | collective-permute-start | bytes 344072 | tf_op jit(solution)/shard_map/ppermute | solution.py:449
  97.4 5.0 %collective-permute-start.30 = (bf16[32,1792]{1,0:T(8,128)(2,1)S(1)}, bf16[32,1792]{1,0:T(8,128)(2,1)S(1)}, u32[]{:S(2)}, u32[]{:S(2)}) collective-permute-start(bf16[32,1792]{1,0:T(8,128)(2,1)S(1)} %shard_map.168.refs_0_), channel_id=1, source_target_pairs={{0,1},{1,0},{2,3},{3,2},{4,5},{5,4},{6,7},{7,6},{8,9},{9,8},{10,11... | collective-permute-start | bytes 344072 | tf_op jit(solution)/shard_map/ppermute | solution.py:449
  99.0 6.0 %collective-permute-start.33 = (bf16[64,1792]{1,0:T(8,128)(2,1)S(1)}, bf16[64,1792]{1,0:T(8,128)(2,1)S(1)}, u32[]{:S(2)}, u32[]{:S(2)}) collective-permute-start(bf16[64,1792]{1,0:T(8,128)(2,1)S(1)} %shard_map.167.after.refs_1_), channel_id=1, source_target_pairs={{0,16},{8,24},{16,0},{24,8},{1,17},{9,25},{17,1},{25,9},{2,18},{10... | collective-permute-start | bytes 688136 | tf_op jit(solution)/shard_map/ppermute | solution.py:449
  102.4 4.0 %collective-permute-start.34 = (bf16[128,1792]{1,0:T(8,128)(2,1)S(1)}, bf16[128,1792]{1,0:T(8,128)(2,1)S(1)}, u32[]{:S(2)}, u32[]{:S(2)}) collective-permute-start(bf16[128,1792]{1,0:T(8,128)(2,1)S(1)} %shard_map.169.refs_0_), channel_id=1, source_target_pairs={{0,8},{8,0},{16,24},{24,16},{1,9},{9,1},{17,25},{25,17},{2,10},{10... | collective-permute-start | bytes 1376264 | tf_op jit(solution)/shard_map/ppermute | solution.py:449
  102.5 2.5 %collective-permute-start.35 = (bf16[64,1792]{1,0:T(8,128)(2,1)S(1)}, bf16[64,1792]{1,0:T(8,128)(2,1)S(1)}, u32[]{:S(2)}, u32[]{:S(2)}) collective-permute-start(bf16[64,1792]{1,0:T(8,128)(2,1)S(1)} %shard_map.167.after.refs_1_), channel_id=1, source_target_pairs={{0,8},{8,0},{16,24},{24,16},{1,9},{9,1},{17,25},{25,17},{2,10},{10... | collective-permute-start | bytes 688136 | tf_op jit(solution)/shard_map/ppermute | solution.py:449
  105.0 1.5 %collective-permute-start.36 = (bf16[64,1792]{1,0:T(8,128)(2,1)S(1)}, bf16[64,1792]{1,0:T(8,128)(2,1)S(1)}, u32[]{:S(2)}, u32[]{:S(2)}) collective-permute-start(bf16[64,1792]{1,0:T(8,128)(2,1)S(1)} %collective-permute-done.33.refs_2_), channel_id=1, source_target_pairs={{0,8},{8,0},{16,24},{24,16},{1,9},{9,1},{17,25},{25,17},{2,10},{10... | collective-permute-start | bytes 688136 | tf_op jit(solution)/shard_map/ppermute | solution.py:449

commit v9 on v8

--- a/solution.py
+++ b/solution.py
@@ -453,13 +453,17 @@
     return sum(x.size * x.dtype.itemsize for x in arrays)
 
 
-def call(kernel, ins, outs, scratch=(), flops=0, room=4, in_hbm=0, out_hbm=0, limit=0):
+def freed(specs, places):
+    return [pl.BlockSpec(memory_space=pl.ANY) if i in places else x for i, x in enumerate(specs)]
+
+
+def call(kernel, ins, outs, scratch=(), flops=0, room=4, in_hbm=0, out_hbm=0, limit=0, free_ins=(), free_outs=()):
     size = nbytes(list(ins) + list(outs))
     return pl.pallas_call(
         kernel,
         out_shape=outs,
-        in_specs=vmem(len(ins) - in_hbm) + [HBM] * in_hbm,
-        out_specs=vmem(len(outs) - out_hbm) + [HBM] * out_hbm,
+        in_specs=freed(vmem(len(ins) - in_hbm) + [HBM] * in_hbm, free_ins),
+        out_specs=freed(vmem(len(outs) - out_hbm) + [HBM] * out_hbm, free_outs),
         scratch_shapes=list(scratch),
         compiler_params=params(limit or 1.1 * size / MIB + room),
         cost_estimate=cost(flops, size),
@@ -571,7 +575,9 @@
         flops=2 * degree * width * count * (ext_rows + width),
         in_hbm=11,
         out_hbm=9,
-        limit=56,
+        free_ins=(1, 2),
+        free_outs=(0, 1, 2),
+        limit=52,
     )
     lent = meet(first_t, second_t)
     mids = gathered(field_t)

time: 109 us -> 108 us (level)
  no operation moved by 1% of the time
where the time goes in v9:
time: 108 us; the launch traced here: 107 us
  starting transfers between devices  41.9 us (39%)
  waiting for transfers between devices  32.8 us (30%)
  Pallas kernels  30.9 us (29%)
  between operations  1.11 us (1%)
    ppermute x34, starting transfers between devices, flip(): return lax.ppermute(value, axis, [(i, i ^ bit) for i in range(size)])  32.5 us
    ppermute x34, waiting for transfers between devices, flip(): return lax.ppermute(value, axis, [(i, i ^ bit) for i in range(size)])  27.2 us
    pallas_call x13, Pallas kernels, call(): pl.pallas_call(kernel, out_shape=outs, in_specs=freed(vmem(len(ins) - in_...  16.9 us
    ppermute x3, starting transfers between devices, meet(): lax.ppermute(second, 'dom', [(i, (i + (1 if i % 2 else size - 1)) % size)...  9.42 us
    pallas_call x1, Pallas kernels, per_device(): pl.pallas_call(functools.partial(readout_kernel, line_span), grid=(steps,...  6.8 us
    ppermute x3, waiting for transfers between devices, meet(): lax.ppermute(second, 'dom', [(i, (i + (1 if i % 2 else size - 1)) % size)...  5.62 us
    pallas_call x1, Pallas kernels, per_device(): pl.pallas_call(decoder_kernel, grid_spec=pltpu.PrefetchScalarGridSpec(num...  5.2 us
  transfers between devices with their start and end apart: 37, of which 20 were waited for; matrix products, arithmetic and copies ran while one was open for 0% of the time, Pallas kernels for 5%

profile of v9, /device:TPU:0, one launch (start us, length us, event | category | flops | bytes accessed | tf_op | source)
XLA Modules:
  0.0 107.4 jit_solution(6477367873994327478)
XLA Ops:
  0.7 2.3 %shard_map.155 = (bf16[512,512]{1,0:T(8,128)(2,1)}, bf16[512,128]{1,0:T(8,128)(2,1)}, bf16[512,128]{1,0:T(8,128)(2,1)}) custom-call(bf16[512,512]{1,0:T(8,128)(2,1)} %bitcast.11, s32[1,128]{1,0:T(1,128)} %bitcast.5, s32[1,128]{1,0:T(1,128)} %bitcast.8), custom_call_target="tpu_custom_call" | custom-call | flops 134217728 | bytes 1311744 | tf_op jit(solution)/shard_map/pallas_call | solution.py:462
  3.0 3.0 %collective-permute-start = (bf16[512,128]{1,0:T(8,128)(2,1)}, bf16[512,128]{1,0:T(8,128)(2,1)S(1)}, u32[]{:S(2)}, u32[]{:S(2)}) collective-permute-start(bf16[512,128]{1,0:T(8,128)(2,1)} %get-tuple-element.44), channel_id=1, source_target_pairs={{0,1},{1,0},{2,3},{3,2},{4,5},{5,4},{6,7},{7,6},{8,9},{9,8},{10,11... | collective-permute-start | bytes 393224 | tf_op jit(solution)/shard_map/ppermute | solution.py:449
  6.0 3.5 %collective-permute-start.1 = (bf16[512,128]{1,0:T(8,128)(2,1)}, bf16[512,128]{1,0:T(8,128)(2,1)S(1)}, u32[]{:S(2)}, u32[]{:S(2)}) collective-permute-start(bf16[512,128]{1,0:T(8,128)(2,1)} %get-tuple-element.45), channel_id=1, source_target_pairs={{0,7},{1,2},{2,1},{3,4},{4,3},{5,6},{6,5},{7,0},{8,15},{9,10},{10,... | collective-permute-start | bytes 393224 | tf_op jit(solution)/shard_map/ppermute | solution.py:443
  9.5 5.2 %shard_map.156 = (bf16[1536,2048]{1,0:T(8,128)(2,1)}, bf16[128,2048]{1,0:T(8,128)(2,1)}, bf16[128,2048]{1,0:T(8,128)(2,1)}, f32[8,128]{1,0:T(8,128)}) custom-call(s32[1]{0:T(128)} %bitcast.3.core, s32[3,4096]{1,0:T(4,128)} %vertices.1, f32[3,4096]{1,0:T(4,128)} %weights.1, bf16[4096,128]{1,0:T(8,128)(2,1)} %base.1, bf16[4096,128]{1,0:T(8,128)(2,1)} %truth.1, ...), custom_call_target="tpu_custom_call" | custom-call | flops 15728640 | bytes 16000000 | tf_op jit(solution)/shard_map/pallas_call | solution.py:546
  14.8 0.7 copy-done.13
  15.5 10.5 %shard_map.157 = (bf16[128,512]{1,0:T(8,128)(2,1)S(1)}, bf16[128,128]{1,0:T(8,128)(2,1)S(1)}, bf16[128,128]{1,0:T(8,128)(2,1)S(1)}, bf16[512,3072]{1,0:T(8,128)(...) custom-call(bf16[512,512]{1,0:T(8,128)(2,1)} %get-tuple-element.43.a, ...), custom_call_target="tpu_custom_call" | custom-call | flops 4026531840 | bytes 12141568 | tf_op jit(solution)/shard_map/pallas_call | solution.py:462
  26.0 1.6 %collective-permute-start.3 = (bf16[128,512]{1,0:T(8,128)(2,1)S(1)}, bf16[128,512]{1,0:T(8,128)(2,1)S(1)}, u32[]{:S(2)}, u32[]{:S(2)}) collective-permute-start(bf16[128,512]{1,0:T(8,128)(2,1)S(1)} %get-tuple-element.47.refs_0_), channel_id=1, source_target_pairs={{0,16},{8,24},{16,0},{24,8},{1,17},{9,25},{17,1},{25,9},{2,18},{10... | collective-permute-start | bytes 393224 | tf_op jit(solution)/shard_map/ppermute | solution.py:449
  27.6 3.0 %collective-permute-start.6 = (bf16[128,128]{1,0:T(8,128)(2,1)S(1)}, bf16[128,128]{1,0:T(8,128)(2,1)S(1)}, u32[]{:S(2)}, u32[]{:S(2)}) collective-permute-start(bf16[128,128]{1,0:T(8,128)(2,1)S(1)} %get-tuple-element.49), channel_id=1, source_target_pairs={{0,7},{1,2},{2,1},{3,4},{4,3},{5,6},{6,5},{7,0},{8,15},{9,10},{10,... | collective-permute-start | bytes 98312 | tf_op jit(solution)/shard_map/ppermute | solution.py:443
  30.6 0.9 collective-permute-done.5.first
  31.5 2.7 %collective-permute-done.6.second = bf16[128,128]{1,0:T(8,128)(2,1)S(1)} collective-permute-done((bf16[128,128]{1,0:T(8,128)(2,1)S(1)}, bf16[128,128]{1,0:T(8,128)(2,1)S(1)}, u32[]{:S(2)}, u32[]{:S(2)}) %collective-permute-start.6) | collective-permute-done | bytes 32800 | tf_op jit(solution)/shard_map/ppermute | solution.py:443
  34.2 0.6 collective-permute-start.8
  34.8 0.5 collective-permute-start.7
  35.4 3.2 %collective-permute-done.8.refs_6_ = bf16[128,256]{1,0:T(8,128)(2,1)S(1)} collective-permute-done((bf16[128,256]{1,0:T(8,128)(2,1)S(1)}, bf16[128,256]{1,0:T(8,128)(2,1)S(1)}, u32[]{:S(2)}, u32[]{:S(2)}) %collective-permute-start.8) | collective-permute-done | bytes 65568 | tf_op jit(solution)/shard_map/ppermute | solution.py:449
  38.6 1.2 %collective-permute-done.9.refs_7_ = bf16[128,256]{1,0:T(8,128)(2,1)S(1)} collective-permute-done((bf16[128,256]{1,0:T(8,128)(2,1)S(1)}, bf16[128,256]{1,0:T(8,128)(2,1)S(1)}, u32[]{:S(2)}, u32[]{:S(2)}) %collective-permute-start.9) | collective-permute-done | bytes 65568 | tf_op jit(solution)/shard_map/ppermute | solution.py:449
  39.9 6.8 %shard_map.159 = (f32[128,512]{1,0:T(8,128)S(1)}, f32[128,256]{1,0:T(8,128)S(1)}, f32[128,512]{1,0:T(8,128)S(1)}, f32[128,256]{1,0:T(8,128)S(1)}, f32[8,1024]{1,0:T(8,128)S(1)}) custom-call(bf16[128,512]{1,0:T(8,128)(2,1)S(1)} %get-tuple-element.47.refs_0_, bf16[128,512]{1,0:T(8,128)(2,1)S(1)} %collective-permute-done.2.refs_1_, ...), custom_call_target="tpu_custom_call" | custom-call | flops 3221225472 | bytes 14000000 | tf_op jit(solution)/shard_map/pallas_call | solution.py:589
  46.7 0.2 collective-permute-start.10
  46.9 0.4 collective-permute-start.11
  47.3 1.2 %collective-permute-done.11.got = f32[128,256]{1,0:T(8,128)S(1)} collective-permute-done((f32[128,256]{1,0:T(8,128)S(1)}, f32[128,256]{1,0:T(8,128)S(1)}, u32[]{:S(2)}, u32[]{:S(2)}) %collective-permute-start.11) | collective-permute-done | bytes 131104 | tf_op jit(solution)/shard_map/ppermute | solution.py:449
  48.5 0.3 collective-permute-start.12
  48.8 2.9 %collective-permute-start.13 = (bf16[128,128]{1,0:T(8,128)(2,1)S(1)}, bf16[128,128]{1,0:T(8,128)(2,1)S(1)}, u32[]{:S(2)}, u32[]{:S(2)}) collective-permute-start(bf16[128,128]{1,0:T(8,128)(2,1)S(1)} %get-tuple-element.58), channel_id=1, source_target_pairs={{0,7},{1,2},{2,1},{3,4},{4,3},{5,6},{6,5},{7,0},{8,15},{9,10},{10,... | collective-permute-start | bytes 98312 | tf_op jit(solution)/shard_map/ppermute | solution.py:443
  51.7 0.8 collective-permute-done.12.from_first
  52.5 2.9 %collective-permute-done.13.from_second = bf16[128,128]{1,0:T(8,128)(2,1)S(1)} collective-permute-done((bf16[128,128]{1,0:T(8,128)(2,1)S(1)}, bf16[128,128]{1,0:T(8,128)(2,1)S(1)}, u32[]{:S(2)}, u32[]{:S(2)}) %collective-permute-start.13) | collective-permute-done | bytes 32800 | tf_op jit(solution)/shard_map/ppermute | solution.py:443
  55.5 3.5 %shard_map.161 = (f32[256,1792]{1,0:T(8,128)S(1)}, bf16[64,1792]{1,0:T(8,128)(2,1)S(1)}, bf16[192,1792]{1,0:T(8,128)(2,1)S(1)}) custom-call(f32[128,512]{1,0:T(8,128)S(1)} %get-tuple-element.53.own_mid, f32[128,512]{1,0:T(8,128)S(1)} %collective-permute-done.10.pair_mid, bf16[128,128]{1,0:T(8,128)(2,1)S(1)} %collective-permute-done.12.from_first, ...), custom_call_target="tpu_custom_call" | custom-call | flops 2415919104 | bytes 13992960 | tf_op jit(solution)/shard_map/pallas_call | solution.py:462
  59.0 0.1 collective-permute-start.14
  59.0 0.5 collective-permute-start.18
  59.5 2.0 %collective-permute-done.18.first = bf16[64,1792]{1,0:T(8,128)(2,1)S(1)} collective-permute-done((bf16[64,1792]{1,0:T(8,128)(2,1)S(1)}, bf16[64,1792]{1,0:T(8,128)(2,1)S(1)}, u32[]{:S(2)}, u32[]{:S(2)}) %collective-permute-start.18) | collective-permute-done | bytes 229408 | tf_op jit(solution)/shard_map/ppermute | solution.py:449
  61.5 0.1 shard_map.163
  61.6 0.6 collective-permute-start.19
  62.2 0.1 shard_map.162
  62.3 0.1 collective-permute-start.15
  62.4 0.1 collective-permute-start.16
  62.5 3.4 %collective-permute-start.17 = (bf16[32,1792]{1,0:T(8,128)(2,1)S(1)}, bf16[32,1792]{1,0:T(8,128)(2,1)S(1)}, u32[]{:S(2)}, u32[]{:S(2)}) collective-permute-start(bf16[32,1792]{1,0:T(8,128)(2,1)S(1)} %get-tuple-element.70), channel_id=1, source_target_pairs={{0,3},{1,2},{2,1},{3,0},{4,7},{5,6},{6,5},{7,4},{8,11},{9,10},{10,... | collective-permute-start | bytes 344072 | tf_op jit(solution)/shard_map/ppermute | solution.py:449
  65.9 3.4 %collective-permute-done.19.far = bf16[64,1792]{1,0:T(8,128)(2,1)S(1)} collective-permute-done((bf16[64,1792]{1,0:T(8,128)(2,1)S(1)}, bf16[64,1792]{1,0:T(8,128)(2,1)S(1)}, u32[]{:S(2)}, u32[]{:S(2)}) %collective-permute-start.19) | collective-permute-done | bytes 229408 | tf_op jit(solution)/shard_map/ppermute | solution.py:449
  69.3 0.1 shard_map.164
  69.4 0.1 collective-permute-start.20
  69.5 2.4 %collective-permute-start.21 = (bf16[16,1792]{1,0:T(8,128)(2,1)S(1)}, bf16[16,1792]{1,0:T(8,128)(2,1)S(1)}, u32[]{:S(2)}, u32[]{:S(2)}) collective-permute-start(bf16[16,1792]{1,0:T(8,128)(2,1)S(1)} %get-tuple-element.73), channel_id=1, source_target_pairs={{0,5},{1,4},{2,7},{3,6},{4,1},{5,0},{6,3},{7,2},{8,13},{9,12},{10,... | collective-permute-start | bytes 172040 | tf_op jit(solution)/shard_map/ppermute | solution.py:449
  71.9 3.4 %collective-permute-start.22 = (bf16[16,1792]{1,0:T(8,128)(2,1)S(1)}, bf16[16,1792]{1,0:T(8,128)(2,1)S(1)}, u32[]{:S(2)}, u32[]{:S(2)}) collective-permute-start(bf16[16,1792]{1,0:T(8,128)(2,1)S(1)} %get-tuple-element.74), channel_id=1, source_target_pairs={{0,6},{1,7},{2,4},{3,5},{4,2},{5,3},{6,0},{7,1},{8,14},{9,15},{10,... | collective-permute-start | bytes 172040 | tf_op jit(solution)/shard_map/ppermute | solution.py:449
  75.3 1.9 %collective-permute-start.23 = (bf16[16,1792]{1,0:T(8,128)(2,1)S(1)}, bf16[16,1792]{1,0:T(8,128)(2,1)S(1)}, u32[]{:S(2)}, u32[]{:S(2)}) collective-permute-start(bf16[16,1792]{1,0:T(8,128)(2,1)S(1)} %get-tuple-element.75), channel_id=1, source_target_pairs={{0,7},{1,6},{2,5},{3,4},{4,3},{5,2},{6,1},{7,0},{8,15},{9,14},{10,... | collective-permute-start | bytes 172040 | tf_op jit(solution)/shard_map/ppermute | solution.py:449
  77.2 0.1 shard_map.165
  77.2 0.6 collective-permute-start.24
  77.8 0.5 collective-permute-done.21.refs_4_
  78.3 0.2 collective-permute-done.22.refs_5_
  78.5 3.7 %collective-permute-done.23.refs_6_ = bf16[16,1792]{1,0:T(8,128)(2,1)S(1)} collective-permute-done((bf16[16,1792]{1,0:T(8,128)(2,1)S(1)}, bf16[16,1792]{1,0:T(8,128)(2,1)S(1)}, u32[]{:S(2)}, u32[]{:S(2)}) %collective-permute-start.23) | collective-permute-done | bytes 57376 | tf_op jit(solution)/shard_map/ppermute | solution.py:449
  82.2 0.1 shard_map.166.mine
  82.3 2.2 %collective-permute-start.29 = (bf16[16,1792]{1,0:T(8,128)(2,1)S(1)}, bf16[16,1792]{1,0:T(8,128)(2,1)S(1)}, u32[]{:S(2)}, u32[]{:S(2)}) collective-permute-start(bf16[16,1792]{1,0:T(8,128)(2,1)S(1)} %shard_map.166.mine), channel_id=1, source_target_pairs={{0,7},{1,6},{2,5},{3,4},{4,3},{5,2},{6,1},{7,0},{8,15},{9,14},{10,... | collective-permute-start | bytes 172040 | tf_op jit(solution)/shard_map/ppermute | solution.py:449
  84.5 1.4 %collective-permute-start.28 = (bf16[16,1792]{1,0:T(8,128)(2,1)S(1)}, bf16[16,1792]{1,0:T(8,128)(2,1)S(1)}, u32[]{:S(2)}, u32[]{:S(2)}) collective-permute-start(bf16[16,1792]{1,0:T(8,128)(2,1)S(1)} %shard_map.166.mine), channel_id=1, source_target_pairs={{0,6},{1,7},{2,4},{3,5},{4,2},{5,3},{6,0},{7,1},{8,14},{9,15},{10,... | collective-permute-start | bytes 172040 | tf_op jit(solution)/shard_map/ppermute | solution.py:449
  85.8 0.5 collective-permute-start.27
  86.4 3.6 %collective-permute-start.26 = (bf16[16,1792]{1,0:T(8,128)(2,1)S(1)}, bf16[16,1792]{1,0:T(8,128)(2,1)S(1)}, u32[]{:S(2)}, u32[]{:S(2)}) collective-permute-start(bf16[16,1792]{1,0:T(8,128)(2,1)S(1)} %shard_map.166.mine), channel_id=1, source_target_pairs={{0,4},{1,5},{2,6},{3,7},{4,0},{5,1},{6,2},{7,3},{8,12},{9,13},{10,... | collective-permute-start | bytes 172040 | tf_op jit(solution)/shard_map/ppermute | solution.py:449
  90.0 0.5 collective-permute-start.25
  90.6 2.6 %collective-permute-done.27.refs_1_ = bf16[16,1792]{1,0:T(8,128)(2,1)S(1)} collective-permute-done((bf16[16,1792]{1,0:T(8,128)(2,1)S(1)}, bf16[16,1792]{1,0:T(8,128)(2,1)S(1)}, u32[]{:S(2)}, u32[]{:S(2)}) %collective-permute-start.27) | collective-permute-done | bytes 57376 | tf_op jit(solution)/shard_map/ppermute | solution.py:449
  93.1 0.6 collective-permute-done.26.refs_0_
  93.7 0.4 collective-permute-done.25.other
  94.2 0.9 collective-permute-start.32
  95.0 1.1 %collective-permute-start.31 = (bf16[32,1792]{1,0:T(8,128)(2,1)S(1)}, bf16[32,1792]{1,0:T(8,128)(2,1)S(1)}, u32[]{:S(2)}, u32[]{:S(2)}) collective-permute-start(bf16[32,1792]{1,0:T(8,128)(2,1)S(1)} %shard_map.168.refs_0_), channel_id=1, source_target_pairs={{0,2},{1,3},{2,0},{3,1},{4,6},{5,7},{6,4},{7,5},{8,10},{9,11},{10,... | collective-permute-start | bytes 344072 | tf_op jit(solution)/shard_map/ppermute | solution.py:449
  96.1 1.6 %collective-permute-start.30 = (bf16[32,1792]{1,0:T(8,128)(2,1)S(1)}, bf16[32,1792]{1,0:T(8,128)(2,1)S(1)}, u32[]{:S(2)}, u32[]{:S(2)}) collective-permute-start(bf16[32,1792]{1,0:T(8,128)(2,1)S(1)} %shard_map.168.refs_0_), channel_id=1, source_target_pairs={{0,1},{1,0},{2,3},{3,2},{4,5},{5,4},{6,7},{7,6},{8,9},{9,8},{10,11... | collective-permute-start | bytes 344072 | tf_op jit(solution)/shard_map/ppermute | solution.py:449
  97.7 0.5 collective-permute-start.33
  98.3 1.7 %collective-permute-done.32.refs_3_ = bf16[32,1792]{1,0:T(8,128)(2,1)S(1)} collective-permute-done((bf16[32,1792]{1,0:T(8,128)(2,1)S(1)}, bf16[32,1792]{1,0:T(8,128)(2,1)S(1)}, u32[]{:S(2)}, u32[]{:S(2)}) %collective-permute-start.32) | collective-permute-done | bytes 114720 | tf_op jit(solution)/shard_map/ppermute | solution.py:449
  100.0 0.7 collective-permute-done.31.refs_2_
  100.6 0.5 collective-permute-done.30.refs_1_
  101.2 0.1 collective-permute-start.34
  101.3 0.5 collective-permute-start.35
  101.8 2.0 %collective-permute-done.33.refs_2_ = bf16[64,1792]{1,0:T(8,128)(2,1)S(1)} collective-permute-done((bf16[64,1792]{1,0:T(8,128)(2,1)S(1)}, bf16[64,1792]{1,0:T(8,128)(2,1)S(1)}, u32[]{:S(2)}, u32[]{:S(2)}) %collective-permute-start.33) | collective-permute-done | bytes 229408 | tf_op jit(solution)/shard_map/ppermute | solution.py:449
  103.8 1.5 %collective-permute-done.36.refs_5_ = bf16[64,1792]{1,0:T(8,128)(2,1)S(1)} collective-permute-done((bf16[64,1792]{1,0:T(8,128)(2,1)S(1)}, bf16[64,1792]{1,0:T(8,128)(2,1)S(1)}, u32[]{:S(2)}, u32[]{:S(2)}) %collective-permute-start.36) | collective-permute-done | bytes 229408 | tf_op jit(solution)/shard_map/ppermute | solution.py:449
  105.2 2.0 %shard_map.170 = (f32[512,512]{1,0:T(8,128)}, f32[512,512]{1,0:T(8,128)}, f32[512,512]{1,0:T(8,128)}, f32[512,128]{1,0:T(8,128)}, f32[1,1]{1,0:T(1,128)}) custom-call(bf16[128,1792]{1,0:T(8,128)(2,1)S(1)} %shard_map.169.refs_0_, bf16[64,1792]{1,0:T(8,128)(2,1)S(1)} %shard_map.167.after.refs_1_, bf16[64,1792]{1,0:T(8,128)(2,1)S(1)} %collective-permute-done.33.refs_2_, ...), custom_call_target="tpu_custom_call" | custom-call | bytes 5505024 | tf_op jit(solution)/shard_map/pallas_call | solution.py:635
  (54 shorter events, 0.2 us)
Async XLA Ops:
  0.6 14.1 %copy-start.8 = (s32[128]{0:T(128)S(1)}, s32[128]{0:T(128)}, u32[]{:S(2)}) copy-start(s32[128]{0:T(128)} %param.15) | copy-start | bytes 1540
  0.6 14.1 %copy-start.7 = (s32[128]{0:T(128)S(1)}, s32[128]{0:T(128)}, u32[]{:S(2)}) copy-start(s32[128]{0:T(128)} %param.14) | copy-start | bytes 1540
  0.7 14.1 %copy-start.6 = (bf16[512,128]{1,0:T(8,128)(2,1)S(1)}, bf16[512,128]{1,0:T(8,128)(2,1)}, u32[]{:S(2)}) copy-start(bf16[512,128]{1,0:T(8,128)(2,1)} %w_decode.1) | copy-start | bytes 393220
  0.7 14.1 %copy-start.12 = (s32[6,512]{1,0:T(8,128)S(1)}, s32[6,512]{1,0:T(8,128)}, u32[]{:S(2)}) copy-start(s32[6,512]{1,0:T(8,128)} %senders_in.1) | copy-start | bytes 36868
  3.0 11.8 %collective-permute-start = (bf16[512,128]{1,0:T(8,128)(2,1)}, bf16[512,128]{1,0:T(8,128)(2,1)S(1)}, u32[]{:S(2)}, u32[]{:S(2)}) collective-permute-start(bf16[512,128]{1,0:T(8,128)(2,1)} %get-tuple-element.44), channel_id=1, source_target_pairs={{0,1},{1,0},{2,3},{3,2},{4,5},{5,4},{6,7},{7,6},{8,9},{9,8},{10,11... | collective-permute-start | bytes 393224 | tf_op jit(solution)/shard_map/ppermute | solution.py:449
  6.0 8.8 %collective-permute-start.1 = (bf16[512,128]{1,0:T(8,128)(2,1)}, bf16[512,128]{1,0:T(8,128)(2,1)S(1)}, u32[]{:S(2)}, u32[]{:S(2)}) collective-permute-start(bf16[512,128]{1,0:T(8,128)(2,1)} %get-tuple-element.45), channel_id=1, source_target_pairs={{0,7},{1,2},{2,1},{3,4},{4,3},{5,6},{6,5},{7,0},{8,15},{9,10},{10,... | collective-permute-start | bytes 393224 | tf_op jit(solution)/shard_map/ppermute | solution.py:443
  14.8 0.7 copy-start.13
  15.5 24.3 %copy-start.9 = (bf16[1536,2048]{1,0:T(8,128)(2,1)S(1)}, bf16[1536,2048]{1,0:T(8,128)(2,1)}, u32[]{:S(2)}) copy-start(bf16[1536,2048]{1,0:T(8,128)(2,1)} %get-tuple-element.50.refs_8_) | copy-start | bytes 18874372
  15.5 24.3 %copy-start.10 = (bf16[128,2048]{1,0:T(8,128)(2,1)S(1)}, bf16[128,2048]{1,0:T(8,128)(2,1)}, u32[]{:S(2)}) copy-start(bf16[128,2048]{1,0:T(8,128)(2,1)} %get-tuple-element.51.refs_9_) | copy-start | bytes 1572868
  15.5 24.3 %copy-start.11 = (bf16[128,2048]{1,0:T(8,128)(2,1)S(1)}, bf16[128,2048]{1,0:T(8,128)(2,1)}, u32[]{:S(2)}) copy-start(bf16[128,2048]{1,0:T(8,128)(2,1)} %get-tuple-element.52.refs_10_) | copy-start | bytes 1572868
  26.0 8.8 %collective-permute-start.3 = (bf16[128,512]{1,0:T(8,128)(2,1)S(1)}, bf16[128,512]{1,0:T(8,128)(2,1)S(1)}, u32[]{:S(2)}, u32[]{:S(2)}) collective-permute-start(bf16[128,512]{1,0:T(8,128)(2,1)S(1)} %get-tuple-element.47.refs_0_), channel_id=1, source_target_pairs={{0,16},{8,24},{16,0},{24,8},{1,17},{9,25},{17,1},{25,9},{2,18},{10... | collective-permute-start | bytes 393224 | tf_op jit(solution)/shard_map/ppermute | solution.py:449
  27.6 3.9 %collective-permute-start.5 = (bf16[128,128]{1,0:T(8,128)(2,1)S(1)}, bf16[128,128]{1,0:T(8,128)(2,1)S(1)}, u32[]{:S(2)}, u32[]{:S(2)}) collective-permute-start(bf16[128,128]{1,0:T(8,128)(2,1)S(1)} %get-tuple-element.48), channel_id=1, source_target_pairs={{0,1},{1,0},{2,3},{3,2},{4,5},{5,4},{6,7},{7,6},{8,9},{9,8},{10,11... | collective-permute-start | bytes 98312 | tf_op jit(solution)/shard_map/ppermute | solution.py:449
  27.6 6.6 %collective-permute-start.6 = (bf16[128,128]{1,0:T(8,128)(2,1)S(1)}, bf16[128,128]{1,0:T(8,128)(2,1)S(1)}, u32[]{:S(2)}, u32[]{:S(2)}) collective-permute-start(bf16[128,128]{1,0:T(8,128)(2,1)S(1)} %get-tuple-element.49), channel_id=1, source_target_pairs={{0,7},{1,2},{2,1},{3,4},{4,3},{5,6},{6,5},{7,0},{8,15},{9,10},{10,... | collective-permute-start | bytes 98312 | tf_op jit(solution)/shard_map/ppermute | solution.py:443
  30.6 8.0 %collective-permute-start.2 = (bf16[128,512]{1,0:T(8,128)(2,1)S(1)}, bf16[128,512]{1,0:T(8,128)(2,1)S(1)}, u32[]{:S(2)}, u32[]{:S(2)}) collective-permute-start(bf16[128,512]{1,0:T(8,128)(2,1)S(1)} %get-tuple-element.47.refs_0_), channel_id=1, source_target_pairs={{0,8},{8,0},{16,24},{24,16},{1,9},{9,1},{17,25},{25,17},{2,10},{10... | collective-permute-start | bytes 393224 | tf_op jit(solution)/shard_map/ppermute | solution.py:449
  34.2 4.3 %collective-permute-start.8 = (bf16[128,256]{1,0:T(8,128)(2,1)S(1)}, bf16[128,256]{1,0:T(8,128)(2,1)S(1)}, u32[]{:S(2)}, u32[]{:S(2)}) collective-permute-start(bf16[128,256]{1,0:T(8,128)(2,1)S(1)} %shard_map.158.refs_4_), channel_id=1, source_target_pairs={{0,16},{8,24},{16,0},{24,8},{1,17},{9,25},{17,1},{25,9},{2,18},{10... | collective-permute-start | bytes 196616 | tf_op jit(solution)/shard_map/ppermute | solution.py:449
  34.8 5.0 %collective-permute-start.4 = (bf16[128,512]{1,0:T(8,128)(2,1)S(1)}, bf16[128,512]{1,0:T(8,128)(2,1)S(1)}, u32[]{:S(2)}, u32[]{:S(2)}) collective-permute-start(bf16[128,512]{1,0:T(8,128)(2,1)S(1)} %collective-permute-done.3.refs_2_), channel_id=1, source_target_pairs={{0,8},{8,0},{16,24},{24,16},{1,9},{9,1},{17,25},{25,17},{2,10},{10... | collective-permute-start | bytes 393224 | tf_op jit(solution)/shard_map/ppermute | solution.py:449
  34.8 3.7 %collective-permute-start.7 = (bf16[128,256]{1,0:T(8,128)(2,1)S(1)}, bf16[128,256]{1,0:T(8,128)(2,1)S(1)}, u32[]{:S(2)}, u32[]{:S(2)}) collective-permute-start(bf16[128,256]{1,0:T(8,128)(2,1)S(1)} %shard_map.158.refs_4_), channel_id=1, source_target_pairs={{0,8},{8,0},{16,24},{24,16},{1,9},{9,1},{17,25},{25,17},{2,10},{10... | collective-permute-start | bytes 196616 | tf_op jit(solution)/shard_map/ppermute | solution.py:449
  38.6 1.3 %collective-permute-start.9 = (bf16[128,256]{1,0:T(8,128)(2,1)S(1)}, bf16[128,256]{1,0:T(8,128)(2,1)S(1)}, u32[]{:S(2)}, u32[]{:S(2)}) collective-permute-start(bf16[128,256]{1,0:T(8,128)(2,1)S(1)} %collective-permute-done.8.refs_6_), channel_id=1, source_target_pairs={{0,8},{8,0},{16,24},{24,16},{1,9},{9,1},{17,25},{25,17},{2,10},{10... | collective-permute-start | bytes 196616 | tf_op jit(solution)/shard_map/ppermute | solution.py:449
  39.8 15.6 %copy-start = (bf16[512,3072]{1,0:T(8,128)(2,1)S(1)}, bf16[512,3072]{1,0:T(8,128)(2,1)}, u32[]{:S(2)}) copy-start(bf16[512,3072]{1,0:T(8,128)(2,1)} %get-tuple-element.60.picked_t) | copy-start | bytes 9437188
  39.9 15.6 %copy-start.1 = (bf16[512,3072]{1,0:T(8,128)(2,1)S(1)}, bf16[512,3072]{1,0:T(8,128)(2,1)}, u32[]{:S(2)}) copy-start(bf16[512,3072]{1,0:T(8,128)(2,1)} %get-tuple-element.61.slope_t) | copy-start | bytes 9437188
  39.9 15.6 %copy-start.2 = (bf16[512,512]{1,0:T(8,128)(2,1)S(1)}, bf16[512,512]{1,0:T(8,128)(2,1)}, u32[]{:S(2)}) copy-start(bf16[512,512]{1,0:T(8,128)(2,1)} %get-tuple-element.43.after.nodes_in.nodes_t) | copy-start | bytes 1572868
  39.9 15.6 %copy-start.3 = (f32[512,512]{1,0:T(8,128)S(1)}, f32[512,512]{1,0:T(8,128)}, u32[]{:S(2)}) copy-start(f32[512,512]{1,0:T(8,128)} %get-tuple-element.62.slope_sum_t) | copy-start | bytes 3145732
  39.9 15.6 %copy-start.4 = (f32[512,512]{1,0:T(8,128)S(1)}, f32[512,512]{1,0:T(8,128)}, u32[]{:S(2)}) copy-start(f32[512,512]{1,0:T(8,128)} %get-tuple-element.64.upd_slope_t) | copy-start | bytes 3145732
  39.9 15.6 %copy-start.5 = (bf16[512,512]{1,0:T(8,128)(2,1)S(1)}, bf16[512,512]{1,0:T(8,128)(2,1)}, u32[]{:S(2)}) copy-start(bf16[512,512]{1,0:T(8,128)(2,1)} %vertex.1) | copy-start | bytes 1572868
  46.7 8.7 %collective-permute-start.10 = (f32[128,512]{1,0:T(8,128)S(1)}, f32[128,512]{1,0:T(8,128)S(1)}, u32[]{:S(2)}, u32[]{:S(2)}) collective-permute-start(f32[128,512]{1,0:T(8,128)S(1)} %get-tuple-element.54), channel_id=1, source_target_pairs={{0,8},{8,0},{16,24},{24,16},{1,9},{9,1},{17,25},{25,17},{2,10},{10... | collective-permute-start | bytes 786440 | tf_op jit(solution)/shard_map/ppermute | solution.py:449
  46.9 1.6 %collective-permute-start.11 = (f32[128,256]{1,0:T(8,128)S(1)}, f32[128,256]{1,0:T(8,128)S(1)}, u32[]{:S(2)}, u32[]{:S(2)}) collective-permute-start(f32[128,256]{1,0:T(8,128)S(1)} %get-tuple-element.56), channel_id=1, source_target_pairs={{0,8},{8,0},{16,24},{24,16},{1,9},{9,1},{17,25},{25,17},{2,10},{10... | collective-permute-start | bytes 393224 | tf_op jit(solution)/shard_map/ppermute | solution.py:449
  48.5 4.0 %collective-permute-start.12 = (bf16[128,128]{1,0:T(8,128)(2,1)S(1)}, bf16[128,128]{1,0:T(8,128)(2,1)S(1)}, u32[]{:S(2)}, u32[]{:S(2)}) collective-permute-start(bf16[128,128]{1,0:T(8,128)(2,1)S(1)} %get-tuple-element.57), channel_id=1, source_target_pairs={{0,1},{1,0},{2,3},{3,2},{4,5},{5,4},{6,7},{7,6},{8,9},{9,8},{10,11... | collective-permute-start | bytes 98312 | tf_op jit(solution)/shard_map/ppermute | solution.py:449
  48.8 6.6 %collective-permute-start.13 = (bf16[128,128]{1,0:T(8,128)(2,1)S(1)}, bf16[128,128]{1,0:T(8,128)(2,1)S(1)}, u32[]{:S(2)}, u32[]{:S(2)}) collective-permute-start(bf16[128,128]{1,0:T(8,128)(2,1)S(1)} %get-tuple-element.58), channel_id=1, source_target_pairs={{0,7},{1,2},{2,1},{3,4},{4,3},{5,6},{6,5},{7,0},{8,15},{9,10},{10,... | collective-permute-start | bytes 98312 | tf_op jit(solution)/shard_map/ppermute | solution.py:443
  59.0 3.3 %collective-permute-start.14 = (bf16[192,1792]{1,0:T(8,128)(2,1)S(1)}, bf16[192,1792]{1,0:T(8,128)(2,1)S(1)}, u32[]{:S(2)}, u32[]{:S(2)}) collective-permute-start(bf16[192,1792]{1,0:T(8,128)(2,1)S(1)} %get-tuple-element.67), channel_id=1, source_target_pairs={{0,8},{8,0},{16,24},{24,16},{1,9},{9,1},{17,25},{25,17},{2,10},{10... | collective-permute-start | bytes 2064392 | tf_op jit(solution)/shard_map/ppermute | solution.py:449
  59.0 2.5 %collective-permute-start.18 = (bf16[64,1792]{1,0:T(8,128)(2,1)S(1)}, bf16[64,1792]{1,0:T(8,128)(2,1)S(1)}, u32[]{:S(2)}, u32[]{:S(2)}) collective-permute-start(bf16[64,1792]{1,0:T(8,128)(2,1)S(1)} %get-tuple-element.71), channel_id=1, source_target_pairs={{0,8},{8,0},{16,24},{24,16},{1,9},{9,1},{17,25},{25,17},{2,10},{10... | collective-permute-start | bytes 688136 | tf_op jit(solution)/shard_map/ppermute | solution.py:449
  61.6 7.7 %collective-permute-start.19 = (bf16[64,1792]{1,0:T(8,128)(2,1)S(1)}, bf16[64,1792]{1,0:T(8,128)(2,1)S(1)}, u32[]{:S(2)}, u32[]{:S(2)}) collective-permute-start(bf16[64,1792]{1,0:T(8,128)(2,1)S(1)} %shard_map.163), channel_id=1, source_target_pairs={{0,16},{8,24},{16,0},{24,8},{1,17},{9,25},{17,1},{25,9},{2,18},{10... | collective-permute-start | bytes 688136 | tf_op jit(solution)/shard_map/ppermute | solution.py:449
  62.3 9.5 %collective-permute-start.15 = (bf16[32,1792]{1,0:T(8,128)(2,1)S(1)}, bf16[32,1792]{1,0:T(8,128)(2,1)S(1)}, u32[]{:S(2)}, u32[]{:S(2)}) collective-permute-start(bf16[32,1792]{1,0:T(8,128)(2,1)S(1)} %get-tuple-element.68), channel_id=1, source_target_pairs={{0,1},{1,0},{2,3},{3,2},{4,5},{5,4},{6,7},{7,6},{8,9},{9,8},{10,11... | collective-permute-start | bytes 344072 | tf_op jit(solution)/shard_map/ppermute | solution.py:449
  62.4 12.9 %collective-permute-start.16 = (bf16[32,1792]{1,0:T(8,128)(2,1)S(1)}, bf16[32,1792]{1,0:T(8,128)(2,1)S(1)}, u32[]{:S(2)}, u32[]{:S(2)}) collective-permute-start(bf16[32,1792]{1,0:T(8,128)(2,1)S(1)} %get-tuple-element.69), channel_id=1, source_target_pairs={{0,2},{1,3},{2,0},{3,1},{4,6},{5,7},{6,4},{7,5},{8,10},{9,11},{10,... | collective-permute-start | bytes 344072 | tf_op jit(solution)/shard_map/ppermute | solution.py:449
  62.5 14.7 %collective-permute-start.17 = (bf16[32,1792]{1,0:T(8,128)(2,1)S(1)}, bf16[32,1792]{1,0:T(8,128)(2,1)S(1)}, u32[]{:S(2)}, u32[]{:S(2)}) collective-permute-start(bf16[32,1792]{1,0:T(8,128)(2,1)S(1)} %get-tuple-element.70), channel_id=1, source_target_pairs={{0,3},{1,2},{2,1},{3,0},{4,7},{5,6},{6,5},{7,4},{8,11},{9,10},{10,... | collective-permute-start | bytes 344072 | tf_op jit(solution)/shard_map/ppermute | solution.py:449
  69.4 8.4 %collective-permute-start.20 = (bf16[16,1792]{1,0:T(8,128)(2,1)S(1)}, bf16[16,1792]{1,0:T(8,128)(2,1)S(1)}, u32[]{:S(2)}, u32[]{:S(2)}) collective-permute-start(bf16[16,1792]{1,0:T(8,128)(2,1)S(1)} %get-tuple-element.72), channel_id=1, source_target_pairs={{0,4},{1,5},{2,6},{3,7},{4,0},{5,1},{6,2},{7,3},{8,12},{9,13},{10,... | collective-permute-start | bytes 172040 | tf_op jit(solution)/shard_map/ppermute | solution.py:449
  69.5 8.8 %collective-permute-start.21 = (bf16[16,1792]{1,0:T(8,128)(2,1)S(1)}, bf16[16,1792]{1,0:T(8,128)(2,1)S(1)}, u32[]{:S(2)}, u32[]{:S(2)}) collective-permute-start(bf16[16,1792]{1,0:T(8,128)(2,1)S(1)} %get-tuple-element.73), channel_id=1, source_target_pairs={{0,5},{1,4},{2,7},{3,6},{4,1},{5,0},{6,3},{7,2},{8,13},{9,12},{10,... | collective-permute-start | bytes 172040 | tf_op jit(solution)/shard_map/ppermute | solution.py:449
  71.9 6.6 %collective-permute-start.22 = (bf16[16,1792]{1,0:T(8,128)(2,1)S(1)}, bf16[16,1792]{1,0:T(8,128)(2,1)S(1)}, u32[]{:S(2)}, u32[]{:S(2)}) collective-permute-start(bf16[16,1792]{1,0:T(8,128)(2,1)S(1)} %get-tuple-element.74), channel_id=1, source_target_pairs={{0,6},{1,7},{2,4},{3,5},{4,2},{5,3},{6,0},{7,1},{8,14},{9,15},{10,... | collective-permute-start | bytes 172040 | tf_op jit(solution)/shard_map/ppermute | solution.py:449
  75.3 6.9 %collective-permute-start.23 = (bf16[16,1792]{1,0:T(8,128)(2,1)S(1)}, bf16[16,1792]{1,0:T(8,128)(2,1)S(1)}, u32[]{:S(2)}, u32[]{:S(2)}) collective-permute-start(bf16[16,1792]{1,0:T(8,128)(2,1)S(1)} %get-tuple-element.75), channel_id=1, source_target_pairs={{0,7},{1,6},{2,5},{3,4},{4,3},{5,2},{6,1},{7,0},{8,15},{9,14},{10,... | collective-permute-start | bytes 172040 | tf_op jit(solution)/shard_map/ppermute | solution.py:449
  77.2 4.9 %collective-permute-start.24 = (bf16[16,1792]{1,0:T(8,128)(2,1)S(1)}, bf16[16,1792]{1,0:T(8,128)(2,1)S(1)}, u32[]{:S(2)}, u32[]{:S(2)}) collective-permute-start(bf16[16,1792]{1,0:T(8,128)(2,1)S(1)} %shard_map.165), channel_id=1, source_target_pairs={{0,16},{8,24},{16,0},{24,8},{1,17},{9,25},{17,1},{25,9},{2,18},{10... | collective-permute-start | bytes 172040 | tf_op jit(solution)/shard_map/ppermute | solution.py:449
  82.3 8.3 %collective-permute-start.29 = (bf16[16,1792]{1,0:T(8,128)(2,1)S(1)}, bf16[16,1792]{1,0:T(8,128)(2,1)S(1)}, u32[]{:S(2)}, u32[]{:S(2)}) collective-permute-start(bf16[16,1792]{1,0:T(8,128)(2,1)S(1)} %shard_map.166.mine), channel_id=1, source_target_pairs={{0,7},{1,6},{2,5},{3,4},{4,3},{5,2},{6,1},{7,0},{8,15},{9,14},{10,... | collective-permute-start | bytes 172040 | tf_op jit(solution)/shard_map/ppermute | solution.py:449
  84.5 6.1 %collective-permute-start.28 = (bf16[16,1792]{1,0:T(8,128)(2,1)S(1)}, bf16[16,1792]{1,0:T(8,128)(2,1)S(1)}, u32[]{:S(2)}, u32[]{:S(2)}) collective-permute-start(bf16[16,1792]{1,0:T(8,128)(2,1)S(1)} %shard_map.166.mine), channel_id=1, source_target_pairs={{0,6},{1,7},{2,4},{3,5},{4,2},{5,3},{6,0},{7,1},{8,14},{9,15},{10,... | collective-permute-start | bytes 172040 | tf_op jit(solution)/shard_map/ppermute | solution.py:449
  85.8 7.3 %collective-permute-start.27 = (bf16[16,1792]{1,0:T(8,128)(2,1)S(1)}, bf16[16,1792]{1,0:T(8,128)(2,1)S(1)}, u32[]{:S(2)}, u32[]{:S(2)}) collective-permute-start(bf16[16,1792]{1,0:T(8,128)(2,1)S(1)} %shard_map.166.mine), channel_id=1, source_target_pairs={{0,5},{1,4},{2,7},{3,6},{4,1},{5,0},{6,3},{7,2},{8,13},{9,12},{10,... | collective-permute-start | bytes 172040 | tf_op jit(solution)/shard_map/ppermute | solution.py:449
  86.4 7.3 %collective-permute-start.26 = (bf16[16,1792]{1,0:T(8,128)(2,1)S(1)}, bf16[16,1792]{1,0:T(8,128)(2,1)S(1)}, u32[]{:S(2)}, u32[]{:S(2)}) collective-permute-start(bf16[16,1792]{1,0:T(8,128)(2,1)S(1)} %shard_map.166.mine), channel_id=1, source_target_pairs={{0,4},{1,5},{2,6},{3,7},{4,0},{5,1},{6,2},{7,3},{8,12},{9,13},{10,... | collective-permute-start | bytes 172040 | tf_op jit(solution)/shard_map/ppermute | solution.py:449
  90.0 4.2 %collective-permute-start.25 = (bf16[16,1792]{1,0:T(8,128)(2,1)S(1)}, bf16[16,1792]{1,0:T(8,128)(2,1)S(1)}, u32[]{:S(2)}, u32[]{:S(2)}) collective-permute-start(bf16[16,1792]{1,0:T(8,128)(2,1)S(1)} %shard_map.166.mine), channel_id=1, source_target_pairs={{0,16},{8,24},{16,0},{24,8},{1,17},{9,25},{17,1},{25,9},{2,18},{10... | collective-permute-start | bytes 172040 | tf_op jit(solution)/shard_map/ppermute | solution.py:449
  94.2 5.8 %collective-permute-start.32 = (bf16[32,1792]{1,0:T(8,128)(2,1)S(1)}, bf16[32,1792]{1,0:T(8,128)(2,1)S(1)}, u32[]{:S(2)}, u32[]{:S(2)}) collective-permute-start(bf16[32,1792]{1,0:T(8,128)(2,1)S(1)} %shard_map.168.refs_0_), channel_id=1, source_target_pairs={{0,3},{1,2},{2,1},{3,0},{4,7},{5,6},{6,5},{7,4},{8,11},{9,10},{10,... | collective-permute-start | bytes 344072 | tf_op jit(solution)/shard_map/ppermute | solution.py:449
  95.0 5.6 %collective-permute-start.31 = (bf16[32,1792]{1,0:T(8,128)(2,1)S(1)}, bf16[32,1792]{1,0:T(8,128)(2,1)S(1)}, u32[]{:S(2)}, u32[]{:S(2)}) collective-permute-start(bf16[32,1792]{1,0:T(8,128)(2,1)S(1)} %shard_map.168.refs_0_), channel_id=1, source_target_pairs={{0,2},{1,3},{2,0},{3,1},{4,6},{5,7},{6,4},{7,5},{8,10},{9,11},{10,... | collective-permute-start | bytes 344072 | tf_op jit(solution)/shard_map/ppermute | solution.py:449
  96.1 5.0 %collective-permute-start.30 = (bf16[32,1792]{1,0:T(8,128)(2,1)S(1)}, bf16[32,1792]{1,0:T(8,128)(2,1)S(1)}, u32[]{:S(2)}, u32[]{:S(2)}) collective-permute-start(bf16[32,1792]{1,0:T(8,128)(2,1)S(1)} %shard_map.168.refs_0_), channel_id=1, source_target_pairs={{0,1},{1,0},{2,3},{3,2},{4,5},{5,4},{6,7},{7,6},{8,9},{9,8},{10,11... | collective-permute-start | bytes 344072 | tf_op jit(solution)/shard_map/ppermute | solution.py:449
  97.7 6.0 %collective-permute-start.33 = (bf16[64,1792]{1,0:T(8,128)(2,1)S(1)}, bf16[64,1792]{1,0:T(8,128)(2,1)S(1)}, u32[]{:S(2)}, u32[]{:S(2)}) collective-permute-start(bf16[64,1792]{1,0:T(8,128)(2,1)S(1)} %shard_map.167.after.refs_1_), channel_id=1, source_target_pairs={{0,16},{8,24},{16,0},{24,8},{1,17},{9,25},{17,1},{25,9},{2,18},{10... | collective-permute-start | bytes 688136 | tf_op jit(solution)/shard_map/ppermute | solution.py:449
  101.2 4.0 %collective-permute-start.34 = (bf16[128,1792]{1,0:T(8,128)(2,1)S(1)}, bf16[128,1792]{1,0:T(8,128)(2,1)S(1)}, u32[]{:S(2)}, u32[]{:S(2)}) collective-permute-start(bf16[128,1792]{1,0:T(8,128)(2,1)S(1)} %shard_map.169.refs_0_), channel_id=1, source_target_pairs={{0,8},{8,0},{16,24},{24,16},{1,9},{9,1},{17,25},{25,17},{2,10},{10... | collective-permute-start | bytes 1376264 | tf_op jit(solution)/shard_map/ppermute | solution.py:449
  101.3 2.5 %collective-permute-start.35 = (bf16[64,1792]{1,0:T(8,128)(2,1)S(1)}, bf16[64,1792]{1,0:T(8,128)(2,1)S(1)}, u32[]{:S(2)}, u32[]{:S(2)}) collective-permute-start(bf16[64,1792]{1,0:T(8,128)(2,1)S(1)} %shard_map.167.after.refs_1_), channel_id=1, source_target_pairs={{0,8},{8,0},{16,24},{24,16},{1,9},{9,1},{17,25},{25,17},{2,10},{10... | collective-permute-start | bytes 688136 | tf_op jit(solution)/shard_map/ppermute | solution.py:449
  103.8 1.5 %collective-permute-start.36 = (bf16[64,1792]{1,0:T(8,128)(2,1)S(1)}, bf16[64,1792]{1,0:T(8,128)(2,1)S(1)}, u32[]{:S(2)}, u32[]{:S(2)}) collective-permute-start(bf16[64,1792]{1,0:T(8,128)(2,1)S(1)} %collective-permute-done.33.refs_2_), channel_id=1, source_target_pairs={{0,8},{8,0},{16,24},{24,16},{1,9},{9,1},{17,25},{25,17},{2,10},{10... | collective-permute-start | bytes 688136 | tf_op jit(solution)/shard_map/ppermute | solution.py:449

commit v10 on v9

--- a/solution.py
+++ b/solution.py
@@ -207,23 +207,16 @@
     table, grad = refs[16:18]
     subs = (len(refs) - 18) // 2
     states, slopes = refs[18 : 18 + subs], refs[18 + subs :]
-    step = pl.program_id(0)
     members = len(mids)
     variables, count = own_mid.shape
     ext_rows = grad.shape[1]
 
-    @pl.when(step == 0)
-    def _():
-        grad[...] = jnp.zeros_like(grad)
-        loss[...] = jnp.zeros_like(loss)
-        for m in range(members):
-            for base in (0, ext_rows):
-                table[m * variables : (m + 1) * variables, base : base + count] = mids[m][...]
-                table[m * variables : (m + 1) * variables, base + count : base + ext_rows] = ends[m][...]
-
-    wide = states[0].shape[1]
-    for i, state in enumerate(states):
-        state[...] = dot(table[...], mat[:, i * wide : (i + 1) * wide])
+    grad[...] = jnp.zeros_like(grad)
+    loss[...] = jnp.zeros_like(loss)
+    for m in range(members):
+        for start in (0, ext_rows):
+            table[m * variables : (m + 1) * variables, start : start + count] = mids[m][...]
+            table[m * variables : (m + 1) * variables, start + count : start + ext_rows] = ends[m][...]
 
     def bend(diff):
         square = diff * diff + EPS
@@ -231,8 +224,18 @@
         return square * inverse, diff * inverse
 
     alone = EPS**0.5
-    for i, (state, slope_out) in enumerate(zip(states, slopes)):
+    wide = states[0].shape[1]
+    blocks = mat.shape[1] // wide
+
+    def decode(i):
+        states[i % 2][...] = dot(table[...], mat[:, i * wide : (i + 1) * wide])
+
+    decode(0)
+    for i in range(blocks):
+        state, slope_out = states[i % 2], slopes[i % 2]
         cols = slice(i * wide, (i + 1) * wide)
+        if i + 1 < blocks:
+            decode(i + 1)
         summed = jnp.zeros((8, wide), F32)
         for start in range(0, variables, TILE):
             rows = slice(start, start + TILE)
@@ -260,15 +263,13 @@
                 slope_out[m * variables + start : m * variables + start + TILE, :] = slope.astype(BF16)
             term = near * (1.0 / members) - (apart[0] + apart[1]) * (1.0 / (2.0 * members * (members - 1)))
             summed += term[:8] + term[8:]
-        loss[:, cols] += summed
+        loss[...] += summed
         grad[...] += dot_nt(slope_out[...], mat[:ext_rows, cols])
 
-    @pl.when(step == pl.num_programs(0) - 1)
-    def _():
-        for i, (mid, end) in enumerate(((own_mid, own_end), (pair_mid, pair_end))):
-            rows = slice(i * variables, (i + 1) * variables)
-            mid[...] = grad[rows, :count]
-            end[...] = grad[rows, count:]
+    for i, (mid, end) in enumerate(((own_mid, own_end), (pair_mid, pair_end))):
+        rows = slice(i * variables, (i + 1) * variables)
+        mid[...] = grad[rows, :count]
+        end[...] = grad[rows, count:]
 
 
 def borrowed_kernel(first, second, end):
@@ -585,23 +586,15 @@
     (end,) = call(borrowed_kernel, list(lent), [sds((variables, 2 * halo), BF16)])
     ends = gathered(end)
 
-    wide = lambda rows: pl.BlockSpec((rows, 2 * block), lambda i, *at: (0, i))
-    grads = pl.pallas_call(
+    grads = call(
         functools.partial(readout_kernel, line_span),
-        grid=(steps,),
-        out_shape=[sds((variables, count), F32), sds((variables, 2 * halo), F32)] * 2 + [sds((8, block), F32)],
-        in_specs=[fixed((variables, count))] * members + [fixed((variables, 2 * halo))] * members + [
-            tall(2 * ext_rows), tall(variables), tall(variables),
-        ],
-        out_specs=[fixed((variables, count)), fixed((variables, 2 * halo))] * 2 + [fixed((8, block))],
-        scratch_shapes=[
-            pltpu.VMEM((members * variables, 2 * ext_rows), BF16), pltpu.VMEM((2 * variables, ext_rows), F32),
-            *[pltpu.VMEM((members * variables, 256), F32)] * (block // 256),
-            *[pltpu.VMEM((2 * variables, 256), BF16)] * (block // 256),
-        ],
-        compiler_params=params(20),
-        cost_estimate=cost(4 * members * variables * ext_rows * half_span, 14e6),
-    )(*mids, *ends, mat, base_t, truth_t)
+        mids + ends + [mat, base_t, truth_t],
+        [sds((variables, count), F32), sds((variables, 2 * halo), F32)] * 2 + [sds((8, 256), F32)],
+        [held((members * variables, 2 * ext_rows)), held((2 * variables, ext_rows), F32)]
+        + [held((members * variables, 256), F32)] * 2 + [held((2 * variables, 256))] * 2,
+        flops=4 * members * variables * ext_rows * half_span,
+        limit=24,
+    )
     own_mid, own_end, pair_mid, pair_end, term = grads
     got_end = flip(pair_end, "ens", 1)
     got_mid = flip(pair_mid, "ens", 1)

time: 108 us -> 107 us (level)
    pallas_call x1 -> x0, Pallas kernels: 6.8 us -> none  [per_device(): pl.pallas_call(functools.partial(readout_kernel, line_span), grid=(steps,...]
    pallas_call x13 -> x14, Pallas kernels: 16.9 us -> 23.5 us  [call(): pl.pallas_call(kernel, out_shape=outs, in_specs=freed(vmem(len(ins) - in_...]
where the time goes in v10:
time: 107 us
  starting transfers between devices  41.9 us (39%)
  waiting for transfers between devices  32.8 us (31%)
  Pallas kernels  30.6 us (29%)
  between operations  1.11 us (1%)
    ppermute x34, starting transfers between devices, flip(): return lax.ppermute(value, axis, [(i, i ^ bit) for i in range(size)])  32.5 us
    ppermute x34, waiting for transfers between devices, flip(): return lax.ppermute(value, axis, [(i, i ^ bit) for i in range(size)])  27.1 us
    pallas_call x14, Pallas kernels, call(): pl.pallas_call(kernel, out_shape=outs, in_specs=freed(vmem(len(ins) - in_...  23.5 us
    ppermute x3, starting transfers between devices, meet(): lax.ppermute(second, 'dom', [(i, (i + (1 if i % 2 else size - 1)) % size)...  9.42 us
    ppermute x3, waiting for transfers between devices, meet(): lax.ppermute(second, 'dom', [(i, (i + (1 if i % 2 else size - 1)) % size)...  5.62 us
    pallas_call x1, Pallas kernels, per_device(): pl.pallas_call(decoder_kernel, grid_spec=pltpu.PrefetchScalarGridSpec(num...  5.2 us
  transfers between devices with their start and end apart: 37, of which 20 were waited for; matrix products, arithmetic and copies ran while one was open for 0% of the time, Pallas kernels for 5%

profile of v10, /device:TPU:0, one launch (start us, length us, event | category | flops | bytes accessed | tf_op | source)
XLA Modules:
  0.0 107.2 jit_solution(8819871616580340485)
XLA Ops:
  0.7 2.3 %shard_map.155 = (bf16[512,512]{1,0:T(8,128)(2,1)}, bf16[512,128]{1,0:T(8,128)(2,1)}, bf16[512,128]{1,0:T(8,128)(2,1)}) custom-call(bf16[512,512]{1,0:T(8,128)(2,1)} %bitcast.11, s32[1,128]{1,0:T(1,128)} %bitcast.5, s32[1,128]{1,0:T(1,128)} %bitcast.8), custom_call_target="tpu_custom_call" | custom-call | flops 134217728 | bytes 1311744 | tf_op jit(solution)/shard_map/pallas_call | solution.py:463
  3.0 3.0 %collective-permute-start = (bf16[512,128]{1,0:T(8,128)(2,1)}, bf16[512,128]{1,0:T(8,128)(2,1)S(1)}, u32[]{:S(2)}, u32[]{:S(2)}) collective-permute-start(bf16[512,128]{1,0:T(8,128)(2,1)} %get-tuple-element.44), channel_id=1, source_target_pairs={{0,1},{1,0},{2,3},{3,2},{4,5},{5,4},{6,7},{7,6},{8,9},{9,8},{10,11... | collective-permute-start | bytes 393224 | tf_op jit(solution)/shard_map/ppermute | solution.py:450
  6.0 3.5 %collective-permute-start.1 = (bf16[512,128]{1,0:T(8,128)(2,1)}, bf16[512,128]{1,0:T(8,128)(2,1)S(1)}, u32[]{:S(2)}, u32[]{:S(2)}) collective-permute-start(bf16[512,128]{1,0:T(8,128)(2,1)} %get-tuple-element.45), channel_id=1, source_target_pairs={{0,7},{1,2},{2,1},{3,4},{4,3},{5,6},{6,5},{7,0},{8,15},{9,10},{10,... | collective-permute-start | bytes 393224 | tf_op jit(solution)/shard_map/ppermute | solution.py:444
  9.5 5.2 %shard_map.156 = (bf16[1536,2048]{1,0:T(8,128)(2,1)}, bf16[128,2048]{1,0:T(8,128)(2,1)}, bf16[128,2048]{1,0:T(8,128)(2,1)}, f32[8,128]{1,0:T(8,128)}) custom-call(s32[1]{0:T(128)} %bitcast.3.core, s32[3,4096]{1,0:T(4,128)} %vertices.1, f32[3,4096]{1,0:T(4,128)} %weights.1, bf16[4096,128]{1,0:T(8,128)(2,1)} %base.1, bf16[4096,128]{1,0:T(8,128)(2,1)} %truth.1, ...), custom_call_target="tpu_custom_call" | custom-call | flops 15728640 | bytes 16000000 | tf_op jit(solution)/shard_map/pallas_call | solution.py:547
  14.8 0.7 copy-done.13
  15.5 10.5 %shard_map.157 = (bf16[128,512]{1,0:T(8,128)(2,1)S(1)}, bf16[128,128]{1,0:T(8,128)(2,1)S(1)}, bf16[128,128]{1,0:T(8,128)(2,1)S(1)}, bf16[512,3072]{1,0:T(8,128)(...) custom-call(bf16[512,512]{1,0:T(8,128)(2,1)} %get-tuple-element.43.a, ...), custom_call_target="tpu_custom_call" | custom-call | flops 4026531840 | bytes 12141568 | tf_op jit(solution)/shard_map/pallas_call | solution.py:463
  26.0 1.6 %collective-permute-start.3 = (bf16[128,512]{1,0:T(8,128)(2,1)S(1)}, bf16[128,512]{1,0:T(8,128)(2,1)S(1)}, u32[]{:S(2)}, u32[]{:S(2)}) collective-permute-start(bf16[128,512]{1,0:T(8,128)(2,1)S(1)} %get-tuple-element.47.refs_0_), channel_id=1, source_target_pairs={{0,16},{8,24},{16,0},{24,8},{1,17},{9,25},{17,1},{25,9},{2,18},{10... | collective-permute-start | bytes 393224 | tf_op jit(solution)/shard_map/ppermute | solution.py:450
  27.6 3.0 %collective-permute-start.6 = (bf16[128,128]{1,0:T(8,128)(2,1)S(1)}, bf16[128,128]{1,0:T(8,128)(2,1)S(1)}, u32[]{:S(2)}, u32[]{:S(2)}) collective-permute-start(bf16[128,128]{1,0:T(8,128)(2,1)S(1)} %get-tuple-element.49), channel_id=1, source_target_pairs={{0,7},{1,2},{2,1},{3,4},{4,3},{5,6},{6,5},{7,0},{8,15},{9,10},{10,... | collective-permute-start | bytes 98312 | tf_op jit(solution)/shard_map/ppermute | solution.py:444
  30.6 0.9 collective-permute-done.5.first
  31.5 2.7 %collective-permute-done.6.second = bf16[128,128]{1,0:T(8,128)(2,1)S(1)} collective-permute-done((bf16[128,128]{1,0:T(8,128)(2,1)S(1)}, bf16[128,128]{1,0:T(8,128)(2,1)S(1)}, u32[]{:S(2)}, u32[]{:S(2)}) %collective-permute-start.6) | collective-permute-done | bytes 32800 | tf_op jit(solution)/shard_map/ppermute | solution.py:444
  34.2 0.6 collective-permute-start.8
  34.8 0.5 collective-permute-start.7
  35.4 3.2 %collective-permute-done.8.refs_6_ = bf16[128,256]{1,0:T(8,128)(2,1)S(1)} collective-permute-done((bf16[128,256]{1,0:T(8,128)(2,1)S(1)}, bf16[128,256]{1,0:T(8,128)(2,1)S(1)}, u32[]{:S(2)}, u32[]{:S(2)}) %collective-permute-start.8) | collective-permute-done | bytes 65568 | tf_op jit(solution)/shard_map/ppermute | solution.py:450
  38.6 1.2 %collective-permute-done.9.refs_7_ = bf16[128,256]{1,0:T(8,128)(2,1)S(1)} collective-permute-done((bf16[128,256]{1,0:T(8,128)(2,1)S(1)}, bf16[128,256]{1,0:T(8,128)(2,1)S(1)}, u32[]{:S(2)}, u32[]{:S(2)}) %collective-permute-start.9) | collective-permute-done | bytes 65568 | tf_op jit(solution)/shard_map/ppermute | solution.py:450
  39.9 6.5 %shard_map.159 = (f32[128,512]{1,0:T(8,128)S(1)}, f32[128,256]{1,0:T(8,128)S(1)}, f32[128,512]{1,0:T(8,128)S(1)}, f32[128,256]{1,0:T(8,128)S(1)}, f32[8,256]{1,0:T(8,128)S(1)}) custom-call(bf16[128,512]{1,0:T(8,128)(2,1)S(1)} %get-tuple-element.47.refs_0_, bf16[128,512]{1,0:T(8,128)(2,1)S(1)} %collective-permute-done.2.refs_1_, ...), custom_call_target="tpu_custom_call" | custom-call | flops 3221225472 | bytes 8921088 | tf_op jit(solution)/shard_map/pallas_call | solution.py:463
  46.4 0.2 collective-permute-start.10
  46.6 0.4 collective-permute-start.11
  47.0 1.2 %collective-permute-done.11.got = f32[128,256]{1,0:T(8,128)S(1)} collective-permute-done((f32[128,256]{1,0:T(8,128)S(1)}, f32[128,256]{1,0:T(8,128)S(1)}, u32[]{:S(2)}, u32[]{:S(2)}) %collective-permute-start.11) | collective-permute-done | bytes 131104 | tf_op jit(solution)/shard_map/ppermute | solution.py:450
  48.2 0.3 collective-permute-start.12
  48.5 2.9 %collective-permute-start.13 = (bf16[128,128]{1,0:T(8,128)(2,1)S(1)}, bf16[128,128]{1,0:T(8,128)(2,1)S(1)}, u32[]{:S(2)}, u32[]{:S(2)}) collective-permute-start(bf16[128,128]{1,0:T(8,128)(2,1)S(1)} %get-tuple-element.58), channel_id=1, source_target_pairs={{0,7},{1,2},{2,1},{3,4},{4,3},{5,6},{6,5},{7,0},{8,15},{9,10},{10,... | collective-permute-start | bytes 98312 | tf_op jit(solution)/shard_map/ppermute | solution.py:444
  51.4 0.8 collective-permute-done.12.from_first
  52.2 2.9 %collective-permute-done.13.from_second = bf16[128,128]{1,0:T(8,128)(2,1)S(1)} collective-permute-done((bf16[128,128]{1,0:T(8,128)(2,1)S(1)}, bf16[128,128]{1,0:T(8,128)(2,1)S(1)}, u32[]{:S(2)}, u32[]{:S(2)}) %collective-permute-start.13) | collective-permute-done | bytes 32800 | tf_op jit(solution)/shard_map/ppermute | solution.py:444
  55.2 3.5 %shard_map.161 = (f32[256,1792]{1,0:T(8,128)S(1)}, bf16[64,1792]{1,0:T(8,128)(2,1)S(1)}, bf16[192,1792]{1,0:T(8,128)(2,1)S(1)}) custom-call(f32[128,512]{1,0:T(8,128)S(1)} %get-tuple-element.53.own_mid, f32[128,512]{1,0:T(8,128)S(1)} %collective-permute-done.10.pair_mid, bf16[128,128]{1,0:T(8,128)(2,1)S(1)} %collective-permute-done.12.from_first, ...), custom_call_target="tpu_custom_call" | custom-call | flops 2415919104 | bytes 13968384 | tf_op jit(solution)/shard_map/pallas_call | solution.py:463
  58.7 0.1 collective-permute-start.14
  58.8 0.5 collective-permute-start.18
  59.3 2.0 %collective-permute-done.18.first = bf16[64,1792]{1,0:T(8,128)(2,1)S(1)} collective-permute-done((bf16[64,1792]{1,0:T(8,128)(2,1)S(1)}, bf16[64,1792]{1,0:T(8,128)(2,1)S(1)}, u32[]{:S(2)}, u32[]{:S(2)}) %collective-permute-start.18) | collective-permute-done | bytes 229408 | tf_op jit(solution)/shard_map/ppermute | solution.py:450
  61.3 0.1 shard_map.163
  61.4 0.6 collective-permute-start.19
  62.0 0.1 shard_map.162
  62.1 0.1 collective-permute-start.15
  62.2 0.1 collective-permute-start.16
  62.3 3.4 %collective-permute-start.17 = (bf16[32,1792]{1,0:T(8,128)(2,1)S(1)}, bf16[32,1792]{1,0:T(8,128)(2,1)S(1)}, u32[]{:S(2)}, u32[]{:S(2)}) collective-permute-start(bf16[32,1792]{1,0:T(8,128)(2,1)S(1)} %get-tuple-element.70), channel_id=1, source_target_pairs={{0,3},{1,2},{2,1},{3,0},{4,7},{5,6},{6,5},{7,4},{8,11},{9,10},{10,... | collective-permute-start | bytes 344072 | tf_op jit(solution)/shard_map/ppermute | solution.py:450
  65.7 3.4 %collective-permute-done.19.far = bf16[64,1792]{1,0:T(8,128)(2,1)S(1)} collective-permute-done((bf16[64,1792]{1,0:T(8,128)(2,1)S(1)}, bf16[64,1792]{1,0:T(8,128)(2,1)S(1)}, u32[]{:S(2)}, u32[]{:S(2)}) %collective-permute-start.19) | collective-permute-done | bytes 229408 | tf_op jit(solution)/shard_map/ppermute | solution.py:450
  69.1 0.1 shard_map.164
  69.2 0.1 collective-permute-start.20
  69.3 2.3 %collective-permute-start.21 = (bf16[16,1792]{1,0:T(8,128)(2,1)S(1)}, bf16[16,1792]{1,0:T(8,128)(2,1)S(1)}, u32[]{:S(2)}, u32[]{:S(2)}) collective-permute-start(bf16[16,1792]{1,0:T(8,128)(2,1)S(1)} %get-tuple-element.73), channel_id=1, source_target_pairs={{0,5},{1,4},{2,7},{3,6},{4,1},{5,0},{6,3},{7,2},{8,13},{9,12},{10,... | collective-permute-start | bytes 172040 | tf_op jit(solution)/shard_map/ppermute | solution.py:450
  71.6 3.4 %collective-permute-start.22 = (bf16[16,1792]{1,0:T(8,128)(2,1)S(1)}, bf16[16,1792]{1,0:T(8,128)(2,1)S(1)}, u32[]{:S(2)}, u32[]{:S(2)}) collective-permute-start(bf16[16,1792]{1,0:T(8,128)(2,1)S(1)} %get-tuple-element.74), channel_id=1, source_target_pairs={{0,6},{1,7},{2,4},{3,5},{4,2},{5,3},{6,0},{7,1},{8,14},{9,15},{10,... | collective-permute-start | bytes 172040 | tf_op jit(solution)/shard_map/ppermute | solution.py:450
  75.1 1.9 %collective-permute-start.23 = (bf16[16,1792]{1,0:T(8,128)(2,1)S(1)}, bf16[16,1792]{1,0:T(8,128)(2,1)S(1)}, u32[]{:S(2)}, u32[]{:S(2)}) collective-permute-start(bf16[16,1792]{1,0:T(8,128)(2,1)S(1)} %get-tuple-element.75), channel_id=1, source_target_pairs={{0,7},{1,6},{2,5},{3,4},{4,3},{5,2},{6,1},{7,0},{8,15},{9,14},{10,... | collective-permute-start | bytes 172040 | tf_op jit(solution)/shard_map/ppermute | solution.py:450
  76.9 0.1 shard_map.165
  77.0 0.6 collective-permute-start.24
  77.6 0.5 collective-permute-done.21.refs_4_
  78.1 0.2 collective-permute-done.22.refs_5_
  78.3 3.7 %collective-permute-done.23.refs_6_ = bf16[16,1792]{1,0:T(8,128)(2,1)S(1)} collective-permute-done((bf16[16,1792]{1,0:T(8,128)(2,1)S(1)}, bf16[16,1792]{1,0:T(8,128)(2,1)S(1)}, u32[]{:S(2)}, u32[]{:S(2)}) %collective-permute-start.23) | collective-permute-done | bytes 57376 | tf_op jit(solution)/shard_map/ppermute | solution.py:450
  82.0 0.1 shard_map.166.mine
  82.0 2.2 %collective-permute-start.29 = (bf16[16,1792]{1,0:T(8,128)(2,1)S(1)}, bf16[16,1792]{1,0:T(8,128)(2,1)S(1)}, u32[]{:S(2)}, u32[]{:S(2)}) collective-permute-start(bf16[16,1792]{1,0:T(8,128)(2,1)S(1)} %shard_map.166.mine), channel_id=1, source_target_pairs={{0,7},{1,6},{2,5},{3,4},{4,3},{5,2},{6,1},{7,0},{8,15},{9,14},{10,... | collective-permute-start | bytes 172040 | tf_op jit(solution)/shard_map/ppermute | solution.py:450
  84.2 1.4 %collective-permute-start.28 = (bf16[16,1792]{1,0:T(8,128)(2,1)S(1)}, bf16[16,1792]{1,0:T(8,128)(2,1)S(1)}, u32[]{:S(2)}, u32[]{:S(2)}) collective-permute-start(bf16[16,1792]{1,0:T(8,128)(2,1)S(1)} %shard_map.166.mine), channel_id=1, source_target_pairs={{0,6},{1,7},{2,4},{3,5},{4,2},{5,3},{6,0},{7,1},{8,14},{9,15},{10,... | collective-permute-start | bytes 172040 | tf_op jit(solution)/shard_map/ppermute | solution.py:450
  85.6 0.5 collective-permute-start.27
  86.1 3.6 %collective-permute-start.26 = (bf16[16,1792]{1,0:T(8,128)(2,1)S(1)}, bf16[16,1792]{1,0:T(8,128)(2,1)S(1)}, u32[]{:S(2)}, u32[]{:S(2)}) collective-permute-start(bf16[16,1792]{1,0:T(8,128)(2,1)S(1)} %shard_map.166.mine), channel_id=1, source_target_pairs={{0,4},{1,5},{2,6},{3,7},{4,0},{5,1},{6,2},{7,3},{8,12},{9,13},{10,... | collective-permute-start | bytes 172040 | tf_op jit(solution)/shard_map/ppermute | solution.py:450
  89.8 0.5 collective-permute-start.25
  90.3 2.6 %collective-permute-done.27.refs_1_ = bf16[16,1792]{1,0:T(8,128)(2,1)S(1)} collective-permute-done((bf16[16,1792]{1,0:T(8,128)(2,1)S(1)}, bf16[16,1792]{1,0:T(8,128)(2,1)S(1)}, u32[]{:S(2)}, u32[]{:S(2)}) %collective-permute-start.27) | collective-permute-done | bytes 57376 | tf_op jit(solution)/shard_map/ppermute | solution.py:450
  92.9 0.6 collective-permute-done.26.refs_0_
  93.5 0.4 collective-permute-done.25.other
  93.9 0.9 collective-permute-start.32
  94.8 1.1 %collective-permute-start.31 = (bf16[32,1792]{1,0:T(8,128)(2,1)S(1)}, bf16[32,1792]{1,0:T(8,128)(2,1)S(1)}, u32[]{:S(2)}, u32[]{:S(2)}) collective-permute-start(bf16[32,1792]{1,0:T(8,128)(2,1)S(1)} %shard_map.168.refs_0_), channel_id=1, source_target_pairs={{0,2},{1,3},{2,0},{3,1},{4,6},{5,7},{6,4},{7,5},{8,10},{9,11},{10,... | collective-permute-start | bytes 344072 | tf_op jit(solution)/shard_map/ppermute | solution.py:450
  95.9 1.6 %collective-permute-start.30 = (bf16[32,1792]{1,0:T(8,128)(2,1)S(1)}, bf16[32,1792]{1,0:T(8,128)(2,1)S(1)}, u32[]{:S(2)}, u32[]{:S(2)}) collective-permute-start(bf16[32,1792]{1,0:T(8,128)(2,1)S(1)} %shard_map.168.refs_0_), channel_id=1, source_target_pairs={{0,1},{1,0},{2,3},{3,2},{4,5},{5,4},{6,7},{7,6},{8,9},{9,8},{10,11... | collective-permute-start | bytes 344072 | tf_op jit(solution)/shard_map/ppermute | solution.py:450
  97.5 0.5 collective-permute-start.33
  98.0 1.7 %collective-permute-done.32.refs_3_ = bf16[32,1792]{1,0:T(8,128)(2,1)S(1)} collective-permute-done((bf16[32,1792]{1,0:T(8,128)(2,1)S(1)}, bf16[32,1792]{1,0:T(8,128)(2,1)S(1)}, u32[]{:S(2)}, u32[]{:S(2)}) %collective-permute-start.32) | collective-permute-done | bytes 114720 | tf_op jit(solution)/shard_map/ppermute | solution.py:450
  99.7 0.7 collective-permute-done.31.refs_2_
  100.4 0.5 collective-permute-done.30.refs_1_
  101.0 0.1 collective-permute-start.34
  101.0 0.5 collective-permute-start.35
  101.5 2.0 %collective-permute-done.33.refs_2_ = bf16[64,1792]{1,0:T(8,128)(2,1)S(1)} collective-permute-done((bf16[64,1792]{1,0:T(8,128)(2,1)S(1)}, bf16[64,1792]{1,0:T(8,128)(2,1)S(1)}, u32[]{:S(2)}, u32[]{:S(2)}) %collective-permute-start.33) | collective-permute-done | bytes 229408 | tf_op jit(solution)/shard_map/ppermute | solution.py:450
  103.5 1.5 %collective-permute-done.36.refs_5_ = bf16[64,1792]{1,0:T(8,128)(2,1)S(1)} collective-permute-done((bf16[64,1792]{1,0:T(8,128)(2,1)S(1)}, bf16[64,1792]{1,0:T(8,128)(2,1)S(1)}, u32[]{:S(2)}, u32[]{:S(2)}) %collective-permute-start.36) | collective-permute-done | bytes 229408 | tf_op jit(solution)/shard_map/ppermute | solution.py:450
  105.0 2.0 %shard_map.170 = (f32[512,512]{1,0:T(8,128)}, f32[512,512]{1,0:T(8,128)}, f32[512,512]{1,0:T(8,128)}, f32[512,128]{1,0:T(8,128)}, f32[1,1]{1,0:T(1,128)}) custom-call(bf16[128,1792]{1,0:T(8,128)(2,1)S(1)} %shard_map.169.refs_0_, bf16[64,1792]{1,0:T(8,128)(2,1)S(1)} %shard_map.167.after.refs_1_, bf16[64,1792]{1,0:T(8,128)(2,1)S(1)} %collective-permute-done.33.refs_2_, ...), custom_call_target="tpu_custom_call" | custom-call | bytes 5505024 | tf_op jit(solution)/shard_map/pallas_call | solution.py:628
  (54 shorter events, 0.2 us)
Async XLA Ops:
  0.6 14.1 %copy-start.8 = (s32[128]{0:T(128)S(1)}, s32[128]{0:T(128)}, u32[]{:S(2)}) copy-start(s32[128]{0:T(128)} %param.15) | copy-start | bytes 1540
  0.6 14.1 %copy-start.7 = (s32[128]{0:T(128)S(1)}, s32[128]{0:T(128)}, u32[]{:S(2)}) copy-start(s32[128]{0:T(128)} %param.14) | copy-start | bytes 1540
  0.7 14.1 %copy-start.6 = (bf16[512,128]{1,0:T(8,128)(2,1)S(1)}, bf16[512,128]{1,0:T(8,128)(2,1)}, u32[]{:S(2)}) copy-start(bf16[512,128]{1,0:T(8,128)(2,1)} %w_decode.1) | copy-start | bytes 393220
  0.7 14.1 %copy-start.12 = (s32[6,512]{1,0:T(8,128)S(1)}, s32[6,512]{1,0:T(8,128)}, u32[]{:S(2)}) copy-start(s32[6,512]{1,0:T(8,128)} %senders_in.1) | copy-start | bytes 36868
  3.0 11.8 %collective-permute-start = (bf16[512,128]{1,0:T(8,128)(2,1)}, bf16[512,128]{1,0:T(8,128)(2,1)S(1)}, u32[]{:S(2)}, u32[]{:S(2)}) collective-permute-start(bf16[512,128]{1,0:T(8,128)(2,1)} %get-tuple-element.44), channel_id=1, source_target_pairs={{0,1},{1,0},{2,3},{3,2},{4,5},{5,4},{6,7},{7,6},{8,9},{9,8},{10,11... | collective-permute-start | bytes 393224 | tf_op jit(solution)/shard_map/ppermute | solution.py:450
  6.0 8.8 %collective-permute-start.1 = (bf16[512,128]{1,0:T(8,128)(2,1)}, bf16[512,128]{1,0:T(8,128)(2,1)S(1)}, u32[]{:S(2)}, u32[]{:S(2)}) collective-permute-start(bf16[512,128]{1,0:T(8,128)(2,1)} %get-tuple-element.45), channel_id=1, source_target_pairs={{0,7},{1,2},{2,1},{3,4},{4,3},{5,6},{6,5},{7,0},{8,15},{9,10},{10,... | collective-permute-start | bytes 393224 | tf_op jit(solution)/shard_map/ppermute | solution.py:444
  14.8 0.7 copy-start.13
  15.5 24.3 %copy-start.9 = (bf16[1536,2048]{1,0:T(8,128)(2,1)S(1)}, bf16[1536,2048]{1,0:T(8,128)(2,1)}, u32[]{:S(2)}) copy-start(bf16[1536,2048]{1,0:T(8,128)(2,1)} %get-tuple-element.50.refs_8_) | copy-start | bytes 18874372
  15.5 24.3 %copy-start.10 = (bf16[128,2048]{1,0:T(8,128)(2,1)S(1)}, bf16[128,2048]{1,0:T(8,128)(2,1)}, u32[]{:S(2)}) copy-start(bf16[128,2048]{1,0:T(8,128)(2,1)} %get-tuple-element.51.refs_9_) | copy-start | bytes 1572868
  15.5 24.3 %copy-start.11 = (bf16[128,2048]{1,0:T(8,128)(2,1)S(1)}, bf16[128,2048]{1,0:T(8,128)(2,1)}, u32[]{:S(2)}) copy-start(bf16[128,2048]{1,0:T(8,128)(2,1)} %get-tuple-element.52.refs_10_) | copy-start | bytes 1572868
  26.0 8.8 %collective-permute-start.3 = (bf16[128,512]{1,0:T(8,128)(2,1)S(1)}, bf16[128,512]{1,0:T(8,128)(2,1)S(1)}, u32[]{:S(2)}, u32[]{:S(2)}) collective-permute-start(bf16[128,512]{1,0:T(8,128)(2,1)S(1)} %get-tuple-element.47.refs_0_), channel_id=1, source_target_pairs={{0,16},{8,24},{16,0},{24,8},{1,17},{9,25},{17,1},{25,9},{2,18},{10... | collective-permute-start | bytes 393224 | tf_op jit(solution)/shard_map/ppermute | solution.py:450
  27.6 3.9 %collective-permute-start.5 = (bf16[128,128]{1,0:T(8,128)(2,1)S(1)}, bf16[128,128]{1,0:T(8,128)(2,1)S(1)}, u32[]{:S(2)}, u32[]{:S(2)}) collective-permute-start(bf16[128,128]{1,0:T(8,128)(2,1)S(1)} %get-tuple-element.48), channel_id=1, source_target_pairs={{0,1},{1,0},{2,3},{3,2},{4,5},{5,4},{6,7},{7,6},{8,9},{9,8},{10,11... | collective-permute-start | bytes 98312 | tf_op jit(solution)/shard_map/ppermute | solution.py:450
  27.6 6.6 %collective-permute-start.6 = (bf16[128,128]{1,0:T(8,128)(2,1)S(1)}, bf16[128,128]{1,0:T(8,128)(2,1)S(1)}, u32[]{:S(2)}, u32[]{:S(2)}) collective-permute-start(bf16[128,128]{1,0:T(8,128)(2,1)S(1)} %get-tuple-element.49), channel_id=1, source_target_pairs={{0,7},{1,2},{2,1},{3,4},{4,3},{5,6},{6,5},{7,0},{8,15},{9,10},{10,... | collective-permute-start | bytes 98312 | tf_op jit(solution)/shard_map/ppermute | solution.py:444
  30.6 8.0 %collective-permute-start.2 = (bf16[128,512]{1,0:T(8,128)(2,1)S(1)}, bf16[128,512]{1,0:T(8,128)(2,1)S(1)}, u32[]{:S(2)}, u32[]{:S(2)}) collective-permute-start(bf16[128,512]{1,0:T(8,128)(2,1)S(1)} %get-tuple-element.47.refs_0_), channel_id=1, source_target_pairs={{0,8},{8,0},{16,24},{24,16},{1,9},{9,1},{17,25},{25,17},{2,10},{10... | collective-permute-start | bytes 393224 | tf_op jit(solution)/shard_map/ppermute | solution.py:450
  34.2 4.3 %collective-permute-start.8 = (bf16[128,256]{1,0:T(8,128)(2,1)S(1)}, bf16[128,256]{1,0:T(8,128)(2,1)S(1)}, u32[]{:S(2)}, u32[]{:S(2)}) collective-permute-start(bf16[128,256]{1,0:T(8,128)(2,1)S(1)} %shard_map.158.refs_4_), channel_id=1, source_target_pairs={{0,16},{8,24},{16,0},{24,8},{1,17},{9,25},{17,1},{25,9},{2,18},{10... | collective-permute-start | bytes 196616 | tf_op jit(solution)/shard_map/ppermute | solution.py:450
  34.8 5.0 %collective-permute-start.4 = (bf16[128,512]{1,0:T(8,128)(2,1)S(1)}, bf16[128,512]{1,0:T(8,128)(2,1)S(1)}, u32[]{:S(2)}, u32[]{:S(2)}) collective-permute-start(bf16[128,512]{1,0:T(8,128)(2,1)S(1)} %collective-permute-done.3.refs_2_), channel_id=1, source_target_pairs={{0,8},{8,0},{16,24},{24,16},{1,9},{9,1},{17,25},{25,17},{2,10},{10... | collective-permute-start | bytes 393224 | tf_op jit(solution)/shard_map/ppermute | solution.py:450
  34.8 3.7 %collective-permute-start.7 = (bf16[128,256]{1,0:T(8,128)(2,1)S(1)}, bf16[128,256]{1,0:T(8,128)(2,1)S(1)}, u32[]{:S(2)}, u32[]{:S(2)}) collective-permute-start(bf16[128,256]{1,0:T(8,128)(2,1)S(1)} %shard_map.158.refs_4_), channel_id=1, source_target_pairs={{0,8},{8,0},{16,24},{24,16},{1,9},{9,1},{17,25},{25,17},{2,10},{10... | collective-permute-start | bytes 196616 | tf_op jit(solution)/shard_map/ppermute | solution.py:450
  38.6 1.3 %collective-permute-start.9 = (bf16[128,256]{1,0:T(8,128)(2,1)S(1)}, bf16[128,256]{1,0:T(8,128)(2,1)S(1)}, u32[]{:S(2)}, u32[]{:S(2)}) collective-permute-start(bf16[128,256]{1,0:T(8,128)(2,1)S(1)} %collective-permute-done.8.refs_6_), channel_id=1, source_target_pairs={{0,8},{8,0},{16,24},{24,16},{1,9},{9,1},{17,25},{25,17},{2,10},{10... | collective-permute-start | bytes 196616 | tf_op jit(solution)/shard_map/ppermute | solution.py:450
  39.8 15.3 %copy-start = (bf16[512,3072]{1,0:T(8,128)(2,1)S(1)}, bf16[512,3072]{1,0:T(8,128)(2,1)}, u32[]{:S(2)}) copy-start(bf16[512,3072]{1,0:T(8,128)(2,1)} %get-tuple-element.60.picked_t) | copy-start | bytes 9437188
  39.9 15.3 %copy-start.1 = (bf16[512,3072]{1,0:T(8,128)(2,1)S(1)}, bf16[512,3072]{1,0:T(8,128)(2,1)}, u32[]{:S(2)}) copy-start(bf16[512,3072]{1,0:T(8,128)(2,1)} %get-tuple-element.61.slope_t) | copy-start | bytes 9437188
  39.9 15.3 %copy-start.2 = (bf16[512,512]{1,0:T(8,128)(2,1)S(1)}, bf16[512,512]{1,0:T(8,128)(2,1)}, u32[]{:S(2)}) copy-start(bf16[512,512]{1,0:T(8,128)(2,1)} %get-tuple-element.43.after.nodes_in.nodes_t) | copy-start | bytes 1572868
  39.9 15.3 %copy-start.3 = (f32[512,512]{1,0:T(8,128)S(1)}, f32[512,512]{1,0:T(8,128)}, u32[]{:S(2)}) copy-start(f32[512,512]{1,0:T(8,128)} %get-tuple-element.62.slope_sum_t) | copy-start | bytes 3145732
  39.9 15.3 %copy-start.4 = (f32[512,512]{1,0:T(8,128)S(1)}, f32[512,512]{1,0:T(8,128)}, u32[]{:S(2)}) copy-start(f32[512,512]{1,0:T(8,128)} %get-tuple-element.64.upd_slope_t) | copy-start | bytes 3145732
  39.9 15.3 %copy-start.5 = (bf16[512,512]{1,0:T(8,128)(2,1)S(1)}, bf16[512,512]{1,0:T(8,128)(2,1)}, u32[]{:S(2)}) copy-start(bf16[512,512]{1,0:T(8,128)(2,1)} %vertex.1) | copy-start | bytes 1572868
  46.4 8.7 %collective-permute-start.10 = (f32[128,512]{1,0:T(8,128)S(1)}, f32[128,512]{1,0:T(8,128)S(1)}, u32[]{:S(2)}, u32[]{:S(2)}) collective-permute-start(f32[128,512]{1,0:T(8,128)S(1)} %get-tuple-element.54), channel_id=1, source_target_pairs={{0,8},{8,0},{16,24},{24,16},{1,9},{9,1},{17,25},{25,17},{2,10},{10... | collective-permute-start | bytes 786440 | tf_op jit(solution)/shard_map/ppermute | solution.py:450
  46.6 1.6 %collective-permute-start.11 = (f32[128,256]{1,0:T(8,128)S(1)}, f32[128,256]{1,0:T(8,128)S(1)}, u32[]{:S(2)}, u32[]{:S(2)}) collective-permute-start(f32[128,256]{1,0:T(8,128)S(1)} %get-tuple-element.56), channel_id=1, source_target_pairs={{0,8},{8,0},{16,24},{24,16},{1,9},{9,1},{17,25},{25,17},{2,10},{10... | collective-permute-start | bytes 393224 | tf_op jit(solution)/shard_map/ppermute | solution.py:450
  48.2 4.0 %collective-permute-start.12 = (bf16[128,128]{1,0:T(8,128)(2,1)S(1)}, bf16[128,128]{1,0:T(8,128)(2,1)S(1)}, u32[]{:S(2)}, u32[]{:S(2)}) collective-permute-start(bf16[128,128]{1,0:T(8,128)(2,1)S(1)} %get-tuple-element.57), channel_id=1, source_target_pairs={{0,1},{1,0},{2,3},{3,2},{4,5},{5,4},{6,7},{7,6},{8,9},{9,8},{10,11... | collective-permute-start | bytes 98312 | tf_op jit(solution)/shard_map/ppermute | solution.py:450
  48.5 6.6 %collective-permute-start.13 = (bf16[128,128]{1,0:T(8,128)(2,1)S(1)}, bf16[128,128]{1,0:T(8,128)(2,1)S(1)}, u32[]{:S(2)}, u32[]{:S(2)}) collective-permute-start(bf16[128,128]{1,0:T(8,128)(2,1)S(1)} %get-tuple-element.58), channel_id=1, source_target_pairs={{0,7},{1,2},{2,1},{3,4},{4,3},{5,6},{6,5},{7,0},{8,15},{9,10},{10,... | collective-permute-start | bytes 98312 | tf_op jit(solution)/shard_map/ppermute | solution.py:444
  58.7 3.3 %collective-permute-start.14 = (bf16[192,1792]{1,0:T(8,128)(2,1)S(1)}, bf16[192,1792]{1,0:T(8,128)(2,1)S(1)}, u32[]{:S(2)}, u32[]{:S(2)}) collective-permute-start(bf16[192,1792]{1,0:T(8,128)(2,1)S(1)} %get-tuple-element.67), channel_id=1, source_target_pairs={{0,8},{8,0},{16,24},{24,16},{1,9},{9,1},{17,25},{25,17},{2,10},{10... | collective-permute-start | bytes 2064392 | tf_op jit(solution)/shard_map/ppermute | solution.py:450
  58.8 2.5 %collective-permute-start.18 = (bf16[64,1792]{1,0:T(8,128)(2,1)S(1)}, bf16[64,1792]{1,0:T(8,128)(2,1)S(1)}, u32[]{:S(2)}, u32[]{:S(2)}) collective-permute-start(bf16[64,1792]{1,0:T(8,128)(2,1)S(1)} %get-tuple-element.71), channel_id=1, source_target_pairs={{0,8},{8,0},{16,24},{24,16},{1,9},{9,1},{17,25},{25,17},{2,10},{10... | collective-permute-start | bytes 688136 | tf_op jit(solution)/shard_map/ppermute | solution.py:450
  61.4 7.7 %collective-permute-start.19 = (bf16[64,1792]{1,0:T(8,128)(2,1)S(1)}, bf16[64,1792]{1,0:T(8,128)(2,1)S(1)}, u32[]{:S(2)}, u32[]{:S(2)}) collective-permute-start(bf16[64,1792]{1,0:T(8,128)(2,1)S(1)} %shard_map.163), channel_id=1, source_target_pairs={{0,16},{8,24},{16,0},{24,8},{1,17},{9,25},{17,1},{25,9},{2,18},{10... | collective-permute-start | bytes 688136 | tf_op jit(solution)/shard_map/ppermute | solution.py:450
  62.1 9.5 %collective-permute-start.15 = (bf16[32,1792]{1,0:T(8,128)(2,1)S(1)}, bf16[32,1792]{1,0:T(8,128)(2,1)S(1)}, u32[]{:S(2)}, u32[]{:S(2)}) collective-permute-start(bf16[32,1792]{1,0:T(8,128)(2,1)S(1)} %get-tuple-element.68), channel_id=1, source_target_pairs={{0,1},{1,0},{2,3},{3,2},{4,5},{5,4},{6,7},{7,6},{8,9},{9,8},{10,11... | collective-permute-start | bytes 344072 | tf_op jit(solution)/shard_map/ppermute | solution.py:450
  62.2 12.9 %collective-permute-start.16 = (bf16[32,1792]{1,0:T(8,128)(2,1)S(1)}, bf16[32,1792]{1,0:T(8,128)(2,1)S(1)}, u32[]{:S(2)}, u32[]{:S(2)}) collective-permute-start(bf16[32,1792]{1,0:T(8,128)(2,1)S(1)} %get-tuple-element.69), channel_id=1, source_target_pairs={{0,2},{1,3},{2,0},{3,1},{4,6},{5,7},{6,4},{7,5},{8,10},{9,11},{10,... | collective-permute-start | bytes 344072 | tf_op jit(solution)/shard_map/ppermute | solution.py:450
  62.3 14.7 %collective-permute-start.17 = (bf16[32,1792]{1,0:T(8,128)(2,1)S(1)}, bf16[32,1792]{1,0:T(8,128)(2,1)S(1)}, u32[]{:S(2)}, u32[]{:S(2)}) collective-permute-start(bf16[32,1792]{1,0:T(8,128)(2,1)S(1)} %get-tuple-element.70), channel_id=1, source_target_pairs={{0,3},{1,2},{2,1},{3,0},{4,7},{5,6},{6,5},{7,4},{8,11},{9,10},{10,... | collective-permute-start | bytes 344072 | tf_op jit(solution)/shard_map/ppermute | solution.py:450
  69.2 8.4 %collective-permute-start.20 = (bf16[16,1792]{1,0:T(8,128)(2,1)S(1)}, bf16[16,1792]{1,0:T(8,128)(2,1)S(1)}, u32[]{:S(2)}, u32[]{:S(2)}) collective-permute-start(bf16[16,1792]{1,0:T(8,128)(2,1)S(1)} %get-tuple-element.72), channel_id=1, source_target_pairs={{0,4},{1,5},{2,6},{3,7},{4,0},{5,1},{6,2},{7,3},{8,12},{9,13},{10,... | collective-permute-start | bytes 172040 | tf_op jit(solution)/shard_map/ppermute | solution.py:450
  69.3 8.8 %collective-permute-start.21 = (bf16[16,1792]{1,0:T(8,128)(2,1)S(1)}, bf16[16,1792]{1,0:T(8,128)(2,1)S(1)}, u32[]{:S(2)}, u32[]{:S(2)}) collective-permute-start(bf16[16,1792]{1,0:T(8,128)(2,1)S(1)} %get-tuple-element.73), channel_id=1, source_target_pairs={{0,5},{1,4},{2,7},{3,6},{4,1},{5,0},{6,3},{7,2},{8,13},{9,12},{10,... | collective-permute-start | bytes 172040 | tf_op jit(solution)/shard_map/ppermute | solution.py:450
  71.6 6.6 %collective-permute-start.22 = (bf16[16,1792]{1,0:T(8,128)(2,1)S(1)}, bf16[16,1792]{1,0:T(8,128)(2,1)S(1)}, u32[]{:S(2)}, u32[]{:S(2)}) collective-permute-start(bf16[16,1792]{1,0:T(8,128)(2,1)S(1)} %get-tuple-element.74), channel_id=1, source_target_pairs={{0,6},{1,7},{2,4},{3,5},{4,2},{5,3},{6,0},{7,1},{8,14},{9,15},{10,... | collective-permute-start | bytes 172040 | tf_op jit(solution)/shard_map/ppermute | solution.py:450
  75.1 6.9 %collective-permute-start.23 = (bf16[16,1792]{1,0:T(8,128)(2,1)S(1)}, bf16[16,1792]{1,0:T(8,128)(2,1)S(1)}, u32[]{:S(2)}, u32[]{:S(2)}) collective-permute-start(bf16[16,1792]{1,0:T(8,128)(2,1)S(1)} %get-tuple-element.75), channel_id=1, source_target_pairs={{0,7},{1,6},{2,5},{3,4},{4,3},{5,2},{6,1},{7,0},{8,15},{9,14},{10,... | collective-permute-start | bytes 172040 | tf_op jit(solution)/shard_map/ppermute | solution.py:450
  77.0 4.9 %collective-permute-start.24 = (bf16[16,1792]{1,0:T(8,128)(2,1)S(1)}, bf16[16,1792]{1,0:T(8,128)(2,1)S(1)}, u32[]{:S(2)}, u32[]{:S(2)}) collective-permute-start(bf16[16,1792]{1,0:T(8,128)(2,1)S(1)} %shard_map.165), channel_id=1, source_target_pairs={{0,16},{8,24},{16,0},{24,8},{1,17},{9,25},{17,1},{25,9},{2,18},{10... | collective-permute-start | bytes 172040 | tf_op jit(solution)/shard_map/ppermute | solution.py:450
  82.0 8.3 %collective-permute-start.29 = (bf16[16,1792]{1,0:T(8,128)(2,1)S(1)}, bf16[16,1792]{1,0:T(8,128)(2,1)S(1)}, u32[]{:S(2)}, u32[]{:S(2)}) collective-permute-start(bf16[16,1792]{1,0:T(8,128)(2,1)S(1)} %shard_map.166.mine), channel_id=1, source_target_pairs={{0,7},{1,6},{2,5},{3,4},{4,3},{5,2},{6,1},{7,0},{8,15},{9,14},{10,... | collective-permute-start | bytes 172040 | tf_op jit(solution)/shard_map/ppermute | solution.py:450
  84.2 6.1 %collective-permute-start.28 = (bf16[16,1792]{1,0:T(8,128)(2,1)S(1)}, bf16[16,1792]{1,0:T(8,128)(2,1)S(1)}, u32[]{:S(2)}, u32[]{:S(2)}) collective-permute-start(bf16[16,1792]{1,0:T(8,128)(2,1)S(1)} %shard_map.166.mine), channel_id=1, source_target_pairs={{0,6},{1,7},{2,4},{3,5},{4,2},{5,3},{6,0},{7,1},{8,14},{9,15},{10,... | collective-permute-start | bytes 172040 | tf_op jit(solution)/shard_map/ppermute | solution.py:450
  85.6 7.3 %collective-permute-start.27 = (bf16[16,1792]{1,0:T(8,128)(2,1)S(1)}, bf16[16,1792]{1,0:T(8,128)(2,1)S(1)}, u32[]{:S(2)}, u32[]{:S(2)}) collective-permute-start(bf16[16,1792]{1,0:T(8,128)(2,1)S(1)} %shard_map.166.mine), channel_id=1, source_target_pairs={{0,5},{1,4},{2,7},{3,6},{4,1},{5,0},{6,3},{7,2},{8,13},{9,12},{10,... | collective-permute-start | bytes 172040 | tf_op jit(solution)/shard_map/ppermute | solution.py:450
  86.1 7.4 %collective-permute-start.26 = (bf16[16,1792]{1,0:T(8,128)(2,1)S(1)}, bf16[16,1792]{1,0:T(8,128)(2,1)S(1)}, u32[]{:S(2)}, u32[]{:S(2)}) collective-permute-start(bf16[16,1792]{1,0:T(8,128)(2,1)S(1)} %shard_map.166.mine), channel_id=1, source_target_pairs={{0,4},{1,5},{2,6},{3,7},{4,0},{5,1},{6,2},{7,3},{8,12},{9,13},{10,... | collective-permute-start | bytes 172040 | tf_op jit(solution)/shard_map/ppermute | solution.py:450
  89.8 4.2 %collective-permute-start.25 = (bf16[16,1792]{1,0:T(8,128)(2,1)S(1)}, bf16[16,1792]{1,0:T(8,128)(2,1)S(1)}, u32[]{:S(2)}, u32[]{:S(2)}) collective-permute-start(bf16[16,1792]{1,0:T(8,128)(2,1)S(1)} %shard_map.166.mine), channel_id=1, source_target_pairs={{0,16},{8,24},{16,0},{24,8},{1,17},{9,25},{17,1},{25,9},{2,18},{10... | collective-permute-start | bytes 172040 | tf_op jit(solution)/shard_map/ppermute | solution.py:450
  93.9 5.8 %collective-permute-start.32 = (bf16[32,1792]{1,0:T(8,128)(2,1)S(1)}, bf16[32,1792]{1,0:T(8,128)(2,1)S(1)}, u32[]{:S(2)}, u32[]{:S(2)}) collective-permute-start(bf16[32,1792]{1,0:T(8,128)(2,1)S(1)} %shard_map.168.refs_0_), channel_id=1, source_target_pairs={{0,3},{1,2},{2,1},{3,0},{4,7},{5,6},{6,5},{7,4},{8,11},{9,10},{10,... | collective-permute-start | bytes 344072 | tf_op jit(solution)/shard_map/ppermute | solution.py:450
  94.8 5.6 %collective-permute-start.31 = (bf16[32,1792]{1,0:T(8,128)(2,1)S(1)}, bf16[32,1792]{1,0:T(8,128)(2,1)S(1)}, u32[]{:S(2)}, u32[]{:S(2)}) collective-permute-start(bf16[32,1792]{1,0:T(8,128)(2,1)S(1)} %shard_map.168.refs_0_), channel_id=1, source_target_pairs={{0,2},{1,3},{2,0},{3,1},{4,6},{5,7},{6,4},{7,5},{8,10},{9,11},{10,... | collective-permute-start | bytes 344072 | tf_op jit(solution)/shard_map/ppermute | solution.py:450
  95.9 5.0 %collective-permute-start.30 = (bf16[32,1792]{1,0:T(8,128)(2,1)S(1)}, bf16[32,1792]{1,0:T(8,128)(2,1)S(1)}, u32[]{:S(2)}, u32[]{:S(2)}) collective-permute-start(bf16[32,1792]{1,0:T(8,128)(2,1)S(1)} %shard_map.168.refs_0_), channel_id=1, source_target_pairs={{0,1},{1,0},{2,3},{3,2},{4,5},{5,4},{6,7},{7,6},{8,9},{9,8},{10,11... | collective-permute-start | bytes 344072 | tf_op jit(solution)/shard_map/ppermute | solution.py:450
  97.5 6.0 %collective-permute-start.33 = (bf16[64,1792]{1,0:T(8,128)(2,1)S(1)}, bf16[64,1792]{1,0:T(8,128)(2,1)S(1)}, u32[]{:S(2)}, u32[]{:S(2)}) collective-permute-start(bf16[64,1792]{1,0:T(8,128)(2,1)S(1)} %shard_map.167.after.refs_1_), channel_id=1, source_target_pairs={{0,16},{8,24},{16,0},{24,8},{1,17},{9,25},{17,1},{25,9},{2,18},{10... | collective-permute-start | bytes 688136 | tf_op jit(solution)/shard_map/ppermute | solution.py:450
  101.0 4.0 %collective-permute-start.34 = (bf16[128,1792]{1,0:T(8,128)(2,1)S(1)}, bf16[128,1792]{1,0:T(8,128)(2,1)S(1)}, u32[]{:S(2)}, u32[]{:S(2)}) collective-permute-start(bf16[128,1792]{1,0:T(8,128)(2,1)S(1)} %shard_map.169.refs_0_), channel_id=1, source_target_pairs={{0,8},{8,0},{16,24},{24,16},{1,9},{9,1},{17,25},{25,17},{2,10},{10... | collective-permute-start | bytes 1376264 | tf_op jit(solution)/shard_map/ppermute | solution.py:450
  101.0 2.5 %collective-permute-start.35 = (bf16[64,1792]{1,0:T(8,128)(2,1)S(1)}, bf16[64,1792]{1,0:T(8,128)(2,1)S(1)}, u32[]{:S(2)}, u32[]{:S(2)}) collective-permute-start(bf16[64,1792]{1,0:T(8,128)(2,1)S(1)} %shard_map.167.after.refs_1_), channel_id=1, source_target_pairs={{0,8},{8,0},{16,24},{24,16},{1,9},{9,1},{17,25},{25,17},{2,10},{10... | collective-permute-start | bytes 688136 | tf_op jit(solution)/shard_map/ppermute | solution.py:450
  103.5 1.5 %collective-permute-start.36 = (bf16[64,1792]{1,0:T(8,128)(2,1)S(1)}, bf16[64,1792]{1,0:T(8,128)(2,1)S(1)}, u32[]{:S(2)}, u32[]{:S(2)}) collective-permute-start(bf16[64,1792]{1,0:T(8,128)(2,1)S(1)} %collective-permute-done.33.refs_2_), channel_id=1, source_target_pairs={{0,8},{8,0},{16,24},{24,16},{1,9},{9,1},{17,25},{25,17},{2,10},{10... | collective-permute-start | bytes 688136 | tf_op jit(solution)/shard_map/ppermute | solution.py:450

commit v11 on v10

--- a/solution.py
+++ b/solution.py
@@ -589,9 +589,9 @@
     grads = call(
         functools.partial(readout_kernel, line_span),
         mids + ends + [mat, base_t, truth_t],
-        [sds((variables, count), F32), sds((variables, 2 * halo), F32)] * 2 + [sds((8, 256), F32)],
+        [sds((variables, count), F32), sds((variables, 2 * halo), F32)] * 2 + [sds((8, 512), F32)],
         [held((members * variables, 2 * ext_rows)), held((2 * variables, ext_rows), F32)]
-        + [held((members * variables, 256), F32)] * 2 + [held((2 * variables, 256))] * 2,
+        + [held((members * variables, 512), F32)] * 2 + [held((2 * variables, 512))] * 2,
         flops=4 * members * variables * ext_rows * half_span,
         limit=24,
     )

time: 107 us -> 107 us (level)
  no operation moved by 1% of the time
where the time goes in v11:
time: 107 us
  starting transfers between devices  41.9 us (39%)
  waiting for transfers between devices  32.8 us (31%)
  Pallas kernels  30 us (28%)
  between operations  1.11 us (1%)
    ppermute x34, starting transfers between devices, flip(): return lax.ppermute(value, axis, [(i, i ^ bit) for i in range(size)])  32.5 us
    ppermute x34, waiting for transfers between devices, flip(): return lax.ppermute(value, axis, [(i, i ^ bit) for i in range(size)])  27.2 us
    pallas_call x14, Pallas kernels, call(): pl.pallas_call(kernel, out_shape=outs, in_specs=freed(vmem(len(ins) - in_...  22.8 us
    ppermute x3, starting transfers between devices, meet(): lax.ppermute(second, 'dom', [(i, (i + (1 if i % 2 else size - 1)) % size)...  9.42 us
    ppermute x3, waiting for transfers between devices, meet(): lax.ppermute(second, 'dom', [(i, (i + (1 if i % 2 else size - 1)) % size)...  5.62 us
    pallas_call x1, Pallas kernels, per_device(): pl.pallas_call(decoder_kernel, grid_spec=pltpu.PrefetchScalarGridSpec(num...  5.2 us
  transfers between devices with their start and end apart: 37, of which 20 were waited for; matrix products, arithmetic and copies ran while one was open for 0% of the time, Pallas kernels for 5%

profile of v11, /device:TPU:0, one launch (start us, length us, event | category | flops | bytes accessed | tf_op | source)
XLA Modules:
  0.0 106.5 jit_solution(4094740257578292796)
XLA Ops:
  0.7 2.3 %shard_map.155 = (bf16[512,512]{1,0:T(8,128)(2,1)}, bf16[512,128]{1,0:T(8,128)(2,1)}, bf16[512,128]{1,0:T(8,128)(2,1)}) custom-call(bf16[512,512]{1,0:T(8,128)(2,1)} %bitcast.11, s32[1,128]{1,0:T(1,128)} %bitcast.5, s32[1,128]{1,0:T(1,128)} %bitcast.8), custom_call_target="tpu_custom_call" | custom-call | flops 134217728 | bytes 1311744 | tf_op jit(solution)/shard_map/pallas_call | solution.py:463
  3.0 3.0 %collective-permute-start = (bf16[512,128]{1,0:T(8,128)(2,1)}, bf16[512,128]{1,0:T(8,128)(2,1)S(1)}, u32[]{:S(2)}, u32[]{:S(2)}) collective-permute-start(bf16[512,128]{1,0:T(8,128)(2,1)} %get-tuple-element.44), channel_id=1, source_target_pairs={{0,1},{1,0},{2,3},{3,2},{4,5},{5,4},{6,7},{7,6},{8,9},{9,8},{10,11... | collective-permute-start | bytes 393224 | tf_op jit(solution)/shard_map/ppermute | solution.py:450
  6.0 3.5 %collective-permute-start.1 = (bf16[512,128]{1,0:T(8,128)(2,1)}, bf16[512,128]{1,0:T(8,128)(2,1)S(1)}, u32[]{:S(2)}, u32[]{:S(2)}) collective-permute-start(bf16[512,128]{1,0:T(8,128)(2,1)} %get-tuple-element.45), channel_id=1, source_target_pairs={{0,7},{1,2},{2,1},{3,4},{4,3},{5,6},{6,5},{7,0},{8,15},{9,10},{10,... | collective-permute-start | bytes 393224 | tf_op jit(solution)/shard_map/ppermute | solution.py:444
  9.5 5.2 %shard_map.156 = (bf16[1536,2048]{1,0:T(8,128)(2,1)}, bf16[128,2048]{1,0:T(8,128)(2,1)}, bf16[128,2048]{1,0:T(8,128)(2,1)}, f32[8,128]{1,0:T(8,128)}) custom-call(s32[1]{0:T(128)} %bitcast.3.core, s32[3,4096]{1,0:T(4,128)} %vertices.1, f32[3,4096]{1,0:T(4,128)} %weights.1, bf16[4096,128]{1,0:T(8,128)(2,1)} %base.1, bf16[4096,128]{1,0:T(8,128)(2,1)} %truth.1, ...), custom_call_target="tpu_custom_call" | custom-call | flops 15728640 | bytes 16000000 | tf_op jit(solution)/shard_map/pallas_call | solution.py:547
  14.8 0.7 copy-done.13
  15.5 10.5 %shard_map.157 = (bf16[128,512]{1,0:T(8,128)(2,1)S(1)}, bf16[128,128]{1,0:T(8,128)(2,1)S(1)}, bf16[128,128]{1,0:T(8,128)(2,1)S(1)}, bf16[512,3072]{1,0:T(8,128)(...) custom-call(bf16[512,512]{1,0:T(8,128)(2,1)} %get-tuple-element.43.a, ...), custom_call_target="tpu_custom_call" | custom-call | flops 4026531840 | bytes 12141568 | tf_op jit(solution)/shard_map/pallas_call | solution.py:463
  26.0 1.6 %collective-permute-start.3 = (bf16[128,512]{1,0:T(8,128)(2,1)S(1)}, bf16[128,512]{1,0:T(8,128)(2,1)S(1)}, u32[]{:S(2)}, u32[]{:S(2)}) collective-permute-start(bf16[128,512]{1,0:T(8,128)(2,1)S(1)} %get-tuple-element.47.refs_0_), channel_id=1, source_target_pairs={{0,16},{8,24},{16,0},{24,8},{1,17},{9,25},{17,1},{25,9},{2,18},{10... | collective-permute-start | bytes 393224 | tf_op jit(solution)/shard_map/ppermute | solution.py:450
  27.6 3.0 %collective-permute-start.6 = (bf16[128,128]{1,0:T(8,128)(2,1)S(1)}, bf16[128,128]{1,0:T(8,128)(2,1)S(1)}, u32[]{:S(2)}, u32[]{:S(2)}) collective-permute-start(bf16[128,128]{1,0:T(8,128)(2,1)S(1)} %get-tuple-element.49), channel_id=1, source_target_pairs={{0,7},{1,2},{2,1},{3,4},{4,3},{5,6},{6,5},{7,0},{8,15},{9,10},{10,... | collective-permute-start | bytes 98312 | tf_op jit(solution)/shard_map/ppermute | solution.py:444
  30.6 0.9 collective-permute-done.5.first
  31.5 2.7 %collective-permute-done.6.second = bf16[128,128]{1,0:T(8,128)(2,1)S(1)} collective-permute-done((bf16[128,128]{1,0:T(8,128)(2,1)S(1)}, bf16[128,128]{1,0:T(8,128)(2,1)S(1)}, u32[]{:S(2)}, u32[]{:S(2)}) %collective-permute-start.6) | collective-permute-done | bytes 32800 | tf_op jit(solution)/shard_map/ppermute | solution.py:444
  34.2 0.6 collective-permute-start.8
  34.8 0.5 collective-permute-start.7
  35.4 3.2 %collective-permute-done.8.refs_6_ = bf16[128,256]{1,0:T(8,128)(2,1)S(1)} collective-permute-done((bf16[128,256]{1,0:T(8,128)(2,1)S(1)}, bf16[128,256]{1,0:T(8,128)(2,1)S(1)}, u32[]{:S(2)}, u32[]{:S(2)}) %collective-permute-start.8) | collective-permute-done | bytes 65568 | tf_op jit(solution)/shard_map/ppermute | solution.py:450
  38.6 1.2 %collective-permute-done.9.refs_7_ = bf16[128,256]{1,0:T(8,128)(2,1)S(1)} collective-permute-done((bf16[128,256]{1,0:T(8,128)(2,1)S(1)}, bf16[128,256]{1,0:T(8,128)(2,1)S(1)}, u32[]{:S(2)}, u32[]{:S(2)}) %collective-permute-start.9) | collective-permute-done | bytes 65568 | tf_op jit(solution)/shard_map/ppermute | solution.py:450
  39.9 6.0 %shard_map.159 = (f32[128,512]{1,0:T(8,128)S(1)}, f32[128,256]{1,0:T(8,128)S(1)}, f32[128,512]{1,0:T(8,128)S(1)}, f32[128,256]{1,0:T(8,128)S(1)}, f32[8,512]{1,0:T(8,128)S(1)}) custom-call(bf16[128,512]{1,0:T(8,128)(2,1)S(1)} %get-tuple-element.47.refs_0_, bf16[128,512]{1,0:T(8,128)(2,1)S(1)} %collective-permute-done.2.refs_1_, ...), custom_call_target="tpu_custom_call" | custom-call | flops 3221225472 | bytes 8929280 | tf_op jit(solution)/shard_map/pallas_call | solution.py:463
  45.9 0.2 collective-permute-start.10
  46.1 0.4 collective-permute-start.11
  46.5 1.2 %collective-permute-done.11.got = f32[128,256]{1,0:T(8,128)S(1)} collective-permute-done((f32[128,256]{1,0:T(8,128)S(1)}, f32[128,256]{1,0:T(8,128)S(1)}, u32[]{:S(2)}, u32[]{:S(2)}) %collective-permute-start.11) | collective-permute-done | bytes 131104 | tf_op jit(solution)/shard_map/ppermute | solution.py:450
  47.7 0.3 collective-permute-start.12
  48.0 2.9 %collective-permute-start.13 = (bf16[128,128]{1,0:T(8,128)(2,1)S(1)}, bf16[128,128]{1,0:T(8,128)(2,1)S(1)}, u32[]{:S(2)}, u32[]{:S(2)}) collective-permute-start(bf16[128,128]{1,0:T(8,128)(2,1)S(1)} %get-tuple-element.58), channel_id=1, source_target_pairs={{0,7},{1,2},{2,1},{3,4},{4,3},{5,6},{6,5},{7,0},{8,15},{9,10},{10,... | collective-permute-start | bytes 98312 | tf_op jit(solution)/shard_map/ppermute | solution.py:444
  50.8 0.8 collective-permute-done.12.from_first
  51.7 2.9 %collective-permute-done.13.from_second = bf16[128,128]{1,0:T(8,128)(2,1)S(1)} collective-permute-done((bf16[128,128]{1,0:T(8,128)(2,1)S(1)}, bf16[128,128]{1,0:T(8,128)(2,1)S(1)}, u32[]{:S(2)}, u32[]{:S(2)}) %collective-permute-start.13) | collective-permute-done | bytes 32800 | tf_op jit(solution)/shard_map/ppermute | solution.py:444
  54.6 3.5 %shard_map.161 = (f32[256,1792]{1,0:T(8,128)S(1)}, bf16[64,1792]{1,0:T(8,128)(2,1)S(1)}, bf16[192,1792]{1,0:T(8,128)(2,1)S(1)}) custom-call(f32[128,512]{1,0:T(8,128)S(1)} %get-tuple-element.53.own_mid, f32[128,512]{1,0:T(8,128)S(1)} %collective-permute-done.10.pair_mid, bf16[128,128]{1,0:T(8,128)(2,1)S(1)} %collective-permute-done.12.from_first, ...), custom_call_target="tpu_custom_call" | custom-call | flops 2415919104 | bytes 13976576 | tf_op jit(solution)/shard_map/pallas_call | solution.py:463
  58.1 0.1 collective-permute-start.14
  58.2 0.5 collective-permute-start.18
  58.7 2.0 %collective-permute-done.18.first = bf16[64,1792]{1,0:T(8,128)(2,1)S(1)} collective-permute-done((bf16[64,1792]{1,0:T(8,128)(2,1)S(1)}, bf16[64,1792]{1,0:T(8,128)(2,1)S(1)}, u32[]{:S(2)}, u32[]{:S(2)}) %collective-permute-start.18) | collective-permute-done | bytes 229408 | tf_op jit(solution)/shard_map/ppermute | solution.py:450
  60.7 0.1 shard_map.163
  60.8 0.6 collective-permute-start.19
  61.4 0.1 shard_map.162
  61.5 0.1 collective-permute-start.15
  61.6 0.1 collective-permute-start.16
  61.6 3.4 %collective-permute-start.17 = (bf16[32,1792]{1,0:T(8,128)(2,1)S(1)}, bf16[32,1792]{1,0:T(8,128)(2,1)S(1)}, u32[]{:S(2)}, u32[]{:S(2)}) collective-permute-start(bf16[32,1792]{1,0:T(8,128)(2,1)S(1)} %get-tuple-element.70), channel_id=1, source_target_pairs={{0,3},{1,2},{2,1},{3,0},{4,7},{5,6},{6,5},{7,4},{8,11},{9,10},{10,... | collective-permute-start | bytes 344072 | tf_op jit(solution)/shard_map/ppermute | solution.py:450
  65.0 3.5 %collective-permute-done.19.far = bf16[64,1792]{1,0:T(8,128)(2,1)S(1)} collective-permute-done((bf16[64,1792]{1,0:T(8,128)(2,1)S(1)}, bf16[64,1792]{1,0:T(8,128)(2,1)S(1)}, u32[]{:S(2)}, u32[]{:S(2)}) %collective-permute-start.19) | collective-permute-done | bytes 229408 | tf_op jit(solution)/shard_map/ppermute | solution.py:450
  68.5 0.1 shard_map.164
  68.6 0.1 collective-permute-start.20
  68.7 2.4 %collective-permute-start.21 = (bf16[16,1792]{1,0:T(8,128)(2,1)S(1)}, bf16[16,1792]{1,0:T(8,128)(2,1)S(1)}, u32[]{:S(2)}, u32[]{:S(2)}) collective-permute-start(bf16[16,1792]{1,0:T(8,128)(2,1)S(1)} %get-tuple-element.73), channel_id=1, source_target_pairs={{0,5},{1,4},{2,7},{3,6},{4,1},{5,0},{6,3},{7,2},{8,13},{9,12},{10,... | collective-permute-start | bytes 172040 | tf_op jit(solution)/shard_map/ppermute | solution.py:450
  71.0 3.4 %collective-permute-start.22 = (bf16[16,1792]{1,0:T(8,128)(2,1)S(1)}, bf16[16,1792]{1,0:T(8,128)(2,1)S(1)}, u32[]{:S(2)}, u32[]{:S(2)}) collective-permute-start(bf16[16,1792]{1,0:T(8,128)(2,1)S(1)} %get-tuple-element.74), channel_id=1, source_target_pairs={{0,6},{1,7},{2,4},{3,5},{4,2},{5,3},{6,0},{7,1},{8,14},{9,15},{10,... | collective-permute-start | bytes 172040 | tf_op jit(solution)/shard_map/ppermute | solution.py:450
  74.5 1.9 %collective-permute-start.23 = (bf16[16,1792]{1,0:T(8,128)(2,1)S(1)}, bf16[16,1792]{1,0:T(8,128)(2,1)S(1)}, u32[]{:S(2)}, u32[]{:S(2)}) collective-permute-start(bf16[16,1792]{1,0:T(8,128)(2,1)S(1)} %get-tuple-element.75), channel_id=1, source_target_pairs={{0,7},{1,6},{2,5},{3,4},{4,3},{5,2},{6,1},{7,0},{8,15},{9,14},{10,... | collective-permute-start | bytes 172040 | tf_op jit(solution)/shard_map/ppermute | solution.py:450
  76.3 0.1 shard_map.165
  76.4 0.6 collective-permute-start.24
  77.0 0.5 collective-permute-done.21.refs_4_
  77.5 0.2 collective-permute-done.22.refs_5_
  77.6 3.7 %collective-permute-done.23.refs_6_ = bf16[16,1792]{1,0:T(8,128)(2,1)S(1)} collective-permute-done((bf16[16,1792]{1,0:T(8,128)(2,1)S(1)}, bf16[16,1792]{1,0:T(8,128)(2,1)S(1)}, u32[]{:S(2)}, u32[]{:S(2)}) %collective-permute-start.23) | collective-permute-done | bytes 57376 | tf_op jit(solution)/shard_map/ppermute | solution.py:450
  81.3 0.1 shard_map.166.mine
  81.4 2.2 %collective-permute-start.29 = (bf16[16,1792]{1,0:T(8,128)(2,1)S(1)}, bf16[16,1792]{1,0:T(8,128)(2,1)S(1)}, u32[]{:S(2)}, u32[]{:S(2)}) collective-permute-start(bf16[16,1792]{1,0:T(8,128)(2,1)S(1)} %shard_map.166.mine), channel_id=1, source_target_pairs={{0,7},{1,6},{2,5},{3,4},{4,3},{5,2},{6,1},{7,0},{8,15},{9,14},{10,... | collective-permute-start | bytes 172040 | tf_op jit(solution)/shard_map/ppermute | solution.py:450
  83.6 1.4 %collective-permute-start.28 = (bf16[16,1792]{1,0:T(8,128)(2,1)S(1)}, bf16[16,1792]{1,0:T(8,128)(2,1)S(1)}, u32[]{:S(2)}, u32[]{:S(2)}) collective-permute-start(bf16[16,1792]{1,0:T(8,128)(2,1)S(1)} %shard_map.166.mine), channel_id=1, source_target_pairs={{0,6},{1,7},{2,4},{3,5},{4,2},{5,3},{6,0},{7,1},{8,14},{9,15},{10,... | collective-permute-start | bytes 172040 | tf_op jit(solution)/shard_map/ppermute | solution.py:450
  85.0 0.5 collective-permute-start.27
  85.5 3.6 %collective-permute-start.26 = (bf16[16,1792]{1,0:T(8,128)(2,1)S(1)}, bf16[16,1792]{1,0:T(8,128)(2,1)S(1)}, u32[]{:S(2)}, u32[]{:S(2)}) collective-permute-start(bf16[16,1792]{1,0:T(8,128)(2,1)S(1)} %shard_map.166.mine), channel_id=1, source_target_pairs={{0,4},{1,5},{2,6},{3,7},{4,0},{5,1},{6,2},{7,3},{8,12},{9,13},{10,... | collective-permute-start | bytes 172040 | tf_op jit(solution)/shard_map/ppermute | solution.py:450
  89.1 0.5 collective-permute-start.25
  89.7 2.6 %collective-permute-done.27.refs_1_ = bf16[16,1792]{1,0:T(8,128)(2,1)S(1)} collective-permute-done((bf16[16,1792]{1,0:T(8,128)(2,1)S(1)}, bf16[16,1792]{1,0:T(8,128)(2,1)S(1)}, u32[]{:S(2)}, u32[]{:S(2)}) %collective-permute-start.27) | collective-permute-done | bytes 57376 | tf_op jit(solution)/shard_map/ppermute | solution.py:450
  92.3 0.6 collective-permute-done.26.refs_0_
  92.9 0.4 collective-permute-done.25.other
  93.3 0.9 collective-permute-start.32
  94.2 1.1 %collective-permute-start.31 = (bf16[32,1792]{1,0:T(8,128)(2,1)S(1)}, bf16[32,1792]{1,0:T(8,128)(2,1)S(1)}, u32[]{:S(2)}, u32[]{:S(2)}) collective-permute-start(bf16[32,1792]{1,0:T(8,128)(2,1)S(1)} %shard_map.168.refs_0_), channel_id=1, source_target_pairs={{0,2},{1,3},{2,0},{3,1},{4,6},{5,7},{6,4},{7,5},{8,10},{9,11},{10,... | collective-permute-start | bytes 344072 | tf_op jit(solution)/shard_map/ppermute | solution.py:450
  95.3 1.6 %collective-permute-start.30 = (bf16[32,1792]{1,0:T(8,128)(2,1)S(1)}, bf16[32,1792]{1,0:T(8,128)(2,1)S(1)}, u32[]{:S(2)}, u32[]{:S(2)}) collective-permute-start(bf16[32,1792]{1,0:T(8,128)(2,1)S(1)} %shard_map.168.refs_0_), channel_id=1, source_target_pairs={{0,1},{1,0},{2,3},{3,2},{4,5},{5,4},{6,7},{7,6},{8,9},{9,8},{10,11... | collective-permute-start | bytes 344072 | tf_op jit(solution)/shard_map/ppermute | solution.py:450
  96.9 0.5 collective-permute-start.33
  97.4 1.7 %collective-permute-done.32.refs_3_ = bf16[32,1792]{1,0:T(8,128)(2,1)S(1)} collective-permute-done((bf16[32,1792]{1,0:T(8,128)(2,1)S(1)}, bf16[32,1792]{1,0:T(8,128)(2,1)S(1)}, u32[]{:S(2)}, u32[]{:S(2)}) %collective-permute-start.32) | collective-permute-done | bytes 114720 | tf_op jit(solution)/shard_map/ppermute | solution.py:450
  99.1 0.7 collective-permute-done.31.refs_2_
  99.8 0.5 collective-permute-done.30.refs_1_
  100.4 0.1 collective-permute-start.34
  100.4 0.5 collective-permute-start.35
  100.9 2.0 %collective-permute-done.33.refs_2_ = bf16[64,1792]{1,0:T(8,128)(2,1)S(1)} collective-permute-done((bf16[64,1792]{1,0:T(8,128)(2,1)S(1)}, bf16[64,1792]{1,0:T(8,128)(2,1)S(1)}, u32[]{:S(2)}, u32[]{:S(2)}) %collective-permute-start.33) | collective-permute-done | bytes 229408 | tf_op jit(solution)/shard_map/ppermute | solution.py:450
  102.9 1.5 %collective-permute-done.36.refs_5_ = bf16[64,1792]{1,0:T(8,128)(2,1)S(1)} collective-permute-done((bf16[64,1792]{1,0:T(8,128)(2,1)S(1)}, bf16[64,1792]{1,0:T(8,128)(2,1)S(1)}, u32[]{:S(2)}, u32[]{:S(2)}) %collective-permute-start.36) | collective-permute-done | bytes 229408 | tf_op jit(solution)/shard_map/ppermute | solution.py:450
  104.4 2.0 %shard_map.170 = (f32[512,512]{1,0:T(8,128)}, f32[512,512]{1,0:T(8,128)}, f32[512,512]{1,0:T(8,128)}, f32[512,128]{1,0:T(8,128)}, f32[1,1]{1,0:T(1,128)}) custom-call(bf16[128,1792]{1,0:T(8,128)(2,1)S(1)} %shard_map.169.refs_0_, bf16[64,1792]{1,0:T(8,128)(2,1)S(1)} %shard_map.167.after.refs_1_, bf16[64,1792]{1,0:T(8,128)(2,1)S(1)} %collective-permute-done.33.refs_2_, ...), custom_call_target="tpu_custom_call" | custom-call | bytes 5505024 | tf_op jit(solution)/shard_map/pallas_call | solution.py:628
  (54 shorter events, 0.2 us)
Async XLA Ops:
  0.6 14.1 %copy-start.8 = (s32[128]{0:T(128)S(1)}, s32[128]{0:T(128)}, u32[]{:S(2)}) copy-start(s32[128]{0:T(128)} %param.15) | copy-start | bytes 1540
  0.6 14.1 %copy-start.7 = (s32[128]{0:T(128)S(1)}, s32[128]{0:T(128)}, u32[]{:S(2)}) copy-start(s32[128]{0:T(128)} %param.14) | copy-start | bytes 1540
  0.7 14.1 %copy-start.6 = (bf16[512,128]{1,0:T(8,128)(2,1)S(1)}, bf16[512,128]{1,0:T(8,128)(2,1)}, u32[]{:S(2)}) copy-start(bf16[512,128]{1,0:T(8,128)(2,1)} %w_decode.1) | copy-start | bytes 393220
  0.7 14.1 %copy-start.12 = (s32[6,512]{1,0:T(8,128)S(1)}, s32[6,512]{1,0:T(8,128)}, u32[]{:S(2)}) copy-start(s32[6,512]{1,0:T(8,128)} %senders_in.1) | copy-start | bytes 36868
  3.0 11.8 %collective-permute-start = (bf16[512,128]{1,0:T(8,128)(2,1)}, bf16[512,128]{1,0:T(8,128)(2,1)S(1)}, u32[]{:S(2)}, u32[]{:S(2)}) collective-permute-start(bf16[512,128]{1,0:T(8,128)(2,1)} %get-tuple-element.44), channel_id=1, source_target_pairs={{0,1},{1,0},{2,3},{3,2},{4,5},{5,4},{6,7},{7,6},{8,9},{9,8},{10,11... | collective-permute-start | bytes 393224 | tf_op jit(solution)/shard_map/ppermute | solution.py:450
  6.0 8.8 %collective-permute-start.1 = (bf16[512,128]{1,0:T(8,128)(2,1)}, bf16[512,128]{1,0:T(8,128)(2,1)S(1)}, u32[]{:S(2)}, u32[]{:S(2)}) collective-permute-start(bf16[512,128]{1,0:T(8,128)(2,1)} %get-tuple-element.45), channel_id=1, source_target_pairs={{0,7},{1,2},{2,1},{3,4},{4,3},{5,6},{6,5},{7,0},{8,15},{9,10},{10,... | collective-permute-start | bytes 393224 | tf_op jit(solution)/shard_map/ppermute | solution.py:444
  14.8 0.7 copy-start.13
  15.5 24.3 %copy-start.9 = (bf16[1536,2048]{1,0:T(8,128)(2,1)S(1)}, bf16[1536,2048]{1,0:T(8,128)(2,1)}, u32[]{:S(2)}) copy-start(bf16[1536,2048]{1,0:T(8,128)(2,1)} %get-tuple-element.50.refs_8_) | copy-start | bytes 18874372
  15.5 24.3 %copy-start.10 = (bf16[128,2048]{1,0:T(8,128)(2,1)S(1)}, bf16[128,2048]{1,0:T(8,128)(2,1)}, u32[]{:S(2)}) copy-start(bf16[128,2048]{1,0:T(8,128)(2,1)} %get-tuple-element.51.refs_9_) | copy-start | bytes 1572868
  15.5 24.3 %copy-start.11 = (bf16[128,2048]{1,0:T(8,128)(2,1)S(1)}, bf16[128,2048]{1,0:T(8,128)(2,1)}, u32[]{:S(2)}) copy-start(bf16[128,2048]{1,0:T(8,128)(2,1)} %get-tuple-element.52.refs_10_) | copy-start | bytes 1572868
  26.0 8.8 %collective-permute-start.3 = (bf16[128,512]{1,0:T(8,128)(2,1)S(1)}, bf16[128,512]{1,0:T(8,128)(2,1)S(1)}, u32[]{:S(2)}, u32[]{:S(2)}) collective-permute-start(bf16[128,512]{1,0:T(8,128)(2,1)S(1)} %get-tuple-element.47.refs_0_), channel_id=1, source_target_pairs={{0,16},{8,24},{16,0},{24,8},{1,17},{9,25},{17,1},{25,9},{2,18},{10... | collective-permute-start | bytes 393224 | tf_op jit(solution)/shard_map/ppermute | solution.py:450
  27.6 3.9 %collective-permute-start.5 = (bf16[128,128]{1,0:T(8,128)(2,1)S(1)}, bf16[128,128]{1,0:T(8,128)(2,1)S(1)}, u32[]{:S(2)}, u32[]{:S(2)}) collective-permute-start(bf16[128,128]{1,0:T(8,128)(2,1)S(1)} %get-tuple-element.48), channel_id=1, source_target_pairs={{0,1},{1,0},{2,3},{3,2},{4,5},{5,4},{6,7},{7,6},{8,9},{9,8},{10,11... | collective-permute-start | bytes 98312 | tf_op jit(solution)/shard_map/ppermute | solution.py:450
  27.6 6.6 %collective-permute-start.6 = (bf16[128,128]{1,0:T(8,128)(2,1)S(1)}, bf16[128,128]{1,0:T(8,128)(2,1)S(1)}, u32[]{:S(2)}, u32[]{:S(2)}) collective-permute-start(bf16[128,128]{1,0:T(8,128)(2,1)S(1)} %get-tuple-element.49), channel_id=1, source_target_pairs={{0,7},{1,2},{2,1},{3,4},{4,3},{5,6},{6,5},{7,0},{8,15},{9,10},{10,... | collective-permute-start | bytes 98312 | tf_op jit(solution)/shard_map/ppermute | solution.py:444
  30.6 8.0 %collective-permute-start.2 = (bf16[128,512]{1,0:T(8,128)(2,1)S(1)}, bf16[128,512]{1,0:T(8,128)(2,1)S(1)}, u32[]{:S(2)}, u32[]{:S(2)}) collective-permute-start(bf16[128,512]{1,0:T(8,128)(2,1)S(1)} %get-tuple-element.47.refs_0_), channel_id=1, source_target_pairs={{0,8},{8,0},{16,24},{24,16},{1,9},{9,1},{17,25},{25,17},{2,10},{10... | collective-permute-start | bytes 393224 | tf_op jit(solution)/shard_map/ppermute | solution.py:450
  34.2 4.3 %collective-permute-start.8 = (bf16[128,256]{1,0:T(8,128)(2,1)S(1)}, bf16[128,256]{1,0:T(8,128)(2,1)S(1)}, u32[]{:S(2)}, u32[]{:S(2)}) collective-permute-start(bf16[128,256]{1,0:T(8,128)(2,1)S(1)} %shard_map.158.refs_4_), channel_id=1, source_target_pairs={{0,16},{8,24},{16,0},{24,8},{1,17},{9,25},{17,1},{25,9},{2,18},{10... | collective-permute-start | bytes 196616 | tf_op jit(solution)/shard_map/ppermute | solution.py:450
  34.8 5.0 %collective-permute-start.4 = (bf16[128,512]{1,0:T(8,128)(2,1)S(1)}, bf16[128,512]{1,0:T(8,128)(2,1)S(1)}, u32[]{:S(2)}, u32[]{:S(2)}) collective-permute-start(bf16[128,512]{1,0:T(8,128)(2,1)S(1)} %collective-permute-done.3.refs_2_), channel_id=1, source_target_pairs={{0,8},{8,0},{16,24},{24,16},{1,9},{9,1},{17,25},{25,17},{2,10},{10... | collective-permute-start | bytes 393224 | tf_op jit(solution)/shard_map/ppermute | solution.py:450
  34.8 3.7 %collective-permute-start.7 = (bf16[128,256]{1,0:T(8,128)(2,1)S(1)}, bf16[128,256]{1,0:T(8,128)(2,1)S(1)}, u32[]{:S(2)}, u32[]{:S(2)}) collective-permute-start(bf16[128,256]{1,0:T(8,128)(2,1)S(1)} %shard_map.158.refs_4_), channel_id=1, source_target_pairs={{0,8},{8,0},{16,24},{24,16},{1,9},{9,1},{17,25},{25,17},{2,10},{10... | collective-permute-start | bytes 196616 | tf_op jit(solution)/shard_map/ppermute | solution.py:450
  38.6 1.3 %collective-permute-start.9 = (bf16[128,256]{1,0:T(8,128)(2,1)S(1)}, bf16[128,256]{1,0:T(8,128)(2,1)S(1)}, u32[]{:S(2)}, u32[]{:S(2)}) collective-permute-start(bf16[128,256]{1,0:T(8,128)(2,1)S(1)} %collective-permute-done.8.refs_6_), channel_id=1, source_target_pairs={{0,8},{8,0},{16,24},{24,16},{1,9},{9,1},{17,25},{25,17},{2,10},{10... | collective-permute-start | bytes 196616 | tf_op jit(solution)/shard_map/ppermute | solution.py:450
  39.8 14.8 %copy-start = (bf16[512,3072]{1,0:T(8,128)(2,1)S(1)}, bf16[512,3072]{1,0:T(8,128)(2,1)}, u32[]{:S(2)}) copy-start(bf16[512,3072]{1,0:T(8,128)(2,1)} %get-tuple-element.60.picked_t) | copy-start | bytes 9437188
  39.9 14.7 %copy-start.1 = (bf16[512,3072]{1,0:T(8,128)(2,1)S(1)}, bf16[512,3072]{1,0:T(8,128)(2,1)}, u32[]{:S(2)}) copy-start(bf16[512,3072]{1,0:T(8,128)(2,1)} %get-tuple-element.61.slope_t) | copy-start | bytes 9437188
  39.9 14.7 %copy-start.2 = (bf16[512,512]{1,0:T(8,128)(2,1)S(1)}, bf16[512,512]{1,0:T(8,128)(2,1)}, u32[]{:S(2)}) copy-start(bf16[512,512]{1,0:T(8,128)(2,1)} %get-tuple-element.43.after.nodes_in.nodes_t) | copy-start | bytes 1572868
  39.9 14.7 %copy-start.3 = (f32[512,512]{1,0:T(8,128)S(1)}, f32[512,512]{1,0:T(8,128)}, u32[]{:S(2)}) copy-start(f32[512,512]{1,0:T(8,128)} %get-tuple-element.62.slope_sum_t) | copy-start | bytes 3145732
  39.9 14.7 %copy-start.4 = (f32[512,512]{1,0:T(8,128)S(1)}, f32[512,512]{1,0:T(8,128)}, u32[]{:S(2)}) copy-start(f32[512,512]{1,0:T(8,128)} %get-tuple-element.64.upd_slope_t) | copy-start | bytes 3145732
  39.9 14.7 %copy-start.5 = (bf16[512,512]{1,0:T(8,128)(2,1)S(1)}, bf16[512,512]{1,0:T(8,128)(2,1)}, u32[]{:S(2)}) copy-start(bf16[512,512]{1,0:T(8,128)(2,1)} %vertex.1) | copy-start | bytes 1572868
  45.9 8.7 %collective-permute-start.10 = (f32[128,512]{1,0:T(8,128)S(1)}, f32[128,512]{1,0:T(8,128)S(1)}, u32[]{:S(2)}, u32[]{:S(2)}) collective-permute-start(f32[128,512]{1,0:T(8,128)S(1)} %get-tuple-element.54), channel_id=1, source_target_pairs={{0,8},{8,0},{16,24},{24,16},{1,9},{9,1},{17,25},{25,17},{2,10},{10... | collective-permute-start | bytes 786440 | tf_op jit(solution)/shard_map/ppermute | solution.py:450
  46.1 1.6 %collective-permute-start.11 = (f32[128,256]{1,0:T(8,128)S(1)}, f32[128,256]{1,0:T(8,128)S(1)}, u32[]{:S(2)}, u32[]{:S(2)}) collective-permute-start(f32[128,256]{1,0:T(8,128)S(1)} %get-tuple-element.56), channel_id=1, source_target_pairs={{0,8},{8,0},{16,24},{24,16},{1,9},{9,1},{17,25},{25,17},{2,10},{10... | collective-permute-start | bytes 393224 | tf_op jit(solution)/shard_map/ppermute | solution.py:450
  47.7 4.0 %collective-permute-start.12 = (bf16[128,128]{1,0:T(8,128)(2,1)S(1)}, bf16[128,128]{1,0:T(8,128)(2,1)S(1)}, u32[]{:S(2)}, u32[]{:S(2)}) collective-permute-start(bf16[128,128]{1,0:T(8,128)(2,1)S(1)} %get-tuple-element.57), channel_id=1, source_target_pairs={{0,1},{1,0},{2,3},{3,2},{4,5},{5,4},{6,7},{7,6},{8,9},{9,8},{10,11... | collective-permute-start | bytes 98312 | tf_op jit(solution)/shard_map/ppermute | solution.py:450
  48.0 6.6 %collective-permute-start.13 = (bf16[128,128]{1,0:T(8,128)(2,1)S(1)}, bf16[128,128]{1,0:T(8,128)(2,1)S(1)}, u32[]{:S(2)}, u32[]{:S(2)}) collective-permute-start(bf16[128,128]{1,0:T(8,128)(2,1)S(1)} %get-tuple-element.58), channel_id=1, source_target_pairs={{0,7},{1,2},{2,1},{3,4},{4,3},{5,6},{6,5},{7,0},{8,15},{9,10},{10,... | collective-permute-start | bytes 98312 | tf_op jit(solution)/shard_map/ppermute | solution.py:444
  58.1 3.3 %collective-permute-start.14 = (bf16[192,1792]{1,0:T(8,128)(2,1)S(1)}, bf16[192,1792]{1,0:T(8,128)(2,1)S(1)}, u32[]{:S(2)}, u32[]{:S(2)}) collective-permute-start(bf16[192,1792]{1,0:T(8,128)(2,1)S(1)} %get-tuple-element.67), channel_id=1, source_target_pairs={{0,8},{8,0},{16,24},{24,16},{1,9},{9,1},{17,25},{25,17},{2,10},{10... | collective-permute-start | bytes 2064392 | tf_op jit(solution)/shard_map/ppermute | solution.py:450
  58.2 2.5 %collective-permute-start.18 = (bf16[64,1792]{1,0:T(8,128)(2,1)S(1)}, bf16[64,1792]{1,0:T(8,128)(2,1)S(1)}, u32[]{:S(2)}, u32[]{:S(2)}) collective-permute-start(bf16[64,1792]{1,0:T(8,128)(2,1)S(1)} %get-tuple-element.71), channel_id=1, source_target_pairs={{0,8},{8,0},{16,24},{24,16},{1,9},{9,1},{17,25},{25,17},{2,10},{10... | collective-permute-start | bytes 688136 | tf_op jit(solution)/shard_map/ppermute | solution.py:450
  60.8 7.7 %collective-permute-start.19 = (bf16[64,1792]{1,0:T(8,128)(2,1)S(1)}, bf16[64,1792]{1,0:T(8,128)(2,1)S(1)}, u32[]{:S(2)}, u32[]{:S(2)}) collective-permute-start(bf16[64,1792]{1,0:T(8,128)(2,1)S(1)} %shard_map.163), channel_id=1, source_target_pairs={{0,16},{8,24},{16,0},{24,8},{1,17},{9,25},{17,1},{25,9},{2,18},{10... | collective-permute-start | bytes 688136 | tf_op jit(solution)/shard_map/ppermute | solution.py:450
  61.5 9.5 %collective-permute-start.15 = (bf16[32,1792]{1,0:T(8,128)(2,1)S(1)}, bf16[32,1792]{1,0:T(8,128)(2,1)S(1)}, u32[]{:S(2)}, u32[]{:S(2)}) collective-permute-start(bf16[32,1792]{1,0:T(8,128)(2,1)S(1)} %get-tuple-element.68), channel_id=1, source_target_pairs={{0,1},{1,0},{2,3},{3,2},{4,5},{5,4},{6,7},{7,6},{8,9},{9,8},{10,11... | collective-permute-start | bytes 344072 | tf_op jit(solution)/shard_map/ppermute | solution.py:450
  61.6 12.9 %collective-permute-start.16 = (bf16[32,1792]{1,0:T(8,128)(2,1)S(1)}, bf16[32,1792]{1,0:T(8,128)(2,1)S(1)}, u32[]{:S(2)}, u32[]{:S(2)}) collective-permute-start(bf16[32,1792]{1,0:T(8,128)(2,1)S(1)} %get-tuple-element.69), channel_id=1, source_target_pairs={{0,2},{1,3},{2,0},{3,1},{4,6},{5,7},{6,4},{7,5},{8,10},{9,11},{10,... | collective-permute-start | bytes 344072 | tf_op jit(solution)/shard_map/ppermute | solution.py:450
  61.6 14.7 %collective-permute-start.17 = (bf16[32,1792]{1,0:T(8,128)(2,1)S(1)}, bf16[32,1792]{1,0:T(8,128)(2,1)S(1)}, u32[]{:S(2)}, u32[]{:S(2)}) collective-permute-start(bf16[32,1792]{1,0:T(8,128)(2,1)S(1)} %get-tuple-element.70), channel_id=1, source_target_pairs={{0,3},{1,2},{2,1},{3,0},{4,7},{5,6},{6,5},{7,4},{8,11},{9,10},{10,... | collective-permute-start | bytes 344072 | tf_op jit(solution)/shard_map/ppermute | solution.py:450
  68.6 8.4 %collective-permute-start.20 = (bf16[16,1792]{1,0:T(8,128)(2,1)S(1)}, bf16[16,1792]{1,0:T(8,128)(2,1)S(1)}, u32[]{:S(2)}, u32[]{:S(2)}) collective-permute-start(bf16[16,1792]{1,0:T(8,128)(2,1)S(1)} %get-tuple-element.72), channel_id=1, source_target_pairs={{0,4},{1,5},{2,6},{3,7},{4,0},{5,1},{6,2},{7,3},{8,12},{9,13},{10,... | collective-permute-start | bytes 172040 | tf_op jit(solution)/shard_map/ppermute | solution.py:450
  68.7 8.8 %collective-permute-start.21 = (bf16[16,1792]{1,0:T(8,128)(2,1)S(1)}, bf16[16,1792]{1,0:T(8,128)(2,1)S(1)}, u32[]{:S(2)}, u32[]{:S(2)}) collective-permute-start(bf16[16,1792]{1,0:T(8,128)(2,1)S(1)} %get-tuple-element.73), channel_id=1, source_target_pairs={{0,5},{1,4},{2,7},{3,6},{4,1},{5,0},{6,3},{7,2},{8,13},{9,12},{10,... | collective-permute-start | bytes 172040 | tf_op jit(solution)/shard_map/ppermute | solution.py:450
  71.0 6.6 %collective-permute-start.22 = (bf16[16,1792]{1,0:T(8,128)(2,1)S(1)}, bf16[16,1792]{1,0:T(8,128)(2,1)S(1)}, u32[]{:S(2)}, u32[]{:S(2)}) collective-permute-start(bf16[16,1792]{1,0:T(8,128)(2,1)S(1)} %get-tuple-element.74), channel_id=1, source_target_pairs={{0,6},{1,7},{2,4},{3,5},{4,2},{5,3},{6,0},{7,1},{8,14},{9,15},{10,... | collective-permute-start | bytes 172040 | tf_op jit(solution)/shard_map/ppermute | solution.py:450
  74.5 6.9 %collective-permute-start.23 = (bf16[16,1792]{1,0:T(8,128)(2,1)S(1)}, bf16[16,1792]{1,0:T(8,128)(2,1)S(1)}, u32[]{:S(2)}, u32[]{:S(2)}) collective-permute-start(bf16[16,1792]{1,0:T(8,128)(2,1)S(1)} %get-tuple-element.75), channel_id=1, source_target_pairs={{0,7},{1,6},{2,5},{3,4},{4,3},{5,2},{6,1},{7,0},{8,15},{9,14},{10,... | collective-permute-start | bytes 172040 | tf_op jit(solution)/shard_map/ppermute | solution.py:450
  76.4 4.9 %collective-permute-start.24 = (bf16[16,1792]{1,0:T(8,128)(2,1)S(1)}, bf16[16,1792]{1,0:T(8,128)(2,1)S(1)}, u32[]{:S(2)}, u32[]{:S(2)}) collective-permute-start(bf16[16,1792]{1,0:T(8,128)(2,1)S(1)} %shard_map.165), channel_id=1, source_target_pairs={{0,16},{8,24},{16,0},{24,8},{1,17},{9,25},{17,1},{25,9},{2,18},{10... | collective-permute-start | bytes 172040 | tf_op jit(solution)/shard_map/ppermute | solution.py:450
  81.4 8.3 %collective-permute-start.29 = (bf16[16,1792]{1,0:T(8,128)(2,1)S(1)}, bf16[16,1792]{1,0:T(8,128)(2,1)S(1)}, u32[]{:S(2)}, u32[]{:S(2)}) collective-permute-start(bf16[16,1792]{1,0:T(8,128)(2,1)S(1)} %shard_map.166.mine), channel_id=1, source_target_pairs={{0,7},{1,6},{2,5},{3,4},{4,3},{5,2},{6,1},{7,0},{8,15},{9,14},{10,... | collective-permute-start | bytes 172040 | tf_op jit(solution)/shard_map/ppermute | solution.py:450
  83.6 6.1 %collective-permute-start.28 = (bf16[16,1792]{1,0:T(8,128)(2,1)S(1)}, bf16[16,1792]{1,0:T(8,128)(2,1)S(1)}, u32[]{:S(2)}, u32[]{:S(2)}) collective-permute-start(bf16[16,1792]{1,0:T(8,128)(2,1)S(1)} %shard_map.166.mine), channel_id=1, source_target_pairs={{0,6},{1,7},{2,4},{3,5},{4,2},{5,3},{6,0},{7,1},{8,14},{9,15},{10,... | collective-permute-start | bytes 172040 | tf_op jit(solution)/shard_map/ppermute | solution.py:450
  85.0 7.3 %collective-permute-start.27 = (bf16[16,1792]{1,0:T(8,128)(2,1)S(1)}, bf16[16,1792]{1,0:T(8,128)(2,1)S(1)}, u32[]{:S(2)}, u32[]{:S(2)}) collective-permute-start(bf16[16,1792]{1,0:T(8,128)(2,1)S(1)} %shard_map.166.mine), channel_id=1, source_target_pairs={{0,5},{1,4},{2,7},{3,6},{4,1},{5,0},{6,3},{7,2},{8,13},{9,12},{10,... | collective-permute-start | bytes 172040 | tf_op jit(solution)/shard_map/ppermute | solution.py:450
  85.5 7.3 %collective-permute-start.26 = (bf16[16,1792]{1,0:T(8,128)(2,1)S(1)}, bf16[16,1792]{1,0:T(8,128)(2,1)S(1)}, u32[]{:S(2)}, u32[]{:S(2)}) collective-permute-start(bf16[16,1792]{1,0:T(8,128)(2,1)S(1)} %shard_map.166.mine), channel_id=1, source_target_pairs={{0,4},{1,5},{2,6},{3,7},{4,0},{5,1},{6,2},{7,3},{8,12},{9,13},{10,... | collective-permute-start | bytes 172040 | tf_op jit(solution)/shard_map/ppermute | solution.py:450
  89.1 4.2 %collective-permute-start.25 = (bf16[16,1792]{1,0:T(8,128)(2,1)S(1)}, bf16[16,1792]{1,0:T(8,128)(2,1)S(1)}, u32[]{:S(2)}, u32[]{:S(2)}) collective-permute-start(bf16[16,1792]{1,0:T(8,128)(2,1)S(1)} %shard_map.166.mine), channel_id=1, source_target_pairs={{0,16},{8,24},{16,0},{24,8},{1,17},{9,25},{17,1},{25,9},{2,18},{10... | collective-permute-start | bytes 172040 | tf_op jit(solution)/shard_map/ppermute | solution.py:450
  93.3 5.8 %collective-permute-start.32 = (bf16[32,1792]{1,0:T(8,128)(2,1)S(1)}, bf16[32,1792]{1,0:T(8,128)(2,1)S(1)}, u32[]{:S(2)}, u32[]{:S(2)}) collective-permute-start(bf16[32,1792]{1,0:T(8,128)(2,1)S(1)} %shard_map.168.refs_0_), channel_id=1, source_target_pairs={{0,3},{1,2},{2,1},{3,0},{4,7},{5,6},{6,5},{7,4},{8,11},{9,10},{10,... | collective-permute-start | bytes 344072 | tf_op jit(solution)/shard_map/ppermute | solution.py:450
  94.2 5.6 %collective-permute-start.31 = (bf16[32,1792]{1,0:T(8,128)(2,1)S(1)}, bf16[32,1792]{1,0:T(8,128)(2,1)S(1)}, u32[]{:S(2)}, u32[]{:S(2)}) collective-permute-start(bf16[32,1792]{1,0:T(8,128)(2,1)S(1)} %shard_map.168.refs_0_), channel_id=1, source_target_pairs={{0,2},{1,3},{2,0},{3,1},{4,6},{5,7},{6,4},{7,5},{8,10},{9,11},{10,... | collective-permute-start | bytes 344072 | tf_op jit(solution)/shard_map/ppermute | solution.py:450
  95.3 5.0 %collective-permute-start.30 = (bf16[32,1792]{1,0:T(8,128)(2,1)S(1)}, bf16[32,1792]{1,0:T(8,128)(2,1)S(1)}, u32[]{:S(2)}, u32[]{:S(2)}) collective-permute-start(bf16[32,1792]{1,0:T(8,128)(2,1)S(1)} %shard_map.168.refs_0_), channel_id=1, source_target_pairs={{0,1},{1,0},{2,3},{3,2},{4,5},{5,4},{6,7},{7,6},{8,9},{9,8},{10,11... | collective-permute-start | bytes 344072 | tf_op jit(solution)/shard_map/ppermute | solution.py:450
  96.9 6.0 %collective-permute-start.33 = (bf16[64,1792]{1,0:T(8,128)(2,1)S(1)}, bf16[64,1792]{1,0:T(8,128)(2,1)S(1)}, u32[]{:S(2)}, u32[]{:S(2)}) collective-permute-start(bf16[64,1792]{1,0:T(8,128)(2,1)S(1)} %shard_map.167.after.refs_1_), channel_id=1, source_target_pairs={{0,16},{8,24},{16,0},{24,8},{1,17},{9,25},{17,1},{25,9},{2,18},{10... | collective-permute-start | bytes 688136 | tf_op jit(solution)/shard_map/ppermute | solution.py:450
  100.4 4.0 %collective-permute-start.34 = (bf16[128,1792]{1,0:T(8,128)(2,1)S(1)}, bf16[128,1792]{1,0:T(8,128)(2,1)S(1)}, u32[]{:S(2)}, u32[]{:S(2)}) collective-permute-start(bf16[128,1792]{1,0:T(8,128)(2,1)S(1)} %shard_map.169.refs_0_), channel_id=1, source_target_pairs={{0,8},{8,0},{16,24},{24,16},{1,9},{9,1},{17,25},{25,17},{2,10},{10... | collective-permute-start | bytes 1376264 | tf_op jit(solution)/shard_map/ppermute | solution.py:450
  100.4 2.5 %collective-permute-start.35 = (bf16[64,1792]{1,0:T(8,128)(2,1)S(1)}, bf16[64,1792]{1,0:T(8,128)(2,1)S(1)}, u32[]{:S(2)}, u32[]{:S(2)}) collective-permute-start(bf16[64,1792]{1,0:T(8,128)(2,1)S(1)} %shard_map.167.after.refs_1_), channel_id=1, source_target_pairs={{0,8},{8,0},{16,24},{24,16},{1,9},{9,1},{17,25},{25,17},{2,10},{10... | collective-permute-start | bytes 688136 | tf_op jit(solution)/shard_map/ppermute | solution.py:450
  102.9 1.5 %collective-permute-start.36 = (bf16[64,1792]{1,0:T(8,128)(2,1)S(1)}, bf16[64,1792]{1,0:T(8,128)(2,1)S(1)}, u32[]{:S(2)}, u32[]{:S(2)}) collective-permute-start(bf16[64,1792]{1,0:T(8,128)(2,1)S(1)} %collective-permute-done.33.refs_2_), channel_id=1, source_target_pairs={{0,8},{8,0},{16,24},{24,16},{1,9},{9,1},{17,25},{25,17},{2,10},{10... | collective-permute-start | bytes 688136 | tf_op jit(solution)/shard_map/ppermute | solution.py:450
